TPU v7x, 32 devices: a whole 2x2x4 slice. The times are simulated.
32 devices in a mesh: dp: 8 (over y, x, core), seq: 4 (over z).
Axes of the slice: x: 2, y: 2, z: 4, core: 2. Of those that a mesh axis runs over, the one named last changes fastest.
Arguments:
- patches: bfloat16 [96, 196, 768], P('dp', 'seq'), may hold values from -6 to 6
- specials: bfloat16 [96, 2, 768], P('dp'), may hold values from -6 to 6
- keep_mask: int32 [96, 2], P('dp'), may hold values 0 or 1
- ln1_gain: bfloat16 [768], replicated, may hold values from 0.5 to 1.5
- ln1_bias: bfloat16 [768], replicated, may hold values from -1 to 1
- qkv_weight: bfloat16 [768, 2304], replicated, may hold values from -0.21875 to 0.21875
- qv_bias: bfloat16 [2, 768], replicated, may hold values from -1 to 1
- proj_weight: bfloat16 [768, 768], replicated, may hold values from -1.75 to 1.75
- proj_bias: bfloat16 [768], replicated, may hold values from -1 to 1
- ln2_gain: bfloat16 [768], replicated, may hold values from 0.5 to 1.5
- ln2_bias: bfloat16 [768], replicated, may hold values from -1 to 1
- fc1_weight: bfloat16 [768, 3072], replicated, may hold values from -0.21875 to 0.21875
- fc1_bias: bfloat16 [3072], replicated, may hold values from -1 to 1
- fc2_weight: bfloat16 [3072, 768], replicated, may hold values from -0.109375 to 0.109375
- fc2_bias: bfloat16 [768], replicated, may hold values from -1 to 1
- grad_patches: bfloat16 [96, 196, 768], P('dp', 'seq'), may hold values from -6 to 6
- grad_specials: bfloat16 [96, 2, 768], P('dp'), may hold values from -6 to 6
Outputs:
- out_patches: bfloat16 [96, 196, 768], P('dp', 'seq')
- out_specials: bfloat16 [96, 2, 768], P('dp')
- dx_patches: bfloat16 [96, 196, 768], P('dp', 'seq')
- dx_specials: bfloat16 [96, 2, 768], P('dp')
- d_ln1_gain: float32 [768], P('dp')
- d_ln1_bias: float32 [768], P('dp')
- d_qkv_weight: float32 [768, 2304], P('dp')
- d_qv_bias: float32 [2, 768], P(None, 'dp')
- d_proj_weight: float32 [768, 768], P('dp')
- d_proj_bias: float32 [768], P('dp')
- d_ln2_gain: float32 [768], P('dp')
- d_ln2_bias: float32 [768], P('dp')
- d_fc1_weight: float32 [768, 3072], P('dp')
- d_fc1_bias: float32 [3072], P('dp')
- d_fc2_weight: float32 [3072, 768], P('dp')
- d_fc2_bias: float32 [768], P('dp')
All inputs are finite; a program needn't handle non-finite values. No bound on the sum of `keep_mask` on one device may be relied on, other than what follows from the above.
Results may differ from a plain program's by a relative error of at most 0.014.
Values may be sent and summed in bfloat16 or wider, within the bound.
No kernel may reach another device: no remote copies, remote signals or barrier semaphores. Data moves between devices by JAX's collectives and lax.ppermute only.
A program may use at most 192 MiB of HBM per device.

v0:
```python
from functools import partial

import jax
import jax.numpy as jnp
from jax import lax
from jax.sharding import PartitionSpec as P

HEAD_DIM = 64


keep_rate = 0.9
epsilon = 1e-06


def norm_forward(row_block, norm_gain, norm_shift):
    center = row_block - jnp.mean(row_block, axis=-1, keepdims=True)
    scale_inv = lax.rsqrt(jnp.mean(center * center, axis=-1, keepdims=True) + epsilon)
    normed = center * scale_inv
    return (normed * norm_gain + norm_shift, normed, scale_inv)


def norm_backward(upstream, normed, scale_inv, norm_gain, row_weight):
    scaled = upstream * norm_gain
    result = scale_inv * (
        scaled
        - jnp.mean(scaled, axis=-1, keepdims=True)
        - normed * jnp.mean(scaled * normed, axis=-1, keepdims=True)
    )
    grad_gain = jnp.sum(upstream * normed * row_weight, axis=(0, 1))
    grad_shift = jnp.sum(upstream * row_weight, axis=(0, 1))
    return (result, grad_gain, grad_shift)


def project(row_block, weight):
    return jnp.einsum("brd,de->bre", row_block, weight, preferred_element_type=jnp.float32)


def project_back(upstream, weight):
    return jnp.einsum("bre,de->brd", upstream, weight, preferred_element_type=jnp.float32)


def weight_grad(row_block, upstream):
    return jnp.einsum("brd,bre->de", row_block, upstream, preferred_element_type=jnp.float32)


def shards(
    patches,
    specials,
    keep_mask,
    ln1_gain,
    ln1_bias,
    qkv_weight,
    qv_bias,
    proj_weight,
    proj_bias,
    ln2_gain,
    ln2_bias,
    fc1_weight,
    fc1_bias,
    fc2_weight,
    fc2_bias,
    grad_patches,
    grad_specials,
):
    images, local_rows, feature_width = patches.shape
    groups = lax.axis_size("seq")
    own_index = lax.axis_index("seq")
    all_rows = local_rows + 2
    head_size = HEAD_DIM
    group_width = feature_width // groups
    heads_here = group_width // head_size
    seq_len = local_rows * groups + 2
    score_scale = head_size ** (-0.5)
    row_weight = jnp.concatenate(
        [jnp.full((2,), 0.25, jnp.float32), jnp.ones((local_rows,), jnp.float32)]
    )[None, :, None]
    row_weight_low = row_weight.astype(jnp.bfloat16)
    gain_one = ln1_gain.astype(jnp.float32)
    gain_two = ln2_gain.astype(jnp.float32)
    attn_keep = (keep_mask[:, 0].astype(jnp.float32) / keep_rate)[:, None, None]
    mlp_keep = (keep_mask[:, 1].astype(jnp.float32) / keep_rate)[:, None, None]
    inputs = jnp.concatenate([specials, patches], axis=1).astype(jnp.float32)
    normed_one, hat_one, inv_one = norm_forward(inputs, gain_one, ln1_bias.astype(jnp.float32))
    normed_one_low = normed_one.astype(jnp.bfloat16)
    qkv_shift = jnp.concatenate(
        [
            qv_bias[0].astype(jnp.float32),
            jnp.zeros((feature_width,), jnp.float32),
            qv_bias[1].astype(jnp.float32),
        ]
    )
    qkv_rows = (project(normed_one_low, qkv_weight) + qkv_shift).astype(jnp.bfloat16)
    qkv_rows = qkv_rows.reshape(images, all_rows, 3, groups, group_width)
    arrived = lax.all_to_all(qkv_rows[:, 2:], "seq", split_axis=3, concat_axis=1, tiled=True)
    special_part = lax.dynamic_slice_in_dim(qkv_rows[:, :2], own_index, 1, 3)
    heads_in = jnp.concatenate([special_part, arrived], axis=1)
    heads_in = heads_in.reshape(images, seq_len, 3, heads_here, head_size)
    queries = heads_in[:, :, 0]
    key_rows = heads_in[:, :, 1]
    value_rows = heads_in[:, :, 2]
    scores = (
        jnp.einsum("blhd,bmhd->bhlm", queries, key_rows, preferred_element_type=jnp.float32)
        * score_scale
    )
    exponent = jnp.exp(scores - jnp.max(scores, axis=-1, keepdims=True))
    attention = exponent / jnp.sum(exponent, axis=-1, keepdims=True)
    attention_low = attention.astype(jnp.bfloat16)
    attended = jnp.einsum(
        "bhlm,bmhd->blhd", attention_low, value_rows, preferred_element_type=jnp.float32
    )
    attended = attended.astype(jnp.bfloat16).reshape(images, seq_len, 1, group_width)
    back_rows = lax.all_to_all(attended[:, 2:], "seq", split_axis=1, concat_axis=2, tiled=True)
    special_out = lax.all_gather(attended[:, :2], "seq", axis=2, tiled=True)
    context = jnp.concatenate([special_out, back_rows], axis=1).reshape(
        images, all_rows, feature_width
    )
    branch = project(context, proj_weight) + proj_bias.astype(jnp.float32)
    middle = inputs + attn_keep * branch
    normed_two, hat_two, inv_two = norm_forward(middle, gain_two, ln2_bias.astype(jnp.float32))
    normed_two_low = normed_two.astype(jnp.bfloat16)
    hidden = project(normed_two_low, fc1_weight) + fc1_bias.astype(jnp.float32)
    activated, gelu_back = jax.vjp(partial(jax.nn.gelu, approximate=False), hidden)
    activated_low = activated.astype(jnp.bfloat16)
    result_rows = middle + mlp_keep * (
        project(activated_low, fc2_weight) + fc2_bias.astype(jnp.float32)
    )
    result_low = result_rows.astype(jnp.bfloat16)
    out_grad = jnp.concatenate([grad_specials, grad_patches], axis=1).astype(jnp.float32)
    grad_mlp_out = (mlp_keep * out_grad).astype(jnp.bfloat16)
    grad_fc2 = weight_grad(activated_low, grad_mlp_out * row_weight_low)
    grad_fc2_bias = jnp.sum(grad_mlp_out.astype(jnp.float32) * row_weight, axis=(0, 1))
    grad_act = project_back(grad_mlp_out, fc2_weight)
    (grad_hidden,) = gelu_back(grad_act)
    grad_hidden_low = grad_hidden.astype(jnp.bfloat16)
    grad_fc1 = weight_grad(normed_two_low, grad_hidden_low * row_weight_low)
    grad_fc1_bias = jnp.sum(grad_hidden_low.astype(jnp.float32) * row_weight, axis=(0, 1))
    grad_norm_two = project_back(grad_hidden_low, fc1_weight)
    grad_mid_part, grad_gain_two, grad_shift_two = norm_backward(
        grad_norm_two, hat_two, inv_two, gain_two, row_weight
    )
    grad_middle = out_grad + grad_mid_part
    grad_branch = (attn_keep * grad_middle).astype(jnp.bfloat16)
    grad_proj = weight_grad(context, grad_branch * row_weight_low)
    grad_proj_bias = jnp.sum(grad_branch.astype(jnp.float32) * row_weight, axis=(0, 1))
    grad_context = project_back(grad_branch, proj_weight).astype(jnp.bfloat16)
    grad_context = grad_context.reshape(images, all_rows, groups, group_width)
    arrived_grad = lax.all_to_all(
        grad_context[:, 2:], "seq", split_axis=2, concat_axis=1, tiled=True
    )
    special_grad = lax.dynamic_slice_in_dim(grad_context[:, :2], own_index, 1, 2)
    grad_attended = jnp.concatenate([special_grad, arrived_grad], axis=1)
    grad_attended = grad_attended.reshape(images, seq_len, heads_here, head_size)
    grad_attention = jnp.einsum(
        "blhd,bmhd->bhlm", grad_attended, value_rows, preferred_element_type=jnp.float32
    )
    grad_scores = attention * (
        grad_attention - jnp.sum(attention * grad_attention, axis=-1, keepdims=True)
    )
    grad_scores = grad_scores.astype(jnp.bfloat16)
    grad_value = jnp.einsum(
        "bhlm,blhd->bmhd", attention_low, grad_attended, preferred_element_type=jnp.float32
    )
    grad_query = (
        jnp.einsum("bhlm,bmhd->blhd", grad_scores, key_rows, preferred_element_type=jnp.float32)
        * score_scale
    )
    grad_key = (
        jnp.einsum("bhlm,blhd->bmhd", grad_scores, queries, preferred_element_type=jnp.float32)
        * score_scale
    )
    grad_heads = jnp.stack([grad_query, grad_key, grad_value], axis=2).astype(jnp.bfloat16)
    grad_heads = grad_heads.reshape(images, seq_len, 3, 1, group_width)
    returned = lax.all_to_all(grad_heads[:, 2:], "seq", split_axis=1, concat_axis=3, tiled=True)
    special_back = lax.all_gather(grad_heads[:, :2], "seq", axis=3, tiled=True)
    grad_mixed = jnp.concatenate([special_back, returned], axis=1).reshape(
        images, all_rows, 3 * feature_width
    )
    grad_qkv = weight_grad(normed_one_low, grad_mixed * row_weight_low)
    grad_flat = jnp.sum(grad_mixed.astype(jnp.float32) * row_weight, axis=(0, 1))
    grad_qv = jnp.stack([grad_flat[:feature_width], grad_flat[2 * feature_width :]])
    grad_norm_one = project_back(grad_mixed, qkv_weight)
    grad_in_part, grad_gain_one, grad_shift_one = norm_backward(
        grad_norm_one, hat_one, inv_one, gain_one, row_weight
    )
    grad_inputs = (grad_middle + grad_in_part).astype(jnp.bfloat16)
    all_shares = (
        lax.psum_scatter(grad_gain_one, "dp", scatter_dimension=0, tiled=True),
        lax.psum_scatter(grad_shift_one, "dp", scatter_dimension=0, tiled=True),
        lax.psum_scatter(grad_qkv, "dp", scatter_dimension=0, tiled=True),
        lax.psum_scatter(grad_qv, "dp", scatter_dimension=1, tiled=True),
        lax.psum_scatter(grad_proj, "dp", scatter_dimension=0, tiled=True),
        lax.psum_scatter(grad_proj_bias, "dp", scatter_dimension=0, tiled=True),
        lax.psum_scatter(grad_gain_two, "dp", scatter_dimension=0, tiled=True),
        lax.psum_scatter(grad_shift_two, "dp", scatter_dimension=0, tiled=True),
        lax.psum_scatter(grad_fc1, "dp", scatter_dimension=0, tiled=True),
        lax.psum_scatter(grad_fc1_bias, "dp", scatter_dimension=0, tiled=True),
        lax.psum_scatter(grad_fc2, "dp", scatter_dimension=0, tiled=True),
        lax.psum_scatter(grad_fc2_bias, "dp", scatter_dimension=0, tiled=True),
    )
    summed = tuple(
        (
            lax.psum(all_shares[0].astype(jnp.bfloat16), "seq").astype(jnp.float32),
            lax.psum(all_shares[1].astype(jnp.bfloat16), "seq").astype(jnp.float32),
            lax.psum(all_shares[2].astype(jnp.bfloat16), "seq").astype(jnp.float32),
            lax.psum(all_shares[3].astype(jnp.bfloat16), "seq").astype(jnp.float32),
            lax.psum(all_shares[4].astype(jnp.bfloat16), "seq").astype(jnp.float32),
            lax.psum(all_shares[5].astype(jnp.bfloat16), "seq").astype(jnp.float32),
            lax.psum(all_shares[6].astype(jnp.bfloat16), "seq").astype(jnp.float32),
            lax.psum(all_shares[7].astype(jnp.bfloat16), "seq").astype(jnp.float32),
            lax.psum(all_shares[8].astype(jnp.bfloat16), "seq").astype(jnp.float32),
            lax.psum(all_shares[9].astype(jnp.bfloat16), "seq").astype(jnp.float32),
            lax.psum(all_shares[10].astype(jnp.bfloat16), "seq").astype(jnp.float32),
            lax.psum(all_shares[11].astype(jnp.bfloat16), "seq").astype(jnp.float32),
        )
    )
    return (
        result_low[:, 2:],
        result_low[:, :2],
        grad_inputs[:, 2:],
        grad_inputs[:, :2],
        summed[0],
        summed[1],
        summed[2],
        summed[3],
        summed[4],
        summed[5],
        summed[6],
        summed[7],
        summed[8],
        summed[9],
        summed[10],
        summed[11],
    )


def solution(mesh):
    return jax.shard_map(
        shards,
        mesh=mesh,
        in_specs=(
            P("dp", "seq", None),
            P("dp", None, None),
            P("dp", None),
            P(),
            P(),
            P(),
            P(),
            P(),
            P(),
            P(),
            P(),
            P(),
            P(),
            P(),
            P(),
            P("dp", "seq", None),
            P("dp", None, None),
        ),
        out_specs=(
            P("dp", "seq", None),
            P("dp", None, None),
            P("dp", "seq", None),
            P("dp", None, None),
            P("dp"),
            P("dp"),
            P("dp", None),
            P(None, "dp"),
            P("dp", None),
            P("dp"),
            P("dp"),
            P("dp"),
            P("dp", None),
            P("dp"),
            P("dp", None),
            P("dp"),
        ),
        check_vma=False,
    )
```

profile of v0, /device:TPU:0, one launch (start us, length us, event | category | flops | bytes accessed | tf_op | source)
XLA Modules:
  0.0 746.6 jit_solution(8357983774487223520)
XLA Ops:
  7.2 1.8 convert_reduce_fusion
  9.0 1.9 fusion.43
  13.7 6.0 add_convert_fusion.1
  19.7 7.1 reshape.179
  26.7 2.0 slice-done
  28.7 2.5 copy.95
  31.2 6.6 all-to-all-start
  41.1 2.5 copy.62
  43.6 86.3 %all-to-all-done = bf16[12,49,3,4,192]{4,1,2,0,3:T(8,128)(2,1)} async-done(((bf16[12,49,3,4,192]{4,1,2,0,3:T(8,128)(2,1)}), bf16[12,49,3,4,192]{4,1,2,0,3:T(8,128)(2,1)}, u32[]{:S(2)}, u32[]{:S(2)}) %all-to-all-start) | async-done | bytes 2709536 | tf_op jit(solution)/shard_map/all_to_all | solution.py:94
  129.9 10.5 %copy.89 = bf16[12,4,49,3,1,192]{2,1,5,0,3,4:T(4,128)(2,1)} copy(bf16[12,4,49,3,1,192]{5,2,3,0,1,4:T(8,128)(2,1)} %bitcast.4) | data formatting | bytes 5419008 | tf_op jit(solution)/shard_map/concatenate | solution.py:96
  140.4 10.3 %reshape.192 = bf16[12,196,3,3,64]{1,4,3,0,2:T(8,128)(2,1)} reshape(bf16[12,4,49,3,1,192]{2,1,5,0,3,4:T(4,128)(2,1)} %copy.89) | data formatting | bytes 5419008 | tf_op jit(solution)/shard_map/concatenate | solution.py:96
  150.7 4.5 fusion.63
  155.2 8.0 %fusion.88 = (f32[12,3,198]{2,1,0:T(4,128)}, f32[12,3,198,198]{2,3,1,0:T(8,128)}) fusion(bf16[12,198,3,64]{1,3,2,0:T(8,128)(2,1)} %get-tuple-element.56, bf16[12,198,3,64]{1,3,2,0:T(8,128)(2,1)} %get-tuple-element.55), kind=kOutput, calls=%fused_computation.156 | convolution fusion | flops 184886272 | bytes 7498656 | tf_op jit(solution)/shard_map/sub | solution.py:105
  163.2 4.8 fusion.51
  170.6 4.3 copy.97
  174.9 4.3 all-to-all-start.1
  183.7 1.9 slice.90
  187.0 34.9 %all_gather.6 = bf16[12,2,4,192]{3,1,0,2:T(2,128)(2,1)S(1)} all-gather(bf16[12,2,1,192]{3,1,0,2:T(2,128)(2,1)S(1)} %copy.96), channel_id=1, replica_groups=mesh['dp'=8,'seq'=4] {'seq'}, dimensions={2}, use_global_device_ids=true | all-gather | bytes 46080 | tf_op jit(solution)/shard_map/all_gather | solution.py:113
  224.1 1.8 copy.102
  227.5 3.8 concatenate.55
  231.3 3.2 fusion.89
  235.0 8.5 %fusion.20 = (u16[51,3072]{1,0:T(8,128)(2,1)S(1)}, u16[51,3072]{1,0:T(8,128)(2,1)S(1)}, f32[12,51,3072]{2,1,0:T(8,128)S(1)}) fusion(f32[3072]{0:T(1024)S(1)} %copy-done.27, bf16[768,3072]{1,0:T(8,128)(2,1)} %param.28, f32[12,51,768]{2,1,0:T(8,128)S(1)} %get-tuple-element.64, f32[768]{0:T(1024)S(1)} %copy-done.17, f32[768]{0:T(1024)S(1)} %copy-done.15, ...), kind=kOutput, calls=%fused_computation.44 | convolution fusion | flops 2916135936 | bytes 14768928 | tf_op jit(solution)/shard_map/brd,de->bre/dot_general | solution.py:35
  243.5 20.0 %multiply_convert_fusion = (bf16[12,51,3072]{2,1,0:T(8,128)(2,1)}, f32[12,51,3072]{2,1,0:T(8,128)}) fusion(f32[12,51,3072]{2,1,0:T(8,128)S(1)} %get-tuple-element.65, f32[3072]{0:T(1024)S(1)} %copy-done.27, u16[51,3072]{1,0:T(8,128)(2,1)S(1)} %get-tuple-element.17, u16[51,3072]{1,0:T(8,128)(2,1)S(1)} %get-tuple-element.16), kind=kLoop, calls=%fused_computation.10 | loop fusion | flops 133484544 | bytes 19439616 | tf_op jit(solution)/shard_map/convert_element_type | solution.py:123
  263.5 12.0 %multiply_reduce_fusion = (f32[3072]{0:T(1024)}, bf16[12,51,3072]{2,1,0:T(8,128)(2,1)}) fusion(f32[51]{0:T(128)S(1)} %copy-done.41, f32[12,51,3072]{2,1,0:T(8,128)} %get-tuple-element.54, bf16[3072,768]{1,0:T(8,128)(2,1)} %param.30, f32[12]{0:T(128)S(1)} %copy-done.40, bf16[12,49,768]{2,1,0:T(8,128)(2,1)S(1)} %copy-done.8, ...), kind=kOutput, calls=%fused_computation.8 | convolution fusion | flops 2924436480 | bytes 24484092 | tf_op jit(solution)/shard_map/bre,de->brd/dot_general | solution.py:39
  275.5 8.0 %multiply_reduce_fusion.6 = (f32[768]{0:T(1024)}, f32[12,51]{1,0:T(8,128)S(1)}, f32[12,51]{1,0:T(8,128)S(1)}, f32[768]{0:T(1024)}, f32[12,51,768]{2,1,0:T(8,128)S(1)}) fusion(f32[12,51,768]{2,1,0:T(8,128)S(1)} %get-tuple-element.64, f32[51]{0:T(128)S(1)} %copy-done.41, f32[12,51]{1,0:T(8,128)S(1)} %add_rsqrt_fusion, ...), kind=kOutput, calls=%fused_computation.85 | convolution fusion | flops 2892945920 | bytes 12258060 | tf_op jit(solution)/shard_map/bre,de->brd/dot_general | solution.py:39
  285.9 2.6 convolution_bitcast_fusion.3
  288.6 10.8 %convolution_bitcast_fusion.1 = f32[768,3072]{1,0:T(8,128)} fusion(bf16[12,51,3072]{2,1,0:T(8,128)(2,1)} %get-tuple-element.71, bf16[51]{0:T(256)(128)(2,1)} %constant.98.clone.1, f32[12,51,768]{2,1,0:T(8,128)} %copy-done.2, f32[768]{0:T(1024)} %convert_element_type.205, f32[768]{0:T(1024)} %convert_element_type.204, f32[12,51]{1,0:T(8,128)S(1)} %add_rsqrt_fusion, ...), kind=kOutput, calls=%fused_computation.31 | convolution fusion | flops 2892008448 | bytes 15088518 | tf_op jit(solution)/shard_map/brd,bre->de/dot_general | solution.py:43
  299.4 10.4 %convolution_bitcast_fusion = f32[3072,768]{1,0:T(8,128)} fusion(bf16[12,51,3072]{2,1,0:T(8,128)(2,1)} %get-tuple-element.53, bf16[51]{0:T(256)(128)(2,1)} %constant.98.clone.1, f32[12]{0:T(128)} %get-tuple-element.59, bf16[12,49,768]{2,1,0:T(8,128)(2,1)} %param.32, bf16[12,2,768]{2,1,0:T(2,128)(2,1)} %param.33), kind=kOutput, calls=%fused_computation.30 | convolution fusion | flops 2892478464 | bytes 14137494 | tf_op jit(solution)/shard_map/brd,bre->de/dot_general | solution.py:43
  309.8 3.6 convolution_convert_fusion
  313.4 3.1 reshape.181
  319.1 4.5 all-to-all-start.2
  325.0 1.8 copy.72
  326.9 26.7 %all-to-all-done.2 = bf16[12,49,4,192]{3,1,0,2:T(8,128)(2,1)} async-done(((bf16[12,49,4,192]{3,1,0,2:T(8,128)(2,1)}), bf16[12,49,4,192]{3,1,0,2:T(8,128)(2,1)}, u32[]{:S(2)}, u32[]{:S(2)}) %all-to-all-start.2) | async-done | bytes 903200 | tf_op jit(solution)/shard_map/all_to_all | solution.py:147
  353.6 4.3 copy.74
  357.9 4.3 concatenate.59
  362.2 9.3 %multiply_reduce_fusion.1 = (f32[12,3,198]{2,1,0:T(4,128)S(1)}, f32[12,3,198,198]{2,3,1,0:T(8,128)}) fusion(f32[12,3,198,198]{2,3,1,0:T(8,128)} %get-tuple-element.62, f32[12,3,198]{2,1,0:T(4,128)} %get-tuple-element.61, bf16[12,196,3,3,64]{1,4,3,0,2:T(8,128)(2,1)} %reshape.192, bf16[12,2,3,3,64]{1,4,3,0,2:T(8,128)(2,1)} %bitcast.110, ...), kind=kOutput, calls=%fused_computation.24 | convolution fusion | flops 188528480 | bytes 14997312 | tf_op jit(solution)/shard_map/blhd,bmhd->bhlm/dot_general | solution.py:153
  371.5 7.0 multiply_convert_fusion.1
  378.6 2.2 multiply_convert_fusion.3
  380.8 2.5 copy.78
  383.3 4.8 multiply_convert_fusion.2
  388.0 2.4 copy.79
  390.5 6.0 fusion.54
  396.5 2.5 copy.80
  399.0 3.2 pad_maximum_fusion
  402.2 4.1 copy.82
  406.3 5.0 all-to-all-start.3
  412.3 112.0 %all_gather.7 = bf16[12,2,3,4,192]{4,1,2,0,3:T(2,128)(2,1)S(1)} all-gather(bf16[12,2,3,1,192]{4,1,2,0,3:T(2,128)(2,1)S(1)} %pad_maximum_fusion.14), channel_id=1, replica_groups=mesh['dp'=8,'seq'=4] {'seq'}, dimensions={3}, use_global_device_ids=true | all-gather | bytes 138240 | tf_op jit(solution)/shard_map/all_gather | solution.py:174
  526.7 4.0 copy.101
  530.7 3.3 copy.84
  533.9 7.3 concatenate.62
  541.2 8.5 %convolution_bitcast_fusion.2 = f32[768,2304]{1,0:T(8,128)} fusion(bf16[51]{0:T(256)(128)(2,1)} %constant.98.clone.1, bf16[12,49,2304]{2,1,0:T(8,128)(2,1)} %concatenate.62, bf16[12,2,2304]{2,1,0:T(2,128)(2,1)} %concatenate.61, f32[768]{0:T(1024)} %copy-done.35, f32[768]{0:T(1024)} %copy-done.32, f32[12,51]{1,0:T(8,128)} %copy-done.30, ...), kind=kOutput, calls=%fused_computation.32 | convolution fusion | flops 2178524160 | bytes 10849158 | tf_op jit(solution)/shard_map/brd,bre->de/dot_general | solution.py:43
  553.6 3.1 multiply_reduce_fusion.3
  559.3 9.3 %add_convert_fusion.2 = bf16[12,51,768]{2,1,0:T(8,128)(2,1)S(1)} fusion(f32[12,51,768]{2,1,0:T(8,128)} %copy-done.2, bf16[12,51,3072]{2,1,0:T(8,128)(2,1)} %get-tuple-element.53, bf16[3072,768]{1,0:T(8,128)(2,1)} %param.30, f32[768]{0:T(1024)} %convert_element_type.209, f32[12]{0:T(128)} %get-tuple-element.59), kind=kOutput, calls=%fused_computation.90 | convolution fusion | flops 2889658368 | bytes 11301936 | tf_op jit(solution)/shard_map/brd,de->bre/dot_general | solution.py:35
  572.1 2.2 convert_element_type.236
  574.3 2.5 convert_element_type.241
  576.8 39.0 %reduce-scatter.8.cloned.1.call-done = f32[96,2304]{1,0:T(8,128)} async-done(((f32[768,2304]{1,0:T(8,128)}), f32[96,2304]{1,0:T(8,128)}) %reduce-scatter.8.cloned.1.call-update) | async-done | bytes 884752 | tf_op jit(solution)/shard_map/reduce_scatter | solution.py:189
  615.8 2.0 convert_element_type.222
  617.9 7.8 %multiply_reduce_fusion.4 = (f32[768]{0:T(1024)}, f32[768]{0:T(1024)}, f32[768]{0:T(1024)}, f32[12,51]{1,0:T(8,128)S(1)}, f32[12,51]{1,0:T(8,128)S(1)}, /*index=5*/f32[768]{0:T(1024)}, f32[12,51,768]{2,1,0:T(8,128)S(1)}) fusion(f32[51]{0:T(128)} %constant.97.clone.1, bf16[12,49,768]{2,1,0:T(8,128)(2,1)} %param.32, bf16[12,2,768]{2,1,0:T(2,128)(2,1)} %param.33, ...), kind=kOutput, calls=%fused_computation.82 | convolution fusion | flops 2184160256 | bytes 11084604 | tf_op jit(solution)/shard_map/bre,de->brd/dot_general | solution.py:39
  625.9 2.1 fusion.40
  629.9 24.8 %all-reduce.7 = (bf16[768]{0:T(1024)(128)(2,1)S(1)}, bf16[768]{0:T(1024)(128)(2,1)}, bf16[768]{0:T(1024)(128)(2,1)}, bf16[768]{0:T(1024)(128)(2,1)}, bf16[768]{0...) all-reduce(f32[768]{0:T(1024)} %get-tuple-element.33, ...), channel_id=2, replica_groups=mesh['dp'=8,'seq'=4] {'dp'}, use_global_device_ids=true, to_apply=%region_12.0.clone | all-reduce | flops 7680 | bytes 46080
  662.0 13.1 %all-reduce.8 = (bf16[96]{0:T(256)(128)(2,1)}, bf16[96]{0:T(256)(128)(2,1)}, bf16[2,96]{1,0:T(2,128)(2,1)}, bf16[96]{0:T(256)(128)(2,1)}, bf16[96]{0:T(256)(128)...) all-reduce(bf16[96]{0:T(256)(128)(2,1)} %dynamic-slice.27, ...), channel_id=1, replica_groups=mesh['dp'=8,'seq'=4] {'seq'}, use_global_device_ids=true, to_apply=%region_13.0 | all-reduce | flops 1152 | bytes 4608 | tf_op jit(solution)/shard_map/psum | solution.py:202
  683.9 49.6 %all-reduce.12.cloned.1.call-done = (bf16[96,2304]{1,0:T(8,128)(2,1)}, bf16[96,768]{1,0:T(8,128)(2,1)}, bf16[96,3072]{1,0:T(8,128)(2,1)}, bf16[384,768]{1,0:T(8,128)(2,1)}) async-done(((bf16[96,2304]{1,0:T(8,128)(2,1)}, bf16[96,768]{1,0:T(8,128)(2,1)}, bf16[96,3072]{1,0:T(8,128)(2,1)}, bf16[384,768]{1,0:T(8,128)(2,1)}), (bf16[96,2304]{1,0:T(8,128)(2,1)}, bf16[96,768]{1,0:T(8,128)(2,1)}, ...) | async-done | bytes 1769488 | tf_op jit(solution)/shard_map/psum | solution.py:204
  733.4 2.2 convert_element_type.237
  735.7 2.2 convert_element_type.242
  (167 shorter events, 56.6 us)
Async XLA Ops:
  7.2 6.5 copy-start
  9.0 4.1 copy-start.21
  10.9 2.2 copy-start.30
  11.6 1.5 copy-start.32
  13.1 0.6 copy-start.35
  26.7 2.0 slice-start
  31.2 98.6 %all-to-all-start = ((bf16[12,49,3,4,192]{4,1,2,0,3:T(8,128)(2,1)}), bf16[12,49,3,4,192]{4,1,2,0,3:T(8,128)(2,1)}, u32[]{:S(2)}, u32[]{:S(2)}) async-start(bf16[12,49,3,4,192]{4,1,2,0,3:T(8,128)(2,1)} %copy.95), calls=%async_computation | async-start | bytes 8257536 | tf_op jit(solution)/shard_map/all_to_all | solution.py:94
  168.0 1.0 copy-start.10
  170.6 8.7 %copy-start.38 = (bf16[768]{0:T(1024)(128)(2,1)S(1)}, bf16[768]{0:T(1024)(128)(2,1)}, u32[]{:S(2)}) copy-start(bf16[768]{0:T(1024)(128)(2,1)} %param.25) | copy-start | bytes 4612
  170.6 10.0 %copy-start.34 = (bf16[3072]{0:T(1024)(128)(2,1)S(1)}, bf16[3072]{0:T(1024)(128)(2,1)}, u32[]{:S(2)}) copy-start(bf16[3072]{0:T(1024)(128)(2,1)} %param.29) | copy-start | bytes 18436
  174.9 49.2 %all-to-all-start.1 = ((bf16[12,196,1,192]{3,0,2,1:T(8,128)(2,1)}), bf16[12,196,1,192]{3,0,2,1:T(8,128)(2,1)}, u32[]{:S(2)}, u32[]{:S(2)}) async-start(bf16[12,196,1,192]{3,0,2,1:T(8,128)(2,1)} %copy.97), calls=%async_computation.1 | async-start | bytes 3211264 | tf_op jit(solution)/shard_map/all_to_all | solution.py:112
  179.2 391.2 %reduce-scatter.10.cloned.1.call-start = ((), (), s32[]{:S(2)}) async-start(), calls=%async_computation.10 | async-start | bytes 2654208 | tf_op jit(solution)/shard_map/reduce_scatter | solution.py:191
  225.9 5.4 copy-start.36
  231.3 3.6 copy-start.15
  231.3 3.6 copy-start.17
  231.3 3.6 copy-start.27
  234.5 49.0 %copy-start.2 = (f32[12,51,768]{2,1,0:T(8,128)}, f32[12,51,768]{2,1,0:T(8,128)S(1)}, u32[]{:S(2)}) copy-start(f32[12,51,768]{2,1,0:T(8,128)S(1)} %get-tuple-element.64) | copy-start | bytes 5640196
  243.5 20.0 %copy-start.8 = (bf16[12,49,768]{2,1,0:T(8,128)(2,1)S(1)}, bf16[12,49,768]{2,1,0:T(8,128)(2,1)}, u32[]{:S(2)}) copy-start(bf16[12,49,768]{2,1,0:T(8,128)(2,1)} %param.32) | copy-start | bytes 2709508
  243.5 20.0 %copy-start.18 = (bf16[12,2,768]{2,1,0:T(2,128)(2,1)S(1)}, bf16[12,2,768]{2,1,0:T(2,128)(2,1)}, u32[]{:S(2)}) copy-start(bf16[12,2,768]{2,1,0:T(2,128)(2,1)} %param.33) | copy-start | bytes 110596
  243.5 20.0 %copy-start.40 = (f32[12]{0:T(128)S(1)}, f32[12]{0:T(128)}, u32[]{:S(2)}) copy-start(f32[12]{0:T(128)} %get-tuple-element.59) | copy-start | bytes 148
  243.5 20.0 %copy-start.41 = (f32[51]{0:T(128)S(1)}, f32[51]{0:T(128)}, u32[]{:S(2)}) copy-start(f32[51]{0:T(128)} %constant.97.clone.1) | copy-start | bytes 616
  275.5 8.0 %copy-start.37 = (f32[12]{0:T(128)S(1)}, f32[12]{0:T(128)}, u32[]{:S(2)}) copy-start(f32[12]{0:T(128)} %get-tuple-element.60) | copy-start | bytes 148
  283.5 1.4 copy-start.5
  283.6 1.4 copy-start.23
  283.6 1.4 copy-start.25
  283.6 2.3 copy-start.12
  283.6 2.3 copy-start.29
  283.6 2.3 copy-start.39
  284.9 1.0 copy-start.11
  288.5 283.6 %reduce-scatter.12.cloned.1.call-start = ((), (), s32[]{:S(2)}) async-start(), calls=%async_computation.11 | async-start | bytes 10616832 | tf_op jit(solution)/shard_map/reduce_scatter | solution.py:195
  299.3 274.9 %reduce-scatter.14.cloned.1.call-start = ((), (), s32[]{:S(2)}) async-start(), calls=%async_computation.12 | async-start | bytes 10616832 | tf_op jit(solution)/shard_map/reduce_scatter | solution.py:197
  316.5 1.3 slice-start.1
  319.1 34.6 %all-to-all-start.2 = ((bf16[12,49,4,192]{3,1,0,2:T(8,128)(2,1)}), bf16[12,49,4,192]{3,1,0,2:T(8,128)(2,1)}, u32[]{:S(2)}, u32[]{:S(2)}) async-start(bf16[12,49,4,192]{3,1,0,2:T(8,128)(2,1)} %copy.98), calls=%async_computation.2 | async-start | bytes 2752512 | tf_op jit(solution)/shard_map/all_to_all | solution.py:147
  362.2 9.3 %copy-start.28 = (f32[12,3,198]{2,1,0:T(4,128)S(1)}, f32[12,3,198]{2,1,0:T(4,128)}, u32[]{:S(2)}) copy-start(f32[12,3,198]{2,1,0:T(4,128)} %get-tuple-element.61) | copy-start | bytes 85540
  371.5 7.1 copy-start.7
  378.6 2.2 copy-start.1
  406.3 120.4 %all-to-all-start.3 = ((bf16[12,196,3,1,192]{4,2,0,3,1:T(4,128)(2,1)}), bf16[12,196,3,1,192]{4,2,0,3,1:T(4,128)(2,1)}, u32[]{:S(2)}, u32[]{:S(2)}) async-start(bf16[12,196,3,1,192]{4,2,0,3,1:T(4,128)(2,1)} %copy.82), calls=%async_computation.3 | async-start | bytes 9633792 | tf_op jit(solution)/shard_map/all_to_all | solution.py:173
  411.3 204.5 %reduce-scatter.8.cloned.1.call-start = ((), (), s32[]{:S(2)}) async-start(), calls=%async_computation.9 | async-start | bytes 7962624 | tf_op jit(solution)/shard_map/reduce_scatter | solution.py:189
  549.7 111.4 %reduce-scatter.16.cloned.1.call-start = ((), (), s32[]{:S(2)}) async-start(), calls=%async_computation.13 | async-start | bytes 442368
  559.1 174.4 %all-reduce.12.cloned.1.call-start = ((), (), s32[]{:S(2)}) async-start(), calls=%async_computation.14 | async-start | bytes 3538944 | tf_op jit(solution)/shard_map/psum | solution.py:204
  617.8 8.0 %copy-start.3 = (f32[12,51,768]{2,1,0:T(8,128)S(1)}, f32[12,51,768]{2,1,0:T(8,128)}, u32[]{:S(2)}) copy-start(f32[12,51,768]{2,1,0:T(8,128)} %copy-done.2) | copy-start | bytes 5640196
  617.8 8.0 %copy-start.4 = (bf16[12,49,768]{2,1,0:T(8,128)(2,1)S(1)}, bf16[12,49,768]{2,1,0:T(8,128)(2,1)}, u32[]{:S(2)}) copy-start(bf16[12,49,768]{2,1,0:T(8,128)(2,1)} %param.17) | copy-start | bytes 2709508
  617.8 8.0 %copy-start.6 = (f32[12,51,768]{2,1,0:T(8,128)S(1)}, f32[12,51,768]{2,1,0:T(8,128)}, u32[]{:S(2)}) copy-start(f32[12,51,768]{2,1,0:T(8,128)} %copy-done.5) | copy-start | bytes 5640196
  617.8 8.0 %copy-start.9 = (bf16[12,49,768]{2,1,0:T(8,128)(2,1)S(1)}, bf16[12,49,768]{2,1,0:T(8,128)(2,1)}, u32[]{:S(2)}) copy-start(bf16[12,49,768]{2,1,0:T(8,128)(2,1)} %param.32) | copy-start | bytes 2709508
  617.8 8.0 %copy-start.14 = (bf16[12,2,768]{2,1,0:T(2,128)(2,1)S(1)}, bf16[12,2,768]{2,1,0:T(2,128)(2,1)}, u32[]{:S(2)}) copy-start(bf16[12,2,768]{2,1,0:T(2,128)(2,1)} %param.18) | copy-start | bytes 110596
  617.8 8.0 %copy-start.16 = (f32[768]{0:T(1024)S(1)}, f32[768]{0:T(1024)}, u32[]{:S(2)}) copy-start(f32[768]{0:T(1024)} %convert_element_type.204) | copy-start | bytes 9220
  617.9 8.0 %copy-start.19 = (bf16[12,2,768]{2,1,0:T(2,128)(2,1)S(1)}, bf16[12,2,768]{2,1,0:T(2,128)(2,1)}, u32[]{:S(2)}) copy-start(bf16[12,2,768]{2,1,0:T(2,128)(2,1)} %param.33) | copy-start | bytes 110596
  617.9 8.0 %copy-start.22 = (f32[12,51]{1,0:T(8,128)S(1)}, f32[12,51]{1,0:T(8,128)}, u32[]{:S(2)}) copy-start(f32[12,51]{1,0:T(8,128)} %copy-done.21) | copy-start | bytes 7348
  617.9 8.0 %copy-start.24 = (f32[12,51]{1,0:T(8,128)S(1)}, f32[12,51]{1,0:T(8,128)}, u32[]{:S(2)}) copy-start(f32[12,51]{1,0:T(8,128)} %copy-done.23) | copy-start | bytes 7348
  617.9 8.0 %copy-start.26 = (f32[12,51]{1,0:T(8,128)S(1)}, f32[12,51]{1,0:T(8,128)}, u32[]{:S(2)}) copy-start(f32[12,51]{1,0:T(8,128)} %copy-done.25) | copy-start | bytes 7348
  617.9 8.0 %copy-start.31 = (f32[12,51]{1,0:T(8,128)S(1)}, f32[12,51]{1,0:T(8,128)}, u32[]{:S(2)}) copy-start(f32[12,51]{1,0:T(8,128)} %copy-done.30) | copy-start | bytes 7348
  617.9 8.0 %copy-start.33 = (f32[768]{0:T(1024)S(1)}, f32[768]{0:T(1024)}, u32[]{:S(2)}) copy-start(f32[768]{0:T(1024)} %copy-done.32) | copy-start | bytes 9220
  733.4 4.4 copy-start.13
  733.4 5.4 copy-start.20
Sparse Core Ops, SparseCore 0:
  288.6 42.6 reduce-scatter.9
  335.2 76.4 reduce-scatter.11
  415.6 76.4 reduce-scatter.13
  549.9 65.8 reduce-scatter.7
  618.7 33.8 reduce-scatter.15
  656.3 77.1 all-reduce.11
where the time goes:
time: 754 us; the launch traced here: 747 us
  waiting for transfers between devices  202 us (27%)
  blocking collectives  185 us (25%)
  matrix products  126 us (17%)
  local copies, waits for them, and re-layouts  119 us (16%)
  other arithmetic  77.8 us (10%)
  starting transfers between devices  20.9 us (3%)
  between operations  16.2 us (2%)
    all_gather x1, blocking collectives, shards(): special_back = lax.all_gather(grad_heads[:, :2], 'seq', axis=3, tiled=True)  112 us
    all_to_all x1, waiting for transfers between devices, shards(): lax.all_to_all(qkv_rows[:, 2:], 'seq', split_axis=3, concat_axis=1, tiled...  86.3 us
    psum x1, waiting for transfers between devices, shards(): lax.psum(all_shares[2].astype(jnp.bfloat16), 'seq').astype(jnp.float32)  49.6 us
    reduce_scatter x1, waiting for transfers between devices, shards(): lax.psum_scatter(grad_qkv, 'dp', scatter_dimension=0, tiled=True)  39 us
    all_gather x1, blocking collectives, shards(): special_out = lax.all_gather(attended[:, :2], 'seq', axis=2, tiled=True)  34.9 us
    dot_general x4, matrix products, weight_grad(): jnp.einsum('brd,bre->de', row_block, upstream, preferred_element_type=jnp...  32.2 us
    dot_general x4, matrix products, project_back(): jnp.einsum('bre,de->brd', upstream, weight, preferred_element_type=jnp.fl...  31.5 us
    dot_general x4, matrix products, project(): jnp.einsum('brd,de->bre', row_block, weight, preferred_element_type=jnp.f...  27.1 us
  transfers between devices with their start and end apart: 10, of which 4 were waited for; matrix products, arithmetic and copies ran while one was open for 24% of the time, Pallas kernels for 0%

commit v1 on v0

v1 whole, which is shorter than its diff:
```python
from functools import partial

import jax
import jax.numpy as jnp
from jax import lax
from jax.experimental import pallas as pl
from jax.experimental.pallas import tpu as pltpu
from jax.sharding import PartitionSpec as P

HEAD_DIM = 64
KEEP = 1.0 / 0.9
EPS = 1e-06
BF = jnp.bfloat16
F32 = jnp.float32
OWNERS = 8
VMEM = 60 * 2**20

ERF_P = 0.425
ERF_C = (
    0.2396707695899643,
    0.2419609266760862,
    0.1999560009093125,
    0.2575598334337707,
    -0.1079240365384954,
    0.4126939875393689,
    -0.3161029975019298,
    0.07218539595215835,
)


def dot(a, b):
    return lax.dot_general(a, b, (((1,), (0,)), ((), ())), preferred_element_type=F32)


def dot_nt(a, b):
    return lax.dot_general(a, b, (((1,), (1,)), ((), ())), preferred_element_type=F32)


def dot_tn(a, b):
    return lax.dot_general(a, b, (((0,), (0,)), ((), ())), preferred_element_type=F32)


def gelu_both(u):
    t = 1.0 / (1.0 + (ERF_P * 0.5**0.5) * jnp.abs(u))
    poly = jnp.full_like(t, 0.5 * ERF_C[-1])
    for c in ERF_C[-2::-1]:
        poly = poly * t + 0.5 * c
    bell = jnp.exp(-0.5 * u * u)
    tail = poly * t * bell
    cdf = jnp.where(u >= 0, 1.0 - tail, tail)
    return u * cdf, cdf + u * (bell * 0.3989422804014327)


def normalize(x):
    center = x - jnp.mean(x, axis=-1, keepdims=True)
    inv = lax.rsqrt(jnp.mean(center * center, axis=-1, keepdims=True) + EPS)
    return center * inv, inv


def norm_back(up, hat, inv, gain):
    e = up * gain
    return inv * (
        e
        - jnp.mean(e, axis=-1, keepdims=True)
        - hat * jnp.mean(e * hat, axis=-1, keepdims=True)
    )


def colsum(v):
    return jnp.sum(v, axis=0, keepdims=True)


def place(b):
    return (b & 1) * (OWNERS // 2) + lax.shift_right_logical(b, 1)


def store_relative(ref, lead, value, d):
    n = value.shape[0] // OWNERS
    for b in range(OWNERS):
        spot = pl.multiple_of(place(b ^ d) * n, n)
        ref[lead, pl.ds(spot, n), :] = value[b * n : (b + 1) * n]


def forward_kernel(
    at, keep, x0, x1, x2, x3, sp, g1, b1, wq, bq, wp, bp, g2, b2,
    xs, a1t, qkv, prob, ot, h, a2, a2t, buf, *, rows, heads,
):
    i = pl.program_id(0)
    d = at[1]
    part = x0.shape[1]
    ns = sp.shape[1]
    width = x0.shape[2]
    buf[...] = jnp.zeros_like(buf)
    buf[0:ns, :] = sp[0].astype(F32)
    for k, ref in enumerate((x0, x1, x2, x3)):
        buf[ns + k * part : ns + (k + 1) * part, :] = ref[0].astype(F32)
    x = buf[...]
    xs[0] = x.astype(BF)
    hat, _ = normalize(x)
    a1 = (hat * g1[...].astype(F32) + b1[...].astype(F32)).astype(BF)
    store_relative(a1t, 0, a1.astype(F32).T.astype(BF), d)
    both = (dot(a1, wq[...]) + bq[...]).astype(BF)
    qkv[0] = both
    padded = x.shape[0]
    low = lax.broadcasted_iota(jnp.int32, (padded, 2 * HEAD_DIM), 1) < HEAD_DIM
    seen = lax.broadcasted_iota(jnp.int32, (padded, padded), 1) < rows
    outs = []
    for j in range(heads // 2):
        c = j * 2 * HEAD_DIM
        q = both[:, c : c + 2 * HEAD_DIM] * BF(HEAD_DIM**-0.5)
        k = both[:, width + c : width + c + 2 * HEAD_DIM]
        v = both[:, 2 * width + c : 2 * width + c + 2 * HEAD_DIM]
        pair = []
        for side in range(2):
            mine = low if side == 0 else ~low
            s = dot_nt(jnp.where(mine, q, BF(0)), k)
            s = jnp.where(seen, s, -1e30)
            e = jnp.exp(s - jnp.max(s, axis=-1, keepdims=True))
            p = (e * (1.0 / jnp.sum(e, axis=-1, keepdims=True))).astype(BF)
            prob[0, 2 * j + side] = p
            pair.append(dot(p, v))
        outs.append(jnp.where(low, pair[0], pair[1]))
    o32 = jnp.concatenate(outs, axis=1)
    store_relative(ot, 0, o32.T.astype(BF), d)
    y = dot(o32.astype(BF), wp[...]) + bp[...].astype(F32)
    m1 = keep[at[0] * pl.num_programs(0) + i, 0].astype(F32) * KEEP
    hh = x + m1 * y
    h[0] = hh
    hat2, _ = normalize(hh)
    n2 = hat2 * g2[...].astype(F32) + b2[...].astype(F32)
    a2[0] = n2.astype(BF)
    store_relative(a2t, 0, n2.T.astype(BF), d)


def feed_kernel(
    at, keep, g0, g1, g2, g3, sg, h, a2, a2t, w1, b1, w2, b2, gain,
    o0, o1, o2, o3, dh, dy, w2s, w2k, w1s, w1k, db1, small,
    dout, dz, z, da2, gl, *, images, rows,
):
    t = pl.program_id(0)
    steps = pl.num_programs(0)
    part = g0.shape[1]
    ns = sg.shape[1]
    padded = h.shape[1]

    @pl.when(t == 0)
    def _():
        for i in range(images):
            m2 = keep[at[0] * images + i, 1].astype(F32) * KEEP
            r = i * padded
            dout[r : r + padded, :] = jnp.zeros((padded, dout.shape[1]), F32)
            dout[r : r + ns, :] = sg[i].astype(F32)
            for k, ref in enumerate((g0, g1, g2, g3)):
                lo = r + ns + k * part
                dout[lo : lo + part, :] = ref[i].astype(F32)
            dz[r : r + padded, :] = (dout[r : r + padded, :] * m2).astype(BF)
        z[...] = jnp.zeros_like(z)
        da2[...] = jnp.zeros_like(da2)

    wa = w1[...]
    wb = w2[...]
    bias = b1[...].astype(F32)
    grad1 = None
    db = None
    for i in range(images):
        r = slice(i * padded, (i + 1) * padded)
        u = dot(a2[i], wa) + bias
        dg = dot_nt(dz[r, :], wb)
        act, slope = gelu_both(u)
        act = act.astype(BF)
        du = (slope * dg).astype(BF)
        gl[r, :] = act
        z[r, :] += dot(act, wb)
        da2[r, :] += dot_nt(du, wa)
        g = dot(a2t[i], du)
        s = colsum(du.astype(F32))
        grad1 = g if grad1 is None else grad1 + g
        db = s if db is None else db + s
    db1[...] = db
    half = grad1.shape[0] // 2
    w1k[...] = grad1[:half].astype(BF)
    w1s[...] = grad1[half:].astype(BF)
    grad2 = dot_tn(gl[...], dz[...]).astype(BF)

    @pl.when(t < steps // 2)
    def _():
        w2s[...] = grad2

    @pl.when(t >= steps // 2)
    def _():
        w2k[...] = grad2

    @pl.when(t == steps - 1)
    def _():
        gains = gain[...].astype(F32)
        sums = [jnp.zeros((1, dout.shape[1]), F32) for _ in range(4)]
        for i in range(images):
            n = at[0] * images + i
            m1 = keep[n, 0].astype(F32) * KEEP
            m2 = keep[n, 1].astype(F32) * KEEP
            r = slice(i * padded, (i + 1) * padded)
            x = h[i]
            z[r, :] = x + m2 * (z[r, :] + b2[...].astype(F32))
            hat, inv = normalize(x)
            up = da2[r, :]
            grad = dout[r, :] + norm_back(up, hat, inv, gains)
            dh[i] = grad
            low = (m1 * grad).astype(BF)
            dy[i] = low
            for j, v in enumerate((up * hat, up, dz[r, :].astype(F32), low.astype(F32))):
                sums[j] = sums[j] + colsum(v)
            for k, ref in enumerate((o0, o1, o2, o3)):
                lo = i * padded + ns + k * part
                ref[i] = jnp.concatenate(
                    [z[lo : lo + part, :], z[i * padded : i * padded + ns, :]], axis=0
                ).astype(BF)
        small[...] = jnp.concatenate(sums, axis=0)


def heads_kernel(
    dy, prob, qkv, a1t, ot, wp,
    dqkv, cs, ck, ds_, dk_, flat,
    acc, accp, *, heads,
):
    i = pl.program_id(0)
    width = dy.shape[2]
    padded = dy.shape[1]
    low = lax.broadcasted_iota(jnp.int32, (padded, 2 * HEAD_DIM), 1) < HEAD_DIM
    do = dot_nt(dy[0], wp[...]).astype(BF)
    for j in range(heads // 2):
        c = j * 2 * HEAD_DIM
        pair = slice(c, c + 2 * HEAD_DIM)
        q = qkv[0, :, c : c + 2 * HEAD_DIM]
        k = qkv[0, :, width + c : width + c + 2 * HEAD_DIM]
        v = qkv[0, :, 2 * width + c : 2 * width + c + 2 * HEAD_DIM]
        g = do[:, pair]
        got = []
        for side in range(2):
            mine = low if side == 0 else ~low
            p = prob[0, 2 * j + side]
            p32 = p.astype(F32)
            dp = dot_nt(jnp.where(mine, g, BF(0)), v)
            w = p32 * dp
            ds = (w - p32 * jnp.sum(w, axis=-1, keepdims=True)).astype(BF)
            got.append((dot(ds, k), dot_tn(ds, q), dot_tn(p, g)))
        scale = HEAD_DIM**-0.5
        dqkv[0, :, c : c + 2 * HEAD_DIM] = (jnp.where(low, got[0][0], got[1][0]) * scale).astype(BF)
        dqkv[0, :, width + c : width + c + 2 * HEAD_DIM] = (
            jnp.where(low, got[0][1], got[1][1]) * scale
        ).astype(BF)
        dqkv[0, :, 2 * width + c : 2 * width + c + 2 * HEAD_DIM] = jnp.where(
            low, got[0][2], got[1][2]
        ).astype(BF)
    grads = dqkv[0]
    more = dot(a1t[0], grads)
    morep = dot(ot[0], dy[0])
    tops = colsum(grads.astype(F32))

    @pl.when(i == 0)
    def _():
        acc[...] = more
        accp[...] = morep
        flat[...] = tops

    @pl.when(i > 0)
    def _():
        acc[...] += more
        accp[...] += morep
        flat[...] += tops

    @pl.when(i == pl.num_programs(0) - 1)
    def _():
        half = acc.shape[0] // 2
        for rows, c_ref, d_ref in ((slice(0, half), ck, dk_), (slice(half, 2 * half), cs, ds_)):
            c_ref[...] = acc[rows, : 2 * width].astype(BF)
            d_ref[:, :width] = acc[rows, 2 * width :].astype(BF)
            d_ref[:, width:] = accp[rows, :].astype(BF)


def input_kernel(dqkv, wq, xs, dh, gain, o0, o1, o2, o3, small, buf, *, part, ns):
    i = pl.program_id(0)
    up = dot_nt(dqkv[0], wq[...])
    hat, inv = normalize(xs[0].astype(F32))
    buf[...] = dh[0] + norm_back(up, hat, inv, gain[...].astype(F32))
    for k, ref in enumerate((o0, o1, o2, o3)):
        lo = ns + k * part
        ref[0] = jnp.concatenate([buf[lo : lo + part, :], buf[0:ns, :]], axis=0).astype(BF)
    sums = jnp.concatenate([colsum(up * hat), colsum(up)], axis=0)

    @pl.when(i == 0)
    def _():
        small[...] = sums

    @pl.when(i > 0)
    def _():
        small[...] += sums


def gather_kernel(at, c0, c1, c2, c3, rows, specials):
    k = pl.program_id(0)
    part = rows.shape[1]
    for j, ref in enumerate((c0, c1, c2, c3)):

        @pl.when(k == j)
        def _(ref=ref):
            rows[...] = ref[:, :part, :]
            specials[...] = ref[:, part:, :]


def whole(shape):
    return pl.BlockSpec(shape, lambda *_: (0,) * len(shape))


def params():
    return pltpu.CompilerParams(
        dimension_semantics=("arbitrary",), vmem_limit_bytes=VMEM
    )


def cost(flops, read):
    return pl.CostEstimate(flops=int(flops), bytes_accessed=int(read), transcendentals=0)


def struct(*shape, dtype=BF):
    return jax.ShapeDtypeStruct(shape, dtype)


def send_around(x, groups):
    me = lax.axis_index("seq")
    n = x.shape[0] // groups
    got = []
    for k in range(1, groups):
        block = lax.dynamic_slice_in_dim(x, n * ((me + k) % groups), n)
        got.append(lax.ppermute(block, "seq", [(s, (s + k) % groups) for s in range(groups)]))
    return got


def send_back(chunks, groups):
    return [chunks[0]] + [
        lax.ppermute(c, "seq", [(s, (s - k) % groups) for s in range(groups)])
        for k, c in enumerate(chunks)
        if k
    ]


def settle(chunks, at, groups, part, ns):
    n, _, width = chunks[0].shape
    return pl.pallas_call(
        gather_kernel,
        grid_spec=pltpu.PrefetchScalarGridSpec(
            num_scalar_prefetch=1,
            grid=(groups,),
            in_specs=[whole(c.shape) for c in chunks],
            out_specs=[
                pl.BlockSpec((n, part, width), lambda k, at: ((at[0] + k) % groups, 0, 0)),
                pl.BlockSpec((n, ns, width), lambda k, at: ((at[0] + k) % groups, 0, 0)),
            ],
        ),
        out_shape=[struct(n * groups, part, width), struct(n * groups, ns, width)],
        compiler_params=params(),
        name="settle",
    )(at, *chunks)


def shards(
    patches, specials, keep_mask, ln1_gain, ln1_bias, qkv_weight, qv_bias, proj_weight, proj_bias,
    ln2_gain, ln2_bias, fc1_weight, fc1_bias, fc2_weight, fc2_bias, grad_patches, grad_specials,
):
    images, part, width = patches.shape
    ns = specials.shape[1]
    groups = lax.axis_size("seq")
    replicas = lax.axis_size("dp")
    hidden = fc1_weight.shape[1]
    heads = width // HEAD_DIM
    n = images // groups
    rows = ns + groups * part
    padded = -(-rows // 16) * 16
    chunk = hidden // OWNERS
    half = width // 2
    direct = replicas == OWNERS
    me = lax.axis_index("seq")
    d = lax.axis_index("dp") if direct else jnp.int32(0)
    at = jnp.stack([me, d]).astype(jnp.int32)

    def row(v):
        return v.reshape(1, -1)

    got = send_around(patches, groups)
    got_grad = send_around(grad_patches, groups)
    zero = jnp.zeros((width,), F32)
    qkv_bias = row(jnp.concatenate([qv_bias[0].astype(F32), zero, qv_bias[1].astype(F32)]))

    own = pl.BlockSpec((1, part, width), lambda i, at, keep: (at[0] * n + i, 0, 0))
    block = pl.BlockSpec((1, part, width), lambda i, at, keep: (i, 0, 0))

    def per_image(*shape):
        return pl.BlockSpec((1, *shape), lambda i, *_: (i,) + (0,) * len(shape))

    xs, a1t, qkv, prob, ot, h, a2, a2t = pl.pallas_call(
        partial(forward_kernel, rows=rows, heads=heads),
        grid_spec=pltpu.PrefetchScalarGridSpec(
            num_scalar_prefetch=2,
            grid=(n,),
            in_specs=[
                own, block, block, block,
                pl.BlockSpec((1, ns, width), lambda i, at, keep: (at[0] * n + i, 0, 0)),
                whole((1, width)), whole((1, width)),
                whole(qkv_weight.shape), whole((1, 3 * width)),
                whole(proj_weight.shape), whole((1, width)), whole((1, width)), whole((1, width)),
            ],
            out_specs=[
                per_image(padded, width), per_image(width, padded), per_image(padded, 3 * width),
                per_image(heads, padded, padded), per_image(width, padded),
                per_image(padded, width), per_image(padded, width), per_image(width, padded),
            ],
            scratch_shapes=[pltpu.VMEM((padded, width), F32)],
        ),
        out_shape=[
            struct(n, padded, width), struct(n, width, padded), struct(n, padded, 3 * width),
            struct(n, heads, padded, padded), struct(n, width, padded),
            struct(n, padded, width, dtype=F32), struct(n, padded, width), struct(n, width, padded),
        ],
        compiler_params=params(),
        cost_estimate=cost(2 * n * padded * width * 6 * width, 20e6),
        name="attention_forward",
    )(
        at, keep_mask, patches, *got, specials, row(ln1_gain), row(ln1_bias), qkv_weight, qkv_bias,
        proj_weight, row(proj_bias), row(ln2_gain), row(ln2_bias),
    )

    steps = OWNERS

    def owner(t, at):
        relative = jnp.where(t < steps // 2, 2 * t + 1, 2 * t - steps)
        return relative ^ at[1]

    total = n * padded
    outs = pl.pallas_call(
        partial(feed_kernel, images=n, rows=rows),
        grid_spec=pltpu.PrefetchScalarGridSpec(
            num_scalar_prefetch=2,
            grid=(steps,),
            in_specs=[
                pl.BlockSpec((n, part, width), lambda t, at, keep: (at[0], 0, 0)),
                *[whole((n, part, width))] * 3,
                pl.BlockSpec((n, ns, width), lambda t, at, keep: (at[0], 0, 0)),
                whole(h.shape), whole(a2.shape), whole(a2t.shape),
                pl.BlockSpec((width, chunk), lambda t, at, keep: (0, owner(t, at))),
                pl.BlockSpec((1, chunk), lambda t, at, keep: (0, owner(t, at))),
                pl.BlockSpec((chunk, width), lambda t, at, keep: (owner(t, at), 0)),
                whole((1, width)), whole((1, width)),
            ],
            out_specs=[
                *[whole((n, part + ns, width))] * 4,
                whole((n, padded, width)), whole((n, padded, width)),
                pl.BlockSpec((chunk, width), lambda t, *_: (jnp.minimum(t, steps // 2 - 1), 0)),
                pl.BlockSpec((chunk, width), lambda t, *_: (jnp.maximum(t - steps // 2, 0), 0)),
                pl.BlockSpec((half, chunk), lambda t, at, keep: (0, owner(t, at))),
                pl.BlockSpec((half, chunk), lambda t, at, keep: (0, owner(t, at))),
                pl.BlockSpec((1, chunk), lambda t, at, keep: (0, owner(t, at))),
                whole((4, width)),
            ],
            scratch_shapes=[
                pltpu.VMEM((total, width), F32), pltpu.VMEM((total, width), BF),
                pltpu.VMEM((total, width), F32), pltpu.VMEM((total, width), F32),
                pltpu.VMEM((total, chunk), BF),
            ],
        ),
        out_shape=[
            *[struct(n, part + ns, width)] * 4,
            struct(n, padded, width, dtype=F32), struct(n, padded, width),
            struct(hidden // 2, width), struct(hidden // 2, width),
            struct(half, hidden), struct(half, hidden),
            struct(1, hidden, dtype=F32), struct(4, width, dtype=F32),
        ],
        compiler_params=params(),
        cost_estimate=cost(12 * total * width * hidden, 40e6),
        name="feed_forward",
    )(
        at, keep_mask, grad_patches, *got_grad, grad_specials, h, a2, a2t, fc1_weight, row(fc1_bias),
        fc2_weight, row(fc2_bias), row(ln2_gain),
    )
    out_chunks, (dh, dy, w2s, w2k, w1s, w1k, db1, small2) = outs[:4], outs[4:]
    out_rows, out_specials = settle(send_back(out_chunks, groups), at, groups, part, ns)

    dqkv, cs, ck, ds_, dk_, flat = pl.pallas_call(
        partial(heads_kernel, heads=heads),
        grid=(n,),
        in_specs=[
            per_image(padded, width), per_image(heads, padded, padded), per_image(padded, 3 * width),
            per_image(width, padded), per_image(width, padded), whole(proj_weight.shape),
        ],
        out_specs=[
            per_image(padded, 3 * width), *[whole((half, 2 * width))] * 4, whole((1, 3 * width)),
        ],
        out_shape=[
            struct(n, padded, 3 * width), *[struct(half, 2 * width)] * 4,
            struct(1, 3 * width, dtype=F32),
        ],
        scratch_shapes=[pltpu.VMEM((width, 3 * width), F32), pltpu.VMEM((width, width), F32)],
        compiler_params=params(),
        cost_estimate=cost(2 * total * width * 6 * width, 20e6),
        name="attention_backward",
    )(dy, prob, qkv, a1t, ot, proj_weight)

    outs = pl.pallas_call(
        partial(input_kernel, part=part, ns=ns),
        grid=(n,),
        in_specs=[
            per_image(padded, 3 * width), whole(qkv_weight.shape), per_image(padded, width),
            per_image(padded, width), whole((1, width)),
        ],
        out_specs=[*[per_image(part + ns, width)] * 4, whole((2, width))],
        out_shape=[*[struct(n, part + ns, width)] * 4, struct(2, width, dtype=F32)],
        scratch_shapes=[pltpu.VMEM((padded, width), F32)],
        compiler_params=params(),
        cost_estimate=cost(2 * total * width * 3 * width, 10e6),
        name="input_backward",
    )(dqkv, qkv_weight, xs, dh, row(ln1_gain))
    dx_rows, dx_specials = settle(send_back(outs[:4], groups), at, groups, part, ns)
    small1 = outs[4]

    def swap(v, bit):
        return lax.ppermute(v, "dp", [(s, s ^ bit) for s in range(replicas)])

    ring = ([(0, 1), (1, 0), (2, 3), (3, 2)], [(0, 3), (3, 0), (1, 2), (2, 1)])

    def total_of(sent, kept, x_first):
        v = kept + swap(sent, 1)
        v = v.reshape(2, 2, -1, v.shape[1])
        if x_first:
            v = v[:, 0] + swap(v[:, 1], 2)
            v = v[0] + swap(v[1], 4)
        else:
            v = v[0] + swap(v[1], 4)
            v = v[0] + swap(v[1], 2)
        for way in ring if x_first else ring[::-1]:
            v = v + lax.ppermute(v, "seq", way)
        return v.astype(F32)

    def natural(sent, kept):
        v = jnp.stack([kept, sent]).reshape(2, OWNERS // 2, -1, kept.shape[1])
        v = v.transpose(1, 0, 2, 3).reshape(-1, kept.shape[1])
        v = lax.psum_scatter(v, "dp", scatter_dimension=0, tiled=True)
        return lax.psum(v, "seq").astype(F32)

    def reduce(sent, kept, x_first):
        return total_of(sent, kept, x_first) if direct else natural(sent, kept)

    d_fc1 = reduce(w1s, w1k, True)
    d_fc2 = reduce(w2s, w2k, False)
    d_qk = reduce(cs, ck, True)
    d_vp = reduce(ds_, dk_, False)
    d_qkv = jnp.concatenate([d_qk, d_vp[:, :width]], axis=1)
    d_proj = d_vp[:, width:]

    flat = flat.reshape(3, width)
    vectors = jnp.concatenate([small1, flat[0:1], flat[2:3], small2, db1.reshape(-1, width)], axis=0)
    vectors = lax.psum(vectors, ("dp", "seq"))
    mine = lax.axis_index("dp")
    wide = vectors[8:].reshape(-1)

    def shard(v):
        size = v.shape[-1] // replicas
        return lax.dynamic_slice_in_dim(v, mine * size, size, axis=v.ndim - 1)

    s = shard(vectors[:8])
    return (
        out_rows, out_specials, dx_rows, dx_specials,
        s[0], s[1], d_qkv, s[2:4], d_proj, s[7], s[4], s[5], d_fc1, shard(wide), d_fc2, s[6],
    )


def solution(mesh):
    rows = P("dp", "seq", None)
    lead = P("dp", None, None)
    flat = P("dp")
    matrix = P("dp", None)
    return jax.shard_map(
        shards,
        mesh=mesh,
        in_specs=(rows, lead, matrix, *[P()] * 12, rows, lead),
        out_specs=(
            rows, lead, rows, lead, flat, flat, matrix, P(None, "dp"), matrix, flat, flat, flat,
            matrix, flat, matrix, flat,
        ),
        check_vma=False,
    )
```

time: 754 us -> 342 us (0.45)
  blocking collectives: 185 us -> 50.2 us
  matrix products: 126 us -> 0 us
  waiting for transfers between devices: 202 us -> 86.8 us
  Pallas kernels: 0 us -> 100 us
  local copies, waits for them, and re-layouts: 119 us -> 24.3 us
  other arithmetic: 77.8 us -> 20.7 us
  starting transfers between devices: 20.9 us -> 57.3 us
  between operations: 16.2 us -> 1.09 us
    all_gather x2 -> x0, blocking collectives: 147 us -> none  [the longest x1 112 us: shards(): special_back = lax.all_gather(grad_heads[:, :2], 'seq', axis=3, tiled=True)]
    dot_general x17 -> x0, matrix products: 118 us -> none  [the longest x4 32.2 us: weight_grad(): jnp.einsum('brd,bre->de', row_block, upstream, preferred_element_type=jnp...]
    all_to_all x4 -> x0, waiting for transfers between devices: 113 us -> none  [the longest x1 86.3 us: shards(): lax.all_to_all(qkv_rows[:, 2:], 'seq', split_axis=3, concat_axis=1, tiled...]
    pallas_call x0 -> x6, Pallas kernels: none -> 100 us  [the longest x1 43.4 us: shards(): pl.pallas_call(partial(feed_kernel, images=n, rows=rows), grid_spec=pltpu...]
    ppermute x0 -> x32, waiting for transfers between devices: none -> 86.8 us  [the longest x8 35.2 us: total_of(): v = v + lax.ppermute(v, 'seq', way)]
    convert_element_type x28 -> x5, other arithmetic: 60.1 us -> 2.29 us  [the longest x4 2.27 us: total_of(): return v.astype(F32)]
    ppermute x0 -> x32, starting transfers between devices: none -> 57.3 us  [the longest x8 28 us: total_of(): v = v + lax.ppermute(v, 'seq', way)]
    psum x1 -> x0, waiting for transfers between devices: 49.6 us -> none  [shards(): lax.psum(all_shares[2].astype(jnp.bfloat16), 'seq').astype(jnp.float32)]
  transfers between devices with their start and end apart: 10 -> 32, of which waited for: 4 -> 11; matrix products, arithmetic and copies ran while one was open for 24% -> 11% of each run, Pallas kernels for 0% -> 9%
where the time goes in v1:
time: 342 us; the launch traced here: 341 us
  Pallas kernels  100 us (29%)
  waiting for transfers between devices  86.8 us (25%)
  starting transfers between devices  57.3 us (17%)
  blocking collectives  50.2 us (15%)
  local copies, waits for them, and re-layouts  24.3 us (7%)
  other arithmetic  20.7 us (6%)
    psum x1, blocking collectives, shards(): vectors = lax.psum(vectors, ('dp', 'seq'))  50.2 us
    pallas_call x1, Pallas kernels, shards(): pl.pallas_call(partial(feed_kernel, images=n, rows=rows), grid_spec=pltpu...  43.4 us
    ppermute x8, waiting for transfers between devices, total_of(): v = v + lax.ppermute(v, 'seq', way)  35.2 us
    ppermute x8, starting transfers between devices, total_of(): v = v + lax.ppermute(v, 'seq', way)  28 us
    pallas_call x1, Pallas kernels, shards(): pl.pallas_call(partial(heads_kernel, heads=heads), grid=(n,), in_specs=[p...  26.1 us
    ppermute x12, waiting for transfers between devices, swap(): return lax.ppermute(v, 'dp', [(s, s ^ bit) for s in range(replicas)])  24.1 us
    ppermute x6, waiting for transfers between devices, send_back(): lax.ppermute(c, 'seq', [(s, (s - k) % groups) for s in range(groups)])  16.8 us
    pallas_call x1, Pallas kernels, shards(): pl.pallas_call(partial(forward_kernel, rows=rows, heads=heads), grid_spec...  15.4 us
  transfers between devices with their start and end apart: 32, of which 11 were waited for; matrix products, arithmetic and copies ran while one was open for 11% of the time, Pallas kernels for 9%

profile of v1, /device:TPU:0, one launch (start us, length us, event | category | flops | bytes accessed | tf_op | source)
XLA Modules:
  0.0 340.9 jit_solution(7964709305792398976)
XLA Ops:
  0.7 1.3 constant_dynamic-slice_fusion.1
  2.1 3.1 collective-permute-start.3
  5.2 2.6 collective-permute-start.4
  7.8 1.3 collective-permute-start.5
  9.2 0.7 collective-permute-start
  16.5 2.8 collective-permute-start.2
  19.3 6.3 %collective-permute-done.4.x2 = bf16[3,49,768]{2,1,0:T(8,128)(2,1)S(1)} collective-permute-done((bf16[3,49,768]{2,1,0:T(8,128)(2,1)S(1)}, bf16[3,49,768]{2,1,0:T(8,128)(2,1)S(1)}, u32[]{:S(2)}, u32[]{:S(2)}) %collective-permute-start.4) | collective-permute-done | bytes 225824 | tf_op jit(solution)/shard_map/ppermute | solution.py:334
  26.2 0.7 copy-done.23
  26.9 15.4 %attention_forward.1 = (bf16[3,208,768]{2,1,0:T(8,128)(2,1)}, bf16[3,768,208]{2,1,0:T(8,128)(2,1)}, bf16[3,208,2304]{2,1,0:T(8,128)(2,1)}, bf16[3,12,208,208]{3,...) custom-call(s32[2]{0:T(128)} %pad_add_fusion.at, ...), custom_call_target="tpu_custom_call" | custom-call | flops 4416602112 | bytes 20000000 | tf_op jit(solution)/shard_map/attention_forward/pallas_call | solution.py:399
  42.4 4.4 %collective-permute-done.1.g2 = bf16[3,49,768]{2,1,0:T(8,128)(2,1)S(1)} collective-permute-done((bf16[3,49,768]{2,1,0:T(8,128)(2,1)S(1)}, bf16[3,49,768]{2,1,0:T(8,128)(2,1)S(1)}, u32[]{:S(2)}, u32[]{:S(2)}) %collective-permute-start.1) | collective-permute-done | bytes 225824 | tf_op jit(solution)/shard_map/ppermute | solution.py:334
  47.6 43.4 %feed_forward.1 = (bf16[3,51,768]{2,1,0:T(8,128)(2,1)}, bf16[3,51,768]{2,1,0:T(8,128)(2,1)}, bf16[3,51,768]{2,1,0:T(8,128)(2,1)}, bf16[3,51,768]{2,1,0:T(8,128)(...) custom-call(s32[2]{0:T(128)} %pad_add_fusion.at, ...), custom_call_target="tpu_custom_call" | custom-call | flops 17666408448 | bytes 40000000 | tf_op jit(solution)/shard_map/feed_forward/pallas_call | solution.py:438
  91.0 26.1 %attention_backward.1 = (bf16[3,208,2304]{2,1,0:T(8,128)(2,1)}, bf16[384,1536]{1,0:T(8,128)(2,1)}, bf16[384,1536]{1,0:T(8,128)(2,1)}, bf16[384,1536]{1,0:T(8,128...) custom-call(bf16[3,208,768]{2,1,0:T(8,128)(2,1)} %get-tuple-element.60.dy, ...), custom_call_target="tpu_custom_call" | custom-call | flops 4416602112 | bytes 20000000 | tf_op jit(solution)/shard_map/attention_backward/pallas_call | solution.py:486
  118.2 1.3 fusion.9
  119.5 1.7 collective-permute-done.12
  121.1 1.0 copy-done.2
  122.2 1.9 add.115
  124.1 0.9 slice_bitcast_fusion.6
  124.9 1.4 collective-permute-start.13
  126.4 8.2 %input_backward.1 = (bf16[3,51,768]{2,1,0:T(8,128)(2,1)}, bf16[3,51,768]{2,1,0:T(8,128)(2,1)}, bf16[3,51,768]{2,1,0:T(8,128)(2,1)}, bf16[3,51,768]{2,1,0:T(8,128)(2,1)}, f32[2,768]{1,0:T(2,128)}) custom-call(bf16[3,208,2304]{2,1,0:T(8,128)(2,1)} %get-tuple-element.65.dqkv, bf16[768,2304]{1,0:T(8,128)(2,1)} %wq.3, bf16[3,208,768]{2,1,0:T(8,128)(2,1)} %get-tuple-element.66.xs, ...), custom_call_target="tpu_custom_call" | custom-call | flops 2208301056 | bytes 10000000 | tf_op jit(solution)/shard_map/input_backward/pallas_call | solution.py:506
  135.1 1.4 reduce.7
  137.1 2.7 concatenate.10
  139.8 50.2 %psum.7 = f32[12,768]{1,0:T(8,128)} all-reduce(f32[12,768]{1,0:T(8,128)} %concatenate.10), channel_id=1, replica_groups=mesh['dp'=8,'seq'=4] {'dp','seq'}, use_global_device_ids=true, to_apply=%region_0.1 | all-reduce | flops 9216 | bytes 73728 | tf_op jit(solution)/shard_map/psum | solution.py:559
  190.0 2.9 collective-permute-start.10
  193.0 1.9 add.120
  195.0 2.3 collective-permute-start.18
  197.3 1.1 fusion.3
  198.5 11.2 %collective-permute-done.18 = bf16[2,96,1536]{2,1,0:T(8,128)(2,1)S(1)} collective-permute-done((bf16[2,96,1536]{2,1,0:T(8,128)(2,1)S(1)}, bf16[2,96,1536]{2,1,0:T(8,128)(2,1)S(1)}, u32[]{:S(2)}, u32[]{:S(2)}) %collective-permute-start.18) | collective-permute-done | bytes 589856 | tf_op jit(solution)/shard_map/ppermute | solution.py:524
  209.6 1.7 collective-permute-start.14
  212.1 0.9 copy-done.1
  213.0 0.7 add.131
  213.8 1.2 fusion.6
  215.8 2.5 add.125
  218.4 1.1 slice_bitcast_fusion
  219.5 1.1 collective-permute-start.23
  220.7 0.7 fusion.5
  221.4 3.8 %collective-permute-start.9 = (bf16[3,51,768]{2,1,0:T(8,128)(2,1)S(1)}, bf16[3,51,768]{2,1,0:T(8,128)(2,1)S(1)}, u32[]{:S(2)}, u32[]{:S(2)}) collective-permute-start(bf16[3,51,768]{2,1,0:T(8,128)(2,1)S(1)} %copy-done.18), channel_id=1, source_target_pairs={{0,3},{1,0},{2,1},{3,2},{4,7},{5,4},{6,5},{7,6},{8,11},{9,8},{10,9... | collective-permute-start | bytes 705032 | tf_op jit(solution)/shard_map/ppermute | solution.py:340
  225.3 0.7 fusion.4
  226.1 5.8 %collective-permute-done.9.c1 = bf16[3,51,768]{2,1,0:T(8,128)(2,1)S(1)} collective-permute-done((bf16[3,51,768]{2,1,0:T(8,128)(2,1)S(1)}, bf16[3,51,768]{2,1,0:T(8,128)(2,1)S(1)}, u32[]{:S(2)}, u32[]{:S(2)}) %collective-permute-start.9) | collective-permute-done | bytes 235040 | tf_op jit(solution)/shard_map/ppermute | solution.py:340
  231.9 0.7 copy-done.6
  233.0 5.0 %collective-permute-done.6.c1 = bf16[3,51,768]{2,1,0:T(8,128)(2,1)} collective-permute-done((bf16[3,51,768]{2,1,0:T(8,128)(2,1)S(1)}, bf16[3,51,768]{2,1,0:T(8,128)(2,1)}, u32[]{:S(2)}, u32[]{:S(2)}) %collective-permute-start.6) | collective-permute-done | bytes 235040 | tf_op jit(solution)/shard_map/ppermute | solution.py:340
  238.1 5.6 %collective-permute-start.15 = (bf16[96,1536]{1,0:T(8,128)(2,1)}, bf16[96,1536]{1,0:T(8,128)(2,1)}, u32[]{:S(2)}, u32[]{:S(2)}) collective-permute-start(bf16[96,1536]{1,0:T(8,128)(2,1)} %fusion.5), channel_id=1, source_target_pairs={{0,1},{1,0},{2,3},{3,2},{4,5},{5,4},{6,7},{7,6},{8,9},{9,8},{10,11... | collective-permute-start | bytes 884744 | tf_op jit(solution)/shard_map/ppermute | solution.py:538
  243.6 6.0 %collective-permute-done.7.c2 = bf16[3,51,768]{2,1,0:T(8,128)(2,1)} collective-permute-done((bf16[3,51,768]{2,1,0:T(8,128)(2,1)S(1)}, bf16[3,51,768]{2,1,0:T(8,128)(2,1)}, u32[]{:S(2)}, u32[]{:S(2)}) %collective-permute-start.7) | collective-permute-done | bytes 235040 | tf_op jit(solution)/shard_map/ppermute | solution.py:340
  250.9 1.3 dynamic_slice.31
  252.8 3.6 %settle.3 = (bf16[12,49,768]{2,1,0:T(8,128)(2,1)}, bf16[12,2,768]{2,1,0:T(2,128)(2,1)}) custom-call(s32[2]{0:T(128)} %pad_add_fusion.at, bf16[3,51,768]{2,1,0:T(8,128)(2,1)} %get-tuple-element.68.c0, bf16[3,51,768]{2,1,0:T(8,128)(2,1)} %copy-done.6, bf16[3,51,768]{2,1,0:T(8,128)(2,1)} %copy-done.4, bf16[3,51,768]{2,1,0:T(8,128)(2,1)} %copy-done.5), custom_call_target="tpu_custom_call" | custom-call | tf_op jit(solution)/shard_map/settle/pallas_call | solution.py:348
  256.4 3.6 %settle.2 = (bf16[12,49,768]{2,1,0:T(8,128)(2,1)}, bf16[12,2,768]{2,1,0:T(2,128)(2,1)}) custom-call(s32[2]{0:T(128)} %pad_add_fusion.at, bf16[3,51,768]{2,1,0:T(8,128)(2,1)} %get-tuple-element.54.c0, bf16[3,51,768]{2,1,0:T(8,128)(2,1)} %collective-permute-done.6.c1, bf16[3,51,768]{2,1,0:T(8,128)(2,1)} %collective-permute-done.7.c2, ...), custom_call_target="tpu_custom_call" | custom-call | tf_op jit(solution)/shard_map/settle/pallas_call | solution.py:348
  260.0 1.1 add.118
  261.2 3.9 %collective-permute-start.16 = (bf16[96,1536]{1,0:T(8,128)(2,1)S(1)}, bf16[96,1536]{1,0:T(8,128)(2,1)S(1)}, u32[]{:S(2)}, u32[]{:S(2)}) collective-permute-start(bf16[96,1536]{1,0:T(8,128)(2,1)S(1)} %add.118), channel_id=1, source_target_pairs={{0,3},{3,0},{1,2},{2,1},{4,7},{7,4},{5,6},{6,5},{8,11},{11,8},{9,1... | collective-permute-start | bytes 884744 | tf_op jit(solution)/shard_map/ppermute | solution.py:538
  265.1 1.1 add.123
  266.2 2.0 collective-permute-start.21
  268.2 1.5 add.132
  269.8 1.3 collective-permute-start.29
  271.0 1.4 fusion
  272.5 0.9 collective-permute-start.24
  273.4 11.3 %collective-permute-done.29 = bf16[384,768]{1,0:T(8,128)(2,1)S(1)} collective-permute-done((bf16[384,768]{1,0:T(8,128)(2,1)S(1)}, bf16[384,768]{1,0:T(8,128)(2,1)S(1)}, u32[]{:S(2)}, u32[]{:S(2)}) %collective-permute-start.29) | collective-permute-done | bytes 589856 | tf_op jit(solution)/shard_map/ppermute | solution.py:524
  284.8 3.4 %collective-permute-start.30 = (bf16[384,768]{1,0:T(8,128)(2,1)S(1)}, bf16[384,768]{1,0:T(8,128)(2,1)S(1)}, u32[]{:S(2)}, u32[]{:S(2)}) collective-permute-start(bf16[384,768]{1,0:T(8,128)(2,1)S(1)} %fusion.1), channel_id=1, source_target_pairs={{0,3},{3,0},{1,2},{2,1},{4,7},{7,4},{5,6},{6,5},{8,11},{11,8},{9,1... | collective-permute-start | bytes 1769480 | tf_op jit(solution)/shard_map/ppermute | solution.py:538
  288.4 14.5 %collective-permute-done.30 = bf16[384,768]{1,0:T(8,128)(2,1)S(1)} collective-permute-done((bf16[384,768]{1,0:T(8,128)(2,1)S(1)}, bf16[384,768]{1,0:T(8,128)(2,1)S(1)}, u32[]{:S(2)}, u32[]{:S(2)}) %collective-permute-start.30) | collective-permute-done | bytes 589856 | tf_op jit(solution)/shard_map/ppermute | solution.py:538
  303.1 9.9 %collective-permute-start.31 = (bf16[384,768]{1,0:T(8,128)(2,1)S(1)}, bf16[384,768]{1,0:T(8,128)(2,1)S(1)}, u32[]{:S(2)}, u32[]{:S(2)}) collective-permute-start(bf16[384,768]{1,0:T(8,128)(2,1)S(1)} %add.134), channel_id=1, source_target_pairs={{0,1},{1,0},{2,3},{3,2},{4,5},{5,4},{6,7},{7,6},{8,9},{9,8},{10,11... | collective-permute-start | bytes 1769480 | tf_op jit(solution)/shard_map/ppermute | solution.py:538
  313.0 0.8 fusion.8
  314.0 3.1 collective-permute-start.26
  317.0 1.0 pad_maximum_fusion
  318.0 9.7 %collective-permute-done.31 = bf16[384,768]{1,0:T(8,128)(2,1)S(1)} collective-permute-done((bf16[384,768]{1,0:T(8,128)(2,1)S(1)}, bf16[384,768]{1,0:T(8,128)(2,1)S(1)}, u32[]{:S(2)}, u32[]{:S(2)}) %collective-permute-start.31) | collective-permute-done | bytes 589856 | tf_op jit(solution)/shard_map/ppermute | solution.py:538
  327.7 1.1 add_convert_fusion
  328.8 11.0 %collective-permute-done.26 = bf16[96,3072]{1,0:T(8,128)(2,1)S(1)} collective-permute-done((bf16[96,3072]{1,0:T(8,128)(2,1)S(1)}, bf16[96,3072]{1,0:T(8,128)(2,1)S(1)}, u32[]{:S(2)}, u32[]{:S(2)}) %collective-permute-start.26) | collective-permute-done | bytes 589856 | tf_op jit(solution)/shard_map/ppermute | solution.py:538
  339.8 1.1 add_convert_fusion.1
  (116 shorter events, 15.2 us)
Async XLA Ops:
  0.6 8.5 %copy-start.3 = (bf16[12,49,768]{2,1,0:T(8,128)(2,1)S(1)}, bf16[12,49,768]{2,1,0:T(8,128)(2,1)}, u32[]{:S(2)}) copy-start(bf16[12,49,768]{2,1,0:T(8,128)(2,1)} %g0.1) | copy-start | bytes 2709508
  0.7 9.6 %copy-start.7 = (bf16[2,768]{1,0:T(2,128)(2,1)S(1)}, bf16[2,768]{1,0:T(2,128)(2,1)}, u32[]{:S(2)}) copy-start(bf16[2,768]{1,0:T(2,128)(2,1)} %param.23) | copy-start | bytes 9220
  2.0 8.9 %copy-start.15 = (s32[12,2]{0,1:T(2,128)S(1)}, s32[12,2]{0,1:T(2,128)}, u32[]{:S(2)}) copy-start(s32[12,2]{0,1:T(2,128)} %param.19) | copy-start | bytes 292
  2.1 9.6 %copy-start.9 = (bf16[768]{0:T(1024)(128)(2,1)S(1)}, bf16[768]{0:T(1024)(128)(2,1)}, u32[]{:S(2)}) copy-start(bf16[768]{0:T(1024)(128)(2,1)} %param.20) | copy-start | bytes 4612
  2.1 10.2 %copy-start.10 = (bf16[768]{0:T(1024)(128)(2,1)S(1)}, bf16[768]{0:T(1024)(128)(2,1)}, u32[]{:S(2)}) copy-start(bf16[768]{0:T(1024)(128)(2,1)} %param.26) | copy-start | bytes 4612
  2.1 10.8 %copy-start.11 = (bf16[768]{0:T(1024)(128)(2,1)S(1)}, bf16[768]{0:T(1024)(128)(2,1)}, u32[]{:S(2)}) copy-start(bf16[768]{0:T(1024)(128)(2,1)} %param.21) | copy-start | bytes 4612
  2.1 11.4 %copy-start.12 = (bf16[768]{0:T(1024)(128)(2,1)S(1)}, bf16[768]{0:T(1024)(128)(2,1)}, u32[]{:S(2)}) copy-start(bf16[768]{0:T(1024)(128)(2,1)} %param.25) | copy-start | bytes 4612
  2.1 11.9 %copy-start.13 = (bf16[768]{0:T(1024)(128)(2,1)S(1)}, bf16[768]{0:T(1024)(128)(2,1)}, u32[]{:S(2)}) copy-start(bf16[768]{0:T(1024)(128)(2,1)} %param.27) | copy-start | bytes 4612
  2.1 12.5 %copy-start.8 = (bf16[3072]{0:T(1024)(128)(2,1)S(1)}, bf16[3072]{0:T(1024)(128)(2,1)}, u32[]{:S(2)}) copy-start(bf16[3072]{0:T(1024)(128)(2,1)} %param.29) | copy-start | bytes 18436
  2.1 13.1 %copy-start.14 = (bf16[768]{0:T(1024)(128)(2,1)S(1)}, bf16[768]{0:T(1024)(128)(2,1)}, u32[]{:S(2)}) copy-start(bf16[768]{0:T(1024)(128)(2,1)} %param.31) | copy-start | bytes 4612
  2.1 14.3 %collective-permute-start.3 = (bf16[3,49,768]{2,1,0:T(8,128)(2,1)S(1)}, bf16[3,49,768]{2,1,0:T(8,128)(2,1)S(1)}, u32[]{:S(2)}, u32[]{:S(2)}) collective-permute-start(bf16[3,49,768]{2,1,0:T(8,128)(2,1)S(1)} %get-tuple-element.94), channel_id=1, source_target_pairs={{0,1},{1,2},{2,3},{3,0},{4,5},{5,6},{6,7},{7,4},{8,9},{9,10},{10,1... | collective-permute-start | bytes 677384 | tf_op jit(solution)/shard_map/ppermute | solution.py:334
  5.2 20.3 %collective-permute-start.4 = (bf16[3,49,768]{2,1,0:T(8,128)(2,1)S(1)}, bf16[3,49,768]{2,1,0:T(8,128)(2,1)S(1)}, u32[]{:S(2)}, u32[]{:S(2)}) collective-permute-start(bf16[3,49,768]{2,1,0:T(8,128)(2,1)S(1)} %get-tuple-element.93), channel_id=1, source_target_pairs={{0,2},{1,3},{2,0},{3,1},{4,6},{5,7},{6,4},{7,5},{8,10},{9,11},{10,... | collective-permute-start | bytes 677384 | tf_op jit(solution)/shard_map/ppermute | solution.py:334
  7.8 17.7 %collective-permute-start.5 = (bf16[3,49,768]{2,1,0:T(8,128)(2,1)S(1)}, bf16[3,49,768]{2,1,0:T(8,128)(2,1)S(1)}, u32[]{:S(2)}, u32[]{:S(2)}) collective-permute-start(bf16[3,49,768]{2,1,0:T(8,128)(2,1)S(1)} %get-tuple-element.92), channel_id=1, source_target_pairs={{0,3},{1,0},{2,1},{3,2},{4,7},{5,4},{6,5},{7,6},{8,11},{9,8},{10,9... | collective-permute-start | bytes 677384 | tf_op jit(solution)/shard_map/ppermute | solution.py:334
  9.2 33.1 %collective-permute-start = (bf16[3,49,768]{2,1,0:T(8,128)(2,1)S(1)}, bf16[3,49,768]{2,1,0:T(8,128)(2,1)S(1)}, u32[]{:S(2)}, u32[]{:S(2)}) collective-permute-start(bf16[3,49,768]{2,1,0:T(8,128)(2,1)S(1)} %get-tuple-element.97), channel_id=1, source_target_pairs={{0,1},{1,2},{2,3},{3,0},{4,5},{5,6},{6,7},{7,4},{8,9},{9,10},{10,1... | collective-permute-start | bytes 677384 | tf_op jit(solution)/shard_map/ppermute | solution.py:334
  10.0 36.8 %collective-permute-start.1 = (bf16[3,49,768]{2,1,0:T(8,128)(2,1)S(1)}, bf16[3,49,768]{2,1,0:T(8,128)(2,1)S(1)}, u32[]{:S(2)}, u32[]{:S(2)}) collective-permute-start(bf16[3,49,768]{2,1,0:T(8,128)(2,1)S(1)} %get-tuple-element.96), channel_id=1, source_target_pairs={{0,2},{1,3},{2,0},{3,1},{4,6},{5,7},{6,4},{7,5},{8,10},{9,11},{10,... | collective-permute-start | bytes 677384 | tf_op jit(solution)/shard_map/ppermute | solution.py:334
  16.5 9.1 %copy-start.21 = (bf16[3,49,768]{2,1,0:T(8,128)(2,1)}, bf16[3,49,768]{2,1,0:T(8,128)(2,1)S(1)}, u32[]{:S(2)}) copy-start(bf16[3,49,768]{2,1,0:T(8,128)(2,1)S(1)} %collective-permute-done.3.x1) | copy-start | bytes 677380
  16.5 30.4 %collective-permute-start.2 = (bf16[3,49,768]{2,1,0:T(8,128)(2,1)S(1)}, bf16[3,49,768]{2,1,0:T(8,128)(2,1)S(1)}, u32[]{:S(2)}, u32[]{:S(2)}) collective-permute-start(bf16[3,49,768]{2,1,0:T(8,128)(2,1)S(1)} %get-tuple-element.95), channel_id=1, source_target_pairs={{0,3},{1,0},{2,1},{3,2},{4,7},{5,4},{6,5},{7,6},{8,11},{9,8},{10,9... | collective-permute-start | bytes 677384 | tf_op jit(solution)/shard_map/ppermute | solution.py:334
  25.5 0.7 copy-start.22
  26.2 0.7 copy-start.23
  42.4 4.5 %copy-start.19 = (bf16[3,49,768]{2,1,0:T(8,128)(2,1)}, bf16[3,49,768]{2,1,0:T(8,128)(2,1)S(1)}, u32[]{:S(2)}) copy-start(bf16[3,49,768]{2,1,0:T(8,128)(2,1)S(1)} %collective-permute-done.g1) | copy-start | bytes 677380
  46.8 0.7 copy-start.20
  46.8 0.8 copy-start.24
  117.1 4.0 %collective-permute-start.12 = (bf16[384,1536]{1,0:T(8,128)(2,1)}, bf16[384,1536]{1,0:T(8,128)(2,1)S(1)}, u32[]{:S(2)}, u32[]{:S(2)}) collective-permute-start(bf16[384,1536]{1,0:T(8,128)(2,1)} %get-tuple-element.79), channel_id=1, source_target_pairs={{0,4},{4,0},{8,12},{12,8},{16,20},{20,16},{24,28},{28,24},{1,5},{5... | collective-permute-start | bytes 3538952 | tf_op jit(solution)/shard_map/ppermute | solution.py:524
  117.2 75.8 %collective-permute-start.17 = (bf16[384,1536]{1,0:T(8,128)(2,1)}, bf16[384,1536]{1,0:T(8,128)(2,1)}, u32[]{:S(2)}, u32[]{:S(2)}) collective-permute-start(bf16[384,1536]{1,0:T(8,128)(2,1)} %get-tuple-element.81), channel_id=1, source_target_pairs={{0,4},{4,0},{8,12},{12,8},{16,20},{20,16},{24,28},{28,24},{1,5},{5... | collective-permute-start | bytes 3538952 | tf_op jit(solution)/shard_map/ppermute | solution.py:524
  117.7 93.8 %collective-permute-start.27 = (bf16[1536,768]{1,0:T(8,128)(2,1)}, bf16[1536,768]{1,0:T(8,128)(2,1)S(1)}, u32[]{:S(2)}, u32[]{:S(2)}) collective-permute-start(bf16[1536,768]{1,0:T(8,128)(2,1)} %get-tuple-element.85), channel_id=1, source_target_pairs={{0,4},{4,0},{8,12},{12,8},{16,20},{20,16},{24,28},{28,24},{1,5},{5... | collective-permute-start | bytes 7077896 | tf_op jit(solution)/shard_map/ppermute | solution.py:524
  117.8 97.2 %collective-permute-start.22 = (bf16[384,3072]{1,0:T(8,128)(2,1)}, bf16[384,3072]{1,0:T(8,128)(2,1)}, u32[]{:S(2)}, u32[]{:S(2)}) collective-permute-start(bf16[384,3072]{1,0:T(8,128)(2,1)} %get-tuple-element.83), channel_id=1, source_target_pairs={{0,4},{4,0},{8,12},{12,8},{16,20},{20,16},{24,28},{28,24},{1,5},{5... | collective-permute-start | bytes 7077896 | tf_op jit(solution)/shard_map/ppermute | solution.py:524
  121.1 1.0 copy-start.2
  124.9 70.1 %collective-permute-start.13 = (bf16[2,96,1536]{2,1,0:T(8,128)(2,1)}, bf16[2,96,1536]{2,1,0:T(8,128)(2,1)}, u32[]{:S(2)}, u32[]{:S(2)}) collective-permute-start(bf16[2,96,1536]{2,1,0:T(8,128)(2,1)} %slice_bitcast_fusion.6), channel_id=1, source_target_pairs={{0,8},{4,12},{8,0},{12,4},{16,24},{20,28},{24,16},{28,20},{1,9},{5... | collective-permute-start | bytes 1769480 | tf_op jit(solution)/shard_map/ppermute | solution.py:524
  190.0 31.4 %collective-permute-start.10 = (bf16[3,51,768]{2,1,0:T(8,128)(2,1)}, bf16[3,51,768]{2,1,0:T(8,128)(2,1)S(1)}, u32[]{:S(2)}, u32[]{:S(2)}) collective-permute-start(bf16[3,51,768]{2,1,0:T(8,128)(2,1)} %get-tuple-element.70), channel_id=1, source_target_pairs={{0,2},{1,3},{2,0},{3,1},{4,6},{5,7},{6,4},{7,5},{8,10},{9,11},{10,... | collective-permute-start | bytes 705032 | tf_op jit(solution)/shard_map/ppermute | solution.py:340
  193.0 32.2 %collective-permute-start.11 = (bf16[3,51,768]{2,1,0:T(8,128)(2,1)}, bf16[3,51,768]{2,1,0:T(8,128)(2,1)S(1)}, u32[]{:S(2)}, u32[]{:S(2)}) collective-permute-start(bf16[3,51,768]{2,1,0:T(8,128)(2,1)} %get-tuple-element.71), channel_id=1, source_target_pairs={{0,1},{1,2},{2,3},{3,0},{4,5},{5,6},{6,7},{7,4},{8,9},{9,10},{10,1... | collective-permute-start | bytes 705032 | tf_op jit(solution)/shard_map/ppermute | solution.py:340
  195.0 14.6 %collective-permute-start.18 = (bf16[2,96,1536]{2,1,0:T(8,128)(2,1)S(1)}, bf16[2,96,1536]{2,1,0:T(8,128)(2,1)S(1)}, u32[]{:S(2)}, u32[]{:S(2)}) collective-permute-start(bf16[2,96,1536]{2,1,0:T(8,128)(2,1)S(1)} %bitcast.70), channel_id=1, source_target_pairs={{0,16},{4,20},{8,24},{12,28},{16,0},{20,4},{24,8},{28,12},{1,17},{... | collective-permute-start | bytes 1769480 | tf_op jit(solution)/shard_map/ppermute | solution.py:524
  209.6 9.9 %collective-permute-start.14 = (bf16[96,1536]{1,0:T(8,128)(2,1)S(1)}, bf16[96,1536]{1,0:T(8,128)(2,1)S(1)}, u32[]{:S(2)}, u32[]{:S(2)}) collective-permute-start(bf16[96,1536]{1,0:T(8,128)(2,1)S(1)} %slice_bitcast_fusion.10), channel_id=1, source_target_pairs={{0,16},{4,20},{8,24},{12,28},{16,0},{20,4},{24,8},{28,12},{1,17},{... | collective-permute-start | bytes 884744 | tf_op jit(solution)/shard_map/ppermute | solution.py:524
  211.4 1.7 copy-start.1
  211.5 13.7 %collective-permute-start.19 = (bf16[96,1536]{1,0:T(8,128)(2,1)S(1)}, bf16[96,1536]{1,0:T(8,128)(2,1)S(1)}, u32[]{:S(2)}, u32[]{:S(2)}) collective-permute-start(bf16[96,1536]{1,0:T(8,128)(2,1)S(1)} %slice_bitcast_fusion.8), channel_id=1, source_target_pairs={{0,8},{4,12},{8,0},{12,4},{16,24},{20,28},{24,16},{28,20},{1,9},{5... | collective-permute-start | bytes 884744 | tf_op jit(solution)/shard_map/ppermute | solution.py:524
  213.8 2.1 copy-start
  214.9 53.2 %collective-permute-start.28 = (bf16[2,384,768]{2,1,0:T(8,128)(2,1)}, bf16[2,384,768]{2,1,0:T(8,128)(2,1)}, u32[]{:S(2)}, u32[]{:S(2)}) collective-permute-start(bf16[2,384,768]{2,1,0:T(8,128)(2,1)} %bitcast.22), channel_id=1, source_target_pairs={{0,16},{4,20},{8,24},{12,28},{16,0},{20,4},{24,8},{28,12},{1,17},{... | collective-permute-start | bytes 3538952 | tf_op jit(solution)/shard_map/ppermute | solution.py:524
  218.4 3.0 copy-start.18
  218.4 6.8 %copy-start.17 = (bf16[3,51,768]{2,1,0:T(8,128)(2,1)S(1)}, bf16[3,51,768]{2,1,0:T(8,128)(2,1)}, u32[]{:S(2)}) copy-start(bf16[3,51,768]{2,1,0:T(8,128)(2,1)} %get-tuple-element.55) | copy-start | bytes 705028
  218.4 6.9 %copy-start.16 = (bf16[3,51,768]{2,1,0:T(8,128)(2,1)S(1)}, bf16[3,51,768]{2,1,0:T(8,128)(2,1)}, u32[]{:S(2)}) copy-start(bf16[3,51,768]{2,1,0:T(8,128)(2,1)} %get-tuple-element.56) | copy-start | bytes 705028
  219.5 30.1 %slice-start = ((f32[12,768]{1,0:T(8,128)}), f32[8,768]{1,0:T(8,128)S(1)}, s32[]{:S(2)}) async-start(f32[12,768]{1,0:T(8,128)} %psum.7), calls=%async_computation | async-start | bytes 49152 | tf_op jit(solution)/shard_map/slice | solution.py:567
  219.5 30.2 %slice-start.1 = ((f32[12,768]{1,0:T(8,128)}), f32[4,768]{1,0:T(4,128)S(1)}, s32[]{:S(2)}) async-start(f32[12,768]{1,0:T(8,128)} %psum.7), calls=%async_computation.1 | async-start | bytes 24576 | tf_op jit(solution)/shard_map/slice | solution.py:561
  219.5 51.5 %collective-permute-start.23 = (bf16[2,96,3072]{2,1,0:T(8,128)(2,1)}, bf16[2,96,3072]{2,1,0:T(8,128)(2,1)}, u32[]{:S(2)}, u32[]{:S(2)}) collective-permute-start(bf16[2,96,3072]{2,1,0:T(8,128)(2,1)} %slice_bitcast_fusion), channel_id=1, source_target_pairs={{0,8},{4,12},{8,0},{12,4},{16,24},{20,28},{24,16},{28,20},{1,9},{5... | collective-permute-start | bytes 3538952 | tf_op jit(solution)/shard_map/ppermute | solution.py:524
  221.4 4.7 %copy-start.4 = (bf16[3,51,768]{2,1,0:T(8,128)(2,1)}, bf16[3,51,768]{2,1,0:T(8,128)(2,1)S(1)}, u32[]{:S(2)}) copy-start(bf16[3,51,768]{2,1,0:T(8,128)(2,1)S(1)} %collective-permute-done.10.c2) | copy-start | bytes 705028
  221.4 10.4 %collective-permute-start.9 = (bf16[3,51,768]{2,1,0:T(8,128)(2,1)S(1)}, bf16[3,51,768]{2,1,0:T(8,128)(2,1)S(1)}, u32[]{:S(2)}, u32[]{:S(2)}) collective-permute-start(bf16[3,51,768]{2,1,0:T(8,128)(2,1)S(1)} %copy-done.18), channel_id=1, source_target_pairs={{0,3},{1,0},{2,1},{3,2},{4,7},{5,4},{6,5},{7,6},{8,11},{9,8},{10,9... | collective-permute-start | bytes 705032 | tf_op jit(solution)/shard_map/ppermute | solution.py:340
  225.2 6.7 %copy-start.5 = (bf16[3,51,768]{2,1,0:T(8,128)(2,1)}, bf16[3,51,768]{2,1,0:T(8,128)(2,1)S(1)}, u32[]{:S(2)}) copy-start(bf16[3,51,768]{2,1,0:T(8,128)(2,1)S(1)} %collective-permute-done.11.c3) | copy-start | bytes 705028
  225.2 12.9 %collective-permute-start.6 = (bf16[3,51,768]{2,1,0:T(8,128)(2,1)S(1)}, bf16[3,51,768]{2,1,0:T(8,128)(2,1)}, u32[]{:S(2)}, u32[]{:S(2)}) collective-permute-start(bf16[3,51,768]{2,1,0:T(8,128)(2,1)S(1)} %copy-done.17), channel_id=1, source_target_pairs={{0,3},{1,0},{2,1},{3,2},{4,7},{5,4},{6,5},{7,6},{8,11},{9,8},{10,9... | collective-permute-start | bytes 705032 | tf_op jit(solution)/shard_map/ppermute | solution.py:340
  225.3 24.3 %collective-permute-start.7 = (bf16[3,51,768]{2,1,0:T(8,128)(2,1)S(1)}, bf16[3,51,768]{2,1,0:T(8,128)(2,1)}, u32[]{:S(2)}, u32[]{:S(2)}) collective-permute-start(bf16[3,51,768]{2,1,0:T(8,128)(2,1)S(1)} %copy-done.16), channel_id=1, source_target_pairs={{0,2},{1,3},{2,0},{3,1},{4,6},{5,7},{6,4},{7,5},{8,10},{9,11},{10,... | collective-permute-start | bytes 705032 | tf_op jit(solution)/shard_map/ppermute | solution.py:340
  231.9 0.7 copy-start.6
  232.6 23.8 %collective-permute-start.8 = (bf16[3,51,768]{2,1,0:T(8,128)(2,1)}, bf16[3,51,768]{2,1,0:T(8,128)(2,1)}, u32[]{:S(2)}, u32[]{:S(2)}) collective-permute-start(bf16[3,51,768]{2,1,0:T(8,128)(2,1)} %get-tuple-element.57), channel_id=1, source_target_pairs={{0,1},{1,2},{2,3},{3,0},{4,5},{5,6},{6,7},{7,4},{8,9},{9,10},{10,1... | collective-permute-start | bytes 705032 | tf_op jit(solution)/shard_map/ppermute | solution.py:340
  238.1 22.0 %collective-permute-start.15 = (bf16[96,1536]{1,0:T(8,128)(2,1)}, bf16[96,1536]{1,0:T(8,128)(2,1)}, u32[]{:S(2)}, u32[]{:S(2)}) collective-permute-start(bf16[96,1536]{1,0:T(8,128)(2,1)} %fusion.5), channel_id=1, source_target_pairs={{0,1},{1,0},{2,3},{3,2},{4,5},{5,4},{6,7},{7,6},{8,9},{9,8},{10,11... | collective-permute-start | bytes 884744 | tf_op jit(solution)/shard_map/ppermute | solution.py:538
  249.6 15.4 %collective-permute-start.20 = (bf16[96,1536]{1,0:T(8,128)(2,1)}, bf16[96,1536]{1,0:T(8,128)(2,1)}, u32[]{:S(2)}, u32[]{:S(2)}) collective-permute-start(bf16[96,1536]{1,0:T(8,128)(2,1)} %fusion.4), channel_id=1, source_target_pairs={{0,3},{3,0},{1,2},{2,1},{4,7},{7,4},{5,6},{6,5},{8,11},{11,8},{9,1... | collective-permute-start | bytes 884744 | tf_op jit(solution)/shard_map/ppermute | solution.py:538
  261.2 12.2 %collective-permute-start.16 = (bf16[96,1536]{1,0:T(8,128)(2,1)S(1)}, bf16[96,1536]{1,0:T(8,128)(2,1)S(1)}, u32[]{:S(2)}, u32[]{:S(2)}) collective-permute-start(bf16[96,1536]{1,0:T(8,128)(2,1)S(1)} %add.118), channel_id=1, source_target_pairs={{0,3},{3,0},{1,2},{2,1},{4,7},{7,4},{5,6},{6,5},{8,11},{11,8},{9,1... | collective-permute-start | bytes 884744 | tf_op jit(solution)/shard_map/ppermute | solution.py:538
  266.2 22.2 %collective-permute-start.21 = (bf16[96,1536]{1,0:T(8,128)(2,1)S(1)}, bf16[96,1536]{1,0:T(8,128)(2,1)S(1)}, u32[]{:S(2)}, u32[]{:S(2)}) collective-permute-start(bf16[96,1536]{1,0:T(8,128)(2,1)S(1)} %add.123), channel_id=1, source_target_pairs={{0,1},{1,0},{2,3},{3,2},{4,5},{5,4},{6,7},{7,6},{8,9},{9,8},{10,11... | collective-permute-start | bytes 884744 | tf_op jit(solution)/shard_map/ppermute | solution.py:538
  269.8 14.9 %collective-permute-start.29 = (bf16[384,768]{1,0:T(8,128)(2,1)S(1)}, bf16[384,768]{1,0:T(8,128)(2,1)S(1)}, u32[]{:S(2)}, u32[]{:S(2)}) collective-permute-start(bf16[384,768]{1,0:T(8,128)(2,1)S(1)} %slice_bitcast_fusion.2), channel_id=1, source_target_pairs={{0,8},{4,12},{8,0},{12,4},{16,24},{20,28},{24,16},{28,20},{1,9},{5... | collective-permute-start | bytes 1769480 | tf_op jit(solution)/shard_map/ppermute | solution.py:524
  272.5 15.7 %collective-permute-start.24 = (bf16[96,3072]{1,0:T(8,128)(2,1)S(1)}, bf16[96,3072]{1,0:T(8,128)(2,1)S(1)}, u32[]{:S(2)}, u32[]{:S(2)}) collective-permute-start(bf16[96,3072]{1,0:T(8,128)(2,1)S(1)} %slice_bitcast_fusion.4), channel_id=1, source_target_pairs={{0,16},{4,20},{8,24},{12,28},{16,0},{20,4},{24,8},{28,12},{1,17},{... | collective-permute-start | bytes 1769480 | tf_op jit(solution)/shard_map/ppermute | solution.py:524
  284.8 18.2 %collective-permute-start.30 = (bf16[384,768]{1,0:T(8,128)(2,1)S(1)}, bf16[384,768]{1,0:T(8,128)(2,1)S(1)}, u32[]{:S(2)}, u32[]{:S(2)}) collective-permute-start(bf16[384,768]{1,0:T(8,128)(2,1)S(1)} %fusion.1), channel_id=1, source_target_pairs={{0,3},{3,0},{1,2},{2,1},{4,7},{7,4},{5,6},{6,5},{8,11},{11,8},{9,1... | collective-permute-start | bytes 1769480 | tf_op jit(solution)/shard_map/ppermute | solution.py:538
  288.3 25.5 %collective-permute-start.25 = (bf16[96,3072]{1,0:T(8,128)(2,1)S(1)}, bf16[96,3072]{1,0:T(8,128)(2,1)S(1)}, u32[]{:S(2)}, u32[]{:S(2)}) collective-permute-start(bf16[96,3072]{1,0:T(8,128)(2,1)S(1)} %fusion.2), channel_id=1, source_target_pairs={{0,1},{1,0},{2,3},{3,2},{4,5},{5,4},{6,7},{7,6},{8,9},{9,8},{10,11... | collective-permute-start | bytes 1769480 | tf_op jit(solution)/shard_map/ppermute | solution.py:538
  303.1 24.6 %collective-permute-start.31 = (bf16[384,768]{1,0:T(8,128)(2,1)S(1)}, bf16[384,768]{1,0:T(8,128)(2,1)S(1)}, u32[]{:S(2)}, u32[]{:S(2)}) collective-permute-start(bf16[384,768]{1,0:T(8,128)(2,1)S(1)} %add.134), channel_id=1, source_target_pairs={{0,1},{1,0},{2,3},{3,2},{4,5},{5,4},{6,7},{7,6},{8,9},{9,8},{10,11... | collective-permute-start | bytes 1769480 | tf_op jit(solution)/shard_map/ppermute | solution.py:538
  314.0 25.9 %collective-permute-start.26 = (bf16[96,3072]{1,0:T(8,128)(2,1)S(1)}, bf16[96,3072]{1,0:T(8,128)(2,1)S(1)}, u32[]{:S(2)}, u32[]{:S(2)}) collective-permute-start(bf16[96,3072]{1,0:T(8,128)(2,1)S(1)} %add.128), channel_id=1, source_target_pairs={{0,3},{3,0},{1,2},{2,1},{4,7},{7,4},{5,6},{6,5},{8,11},{11,8},{9,1... | collective-permute-start | bytes 1769480 | tf_op jit(solution)/shard_map/ppermute | solution.py:538

commit v2 on v1

v2 whole, which is shorter than its diff:
```python
from functools import partial

import jax
import jax.numpy as jnp
from jax import lax
from jax.experimental import pallas as pl
from jax.experimental.pallas import tpu as pltpu
from jax.sharding import PartitionSpec as P

HEAD_DIM = 64
KEEP = 1.0 / 0.9
EPS = 1e-06
BF = jnp.bfloat16
F32 = jnp.float32
COLUMNS = 128
PACE = 0.3
OWNERS = 8
VMEM = 60 * 2**20

ERF_P = 0.425
ERF_C = (
    0.2396707695899643,
    0.2419609266760862,
    0.1999560009093125,
    0.2575598334337707,
    -0.1079240365384954,
    0.4126939875393689,
    -0.3161029975019298,
    0.07218539595215835,
)


def dot(a, b):
    return lax.dot_general(a, b, (((1,), (0,)), ((), ())), preferred_element_type=F32)


def dot_nt(a, b):
    return lax.dot_general(a, b, (((1,), (1,)), ((), ())), preferred_element_type=F32)


def dot_tn(a, b):
    return lax.dot_general(a, b, (((0,), (0,)), ((), ())), preferred_element_type=F32)


def gelu_both(u):
    t = 1.0 / (1.0 + (ERF_P * 0.5**0.5) * jnp.abs(u))
    poly = jnp.full_like(t, 0.5 * ERF_C[-1])
    for c in ERF_C[-2::-1]:
        poly = poly * t + 0.5 * c
    bell = jnp.exp(-0.5 * u * u)
    tail = poly * t * bell
    cdf = jnp.where(u >= 0, 1.0 - tail, tail)
    return u * cdf, cdf + u * (bell * 0.3989422804014327)


def normalize(x):
    center = x - jnp.mean(x, axis=-1, keepdims=True)
    inv = lax.rsqrt(jnp.mean(center * center, axis=-1, keepdims=True) + EPS)
    return center * inv, inv


def norm_back(up, hat, inv, gain):
    e = up * gain
    return inv * (
        e
        - jnp.mean(e, axis=-1, keepdims=True)
        - hat * jnp.mean(e * hat, axis=-1, keepdims=True)
    )


def both_heads(v, low):
    return jnp.concatenate([jnp.where(low, v, BF(0)), jnp.where(low, BF(0), v)], axis=0)


def colsum(v):
    return jnp.sum(v, axis=0, keepdims=True)


def place(b):
    return (b & 1) * (OWNERS // 2) + lax.shift_right_logical(b, 1)


def store_relative(ref, lead, value, d):
    n = value.shape[0] // OWNERS
    for b in range(OWNERS):
        spot = pl.multiple_of(place(b ^ d) * n, n)
        ref[lead, pl.ds(spot, n), :] = value[b * n : (b + 1) * n]


def forward_kernel(
    at, keep, x0, x1, x2, x3, sp, g1, b1, wq, bq, wp, bp, g2, b2,
    *refs, rows, heads, lo, images,
):
    xs, a1t, qkv, prob, ot, h, a2, a2t, buf = refs[-9:]
    i = lo + pl.program_id(0)
    d = at[1]
    part = x0.shape[1]
    ns = sp.shape[1]
    width = x0.shape[2]
    buf[...] = jnp.zeros_like(buf)
    buf[0:ns, :] = sp[0].astype(F32)
    for k, ref in enumerate((x0, x1, x2, x3)):
        buf[ns + k * part : ns + (k + 1) * part, :] = ref[0].astype(F32)
    x = buf[...]
    xs[0] = x.astype(BF)
    hat, _ = normalize(x)
    a1 = (hat * g1[...].astype(F32) + b1[...].astype(F32)).astype(BF)
    store_relative(a1t, 0, a1.astype(F32).T.astype(BF), d)
    both = (dot(a1, wq[...]) + bq[...]).astype(BF)
    qkv[0] = both
    padded = x.shape[0]
    low = lax.broadcasted_iota(jnp.int32, (padded, 2 * HEAD_DIM), 1) < HEAD_DIM
    seen = lax.broadcasted_iota(jnp.int32, (2 * padded, padded), 1) < rows
    outs = []
    for j in range(heads // 2):
        c = j * 2 * HEAD_DIM
        q = both[:, c : c + 2 * HEAD_DIM] * BF(HEAD_DIM**-0.5)
        k = both[:, width + c : width + c + 2 * HEAD_DIM]
        v = both[:, 2 * width + c : 2 * width + c + 2 * HEAD_DIM]
        s = jnp.where(seen, dot_nt(both_heads(q, low), k), -1e30)
        e = jnp.exp(s - jnp.max(s, axis=-1, keepdims=True))
        p = (e * (1.0 / jnp.sum(e, axis=-1, keepdims=True))).astype(BF)
        prob[0, j] = p
        pv = dot(p, v)
        outs.append(jnp.where(low, pv[:padded], pv[padded:]))
    o32 = jnp.concatenate(outs, axis=1)
    store_relative(ot, 0, o32.T.astype(BF), d)
    y = dot(o32.astype(BF), wp[...]) + bp[...].astype(F32)
    m1 = keep[at[0] * images + i, 0].astype(F32) * KEEP
    hh = x + m1 * y
    h[0] = hh
    hat2, _ = normalize(hh)
    n2 = hat2 * g2[...].astype(F32) + b2[...].astype(F32)
    a2[0] = n2.astype(BF)
    store_relative(a2t, 0, n2.T.astype(BF), d)


def feed_kernel(
    at, keep, h, a2, w1, b1, w2, b2, act, slope, o0, o1, o2, o3, z, *, images, part, ns
):
    t = pl.program_id(0)
    padded = h.shape[1]
    wa = w1[...]
    wb = w2[...]
    bias = b1[...].astype(F32)
    for i in range(images):
        r = slice(i * padded, (i + 1) * padded)
        g, dg = gelu_both(dot(a2[i], wa) + bias)
        g = g.astype(BF)
        act[i] = g
        slope[i] = dg.astype(BF)
        more = dot(g, wb)

        @pl.when(t == 0)
        def _(r=r, more=more):
            z[r, :] = more

        @pl.when(t > 0)
        def _(r=r, more=more):
            z[r, :] += more

    @pl.when(t == pl.num_programs(0) - 1)
    def _():
        for i in range(images):
            m2 = keep[at[0] * images + i, 1].astype(F32) * KEEP
            r = slice(i * padded, (i + 1) * padded)
            z[r, :] = h[i] + m2 * (z[r, :] + b2[...].astype(F32))
            for k, ref in enumerate((o0, o1, o2, o3)):
                lo = i * padded + ns + k * part
                ref[i] = jnp.concatenate(
                    [z[lo : lo + part, :], z[i * padded : i * padded + ns, :]], axis=0
                ).astype(BF)


def feed_back_kernel(
    at, keep, g0, g1, g2, g3, sg, h, a2t, act, slope, w1, w2, gain,
    dh, dy, w2s, w2k, w1s, w1k, db1, small,
    dout, dz, da2, *, images,
):
    t = pl.program_id(0)
    part = g0.shape[1]
    ns = sg.shape[1]
    padded = h.shape[1]

    @pl.when(t == 0)
    def _():
        for i in range(images):
            m2 = keep[at[0] * images + i, 1].astype(F32) * KEEP
            r = i * padded
            dout[r : r + padded, :] = jnp.zeros((padded, dout.shape[1]), F32)
            dout[r : r + ns, :] = sg[i].astype(F32)
            for k, ref in enumerate((g0, g1, g2, g3)):
                lo = r + ns + k * part
                dout[lo : lo + part, :] = ref[i].astype(F32)
            dz[r : r + padded, :] = (dout[r : r + padded, :] * m2).astype(BF)
        da2[...] = jnp.zeros_like(da2)

    wa = w1[...]
    wb = w2[...]
    grad1 = None
    db = None
    for i in range(images):
        r = slice(i * padded, (i + 1) * padded)
        du = (slope[i].astype(F32) * dot_nt(dz[r, :], wb)).astype(BF)
        da2[r, :] += dot_nt(du, wa)
        g = dot(a2t[i], du)
        s = colsum(du.astype(F32))
        grad1 = g if grad1 is None else grad1 + g
        db = s if db is None else db + s
    db1[...] = db
    n = w1k.shape[2]
    for p in range(w1k.shape[0]):
        w1k[p, 0] = grad1[p * n : (p + 1) * n].astype(BF)
        w1s[p, 0] = grad1[grad1.shape[0] // 2 + p * n :][:n].astype(BF)
    grad2 = dot_tn(act[...].reshape(images * padded, -1), dz[...]).astype(BF)
    half = grad2.shape[0] // 2
    odd = at[1] & 1

    @pl.when(odd == 0)
    def _():
        w2k[...] = grad2[:half]
        w2s[...] = grad2[half:]

    @pl.when(odd == 1)
    def _():
        w2k[...] = grad2[half:]
        w2s[...] = grad2[:half]

    @pl.when(t == pl.num_programs(0) - 1)
    def _():
        gains = gain[...].astype(F32)
        sums = [jnp.zeros((1, dout.shape[1]), F32) for _ in range(4)]
        for i in range(images):
            m1 = keep[at[0] * images + i, 0].astype(F32) * KEEP
            r = slice(i * padded, (i + 1) * padded)
            hat, inv = normalize(h[i])
            up = da2[r, :]
            grad = dout[r, :] + norm_back(up, hat, inv, gains)
            dh[i] = grad
            low = (m1 * grad).astype(BF)
            dy[i] = low
            for j, v in enumerate((up * hat, up, dz[r, :].astype(F32), low.astype(F32))):
                sums[j] = sums[j] + colsum(v)
        small[...] = jnp.concatenate(sums, axis=0)


def heads_kernel(dy, prob, qkv, wp, wq, xs, dh, gain, *refs, heads, part, ns):
    dqkv, o0, o1, o2, o3, flat, small, buf = refs[-8:]
    i = pl.program_id(0)
    width = dy.shape[2]
    padded = dy.shape[1]
    low = lax.broadcasted_iota(jnp.int32, (padded, 2 * HEAD_DIM), 1) < HEAD_DIM
    do = dot_nt(dy[0], wp[...]).astype(BF)
    for j in range(heads // 2):
        c = j * 2 * HEAD_DIM
        q = qkv[0, :, c : c + 2 * HEAD_DIM]
        k = qkv[0, :, width + c : width + c + 2 * HEAD_DIM]
        v = qkv[0, :, 2 * width + c : 2 * width + c + 2 * HEAD_DIM]
        g = both_heads(do[:, c : c + 2 * HEAD_DIM], low)
        p = prob[0, j]
        p32 = p.astype(F32)
        w = p32 * dot_nt(g, v)
        ds = (w - p32 * jnp.sum(w, axis=-1, keepdims=True)).astype(BF)
        dq = dot(ds, k)
        dq = jnp.where(low, dq[:padded], dq[padded:]) * HEAD_DIM**-0.5
        dk = dot_tn(ds, both_heads(q, low)) * HEAD_DIM**-0.5
        dqkv[0, :, c : c + 2 * HEAD_DIM] = dq.astype(BF)
        dqkv[0, :, width + c : width + c + 2 * HEAD_DIM] = dk.astype(BF)
        dqkv[0, :, 2 * width + c : 2 * width + c + 2 * HEAD_DIM] = dot_tn(p, g).astype(BF)
    grads = dqkv[0]
    tops = colsum(grads.astype(F32))
    up = dot_nt(grads, wq[...])
    hat, inv = normalize(xs[0].astype(F32))
    buf[...] = dh[0] + norm_back(up, hat, inv, gain[...].astype(F32))
    for k, ref in enumerate((o0, o1, o2, o3)):
        lo = ns + k * part
        ref[0] = jnp.concatenate([buf[lo : lo + part, :], buf[0:ns, :]], axis=0).astype(BF)
    sums = jnp.concatenate([colsum(up * hat), colsum(up)], axis=0)

    @pl.when(i == 0)
    def _():
        flat[...] = tops
        small[...] = sums

    @pl.when(i > 0)
    def _():
        flat[...] += tops
        small[...] += sums


def weights_kernel(
    at, dqkv, dy, a1k, a1s, ok, os_, flat_a, flat_b, small_a, small_b, small2, db1,
    cs, ck, ds_, dk_, cols,
):
    t = pl.program_id(0)
    images, _, width = dy.shape

    @pl.when(t == 0)
    def _():
        n = width // OWNERS
        per = db1.shape[1] // width
        flat = flat_a[...] + flat_b[...]
        eight = jnp.concatenate(
            [small_a[...] + small_b[...], flat[:, :width], flat[:, 2 * width :], small2[...]], axis=0
        ).T
        long = jnp.broadcast_to(db1[...], (8, db1.shape[1])).T
        cols[...] = jnp.zeros_like(cols)
        for b in range(OWNERS):
            rows = pl.ds(pl.multiple_of(place(b ^ at[1]) * n, n), n)
            cols[rows, 0:8] = eight[b * n : (b + 1) * n]
            for j in range(per):
                lo = (b * per + j) * n
                cols[rows, 8 + j : 9 + j] = long[lo : lo + n, 0:1]

    block = cs.shape[0]
    for side, (a1, o, c_ref, d_ref) in enumerate(((a1s, os_, cs, ds_), (a1k, ok, ck, dk_))):
        g = dot(a1[0], dqkv[0])
        p = dot(o[0], dy[0])
        for i in range(1, images):
            g = g + dot(a1[i], dqkv[i])
            p = p + dot(o[i], dy[i])
        c_ref[:, : 2 * width] = g[:, : 2 * width].astype(BF)
        c_ref[:, 2 * width :] = jnp.zeros((block, COLUMNS), BF)
        d_ref[:, :width] = g[:, 2 * width :].astype(BF)
        d_ref[:, width : 2 * width] = p.astype(BF)
        lo = pl.multiple_of((1 - side) * (width // 2) + t * block, block)
        d_ref[:, 2 * width :] = cols[pl.ds(lo, block), :].astype(BF)


def gather_kernel(at, c0, c1, c2, c3, rows, specials):
    k = pl.program_id(0)
    part = rows.shape[1]
    for j, ref in enumerate((c0, c1, c2, c3)):

        @pl.when(k == j)
        def _(ref=ref):
            rows[...] = ref[:, :part, :]
            specials[...] = ref[:, part:, :]


def sum_kernel(*refs, terms, pick):
    if pick:
        at, *refs = refs
        even = (at[0] & 1) == 0
    ins, outs = refs[: sum(terms)], refs[sum(terms) :]
    values = []
    for count in terms:
        mine, ins = ins[:count], ins[count:]
        total = mine[0][...].astype(F32)
        for ref in mine[1:]:
            total = total + ref[...].astype(F32)
        values.append(total)
    if pick:
        values = [jnp.where(even, *values), jnp.where(even, *values[::-1])]
    for ref, v in zip(outs, values):
        ref[...] = v.astype(BF)


def sums(jobs, at=None):
    specs, arrays, out_specs, out_shapes = [], [], [], []
    for job in jobs:
        for v, lead in job:
            tail = v.shape[len(lead) + 1 :]
            block = tuple(v.shape[i] if j is None else None for i, j in enumerate(lead))
            place_ = tuple(j or 0 for j in lead)
            specs.append(
                pl.BlockSpec((*block, None, *tail), lambda m, p=place_: (*p, m, 0, 0))
            )
            arrays.append(v)
        keep = tuple(b for b in block if b is not None)
        out_shapes.append(struct(*keep, v.shape[len(lead)], *tail))
        out_specs.append(
            pl.BlockSpec((*keep, None, *tail), lambda m, z=len(keep): (*(0,) * z, m, 0, 0))
        )
    if at is not None:
        specs.insert(0, pl.BlockSpec(memory_space=pltpu.SMEM))
        arrays.insert(0, at)
    return pl.pallas_call(
        partial(sum_kernel, terms=[len(job) for job in jobs], pick=at is not None),
        grid=(out_shapes[0].shape[-3],),
        in_specs=specs,
        out_specs=out_specs,
        out_shape=out_shapes,
        compiler_params=params(24),
        cost_estimate=cost(2),
        name="sums",
    )(*arrays)


def finish_feed_kernel(at, mine, other, fc1, fc2):
    even = (at[0] & 1) == 0
    n = fc1.shape[0]
    width = fc2.shape[1]
    for m in range(mine.shape[0]):
        p, q = mine[m].astype(F32), other[m].astype(F32)
        fc1[:, m * width : (m + 1) * width] = jnp.where(even, p, q)
        fc2[m * n : (m + 1) * n, :] = jnp.where(even, q, p)


def finish_kernel(at, mine, other, qkv, proj, *rest):
    vectors, long = rest[:-1], rest[-1]
    width = proj.shape[1]
    even = (at[0] & 1) == 0
    p, q = mine[...].astype(F32), other[...].astype(F32)
    c, d = jnp.where(even, p, q), jnp.where(even, q, p)
    qkv[:, : 2 * width] = c[:, : 2 * width]
    qkv[:, 2 * width :] = d[:, :width]
    proj[...] = d[:, width : 2 * width]
    n = c.shape[0]
    flat = d[:, 2 * width :].T
    row = 0
    for ref in vectors:
        ref[...] = flat[row : row + ref.shape[0]]
        row += ref.shape[0]
    for j in range(long.shape[1] // n):
        long[:, j * n : (j + 1) * n] = flat[row + j : row + j + 1]


def whole(shape):
    return pl.BlockSpec(shape, lambda *_: (0,) * len(shape))


def params(mib=60):
    return pltpu.CompilerParams(
        dimension_semantics=("arbitrary",), vmem_limit_bytes=mib * 2**20
    )


def cost(us):
    return pl.CostEstimate(flops=int(us * 1e9 * PACE), bytes_accessed=1, transcendentals=0)


ANY = pl.BlockSpec(memory_space=pl.ANY)


def struct(*shape, dtype=BF):
    return jax.ShapeDtypeStruct(shape, dtype)


def after(v, *others):
    return lax.optimization_barrier((v, *others))[0]


def together(*vs):
    return lax.optimization_barrier(vs)


def swap(v, bit):
    return lax.ppermute(v, "dp", [(s, s ^ bit) for s in range(lax.axis_size("dp"))])


def send_around(x, groups, lo, count):
    me = lax.axis_index("seq")
    n = x.shape[0] // groups
    got = []
    for k in range(1, groups):
        block = lax.dynamic_slice_in_dim(x, n * ((me + k) % groups) + lo, count)
        got.append(lax.ppermute(block, "seq", [(s, (s + k) % groups) for s in range(groups)]))
    return got


def send_back(chunks, groups):
    return [chunks[0]] + [
        lax.ppermute(c, "seq", [(s, (s - k) % groups) for s in range(groups)])
        for k, c in enumerate(chunks)
        if k
    ]


def settle(chunks, at, groups, part, ns):
    n, _, width = chunks[0].shape
    return pl.pallas_call(
        gather_kernel,
        grid_spec=pltpu.PrefetchScalarGridSpec(
            num_scalar_prefetch=1,
            grid=(groups,),
            in_specs=[whole(c.shape) for c in chunks],
            out_specs=[
                pl.BlockSpec((n, part, width), lambda k, at: ((at[0] + k) % groups, 0, 0)),
                pl.BlockSpec((n, ns, width), lambda k, at: ((at[0] + k) % groups, 0, 0)),
            ],
        ),
        out_shape=[struct(n * groups, part, width), struct(n * groups, ns, width)],
        compiler_params=params(16),
        cost_estimate=cost(2),
        name="settle",
    )(at, *chunks)


def shards(
    patches, specials, keep_mask, ln1_gain, ln1_bias, qkv_weight, qv_bias, proj_weight, proj_bias,
    ln2_gain, ln2_bias, fc1_weight, fc1_bias, fc2_weight, fc2_bias, grad_patches, grad_specials,
):
    images, part, width = patches.shape
    ns = specials.shape[1]
    groups = lax.axis_size("seq")
    replicas = lax.axis_size("dp")
    hidden = fc1_weight.shape[1]
    heads = width // HEAD_DIM
    n = images // groups
    rows = ns + groups * part
    padded = -(-rows // 16) * 16
    steps = OWNERS // 2
    chunk = hidden // steps
    half = width // 2
    direct = replicas == OWNERS
    me = lax.axis_index("seq")
    d = lax.axis_index("dp") if direct else jnp.int32(0)
    at = jnp.stack([me, d]).astype(jnp.int32)

    def row(v):
        return v.reshape(1, -1)

    def per_image(lo, *shape):
        return pl.BlockSpec((1, *shape), lambda i, *_: (lo + i,) + (0,) * len(shape))

    got = together(*send_around(patches, groups, 0, n))
    zero = jnp.zeros((width,), F32)
    qkv_bias = row(jnp.concatenate([qv_bias[0].astype(F32), zero, qv_bias[1].astype(F32)]))

    shapes = [
        ((padded, width), BF), ((width, padded), BF), ((padded, 3 * width), BF),
        ((heads // 2, 2 * padded, padded), BF), ((width, padded), BF),
        ((padded, width), F32), ((padded, width), BF), ((width, padded), BF),
    ]

    def forward(got, lo, count, before=()):
        own = pl.BlockSpec((1, part, width), lambda i, at, keep: (at[0] * n + lo + i, 0, 0))
        ins = 15
        return pl.pallas_call(
            partial(forward_kernel, rows=rows, heads=heads, lo=lo, images=n),
            grid_spec=pltpu.PrefetchScalarGridSpec(
                num_scalar_prefetch=2,
                grid=(count,),
                in_specs=[
                    own, *[per_image(0, part, width)] * 3,
                    pl.BlockSpec((1, ns, width), lambda i, at, keep: (at[0] * n + lo + i, 0, 0)),
                    whole((1, width)), whole((1, width)),
                    whole(qkv_weight.shape), whole((1, 3 * width)),
                    whole(proj_weight.shape), *[whole((1, width))] * 3,
                    *[ANY] * len(before),
                ],
                out_specs=[per_image(lo, *shape) for shape, _ in shapes],
                scratch_shapes=[pltpu.VMEM((padded, width), F32)],
            ),
            out_shape=[struct(n, *shape, dtype=dtype) for shape, dtype in shapes],
            input_output_aliases={ins + j: j for j in range(len(before))},
            compiler_params=params(60),
            cost_estimate=cost(5 * count),
            name="attention_forward",
        )(
            at, keep_mask, patches, *got, specials, row(ln1_gain), row(ln1_bias), qkv_weight, qkv_bias,
            proj_weight, row(proj_bias), row(ln2_gain), row(ln2_bias), *before,
        )

    got_grad = send_around(after(grad_patches, *got), groups, 0, n)
    xs, a1t, qkv, prob, ot, h, a2, a2t = forward(got, 0, n)

    total = n * padded
    act, slope, *out_chunks = pl.pallas_call(
        partial(feed_kernel, images=n, part=part, ns=ns),
        grid_spec=pltpu.PrefetchScalarGridSpec(
            num_scalar_prefetch=2,
            grid=(steps,),
            in_specs=[
                whole(h.shape), whole(a2.shape),
                pl.BlockSpec((width, chunk), lambda t, *_: (0, t)),
                pl.BlockSpec((1, chunk), lambda t, *_: (0, t)),
                pl.BlockSpec((chunk, width), lambda t, *_: (t, 0)),
                whole((1, width)),
            ],
            out_specs=[
                *[pl.BlockSpec((n, padded, chunk), lambda t, *_: (0, 0, t))] * 2,
                *[whole((n, part + ns, width))] * 4,
            ],
            scratch_shapes=[pltpu.VMEM((total, width), F32)],
        ),
        out_shape=[*[struct(n, padded, hidden)] * 2, *[struct(n, part + ns, width)] * 4],
        compiler_params=params(60),
        cost_estimate=cost(20),
        name="feed_forward",
    )(
        at, keep_mask, h, a2, fc1_weight, row(fc1_bias), fc2_weight, row(fc2_bias)
    )
    act, slope, *got_grad = together(act, slope, *got_grad)
    back_out = send_back(out_chunks, groups)

    def owner(t, at):
        return t ^ lax.shift_right_logical(at[1], 1)

    dh, dy, w2s, w2k, w1s, w1k, db1, small2 = pl.pallas_call(
        partial(feed_back_kernel, images=n),
        grid_spec=pltpu.PrefetchScalarGridSpec(
            num_scalar_prefetch=2,
            grid=(steps,),
            in_specs=[
                pl.BlockSpec((n, part, width), lambda t, at, keep: (at[0], 0, 0)),
                *[whole((n, part, width))] * 3,
                pl.BlockSpec((n, ns, width), lambda t, at, keep: (at[0], 0, 0)),
                whole(h.shape), whole(a2t.shape),
                *[pl.BlockSpec((n, padded, chunk), lambda t, at, keep: (0, 0, owner(t, at)))] * 2,
                pl.BlockSpec((width, chunk), lambda t, at, keep: (0, owner(t, at))),
                pl.BlockSpec((chunk, width), lambda t, at, keep: (owner(t, at), 0)),
                whole((1, width)),
            ],
            out_specs=[
                whole((n, padded, width)), whole((n, padded, width)),
                *[pl.BlockSpec((chunk // 2, width), lambda t, *_: (t, 0))] * 2,
                *[pl.BlockSpec((steps, 1, width // OWNERS, chunk), lambda t, at, keep: (0, owner(t, at), 0, 0))] * 2,
                pl.BlockSpec((1, chunk), lambda t, at, keep: (0, owner(t, at))),
                whole((4, width)),
            ],
            scratch_shapes=[
                pltpu.VMEM((total, width), F32), pltpu.VMEM((total, width), BF),
                pltpu.VMEM((total, width), F32),
            ],
        ),
        out_shape=[
            struct(n, padded, width, dtype=F32), struct(n, padded, width),
            *[struct(hidden // 2, width)] * 2, *[struct(steps, steps, width // OWNERS, chunk)] * 2,
            struct(1, hidden, dtype=F32), struct(4, width, dtype=F32),
        ],
        compiler_params=params(60),
        cost_estimate=cost(25),
        name="feed_backward",
    )(
        at, keep_mask, grad_patches, *got_grad, grad_specials, h, a2t, act, slope, fc1_weight,
        fc2_weight, row(ln2_gain),
    )

    dy, w1s, w2s, *back_out = together(dy, w1s, w2s, *back_out)

    def backward(dy, lo, count, before=()):
        ins = 8
        return pl.pallas_call(
            partial(heads_kernel, heads=heads, part=part, ns=ns),
            grid=(count,),
            in_specs=[
                per_image(lo, padded, width), per_image(lo, heads // 2, 2 * padded, padded),
                per_image(lo, padded, 3 * width), whole(proj_weight.shape), whole(qkv_weight.shape),
                per_image(lo, padded, width), per_image(lo, padded, width), whole((1, width)),
                *[ANY] * len(before),
            ],
            out_specs=[
                per_image(lo, padded, 3 * width), *[per_image(lo, part + ns, width)] * 4,
                whole((1, 3 * width)), whole((2, width)),
            ],
            out_shape=[
                struct(n, padded, 3 * width), *[struct(n, part + ns, width)] * 4,
                struct(1, 3 * width, dtype=F32), struct(2, width, dtype=F32),
            ],
            scratch_shapes=[pltpu.VMEM((padded, width), F32)],
            input_output_aliases={ins + j: j for j in range(len(before))},
            compiler_params=params(60),
            cost_estimate=cost(7 * count),
            name="attention_backward",
        )(dy, prob, qkv, proj_weight, qkv_weight, xs, dh, row(ln1_gain), *before)

    n1 = width // OWNERS
    x_half, y_half = (None, 1), (1, None)
    if direct:
        ra, rb = swap(w1s, 1), swap(w2s, 1)
    *made, flat_a, small_a = backward(dy, 0, 1)
    if direct:
        ra, rb, dy, *made = together(ra, rb, dy, *made)
        wa, wb, ra, rb = (v.reshape(2, 2, steps, n1, chunk) for v in (w1k, w2k, ra, rb))
        as_, bs = sums([[(wa, x_half), (ra, x_half)], [(wb, y_half), (rb, y_half)]])
        dy, as_, bs = together(dy, as_, bs)
        qa, qb = swap(as_, 2), swap(bs, 4)
    dqkv, *back_dx, flat_b, small_b = backward(dy, 1, n - 1, made)
    back_dx = send_back(back_dx, groups)

    rows_k = pl.BlockSpec((n, half // 2, padded), lambda t, at: (0, t, 0))
    rows_s = pl.BlockSpec((n, half // 2, padded), lambda t, at: (0, 2 + t, 0))
    wide = 2 * width + COLUMNS
    cs, ck, ds_, dk_ = pl.pallas_call(
        weights_kernel,
        grid_spec=pltpu.PrefetchScalarGridSpec(
            num_scalar_prefetch=1,
            grid=(2,),
            in_specs=[
                whole(dqkv.shape), whole(dy.shape), rows_k, rows_s, rows_k, rows_s,
                *[whole((1, 3 * width))] * 2, *[whole((2, width))] * 2, whole((4, width)),
                whole((1, hidden)),
            ],
            out_specs=[pl.BlockSpec((half // 2, wide), lambda t, at: (t, 0))] * 4,
            scratch_shapes=[pltpu.VMEM((width, COLUMNS), F32)],
        ),
        out_shape=[struct(half, wide)] * 4,
        compiler_params=params(60),
        cost_estimate=cost(6),
        name="attention_weights",
    )(at, dqkv, dy, a1t, a1t, ot, ot, flat_a, flat_b, small_a, small_b, small2, db1)

    if not direct:
        out_rows, out_specials = settle(back_out, at, groups, part, ns)
        dx_rows, dx_specials = settle(back_dx, at, groups, part, ns)
        return (
            out_rows, out_specials, dx_rows, dx_specials,
            *natural_sums(
                w1s, w1k, w2s, w2k, cs, ck, ds_, dk_, flat_a + flat_b, small_a + small_b, small2, db1
            ),
        )

    def near(v):
        return lax.ppermute(v, "seq", [(s, s ^ 1) for s in range(groups)])

    def far(v):
        return lax.ppermute(v, "seq", [(s, s ^ 2) for s in range(groups)])

    qa, qb, cs, ds_ = together(qa, qb, cs, ds_)
    as_, bs = sums(
        [[(wa, (1, 0)), (ra, (1, 0)), (qa, (1,))], [(wb, (0, 1)), (rb, (0, 1)), (qb, (1,))]]
    )
    as_, bs, cs, ds_, back_dx[1], back_dx[3] = together(as_, bs, cs, ds_, back_dx[1], back_dx[3])
    ta, tb = swap(as_, 4), swap(bs, 2)
    rc, rd = swap(cs, 1), swap(ds_, 1)
    rc, rd, ck, dk_ = together(rc, rd, ck, dk_)
    wc, wd, rc, rd = (v.reshape(2, 2, 2, n1 // 2, -1) for v in (ck, dk_, rc, rd))
    cs, ds_ = sums([[(wc, x_half), (rc, x_half)], [(wd, y_half), (rd, y_half)]])
    ta, tb, cs, ds_ = together(ta, tb, cs, ds_)
    qc, qd = swap(cs, 2), swap(ds_, 4)
    e1, es = sums(
        [
            [(wa, (0, 0)), (ra, (0, 0)), (qa, (0,)), (ta, ())],
            [(wb, (0, 0)), (rb, (0, 0)), (qb, (0,)), (tb, ())],
        ],
        at,
    )
    re = near(es)
    back_out = together(*back_out, e1)[:groups]
    out_rows, out_specials = settle(back_out, at, groups, part, ns)
    re, out_rows, *back_dx = together(re, out_rows, *back_dx)
    e1 = e1 + re
    e1, qc, qd = together(e1, qc, qd)
    re = far(e1)
    cs, ds_ = sums(
        [[(wc, (1, 0)), (rc, (1, 0)), (qc, (1,))], [(wd, (0, 1)), (rd, (0, 1)), (qd, (1,))]]
    )
    tc, td = swap(cs, 4), swap(ds_, 2)
    tc, td = together(tc, td)
    f1, fs = sums(
        [
            [(wc, (0, 0)), (rc, (0, 0)), (qc, (0,)), (tc, ())],
            [(wd, (0, 0)), (rd, (0, 0)), (qd, (0,)), (td, ())],
        ],
        at,
    )
    rf = near(fs)
    back_dx = together(*back_dx, f1)[:groups]
    dx_rows, dx_specials = settle(back_dx, at, groups, part, ns)
    rf, re, dx_rows = together(rf, re, dx_rows)
    f1 = f1 + rf
    rf = far(f1)
    e1 = e1 + re
    re = near(e1)
    re, f1 = together(re, f1)
    smem = pl.BlockSpec(memory_space=pltpu.SMEM)
    vmem = pl.BlockSpec(memory_space=pltpu.VMEM)
    d_fc1, d_fc2 = pl.pallas_call(
        finish_feed_kernel,
        in_specs=[smem, vmem, vmem],
        out_shape=[struct(n1, hidden, dtype=F32), struct(hidden // OWNERS, width, dtype=F32)],
        compiler_params=pltpu.CompilerParams(vmem_limit_bytes=24 * 2**20),
        cost_estimate=cost(2),
        name="finish_feed",
    )(at, e1, re)
    rf, d_fc1 = together(rf, d_fc1)
    f1 = f1 + rf
    rf = near(f1)
    done = pl.pallas_call(
        finish_kernel,
        in_specs=[smem, vmem, vmem],
        out_shape=[
            struct(n1, 3 * width, dtype=F32), struct(n1, width, dtype=F32),
            *[struct(1, n1, dtype=F32)] * 2, struct(2, n1, dtype=F32),
            *[struct(1, n1, dtype=F32)] * 4, struct(1, hidden // OWNERS, dtype=F32),
        ],
        compiler_params=pltpu.CompilerParams(vmem_limit_bytes=24 * 2**20),
        cost_estimate=cost(2),
        name="finish",
    )(at, f1.reshape(n1, -1), rf.reshape(n1, -1))
    d_qkv, d_proj, gain1, bias1, d_qv, gain2, bias2, d_fc2b, d_projb, d_fc1b = done

    def one(v):
        return v.reshape(-1)

    return (
        out_rows, out_specials, dx_rows, dx_specials,
        one(gain1), one(bias1), d_qkv, d_qv, d_proj, one(d_projb), one(gain2), one(bias2),
        d_fc1, one(d_fc1b), d_fc2, one(d_fc2b),
    )


def natural_sums(w1s, w1k, w2s, w2k, cs, ck, ds_, dk_, flat, small1, small2, db1):
    width = small1.shape[1]
    replicas = lax.axis_size("dp")

    def natural(sent, kept):
        if kept.ndim == 4:
            kept, sent = (v.transpose(0, 2, 1, 3).reshape(width // 2, -1) for v in (kept, sent))
        v = jnp.stack([kept, sent]).reshape(2, OWNERS // 2, -1, kept.shape[1])
        v = v.transpose(1, 0, 2, 3).reshape(-1, kept.shape[1])
        v = lax.psum_scatter(v, "dp", scatter_dimension=0, tiled=True)
        return lax.psum(v, "seq").astype(F32)

    d_fc1, d_fc2 = natural(w1s, w1k), natural(w2s, w2k)
    d_qk, d_vp = natural(cs, ck), natural(ds_, dk_)
    d_qkv = jnp.concatenate([d_qk[:, : 2 * width], d_vp[:, :width]], axis=1)
    d_proj = d_vp[:, width : 2 * width]
    flat = flat.reshape(3, width)
    vectors = jnp.concatenate([small1, flat[0:1], flat[2:3], small2, db1.reshape(-1, width)], axis=0)
    vectors = lax.psum(vectors, ("dp", "seq"))
    mine = lax.axis_index("dp")

    def shard(v):
        size = v.shape[-1] // replicas
        return lax.dynamic_slice_in_dim(v, mine * size, size, axis=v.ndim - 1)

    s = shard(vectors[:8])
    d_fc1b = shard(vectors[8:].reshape(-1))
    return s[0], s[1], d_qkv, s[2:4], d_proj, s[7], s[4], s[5], d_fc1, d_fc1b, d_fc2, s[6]


def solution(mesh):
    rows = P("dp", "seq", None)
    lead = P("dp", None, None)
    flat = P("dp")
    matrix = P("dp", None)
    return jax.shard_map(
        shards,
        mesh=mesh,
        in_specs=(rows, lead, matrix, *[P()] * 12, rows, lead),
        out_specs=(
            rows, lead, rows, lead, flat, flat, matrix, P(None, "dp"), matrix, flat, flat, flat,
            matrix, flat, matrix, flat,
        ),
        check_vma=False,
    )
```

time: 342 us -> 258 us (0.75)
  blocking collectives: 50.2 us -> 0 us
  Pallas kernels: 100 us -> 120 us
  other arithmetic: 20.7 us -> 2.41 us
  starting transfers between devices: 57.3 us -> 43 us
  waiting for transfers between devices: 86.8 us -> 73.9 us
  local copies, waits for them, and re-layouts: 24.3 us -> 17.2 us
    psum x1 -> x0, blocking collectives: 50.2 us -> none  [shards(): vectors = lax.psum(vectors, ('dp', 'seq'))]
    pallas_call x4 -> x14, Pallas kernels: 93.1 us -> 114 us  [the longest x1 27.7 us: shards(): pl.pallas_call(partial(feed_back_kernel, images=n), grid_spec=pltpu.Prefe...]
    ppermute x20 -> x18, starting transfers between devices: 39.1 us -> 23 us  [the longest x12 9.61 us: swap(): lax.ppermute(v, 'dp', [(s, s ^ bit) for s in range(lax.axis_size('dp'))])]
    add x16 -> x4, other arithmetic: 15.4 us -> 0.44 us  [the longest x2 0.27 us: shards(): e1 = e1 + re]
    ppermute x20 -> x18, waiting for transfers between devices: 59.4 us -> 53.7 us  [the longest x4 23.1 us: near(): return lax.ppermute(v, 'seq', [(s, s ^ 1) for s in range(groups)])]
    ppermute x6, waiting for transfers between devices: 16.8 us -> 11.5 us  [send_back(): lax.ppermute(c, 'seq', [(s, (s - k) % groups) for s in range(groups)])]
    reshape x8, local copies, waits for them, and re-layouts: 4.77 us -> 9.57 us  [row(): return v.reshape(1, -1)]
    slice x9 -> x0, local copies, waits for them, and re-layouts: 3.85 us -> none  [the longest x1 1.28 us: shards(): flat[2:3]]
  transfers between devices with their start and end apart: 32 -> 30, of which waited for: 11 -> 12; matrix products, arithmetic and copies ran while one was open for 11% -> 5% of each run, Pallas kernels for 9% -> 44%
where the time goes in v2:
time: 258 us; the launch traced here: 257 us
  Pallas kernels  120 us (47%)
  waiting for transfers between devices  73.9 us (29%)
  starting transfers between devices  43 us (17%)
  local copies, waits for them, and re-layouts  17.2 us (7%)
    pallas_call x1, Pallas kernels, shards(): pl.pallas_call(partial(feed_back_kernel, images=n), grid_spec=pltpu.Prefe...  27.7 us
    pallas_call x2, Pallas kernels, backward(): pl.pallas_call(partial(heads_kernel, heads=heads, part=part, ns=ns), grid...  23.9 us
    ppermute x4, waiting for transfers between devices, near(): return lax.ppermute(v, 'seq', [(s, s ^ 1) for s in range(groups)])  23.1 us
    pallas_call x1, Pallas kernels, shards(): pl.pallas_call(partial(feed_kernel, images=n, part=part, ns=ns), grid_spe...  22 us
    ppermute x12, waiting for transfers between devices, swap(): lax.ppermute(v, 'dp', [(s, s ^ bit) for s in range(lax.axis_size('dp'))])  16.7 us
    pallas_call x1, Pallas kernels, forward(): pl.pallas_call(partial(forward_kernel, rows=rows, heads=heads, lo=lo, ima...  14.9 us
    ppermute x2, waiting for transfers between devices, far(): return lax.ppermute(v, 'seq', [(s, s ^ 2) for s in range(groups)])  14 us
    pallas_call x6, Pallas kernels, sums(): pl.pallas_call(partial(sum_kernel, terms=[len(job) for job in jobs], pick...  12 us
  transfers between devices with their start and end apart: 30, of which 12 were waited for; matrix products, arithmetic and copies ran while one was open for 5% of the time, Pallas kernels for 44%

profile of v2, /device:TPU:0, one launch (start us, length us, event | category | flops | bytes accessed | tf_op | source)
XLA Modules:
  0.0 257.0 jit_solution(2958702644238198357)
XLA Ops:
  0.7 1.3 constant_dynamic-slice_fusion.3
  2.0 5.1 %collective-permute-start.2 = (bf16[3,49,768]{2,1,0:T(8,128)(2,1)S(1)}, bf16[3,49,768]{2,1,0:T(8,128)(2,1)S(1)}, u32[]{:S(2)}, u32[]{:S(2)}) collective-permute-start(bf16[3,49,768]{2,1,0:T(8,128)(2,1)S(1)} %get-tuple-element.299), channel_id=1, source_target_pairs={{0,3},{1,0},{2,1},{3,2},{4,7},{5,4},{6,5},{7,6},{8,11},{9,8},{10,9... | collective-permute-start | bytes 677384 | tf_op jit(solution)/shard_map/ppermute | solution.py:458
  7.1 1.0 collective-permute-start
  8.2 0.8 convert_reduce_fusion.1
  8.9 1.3 reshape.114.g1.gain
  10.2 1.3 reshape.118.g2.gain
  11.5 1.3 reshape.115.b1
  12.8 1.3 reshape.117.bp
  14.1 1.3 reshape.119.b2
  15.3 1.3 reshape.121.b2
  16.6 1.4 copy.40.keep
  18.0 0.6 reshape.116.bq
  18.6 1.3 reshape.120.b1
  19.9 0.6 pad_add_fusion.at.refs_0_
  20.5 8.6 %collective-permute-done.1.x2 = bf16[3,49,768]{2,1,0:T(8,128)(2,1)S(1)} collective-permute-done((bf16[3,49,768]{2,1,0:T(8,128)(2,1)S(1)}, bf16[3,49,768]{2,1,0:T(8,128)(2,1)S(1)}, u32[]{:S(2)}, u32[]{:S(2)}) %collective-permute-start.1) | collective-permute-done | bytes 225824 | tf_op jit(solution)/shard_map/ppermute | solution.py:458
  29.3 2.8 %collective-permute-start.4 = (bf16[3,49,768]{2,1,0:T(8,128)(2,1)S(1)}, bf16[3,49,768]{2,1,0:T(8,128)(2,1)S(1)}, u32[]{:S(2)}, u32[]{:S(2)}) collective-permute-start(bf16[3,49,768]{2,1,0:T(8,128)(2,1)S(1)} %get-tuple-element.297), channel_id=1, source_target_pairs={{0,2},{1,3},{2,0},{3,1},{4,6},{5,7},{6,4},{7,5},{8,10},{9,11},{10,... | collective-permute-start | bytes 677384 | tf_op jit(solution)/shard_map/ppermute | solution.py:458
  32.1 1.9 collective-permute-start.3
  34.1 14.9 %attention_forward.1 = (bf16[3,208,768]{2,1,0:T(8,128)(2,1)}, bf16[3,768,208]{2,1,0:T(8,128)(2,1)}, bf16[3,208,2304]{2,1,0:T(8,128)(2,1)}, bf16[3,6,416,208]{3,2...) custom-call(s32[2]{0:T(128)} %pad_add_fusion.at.refs_0_, ...), custom_call_target="tpu_custom_call" | custom-call | flops 4499999744 | bytes 1 | tf_op jit(solution)/shard_map/attention_forward/pallas_call | solution.py:530
  49.0 22.0 %feed_forward.1 = (bf16[3,208,3072]{2,1,0:T(8,128)(2,1)}, bf16[3,208,3072]{2,1,0:T(8,128)(2,1)}, bf16[3,51,768]{2,1,0:T(8,128)(2,1)}, bf16[3,51,768]{2,1,0:T(8,1...) custom-call(s32[2]{0:T(128)} %pad_add_fusion.at.refs_0_, s32[12,2]{1,0:T(8,128)} %copy.40.keep, ...), custom_call_target="tpu_custom_call" | custom-call | flops 6000000000 | bytes 1 | tf_op jit(solution)/shard_map/feed_forward/pallas_call | solution.py:560
  71.0 1.9 collective-permute-start.6
  72.9 0.6 collective-permute-start.8
  73.6 0.6 copy-done.19
  74.3 27.7 %feed_backward.1 = (f32[3,208,768]{2,1,0:T(8,128)}, bf16[3,208,768]{2,1,0:T(8,128)(2,1)}, bf16[1536,768]{1,0:T(8,128)(2,1)}, bf16[1536,768]{1,0:T(8,128)(2,1)}, ...) custom-call(s32[2]{0:T(128)} %pad_add_fusion.at.refs_0_, ...), custom_call_target="tpu_custom_call" | custom-call | flops 7500000256 | bytes 1 | tf_op jit(solution)/shard_map/feed_backward/pallas_call | solution.py:591
  102.1 0.7 copy-done.8
  103.3 8.9 %attention_backward.2 = (bf16[3,208,2304]{2,1,0:T(8,128)(2,1)}, bf16[3,51,768]{2,1,0:T(8,128)(2,1)}, bf16[3,51,768]{2,1,0:T(8,128)(2,1)}, bf16[3,51,768]{2,1,0:T...) custom-call(bf16[3,208,768]{2,1,0:T(8,128)(2,1)} %get-tuple-element.197.dy, ...), custom_call_target="tpu_custom_call" | custom-call | flops 2100000000 | bytes 1 | tf_op jit(solution)/shard_map/attention_backward/pallas_call | solution.py:635
  112.3 1.7 copy-done.1
  114.0 4.1 %sums.6 = (bf16[2,4,96,768]{3,2,1,0:T(8,128)(2,1)}, bf16[2,4,96,768]{3,2,1,0:T(8,128)(2,1)}) custom-call(bf16[2,2,4,96,768]{4,3,2,1,0:T(8,128)(2,1)S(1)} %bitcast.21, bf16[2,2,4,96,768]{4,3,2,1,0:T(8,128)(2,1)} %bitcast.3.refs_1_.refs_2_, bf16[2,2,4,96,768]{4,3,2,1,0:T(8,128)(2,1)S(1)} %bitcast.18, bf16[2,2,4,96,768]{4,3,2,1,0:T(8,128)(2,1)} %bitcast.5.refs_3_.refs_4_.refs_6_), custom_call_target="tpu_custom_call" | custom-call | flops 600000000 | bytes 1 | tf_op jit(solution)/shard_map/sums/pallas_call | solution.py:378
  118.1 1.5 collective-permute-start.11
  119.6 1.5 collective-permute-start.12
  121.1 14.9 %attention_backward.3 = (bf16[3,208,2304]{2,1,0:T(8,128)(2,1)}, bf16[3,51,768]{2,1,0:T(8,128)(2,1)}, bf16[3,51,768]{2,1,0:T(8,128)(2,1)}, bf16[3,51,768]{2,1,0:T...) custom-call(bf16[3,208,768]{2,1,0:T(8,128)(2,1)} %get-tuple-element., ...), custom_call_target="tpu_custom_call", output_to_operand_aliasing={{0}: (8, {}), {1}: (9, {}), {2}: (10, {}), {3}: (11, {}), {... | custom-call | flops 4200000000 | bytes 1 | tf_op jit(solution)/shard_map/attention_backward/pallas_call | solution.py:635
  136.0 3.5 %collective-permute-start.13 = (bf16[3,51,768]{2,1,0:T(8,128)(2,1)}, bf16[3,51,768]{2,1,0:T(8,128)(2,1)}, u32[]{:S(2)}, u32[]{:S(2)}) collective-permute-start(bf16[3,51,768]{2,1,0:T(8,128)(2,1)} %get-tuple-element.220), channel_id=1, source_target_pairs={{0,3},{1,0},{2,1},{3,2},{4,7},{5,4},{6,5},{7,6},{8,11},{9,8},{10,9... | collective-permute-start | bytes 705032 | tf_op jit(solution)/shard_map/ppermute | solution.py:464
  139.5 9.7 %attention_weights.1 = (bf16[384,1664]{1,0:T(8,128)(2,1)}, bf16[384,1664]{1,0:T(8,128)(2,1)}, bf16[384,1664]{1,0:T(8,128)(2,1)}, bf16[384,1664]{1,0:T(8,128)(2,1)}) custom-call(s32[2]{0:T(128)} %pad_add_fusion.at.refs_0_, bf16[3,208,2304]{2,1,0:T(8,128)(2,1)} %get-tuple-element.203.dqkv, bf16[3,208,768]{2,1,0:T(8,128)(2,1)} %get-tuple-element.197.dy, ...), custom_call_target="tpu_custom_call" | custom-call | flops 1800000000 | bytes 1 | tf_op jit(solution)/shard_map/attention_weights/pallas_call | solution.py:676
  149.3 1.7 copy-done.2
  150.9 3.2 %sums.7 = (bf16[4,96,768]{2,1,0:T(8,128)(2,1)S(1)}, bf16[4,96,768]{2,1,0:T(8,128)(2,1)S(1)}) custom-call(bf16[2,2,4,96,768]{4,3,2,1,0:T(8,128)(2,1)S(1)} %bitcast.22, bf16[2,2,4,96,768]{4,3,2,1,0:T(8,128)(2,1)} %bitcast.3.refs_1_.refs_2_, bf16[2,4,96,768]{3,2,1,0:T(8,128)(2,1)S(1)} %collective-permute-done.11.refs_2_.refs_3_, ...), custom_call_target="tpu_custom_call" | custom-call | flops 600000000 | bytes 1 | tf_op jit(solution)/shard_map/sums/pallas_call | solution.py:378
  155.3 0.5 collective-permute-start.16
  155.8 1.5 collective-permute-done.17
  157.3 1.8 collective-permute-done.18
  159.1 0.7 sums.8
  159.8 10.3 %collective-permute-done.15.refs_4_ = bf16[4,96,768]{2,1,0:T(8,128)(2,1)S(1)} collective-permute-done((bf16[4,96,768]{2,1,0:T(8,128)(2,1)S(1)}, bf16[4,96,768]{2,1,0:T(8,128)(2,1)S(1)}, u32[]{:S(2)}, u32[]{:S(2)}) %collective-permute-start.15) | collective-permute-done | bytes 589856 | tf_op jit(solution)/shard_map/ppermute | solution.py:449
  170.3 0.5 collective-permute-start.21
  170.9 1.5 collective-permute-start.22
  172.4 2.7 %sums.9 = (bf16[4,96,768]{2,1,0:T(8,128)(2,1)S(1)}, bf16[4,96,768]{2,1,0:T(8,128)(2,1)S(1)}) custom-call(s32[2]{0:T(128)S(1)} %copy-done.7, bf16[2,2,4,96,768]{4,3,2,1,0:T(8,128)(2,1)S(1)} %bitcast.23, bf16[2,2,4,96,768]{4,3,2,1,0:T(8,128)(2,1)} %bitcast.3.refs_1_.refs_2_, bf16[2,4,96,768]{3,2,1,0:T(8,128)(2,1)S(1)} %collective-permute-done.11.refs_2_.refs_3_, ...), custom_call_target="tpu_custom_call" | custom-call | flops 600000000 | bytes 1 | tf_op jit(solution)/shard_map/sums/pallas_call | solution.py:378
  175.2 1.5 collective-permute-start.19
  176.7 2.9 %collective-permute-start.20 = (bf16[3,51,768]{2,1,0:T(8,128)(2,1)S(1)}, bf16[3,51,768]{2,1,0:T(8,128)(2,1)S(1)}, u32[]{:S(2)}, u32[]{:S(2)}) collective-permute-start(bf16[3,51,768]{2,1,0:T(8,128)(2,1)S(1)} %copy-done.12), channel_id=1, source_target_pairs={{0,2},{1,3},{2,0},{3,1},{4,6},{5,7},{6,4},{7,5},{8,10},{9,11},{10,... | collective-permute-start | bytes 705032 | tf_op jit(solution)/shard_map/ppermute | solution.py:464
  179.6 2.2 settle.2
  181.8 11.5 %collective-permute-done.20.c2 = bf16[3,51,768]{2,1,0:T(8,128)(2,1)S(1)} collective-permute-done((bf16[3,51,768]{2,1,0:T(8,128)(2,1)S(1)}, bf16[3,51,768]{2,1,0:T(8,128)(2,1)S(1)}, u32[]{:S(2)}, u32[]{:S(2)}) %collective-permute-start.20) | collective-permute-done | bytes 235040 | tf_op jit(solution)/shard_map/ppermute | solution.py:464
  193.3 1.0 collective-permute-done.19
  194.8 0.9 collective-permute-start.23
  195.7 1.5 collective-permute-start.24
  197.2 2.6 %collective-permute-start.26 = (bf16[4,96,768]{2,1,0:T(8,128)(2,1)S(1)}, bf16[4,96,768]{2,1,0:T(8,128)(2,1)S(1)}, u32[]{:S(2)}, u32[]{:S(2)}) collective-permute-start(bf16[4,96,768]{2,1,0:T(8,128)(2,1)S(1)} %add.58), channel_id=1, source_target_pairs={{0,2},{1,3},{2,0},{3,1},{4,6},{5,7},{6,4},{7,5},{8,10},{9,11},{10,... | collective-permute-start | bytes 1769480 | tf_op jit(solution)/shard_map/ppermute | solution.py:709
  199.9 2.0 collective-permute-done.23.refs_4_
  201.9 0.8 collective-permute-done.24.refs_8_
  202.7 0.9 sums.11
  203.7 2.6 %collective-permute-start.25 = (bf16[2,48,1664]{2,1,0:T(8,128)(2,1)S(1)}, bf16[2,48,1664]{2,1,0:T(8,128)(2,1)S(1)}, u32[]{:S(2)}, u32[]{:S(2)}) collective-permute-start(bf16[2,48,1664]{2,1,0:T(8,128)(2,1)S(1)} %get-tuple-element.262), channel_id=1, source_target_pairs={{0,1},{1,0},{2,3},{3,2},{4,5},{5,4},{6,7},{7,6},{8,9},{9,8},{10,11... | collective-permute-start | bytes 958472 | tf_op jit(solution)/shard_map/ppermute | solution.py:706
  206.3 3.3 %settle.3 = (bf16[12,49,768]{2,1,0:T(8,128)(2,1)}, bf16[12,2,768]{2,1,0:T(2,128)(2,1)}) custom-call(s32[2]{0:T(128)S(1)} %copy-done.7, bf16[3,51,768]{2,1,0:T(8,128)(2,1)S(1)} %copy-done.6, bf16[3,51,768]{2,1,0:T(8,128)(2,1)} %collective-permute-done.13.c1, bf16[3,51,768]{2,1,0:T(8,128)(2,1)S(1)} %collective-permute-done.20.c2, ...), custom_call_target="tpu_custom_call" | custom-call | flops 600000000 | bytes 1 | tf_op jit(solution)/shard_map/settle/pallas_call | solution.py:472
  209.5 14.0 %collective-permute-done.26 = bf16[4,96,768]{2,1,0:T(8,128)(2,1)S(1)} collective-permute-done((bf16[4,96,768]{2,1,0:T(8,128)(2,1)S(1)}, bf16[4,96,768]{2,1,0:T(8,128)(2,1)S(1)}, u32[]{:S(2)}, u32[]{:S(2)}) %collective-permute-start.26) | collective-permute-done | bytes 589856 | tf_op jit(solution)/shard_map/ppermute | solution.py:709
  223.6 0.8 collective-permute-start.27
  224.6 4.6 %collective-permute-start.28 = (bf16[2,48,1664]{2,1,0:T(8,128)(2,1)S(1)}, bf16[2,48,1664]{2,1,0:T(8,128)(2,1)S(1)}, u32[]{:S(2)}, u32[]{:S(2)}) collective-permute-start(bf16[2,48,1664]{2,1,0:T(8,128)(2,1)S(1)} %add.60), channel_id=1, source_target_pairs={{0,2},{1,3},{2,0},{3,1},{4,6},{5,7},{6,4},{7,5},{8,10},{9,11},{10,... | collective-permute-start | bytes 958472 | tf_op jit(solution)/shard_map/ppermute | solution.py:709
  229.2 15.7 %collective-permute-done.27.other = bf16[4,96,768]{2,1,0:T(8,128)(2,1)S(1)} collective-permute-done((bf16[4,96,768]{2,1,0:T(8,128)(2,1)S(1)}, bf16[4,96,768]{2,1,0:T(8,128)(2,1)S(1)}, u32[]{:S(2)}, u32[]{:S(2)}) %collective-permute-start.27) | collective-permute-done | bytes 589856 | tf_op jit(solution)/shard_map/ppermute | solution.py:706
  244.8 2.2 finish_feed.1
  247.1 1.3 collective-permute-start.29
  248.4 6.4 %collective-permute-done.29 = bf16[2,48,1664]{2,1,0:T(8,128)(2,1)S(1)} collective-permute-done((bf16[2,48,1664]{2,1,0:T(8,128)(2,1)S(1)}, bf16[2,48,1664]{2,1,0:T(8,128)(2,1)S(1)}, u32[]{:S(2)}, u32[]{:S(2)}) %collective-permute-start.29) | collective-permute-done | bytes 319520 | tf_op jit(solution)/shard_map/ppermute | solution.py:706
  254.7 1.7 finish.1
  256.4 0.6 reduce.2
  (74 shorter events, 2.9 us)
Async XLA Ops:
  0.6 28.5 %copy-start.11 = (bf16[12,49,768]{2,1,0:T(8,128)(2,1)S(1)}, bf16[12,49,768]{2,1,0:T(8,128)(2,1)}, u32[]{:S(2)}) copy-start(bf16[12,49,768]{2,1,0:T(8,128)(2,1)} %g0.1) | copy-start | bytes 2709508
  2.0 18.4 %collective-permute-start.2 = (bf16[3,49,768]{2,1,0:T(8,128)(2,1)S(1)}, bf16[3,49,768]{2,1,0:T(8,128)(2,1)S(1)}, u32[]{:S(2)}, u32[]{:S(2)}) collective-permute-start(bf16[3,49,768]{2,1,0:T(8,128)(2,1)S(1)} %get-tuple-element.299), channel_id=1, source_target_pairs={{0,3},{1,0},{2,1},{3,2},{4,7},{5,4},{6,5},{7,6},{8,11},{9,8},{10,9... | collective-permute-start | bytes 677384 | tf_op jit(solution)/shard_map/ppermute | solution.py:458
  7.1 22.0 %collective-permute-start.1 = (bf16[3,49,768]{2,1,0:T(8,128)(2,1)S(1)}, bf16[3,49,768]{2,1,0:T(8,128)(2,1)S(1)}, u32[]{:S(2)}, u32[]{:S(2)}) collective-permute-start(bf16[3,49,768]{2,1,0:T(8,128)(2,1)S(1)} %get-tuple-element.300), channel_id=1, source_target_pairs={{0,2},{1,3},{2,0},{3,1},{4,6},{5,7},{6,4},{7,5},{8,10},{9,11},{10,... | collective-permute-start | bytes 677384 | tf_op jit(solution)/shard_map/ppermute | solution.py:458
  7.1 22.0 %collective-permute-start = (bf16[3,49,768]{2,1,0:T(8,128)(2,1)S(1)}, bf16[3,49,768]{2,1,0:T(8,128)(2,1)S(1)}, u32[]{:S(2)}, u32[]{:S(2)}) collective-permute-start(bf16[3,49,768]{2,1,0:T(8,128)(2,1)S(1)} %get-tuple-element.301), channel_id=1, source_target_pairs={{0,1},{1,2},{2,3},{3,0},{4,5},{5,6},{6,7},{7,4},{8,9},{9,10},{10,1... | collective-permute-start | bytes 677384 | tf_op jit(solution)/shard_map/ppermute | solution.py:458
  20.5 13.6 %copy-start.15 = (bf16[3,49,768]{2,1,0:T(8,128)(2,1)}, bf16[3,49,768]{2,1,0:T(8,128)(2,1)S(1)}, u32[]{:S(2)}) copy-start(bf16[3,49,768]{2,1,0:T(8,128)(2,1)S(1)} %collective-permute-done.2.x3) | copy-start | bytes 677380
  29.1 5.0 %copy-start.16 = (bf16[3,49,768]{2,1,0:T(8,128)(2,1)}, bf16[3,49,768]{2,1,0:T(8,128)(2,1)S(1)}, u32[]{:S(2)}) copy-start(bf16[3,49,768]{2,1,0:T(8,128)(2,1)S(1)} %collective-permute-done.1.x2) | copy-start | bytes 677380
  29.1 5.0 %copy-start.17 = (bf16[3,49,768]{2,1,0:T(8,128)(2,1)}, bf16[3,49,768]{2,1,0:T(8,128)(2,1)S(1)}, u32[]{:S(2)}) copy-start(bf16[3,49,768]{2,1,0:T(8,128)(2,1)S(1)} %collective-permute-done.x1) | copy-start | bytes 677380
  29.2 43.7 %collective-permute-start.5 = (bf16[3,49,768]{2,1,0:T(8,128)(2,1)S(1)}, bf16[3,49,768]{2,1,0:T(8,128)(2,1)S(1)}, u32[]{:S(2)}, u32[]{:S(2)}) collective-permute-start(bf16[3,49,768]{2,1,0:T(8,128)(2,1)S(1)} %get-tuple-element.296), channel_id=1, source_target_pairs={{0,3},{1,0},{2,1},{3,2},{4,7},{5,4},{6,5},{7,6},{8,11},{9,8},{10,9... | collective-permute-start | bytes 677384 | tf_op jit(solution)/shard_map/ppermute | solution.py:458
  29.3 44.3 %collective-permute-start.4 = (bf16[3,49,768]{2,1,0:T(8,128)(2,1)S(1)}, bf16[3,49,768]{2,1,0:T(8,128)(2,1)S(1)}, u32[]{:S(2)}, u32[]{:S(2)}) collective-permute-start(bf16[3,49,768]{2,1,0:T(8,128)(2,1)S(1)} %get-tuple-element.297), channel_id=1, source_target_pairs={{0,2},{1,3},{2,0},{3,1},{4,6},{5,7},{6,4},{7,5},{8,10},{9,11},{10,... | collective-permute-start | bytes 677384 | tf_op jit(solution)/shard_map/ppermute | solution.py:458
  32.1 41.4 %collective-permute-start.3 = (bf16[3,49,768]{2,1,0:T(8,128)(2,1)S(1)}, bf16[3,49,768]{2,1,0:T(8,128)(2,1)S(1)}, u32[]{:S(2)}, u32[]{:S(2)}) collective-permute-start(bf16[3,49,768]{2,1,0:T(8,128)(2,1)S(1)} %get-tuple-element.298), channel_id=1, source_target_pairs={{0,1},{1,2},{2,3},{3,0},{4,5},{5,6},{6,7},{7,4},{8,9},{9,10},{10,1... | collective-permute-start | bytes 677384 | tf_op jit(solution)/shard_map/ppermute | solution.py:458
  71.0 31.1 %collective-permute-start.6 = (bf16[3,51,768]{2,1,0:T(8,128)(2,1)}, bf16[3,51,768]{2,1,0:T(8,128)(2,1)S(1)}, u32[]{:S(2)}, u32[]{:S(2)}) collective-permute-start(bf16[3,51,768]{2,1,0:T(8,128)(2,1)} %get-tuple-element.174), channel_id=1, source_target_pairs={{0,3},{1,0},{2,1},{3,2},{4,7},{5,4},{6,5},{7,6},{8,11},{9,8},{10,9... | collective-permute-start | bytes 705032 | tf_op jit(solution)/shard_map/ppermute | solution.py:464
  72.9 29.2 %collective-permute-start.7 = (bf16[3,51,768]{2,1,0:T(8,128)(2,1)}, bf16[3,51,768]{2,1,0:T(8,128)(2,1)S(1)}, u32[]{:S(2)}, u32[]{:S(2)}) collective-permute-start(bf16[3,51,768]{2,1,0:T(8,128)(2,1)} %get-tuple-element.175), channel_id=1, source_target_pairs={{0,2},{1,3},{2,0},{3,1},{4,6},{5,7},{6,4},{7,5},{8,10},{9,11},{10,... | collective-permute-start | bytes 705032 | tf_op jit(solution)/shard_map/ppermute | solution.py:464
  72.9 0.7 copy-start.18
  72.9 29.2 %collective-permute-start.8 = (bf16[3,51,768]{2,1,0:T(8,128)(2,1)}, bf16[3,51,768]{2,1,0:T(8,128)(2,1)S(1)}, u32[]{:S(2)}, u32[]{:S(2)}) collective-permute-start(bf16[3,51,768]{2,1,0:T(8,128)(2,1)} %get-tuple-element.176), channel_id=1, source_target_pairs={{0,1},{1,2},{2,3},{3,0},{4,5},{5,6},{6,7},{7,4},{8,9},{9,10},{10,1... | collective-permute-start | bytes 705032 | tf_op jit(solution)/shard_map/ppermute | solution.py:464
  73.5 0.7 copy-start.19
  73.6 0.8 copy-start.20
  102.1 0.7 copy-start.8
  102.8 9.4 %collective-permute-start.9 = (bf16[4,4,96,768]{3,2,1,0:T(8,128)(2,1)}, bf16[4,4,96,768]{3,2,1,0:T(8,128)(2,1)}, u32[]{:S(2)}, u32[]{:S(2)}) collective-permute-start(bf16[4,4,96,768]{3,2,1,0:T(8,128)(2,1)} %get-tuple-element.177), channel_id=1, source_target_pairs={{0,4},{4,0},{8,12},{12,8},{16,20},{20,16},{24,28},{28,24},{1,5},{5... | collective-permute-start | bytes 7077896 | tf_op jit(solution)/shard_map/ppermute | solution.py:449
  102.8 9.4 %collective-permute-start.10 = (bf16[1536,768]{1,0:T(8,128)(2,1)}, bf16[1536,768]{1,0:T(8,128)(2,1)}, u32[]{:S(2)}, u32[]{:S(2)}) collective-permute-start(bf16[1536,768]{1,0:T(8,128)(2,1)} %get-tuple-element.178), channel_id=1, source_target_pairs={{0,4},{4,0},{8,12},{12,8},{16,20},{20,16},{24,28},{28,24},{1,5},{5... | collective-permute-start | bytes 7077896 | tf_op jit(solution)/shard_map/ppermute | solution.py:449
  103.3 9.0 %copy-start = (bf16[1536,768]{1,0:T(8,128)(2,1)S(1)}, bf16[1536,768]{1,0:T(8,128)(2,1)}, u32[]{:S(2)}) copy-start(bf16[1536,768]{1,0:T(8,128)(2,1)} %get-tuple-element.191) | copy-start | bytes 7077892
  112.3 1.7 copy-start.1
  118.1 31.2 %collective-permute-start.11 = (bf16[2,4,96,768]{3,2,1,0:T(8,128)(2,1)}, bf16[2,4,96,768]{3,2,1,0:T(8,128)(2,1)S(1)}, u32[]{:S(2)}, u32[]{:S(2)}) collective-permute-start(bf16[2,4,96,768]{3,2,1,0:T(8,128)(2,1)} %get-tuple-element.195), channel_id=1, source_target_pairs={{0,8},{4,12},{8,0},{12,4},{16,24},{20,28},{24,16},{28,20},{1,9},{5... | collective-permute-start | bytes 3538952 | tf_op jit(solution)/shard_map/ppermute | solution.py:449
  119.6 29.7 %collective-permute-start.12 = (bf16[2,4,96,768]{3,2,1,0:T(8,128)(2,1)}, bf16[2,4,96,768]{3,2,1,0:T(8,128)(2,1)}, u32[]{:S(2)}, u32[]{:S(2)}) collective-permute-start(bf16[2,4,96,768]{3,2,1,0:T(8,128)(2,1)} %get-tuple-element.196), channel_id=1, source_target_pairs={{0,16},{4,20},{8,24},{12,28},{16,0},{20,4},{24,8},{28,12},{1,17},{... | collective-permute-start | bytes 3538952 | tf_op jit(solution)/shard_map/ppermute | solution.py:449
  136.0 18.2 %collective-permute-start.13 = (bf16[3,51,768]{2,1,0:T(8,128)(2,1)}, bf16[3,51,768]{2,1,0:T(8,128)(2,1)}, u32[]{:S(2)}, u32[]{:S(2)}) collective-permute-start(bf16[3,51,768]{2,1,0:T(8,128)(2,1)} %get-tuple-element.220), channel_id=1, source_target_pairs={{0,3},{1,0},{2,1},{3,2},{4,7},{5,4},{6,5},{7,6},{8,11},{9,8},{10,9... | collective-permute-start | bytes 705032 | tf_op jit(solution)/shard_map/ppermute | solution.py:464
  139.5 14.7 %collective-permute-start.14 = (bf16[3,51,768]{2,1,0:T(8,128)(2,1)}, bf16[3,51,768]{2,1,0:T(8,128)(2,1)}, u32[]{:S(2)}, u32[]{:S(2)}) collective-permute-start(bf16[3,51,768]{2,1,0:T(8,128)(2,1)} %get-tuple-element.221), channel_id=1, source_target_pairs={{0,1},{1,2},{2,3},{3,0},{4,5},{5,6},{6,7},{7,4},{8,9},{9,10},{10,1... | collective-permute-start | bytes 705032 | tf_op jit(solution)/shard_map/ppermute | solution.py:464
  149.3 1.7 copy-start.2
  150.9 3.3 %copy-start.14 = (bf16[384,1664]{1,0:T(8,128)(2,1)S(1)}, bf16[384,1664]{1,0:T(8,128)(2,1)}, u32[]{:S(2)}) copy-start(bf16[384,1664]{1,0:T(8,128)(2,1)} %get-tuple-element.224) | copy-start | bytes 3833860
  150.9 3.4 %copy-start.13 = (bf16[384,1664]{1,0:T(8,128)(2,1)S(1)}, bf16[384,1664]{1,0:T(8,128)(2,1)}, u32[]{:S(2)}) copy-start(bf16[384,1664]{1,0:T(8,128)(2,1)} %get-tuple-element.225) | copy-start | bytes 3833860
  150.9 8.2 %copy-start.4 = (bf16[384,1664]{1,0:T(8,128)(2,1)S(1)}, bf16[384,1664]{1,0:T(8,128)(2,1)}, u32[]{:S(2)}) copy-start(bf16[384,1664]{1,0:T(8,128)(2,1)} %get-tuple-element.228) | copy-start | bytes 3833860
  150.9 8.2 %copy-start.5 = (bf16[384,1664]{1,0:T(8,128)(2,1)S(1)}, bf16[384,1664]{1,0:T(8,128)(2,1)}, u32[]{:S(2)}) copy-start(bf16[384,1664]{1,0:T(8,128)(2,1)} %get-tuple-element.230) | copy-start | bytes 3833860
  154.2 3.1 %collective-permute-start.17 = (bf16[384,1664]{1,0:T(8,128)(2,1)S(1)}, bf16[384,1664]{1,0:T(8,128)(2,1)S(1)}, u32[]{:S(2)}, u32[]{:S(2)}) collective-permute-start(bf16[384,1664]{1,0:T(8,128)(2,1)S(1)} %copy-done.14), channel_id=1, source_target_pairs={{0,4},{4,0},{8,12},{12,8},{16,20},{20,16},{24,28},{28,24},{1,5},{5... | collective-permute-start | bytes 3833864 | tf_op jit(solution)/shard_map/ppermute | solution.py:449
  154.3 4.8 %collective-permute-start.18 = (bf16[384,1664]{1,0:T(8,128)(2,1)S(1)}, bf16[384,1664]{1,0:T(8,128)(2,1)S(1)}, u32[]{:S(2)}, u32[]{:S(2)}) collective-permute-start(bf16[384,1664]{1,0:T(8,128)(2,1)S(1)} %copy-done.13), channel_id=1, source_target_pairs={{0,4},{4,0},{8,12},{12,8},{16,20},{20,16},{24,28},{28,24},{1,5},{5... | collective-permute-start | bytes 3833864 | tf_op jit(solution)/shard_map/ppermute | solution.py:449
  154.8 15.3 %collective-permute-start.15 = (bf16[4,96,768]{2,1,0:T(8,128)(2,1)S(1)}, bf16[4,96,768]{2,1,0:T(8,128)(2,1)S(1)}, u32[]{:S(2)}, u32[]{:S(2)}) collective-permute-start(bf16[4,96,768]{2,1,0:T(8,128)(2,1)S(1)} %get-tuple-element.222), channel_id=1, source_target_pairs={{0,16},{4,20},{8,24},{12,28},{16,0},{20,4},{24,8},{28,12},{1,17},{... | collective-permute-start | bytes 1769480 | tf_op jit(solution)/shard_map/ppermute | solution.py:449
  155.3 15.0 %collective-permute-start.16 = (bf16[4,96,768]{2,1,0:T(8,128)(2,1)S(1)}, bf16[4,96,768]{2,1,0:T(8,128)(2,1)S(1)}, u32[]{:S(2)}, u32[]{:S(2)}) collective-permute-start(bf16[4,96,768]{2,1,0:T(8,128)(2,1)S(1)} %get-tuple-element.223), channel_id=1, source_target_pairs={{0,8},{4,12},{8,0},{12,4},{16,24},{20,28},{24,16},{28,20},{1,9},{5... | collective-permute-start | bytes 1769480 | tf_op jit(solution)/shard_map/ppermute | solution.py:449
  159.1 13.3 %copy-start.3 = (bf16[4,4,96,768]{3,2,1,0:T(8,128)(2,1)S(1)}, bf16[4,4,96,768]{3,2,1,0:T(8,128)(2,1)}, u32[]{:S(2)}) copy-start(bf16[4,4,96,768]{3,2,1,0:T(8,128)(2,1)} %get-tuple-element.169) | copy-start | bytes 7077892
  159.1 13.3 %copy-start.7 = (s32[2]{0:T(128)S(1)}, s32[2]{0:T(128)}, u32[]{:S(2)}) copy-start(s32[2]{0:T(128)} %pad_add_fusion.at.refs_0_) | copy-start | bytes 28
  170.3 6.3 %copy-start.12 = (bf16[3,51,768]{2,1,0:T(8,128)(2,1)S(1)}, bf16[3,51,768]{2,1,0:T(8,128)(2,1)}, u32[]{:S(2)}) copy-start(bf16[3,51,768]{2,1,0:T(8,128)(2,1)} %get-tuple-element.249) | copy-start | bytes 705028
  170.3 9.3 %copy-start.9 = (bf16[3,51,768]{2,1,0:T(8,128)(2,1)S(1)}, bf16[3,51,768]{2,1,0:T(8,128)(2,1)}, u32[]{:S(2)}) copy-start(bf16[3,51,768]{2,1,0:T(8,128)(2,1)} %copy-done.8) | copy-start | bytes 705028
  170.3 9.3 %copy-start.10 = (bf16[3,51,768]{2,1,0:T(8,128)(2,1)S(1)}, bf16[3,51,768]{2,1,0:T(8,128)(2,1)}, u32[]{:S(2)}) copy-start(bf16[3,51,768]{2,1,0:T(8,128)(2,1)} %get-tuple-element.242.c0) | copy-start | bytes 705028
  170.3 24.1 %collective-permute-start.21 = (bf16[2,2,48,1664]{3,2,1,0:T(8,128)(2,1)S(1)}, bf16[2,2,48,1664]{3,2,1,0:T(8,128)(2,1)S(1)}, u32[]{:S(2)}, u32[]{:S(2)}) collective-permute-start(bf16[2,2,48,1664]{3,2,1,0:T(8,128)(2,1)S(1)} %get-tuple-element.254), channel_id=1, source_target_pairs={{0,8},{4,12},{8,0},{12,4},{16,24},{20,28},{24,16},{28,20},{1,9},{5... | collective-permute-start | bytes 1916936 | tf_op jit(solution)/shard_map/ppermute | solution.py:449
  170.9 23.6 %collective-permute-start.22 = (bf16[2,2,48,1664]{3,2,1,0:T(8,128)(2,1)S(1)}, bf16[2,2,48,1664]{3,2,1,0:T(8,128)(2,1)S(1)}, u32[]{:S(2)}, u32[]{:S(2)}) collective-permute-start(bf16[2,2,48,1664]{3,2,1,0:T(8,128)(2,1)S(1)} %get-tuple-element.255), channel_id=1, source_target_pairs={{0,16},{4,20},{8,24},{12,28},{16,0},{20,4},{24,8},{28,12},{1,17},{... | collective-permute-start | bytes 1916936 | tf_op jit(solution)/shard_map/ppermute | solution.py:449
  175.2 19.2 %collective-permute-start.19 = (bf16[4,96,768]{2,1,0:T(8,128)(2,1)S(1)}, bf16[4,96,768]{2,1,0:T(8,128)(2,1)S(1)}, u32[]{:S(2)}, u32[]{:S(2)}) collective-permute-start(bf16[4,96,768]{2,1,0:T(8,128)(2,1)S(1)} %get-tuple-element.236), channel_id=1, source_target_pairs={{0,1},{1,0},{2,3},{3,2},{4,5},{5,4},{6,7},{7,6},{8,9},{9,8},{10,11... | collective-permute-start | bytes 1769480 | tf_op jit(solution)/shard_map/ppermute | solution.py:706
  176.7 16.6 %collective-permute-start.20 = (bf16[3,51,768]{2,1,0:T(8,128)(2,1)S(1)}, bf16[3,51,768]{2,1,0:T(8,128)(2,1)S(1)}, u32[]{:S(2)}, u32[]{:S(2)}) collective-permute-start(bf16[3,51,768]{2,1,0:T(8,128)(2,1)S(1)} %copy-done.12), channel_id=1, source_target_pairs={{0,2},{1,3},{2,0},{3,1},{4,6},{5,7},{6,4},{7,5},{8,10},{9,11},{10,... | collective-permute-start | bytes 705032 | tf_op jit(solution)/shard_map/ppermute | solution.py:464
  194.8 7.1 %collective-permute-start.23 = (bf16[2,48,1664]{2,1,0:T(8,128)(2,1)S(1)}, bf16[2,48,1664]{2,1,0:T(8,128)(2,1)S(1)}, u32[]{:S(2)}, u32[]{:S(2)}) collective-permute-start(bf16[2,48,1664]{2,1,0:T(8,128)(2,1)S(1)} %get-tuple-element.258), channel_id=1, source_target_pairs={{0,16},{4,20},{8,24},{12,28},{16,0},{20,4},{24,8},{28,12},{1,17},{... | collective-permute-start | bytes 958472 | tf_op jit(solution)/shard_map/ppermute | solution.py:449
  195.7 10.5 %copy-start.6 = (bf16[3,51,768]{2,1,0:T(8,128)(2,1)S(1)}, bf16[3,51,768]{2,1,0:T(8,128)(2,1)}, u32[]{:S(2)}) copy-start(bf16[3,51,768]{2,1,0:T(8,128)(2,1)} %get-tuple-element.269.c0) | copy-start | bytes 705028
  195.7 7.0 %collective-permute-start.24 = (bf16[2,48,1664]{2,1,0:T(8,128)(2,1)S(1)}, bf16[2,48,1664]{2,1,0:T(8,128)(2,1)S(1)}, u32[]{:S(2)}, u32[]{:S(2)}) collective-permute-start(bf16[2,48,1664]{2,1,0:T(8,128)(2,1)S(1)} %get-tuple-element.259), channel_id=1, source_target_pairs={{0,8},{4,12},{8,0},{12,4},{16,24},{20,28},{24,16},{28,20},{1,9},{5... | collective-permute-start | bytes 958472 | tf_op jit(solution)/shard_map/ppermute | solution.py:449
  197.2 26.3 %collective-permute-start.26 = (bf16[4,96,768]{2,1,0:T(8,128)(2,1)S(1)}, bf16[4,96,768]{2,1,0:T(8,128)(2,1)S(1)}, u32[]{:S(2)}, u32[]{:S(2)}) collective-permute-start(bf16[4,96,768]{2,1,0:T(8,128)(2,1)S(1)} %add.58), channel_id=1, source_target_pairs={{0,2},{1,3},{2,0},{3,1},{4,6},{5,7},{6,4},{7,5},{8,10},{9,11},{10,... | collective-permute-start | bytes 1769480 | tf_op jit(solution)/shard_map/ppermute | solution.py:709
  203.7 19.8 %collective-permute-start.25 = (bf16[2,48,1664]{2,1,0:T(8,128)(2,1)S(1)}, bf16[2,48,1664]{2,1,0:T(8,128)(2,1)S(1)}, u32[]{:S(2)}, u32[]{:S(2)}) collective-permute-start(bf16[2,48,1664]{2,1,0:T(8,128)(2,1)S(1)} %get-tuple-element.262), channel_id=1, source_target_pairs={{0,1},{1,0},{2,3},{3,2},{4,5},{5,4},{6,7},{7,6},{8,9},{9,8},{10,11... | collective-permute-start | bytes 958472 | tf_op jit(solution)/shard_map/ppermute | solution.py:706
  223.6 21.2 %collective-permute-start.27 = (bf16[4,96,768]{2,1,0:T(8,128)(2,1)S(1)}, bf16[4,96,768]{2,1,0:T(8,128)(2,1)S(1)}, u32[]{:S(2)}, u32[]{:S(2)}) collective-permute-start(bf16[4,96,768]{2,1,0:T(8,128)(2,1)S(1)} %add.59.mine), channel_id=1, source_target_pairs={{0,1},{1,0},{2,3},{3,2},{4,5},{5,4},{6,7},{7,6},{8,9},{9,8},{10,11... | collective-permute-start | bytes 1769480 | tf_op jit(solution)/shard_map/ppermute | solution.py:706
  224.6 22.5 %collective-permute-start.28 = (bf16[2,48,1664]{2,1,0:T(8,128)(2,1)S(1)}, bf16[2,48,1664]{2,1,0:T(8,128)(2,1)S(1)}, u32[]{:S(2)}, u32[]{:S(2)}) collective-permute-start(bf16[2,48,1664]{2,1,0:T(8,128)(2,1)S(1)} %add.60), channel_id=1, source_target_pairs={{0,2},{1,3},{2,0},{3,1},{4,6},{5,7},{6,4},{7,5},{8,10},{9,11},{10,... | collective-permute-start | bytes 958472 | tf_op jit(solution)/shard_map/ppermute | solution.py:709
  247.1 7.6 %collective-permute-start.29 = (bf16[2,48,1664]{2,1,0:T(8,128)(2,1)S(1)}, bf16[2,48,1664]{2,1,0:T(8,128)(2,1)S(1)}, u32[]{:S(2)}, u32[]{:S(2)}) collective-permute-start(bf16[2,48,1664]{2,1,0:T(8,128)(2,1)S(1)} %add.61), channel_id=1, source_target_pairs={{0,1},{1,0},{2,3},{3,2},{4,5},{5,4},{6,7},{7,6},{8,9},{9,8},{10,11... | collective-permute-start | bytes 958472 | tf_op jit(solution)/shard_map/ppermute | solution.py:706

commit v3 on v2

v3 whole, which is shorter than its diff:
```python
from functools import partial

import jax
import jax.numpy as jnp
from jax import lax
from jax.experimental import pallas as pl
from jax.experimental.pallas import tpu as pltpu
from jax.sharding import PartitionSpec as P

HEAD_DIM = 64
KEEP = 1.0 / 0.9
EPS = 1e-06
BF = jnp.bfloat16
F32 = jnp.float32
COLUMNS = 128
PACE = 0.3
OWNERS = 8
VMEM = 60 * 2**20

def dot(a, b):
    return lax.dot_general(a, b, (((1,), (0,)), ((), ())), preferred_element_type=F32)


def dot_nt(a, b):
    return lax.dot_general(a, b, (((1,), (1,)), ((), ())), preferred_element_type=F32)


def dot_tn(a, b):
    return lax.dot_general(a, b, (((0,), (0,)), ((), ())), preferred_element_type=F32)


def gelu_both(u):
    cdf = 0.5 + 0.5 * lax.erf(u * 0.5**0.5)
    return u * cdf, cdf + u * (jnp.exp(-0.5 * u * u) * 0.3989422804014327)


def normalize(x):
    center = x - jnp.mean(x, axis=-1, keepdims=True)
    inv = lax.rsqrt(jnp.mean(center * center, axis=-1, keepdims=True) + EPS)
    return center * inv, inv


def norm_back(up, hat, inv, gain):
    e = up * gain
    return inv * (
        e
        - jnp.mean(e, axis=-1, keepdims=True)
        - hat * jnp.mean(e * hat, axis=-1, keepdims=True)
    )


def both_heads(v, low):
    return jnp.concatenate([jnp.where(low, v, BF(0)), jnp.where(low, BF(0), v)], axis=0)


def colsum(v):
    return jnp.sum(v, axis=0, keepdims=True)


def place(b):
    return (b & 1) * (OWNERS // 2) + lax.shift_right_logical(b, 1)


def store_relative(ref, lead, value, d):
    n = value.shape[0] // OWNERS
    for b in range(OWNERS):
        spot = pl.multiple_of(place(b ^ d) * n, n)
        ref[lead, pl.ds(spot, n), :] = value[b * n : (b + 1) * n]


def forward_kernel(
    at, keep, x0, x1, x2, x3, sp, g1, b1, wq, bq, wp, bp, g2, b2,
    xs, a1t, qkv, prob, ot, h, a2, a2t, buf, *, rows, heads,
):
    i = pl.program_id(0)
    d = at[1]
    part = x0.shape[1]
    ns = sp.shape[1]
    width = x0.shape[2]
    buf[...] = jnp.zeros_like(buf)
    buf[0:ns, :] = sp[0].astype(F32)
    came = [ref[0].astype(F32) for ref in (x0, x1, x2, x3)]
    for s in range(len(came)):
        k = (at[0] - s) & 3
        near, far = (jnp.where((k & 1) == 0, came[j], came[j + 1]) for j in (0, 2))
        buf[ns + s * part : ns + (s + 1) * part, :] = jnp.where(k < 2, near, far)
    x = buf[...]
    xs[0] = x.astype(BF)
    hat, _ = normalize(x)
    a1 = (hat * g1[...].astype(F32) + b1[...].astype(F32)).astype(BF)
    store_relative(a1t, 0, a1.T, d)
    both = (dot(a1, wq[...]) + bq[...]).astype(BF)
    qkv[0] = both
    padded = x.shape[0]
    low = lax.broadcasted_iota(jnp.int32, (padded, 2 * HEAD_DIM), 1) < HEAD_DIM
    seen = lax.broadcasted_iota(jnp.int32, (2 * padded, padded), 1) < rows
    outs = []
    for j in range(heads // 2):
        c = j * 2 * HEAD_DIM
        q = both[:, c : c + 2 * HEAD_DIM] * BF(HEAD_DIM**-0.5)
        k = both[:, width + c : width + c + 2 * HEAD_DIM]
        v = both[:, 2 * width + c : 2 * width + c + 2 * HEAD_DIM]
        s = jnp.where(seen, dot_nt(both_heads(q, low), k), -1e30)
        e = jnp.exp(s - jnp.max(s, axis=-1, keepdims=True))
        p = (e * (1.0 / jnp.sum(e, axis=-1, keepdims=True))).astype(BF)
        prob[0, j] = p
        pv = dot(p, v)
        outs.append(jnp.where(low, pv[:padded], pv[padded:]))
    o32 = jnp.concatenate(outs, axis=1)
    o = o32.astype(BF)
    store_relative(ot, 0, o.T, d)
    y = dot(o, wp[...]) + bp[...].astype(F32)
    m1 = keep[at[0] * pl.num_programs(0) + i, 0].astype(F32) * KEEP
    hh = x + m1 * y
    h[0] = hh
    hat2, _ = normalize(hh)
    n2 = (hat2 * g2[...].astype(F32) + b2[...].astype(F32)).astype(BF)
    a2[0] = n2
    store_relative(a2t, 0, n2.T, d)


def feed_kernel(
    at, keep, g0, g1, g2, g3, sg, h, a2, a2t, w1, b1, w2, b2, gain,
    out, dh, dy, w2s, w2k, w1s, w1k, db1, small,
    dout, dz, z, da2, acts, dus, across, *, images,
):
    t = pl.program_id(0)
    part = g0.shape[1]
    ns = sg.shape[1]
    padded = h.shape[1]

    @pl.when(t == 0)
    def _():
        for i in range(images):
            m2 = keep[at[0] * images + i, 1].astype(F32) * KEEP
            r = i * padded
            dout[r : r + padded, :] = jnp.zeros((padded, dout.shape[1]), F32)
            dout[r : r + ns, :] = sg[i].astype(F32)
            for k, ref in enumerate((g0, g1, g2, g3)):
                lo = r + ns + k * part
                dout[lo : lo + part, :] = ref[i].astype(F32)
            dz[r : r + padded, :] = (dout[r : r + padded, :] * m2).astype(BF)
            across[:, r : r + padded] = a2t[i]
        z[...] = jnp.zeros_like(z)
        da2[...] = jnp.zeros_like(da2)

    wa = w1[...]
    wb = w2[...]
    bias = b1[...].astype(F32)
    db = None
    for i in range(images):
        r = slice(i * padded, (i + 1) * padded)
        g, slope = gelu_both(dot(a2[i], wa) + bias)
        acts[r, :] = g.astype(BF)
        du = (slope * dot_nt(dz[r, :], wb)).astype(BF)
        dus[r, :] = du
        s = colsum(du.astype(F32))
        db = s if db is None else db + s
    db1[...] = db
    z[...] += dot(acts[...], wb)
    da2[...] += dot_nt(dus[...], wa)
    half = across.shape[0] // 2
    w1k[...] = dot(across[:half, :], dus[...]).astype(BF).reshape(w1k.shape)
    w1s[...] = dot(across[half:, :], dus[...]).astype(BF).reshape(w1s.shape)
    half = acts.shape[1] // 2
    for side, ref in enumerate((w2k, w2s)):
        lo = pl.multiple_of(((at[1] & 1) ^ side) * half, half)
        ref[...] = dot_tn(acts[:, pl.ds(lo, half)], dz[...]).astype(BF)

    @pl.when(t == pl.num_programs(0) - 1)
    def _():
        gains = gain[...].astype(F32)
        sums = [jnp.zeros((1, dout.shape[1]), F32) for _ in range(4)]
        for i in range(images):
            m1 = keep[at[0] * images + i, 0].astype(F32) * KEEP
            m2 = keep[at[0] * images + i, 1].astype(F32) * KEEP
            r = slice(i * padded, (i + 1) * padded)
            x = h[i]
            z[r, :] = x + m2 * (z[r, :] + b2[...].astype(F32))
            for k in range(out.shape[0] // images):
                lo = i * padded + ns + k * part
                out[k * images + i] = jnp.concatenate(
                    [z[lo : lo + part, :], z[i * padded : i * padded + ns, :]], axis=0
                ).astype(BF)
            hat, inv = normalize(x)
            up = da2[r, :]
            grad = dout[r, :] + norm_back(up, hat, inv, gains)
            dh[i] = grad
            low = (m1 * grad).astype(BF)
            dy[i] = low
            for j, v in enumerate((up * hat, up, dz[r, :].astype(F32), low.astype(F32))):
                sums[j] = sums[j] + colsum(v)
        small[...] = jnp.concatenate(sums, axis=0)


def heads_kernel(
    at, dy, prob, qkv, wp_any, wq_any, xs, dh, gain, a1t_any, ot_any, small2, db1,
    out, small, flat, cs, ck, ds_, dk_,
    buf, dqkv, dys, wp, wq, a1t, ot, a1, o, cols, sems, *, images, heads, part, ns,
):
    i = pl.program_id(0)
    width = dy.shape[2]
    padded = dy.shape[1]
    fetches = [
        pltpu.make_async_copy(src, dst, sems.at[j])
        for j, (src, dst) in enumerate(((wp_any, wp), (wq_any, wq), (a1t_any, a1t), (ot_any, ot)))
    ]

    @pl.when(i == 0)
    def _():
        for fetch in fetches:
            fetch.start()
        fetches[0].wait()

    @pl.when(i < images)
    def _():
        low = lax.broadcasted_iota(jnp.int32, (padded, 2 * HEAD_DIM), 1) < HEAD_DIM
        mine = pl.ds(pl.multiple_of(i * padded, padded), padded)
        dys[mine, :] = dy[0]
        do = dot_nt(dy[0], wp[...]).astype(BF)
        for j in range(heads // 2):
            c = j * 2 * HEAD_DIM
            q = qkv[0, :, c : c + 2 * HEAD_DIM]
            k = qkv[0, :, width + c : width + c + 2 * HEAD_DIM]
            v = qkv[0, :, 2 * width + c : 2 * width + c + 2 * HEAD_DIM]
            g = both_heads(do[:, c : c + 2 * HEAD_DIM], low)
            p = prob[0, j]
            p32 = p.astype(F32)
            w = p32 * dot_nt(g, v)
            ds = (w - p32 * jnp.sum(w, axis=-1, keepdims=True)).astype(BF)
            dq = dot(ds, k)
            dq = jnp.where(low, dq[:padded], dq[padded:]) * HEAD_DIM**-0.5
            dk = dot_tn(ds, both_heads(q, low)) * HEAD_DIM**-0.5
            dqkv[mine, c : c + 2 * HEAD_DIM] = dq.astype(BF)
            dqkv[mine, width + c : width + c + 2 * HEAD_DIM] = dk.astype(BF)
            dqkv[mine, 2 * width + c : 2 * width + c + 2 * HEAD_DIM] = dot_tn(p, g).astype(BF)

        @pl.when(i == 0)
        def _():
            fetches[1].wait()

        grads = dqkv[mine, :]
        tops = colsum(grads.astype(F32))
        up = dot_nt(grads, wq[...])
        hat, inv = normalize(xs[0].astype(F32))
        buf[...] = dh[0] + norm_back(up, hat, inv, gain[...].astype(F32))
        for k in range(out.shape[0] // images):
            lo = ns + k * part
            out[k * images + i] = jnp.concatenate(
                [buf[lo : lo + part, :], buf[0:ns, :]], axis=0
            ).astype(BF)
        sums = jnp.concatenate([colsum(up * hat), colsum(up)], axis=0)

        @pl.when(i == 0)
        def _():
            flat[...] = tops
            small[...] = sums

        @pl.when(i > 0)
        def _():
            flat[...] += tops
            small[...] += sums

    @pl.when(i == images)
    def _():
        n = width // OWNERS
        per = db1.shape[1] // width
        eight = jnp.concatenate(
            [small[...], flat[:, :width], flat[:, 2 * width :], small2[...]], axis=0
        ).T
        long = jnp.broadcast_to(db1[...], (8, db1.shape[1])).T
        cols[...] = jnp.zeros_like(cols)
        for b in range(OWNERS):
            rows = pl.ds(pl.multiple_of(place(b ^ at[1]) * n, n), n)
            cols[rows, 0:8] = eight[b * n : (b + 1) * n]
            for j in range(per):
                lo = (b * per + j) * n
                cols[rows, 8 + j : 9 + j] = long[lo : lo + n, 0:1]
        fetches[2].wait()
        fetches[3].wait()

    half = cs.shape[0]
    for step, lo, c_ref, d_ref in ((images, half, cs, ds_), (images + 1, 0, ck, dk_)):

        @pl.when(i == step)
        def _(lo=lo, c_ref=c_ref, d_ref=d_ref):
            for n in range(images):
                lanes = slice(n * padded, (n + 1) * padded)
                a1[:, lanes] = a1t[n, lo : lo + half, :]
                o[:, lanes] = ot[n, lo : lo + half, :]
            c_ref[:, : 2 * width] = dot(a1[...], dqkv[:, : 2 * width]).astype(BF)
            c_ref[:, 2 * width :] = jnp.zeros((half, COLUMNS), BF)
            d_ref[:, :width] = dot(a1[...], dqkv[:, 2 * width :]).astype(BF)
            d_ref[:, width : 2 * width] = dot(o[...], dys[...]).astype(BF)
            d_ref[:, 2 * width :] = cols[lo : lo + half, :].astype(BF)


def settle_kernel(both, rows, specials):
    part = rows.shape[1]
    rows[...] = both[:, :part, :]
    specials[...] = both[:, part:, :]


def sum_kernel(*refs, jobs, pick):
    if pick:
        at, *refs = refs
        even = (at[0] & 1) == 0
    terms = [lead for job in jobs for lead in job]
    count = len(terms)
    arrays, outs, bufs, sems = refs[:count], refs[count : -count - 1], refs[-count - 1 : -1], refs[-1]
    fetches = [
        pltpu.make_async_copy(array.at[lead], buf, sems.at[k])
        for k, (array, lead, buf) in enumerate(zip(arrays, terms, bufs))
    ]
    for fetch in fetches:
        fetch.start()
    for fetch in fetches:
        fetch.wait()
    values = []
    for job in jobs:
        total = None
        for ref in bufs[: len(job)]:
            v = ref[...].astype(F32)
            total = v if total is None else total + v
        bufs = bufs[len(job) :]
        values.append(total)
    if pick:
        values = [jnp.where(even, *values), jnp.where(even, *values[::-1])]
    pieces = len(outs) // len(values)
    for k, ref in enumerate(outs):
        v, n = values[k // pieces], ref.shape[0]
        lo = k % pieces * n if pieces > 1 else 0
        ref[...] = (v if pieces == 1 else v[lo : lo + n]).astype(BF).reshape(ref.shape)


def sums(jobs, at=None, mib=60, pieces=1):
    arrays, bufs, out_shapes, leads = [], [], [], []
    for job in jobs:
        leads.append([])
        for v, lead in job:
            index = tuple(slice(None) if j is None else j for j in lead)
            kept = tuple(v.shape[k] for k, j in enumerate(lead) if j is None) + v.shape[len(lead) :]
            leads[-1].append(index)
            arrays.append(v)
            bufs.append(pltpu.VMEM(kept, BF))
        out_shapes += [struct(kept[0] // pieces, *kept[1:])] * pieces
    specs = [ANY] * len(arrays)
    if at is not None:
        specs.insert(0, pl.BlockSpec(memory_space=pltpu.SMEM))
        arrays.insert(0, at)
    return pl.pallas_call(
        partial(sum_kernel, jobs=leads, pick=at is not None),
        in_specs=specs,
        out_shape=out_shapes,
        scratch_shapes=[*bufs, pltpu.SemaphoreType.DMA((len(bufs),))],
        compiler_params=pltpu.CompilerParams(vmem_limit_bytes=mib * 2**20),
        cost_estimate=cost(2),
        name="sums",
    )(*arrays)


def finish_feed_kernel(at, mine_a, other_a, mine_b, other_b, fc1, fc2):
    even = (at[0] & 1) == 0
    n = fc1.shape[0]
    width = fc2.shape[1]
    half = mine_a.shape[0]
    for m in range(2 * half):
        mine, other = (mine_a, other_a) if m < half else (mine_b, other_b)
        p, q = mine[m % half].astype(F32), other[m % half].astype(F32)
        fc1[:, m * width : (m + 1) * width] = jnp.where(even, p, q)
        fc2[m * n : (m + 1) * n, :] = jnp.where(even, q, p)


def finish_kernel(at, mine, other, qkv, proj, *rest):
    vectors, long = rest[:-1], rest[-1]
    width = proj.shape[1]
    even = (at[0] & 1) == 0
    p, q = mine[...].astype(F32), other[...].astype(F32)
    c, d = jnp.where(even, p, q), jnp.where(even, q, p)
    qkv[:, : 2 * width] = c[:, : 2 * width]
    qkv[:, 2 * width :] = d[:, :width]
    proj[...] = d[:, width : 2 * width]
    n = c.shape[0]
    flat = d[:, 2 * width :].T
    row = 0
    for ref in vectors:
        ref[...] = flat[row : row + ref.shape[0]]
        row += ref.shape[0]
    for j in range(long.shape[1] // n):
        long[:, j * n : (j + 1) * n] = flat[row + j : row + j + 1]


def whole(shape, mode=None):
    return pl.BlockSpec(shape, lambda *_: (0,) * len(shape), pipeline_mode=mode)


def params(mib=60):
    return pltpu.CompilerParams(
        dimension_semantics=("arbitrary",), vmem_limit_bytes=mib * 2**20
    )


def cost(us):
    return pl.CostEstimate(flops=int(us * 1e9 * PACE), bytes_accessed=1, transcendentals=0)


ANY = pl.BlockSpec(memory_space=pl.ANY)


def struct(*shape, dtype=BF):
    return jax.ShapeDtypeStruct(shape, dtype)


def after(v, *others):
    return lax.optimization_barrier((v, *others))[0]


def together(*vs):
    return lax.optimization_barrier(vs)


def swap(v, bit):
    return lax.ppermute(v, "dp", [(s, s ^ bit) for s in range(lax.axis_size("dp"))])


def exchange(x):
    return lax.all_to_all(x, "seq", split_axis=0, concat_axis=0, tiled=True)


def settle(both, ns):
    images, rows, width = both.shape
    n = images // 4
    return pl.pallas_call(
        settle_kernel,
        grid=(images // n,),
        in_specs=[pl.BlockSpec((n, rows, width), lambda i: (i, 0, 0))],
        out_specs=[
            pl.BlockSpec((n, rows - ns, width), lambda i: (i, 0, 0)),
            pl.BlockSpec((n, ns, width), lambda i: (i, 0, 0)),
        ],
        out_shape=[struct(images, rows - ns, width), struct(images, ns, width)],
        compiler_params=params(60),
        cost_estimate=cost(2),
        name="settle",
    )(both)


def shards(
    patches, specials, keep_mask, ln1_gain, ln1_bias, qkv_weight, qv_bias, proj_weight, proj_bias,
    ln2_gain, ln2_bias, fc1_weight, fc1_bias, fc2_weight, fc2_bias, grad_patches, grad_specials,
):
    images, part, width = patches.shape
    ns = specials.shape[1]
    groups = lax.axis_size("seq")
    replicas = lax.axis_size("dp")
    hidden = fc1_weight.shape[1]
    heads = width // HEAD_DIM
    n = images // groups
    rows = ns + groups * part
    padded = -(-rows // 16) * 16
    steps = OWNERS // 2
    chunk = hidden // steps
    half = width // 2
    direct = replicas == OWNERS
    me = lax.axis_index("seq")
    d = lax.axis_index("dp") if direct else jnp.int32(0)
    at = jnp.stack([me, d]).astype(jnp.int32)

    def per_image(lo, *shape):
        return pl.BlockSpec((1, *shape), lambda i, *_: (lo + i,) + (0,) * len(shape))

    moved = []
    for k in range(1, groups):
        block = lax.dynamic_slice_in_dim(patches, n * ((me + k) % groups), n)
        moved.append(lax.ppermute(block, "seq", [(s, (s + k) % groups) for s in range(groups)]))
    moved = together(*moved)
    grads = exchange(after(grad_patches, *moved))
    vectors = (
        fc1_bias, ln1_gain, ln1_bias, qv_bias[0], jnp.zeros_like(proj_bias), qv_bias[1], proj_bias,
        ln2_gain, ln2_bias, fc2_bias,
    )
    vectors = jnp.concatenate([v.astype(F32) for v in vectors]).reshape(1, -1)
    first = hidden // width

    def vector(k, wide=1):
        return pl.BlockSpec((1, wide * width), lambda *_: (0, (first + k) // wide))

    shapes = [
        ((padded, width), BF), ((width, padded), BF), ((padded, 3 * width), BF),
        ((heads // 2, 2 * padded, padded), BF), ((width, padded), BF),
        ((padded, width), F32), ((padded, width), BF), ((width, padded), BF),
    ]

    xs, a1t, qkv, prob, ot, h, a2, a2t = pl.pallas_call(
        partial(forward_kernel, rows=rows, heads=heads),
        grid_spec=pltpu.PrefetchScalarGridSpec(
            num_scalar_prefetch=2,
            grid=(n,),
            in_specs=[
                pl.BlockSpec((1, part, width), lambda i, at, keep: (at[0] * n + i, 0, 0)),
                *[per_image(0, part, width)] * (groups - 1),
                pl.BlockSpec((1, ns, width), lambda i, at, keep: (at[0] * n + i, 0, 0)),
                vector(0), vector(1), whole(qkv_weight.shape), vector(2, 3),
                whole(proj_weight.shape), vector(5), vector(6), vector(7),
            ],
            out_specs=[per_image(0, *shape) for shape, _ in shapes],
            scratch_shapes=[pltpu.VMEM((padded, width), F32)],
        ),
        out_shape=[struct(n, *shape, dtype=dtype) for shape, dtype in shapes],
        compiler_params=params(60),
        cost_estimate=cost(15),
        name="attention_forward",
    )(
        at, keep_mask, patches, *moved, specials, vectors, vectors, qkv_weight, vectors, proj_weight,
        vectors, vectors, vectors,
    )

    total = n * padded
    h, grads = together(h, grads)

    def owner(t, at):
        return t ^ lax.shift_right_logical(at[1], 1)

    once = pl.Buffered(1)
    out_rows, dh, dy, w2s, w2k, w1s, w1k, db1, small2 = pl.pallas_call(
        partial(feed_kernel, images=n),
        grid_spec=pltpu.PrefetchScalarGridSpec(
            num_scalar_prefetch=2,
            grid=(steps,),
            in_specs=[
                *[
                    pl.BlockSpec((n, part, width), lambda t, at, keep, k=k: (k, 0, 0), pipeline_mode=once)
                    for k in range(groups)
                ],
                pl.BlockSpec((n, ns, width), lambda t, at, keep: (at[0], 0, 0)),
                whole(h.shape, once), whole(a2.shape, once), whole(a2t.shape, once),
                pl.BlockSpec((width, chunk), lambda t, at, keep: (0, owner(t, at))),
                pl.BlockSpec((1, chunk), lambda t, at, keep: (0, owner(t, at))),
                pl.BlockSpec((chunk, width), lambda t, at, keep: (owner(t, at), 0)),
                vector(8), vector(6),
            ],
            out_specs=[
                whole((images, part + ns, width)),
                whole((n, padded, width)), whole((n, padded, width)),
                *[pl.BlockSpec((chunk // 2, width), lambda t, *_: (t, 0))] * 2,
                *[pl.BlockSpec((steps, 1, width // OWNERS, chunk), lambda t, at, keep: (0, owner(t, at), 0, 0))] * 2,
                pl.BlockSpec((1, chunk), lambda t, at, keep: (0, owner(t, at))),
                whole((4, width)),
            ],
            scratch_shapes=[
                pltpu.VMEM((total, width), F32), pltpu.VMEM((total, width), BF),
                pltpu.VMEM((total, width), F32), pltpu.VMEM((total, width), F32),
                pltpu.VMEM((total, chunk), BF), pltpu.VMEM((total, chunk), BF),
                pltpu.VMEM((width, total), BF),
            ],
        ),
        out_shape=[
            struct(images, part + ns, width),
            struct(n, padded, width, dtype=F32), struct(n, padded, width),
            *[struct(hidden // 2, width)] * 2, *[struct(steps, steps, width // OWNERS, chunk)] * 2,
            struct(1, hidden, dtype=F32), struct(4, width, dtype=F32),
        ],
        compiler_params=params(60),
        cost_estimate=cost(30),
        name="feed_forward",
    )(
        at, keep_mask, *[grads] * groups, grad_specials, h, a2, a2t, fc1_weight, vectors,
        fc2_weight, vectors, vectors,
    )

    n1 = width // OWNERS
    x_half, y_half = (None, 1), (1, None)
    if direct:
        ra, rb = swap(w1s, 1), swap(w2s, 1)
        ra, rb = together(ra, rb)
        wa, wb, ra, rb = (v.reshape(2, 2, steps, n1, chunk) for v in (w1k, w2k, ra, rb))
        as_, bs = sums([[(wa, x_half), (ra, x_half)], [(wb, y_half), (rb, y_half)]], mib=60)
        dy, as_, bs = together(dy, as_, bs)
        qa, qb = swap(as_, 2), swap(bs, 4)
    out_rows = exchange(out_rows)

    def per_image_last(*shape):
        return pl.BlockSpec(
            (1, *shape), lambda i, *_: (jnp.minimum(i, n - 1),) + (0,) * len(shape)
        )

    wide = 2 * width + COLUMNS
    dx_rows, small1, flat, cs, ck, ds_, dk_ = pl.pallas_call(
        partial(heads_kernel, images=n, heads=heads, part=part, ns=ns),
        grid_spec=pltpu.PrefetchScalarGridSpec(
            num_scalar_prefetch=1,
            grid=(n + 2,),
            in_specs=[
                per_image_last(padded, width), per_image_last(heads // 2, 2 * padded, padded),
                per_image_last(padded, 3 * width), ANY, ANY, per_image_last(padded, width),
                per_image_last(padded, width), vector(0), ANY, ANY, whole((4, width)),
                whole((1, hidden)),
            ],
            out_specs=[
                whole((images, part + ns, width)), whole((2, width)), whole((1, 3 * width)),
                *[whole((half, wide))] * 4,
            ],
            scratch_shapes=[
                pltpu.VMEM((padded, width), F32), pltpu.VMEM((total, 3 * width), BF),
                pltpu.VMEM((total, width), BF), pltpu.VMEM(proj_weight.shape, BF),
                pltpu.VMEM(qkv_weight.shape, BF), pltpu.VMEM(a1t.shape, BF), pltpu.VMEM(ot.shape, BF),
                pltpu.VMEM((half, total), BF), pltpu.VMEM((half, total), BF),
                pltpu.VMEM((width, COLUMNS), F32), pltpu.SemaphoreType.DMA((4,)),
            ],
        ),
        out_shape=[
            struct(images, part + ns, width), struct(2, width, dtype=F32),
            struct(1, 3 * width, dtype=F32), *[struct(half, wide)] * 4,
        ],
        compiler_params=params(60),
        cost_estimate=cost(22),
        name="attention_backward",
    )(at, dy, prob, qkv, proj_weight, qkv_weight, xs, dh, vectors, a1t, ot, small2, db1)

    cs, ds_, out_rows = together(cs, ds_, out_rows)
    dx_rows = exchange(dx_rows)

    if not direct:
        out_rows, out_specials = settle(out_rows, ns)
        dx_rows, dx_specials = settle(dx_rows, ns)
        return (
            out_rows, out_specials, dx_rows, dx_specials,
            *natural_sums(
                w1s, w1k, w2s, w2k, cs, ck, ds_, dk_, flat, small1, small2, db1
            ),
        )

    def near(v):
        return lax.ppermute(v, "seq", [(s, s ^ 1) for s in range(groups)])

    def far(v):
        return lax.ppermute(v, "seq", [(s, s ^ 2) for s in range(groups)])

    qa, qb, cs, ds_ = together(qa, qb, cs, ds_)
    as_, bs = sums(
        [[(wa, (1, 0)), (ra, (1, 0)), (qa, (1,))], [(wb, (0, 1)), (rb, (0, 1)), (qb, (1,))]]
    )
    as_, bs, cs, ds_ = together(as_, bs, cs, ds_)
    ta, tb = swap(as_, 4), swap(bs, 2)
    rc, rd = swap(cs, 1), swap(ds_, 1)
    rc, rd, ck, dk_ = together(rc, rd, ck, dk_)
    wc, wd, rc, rd = (v.reshape(2, 2, 2, n1 // 2, -1) for v in (ck, dk_, rc, rd))
    cs, ds_ = sums([[(wc, x_half), (rc, x_half)], [(wd, y_half), (rd, y_half)]])
    qc, qd = swap(cs, 2), swap(ds_, 4)
    out_rows, out_specials = settle(after(out_rows, cs), ns)
    ta, tb, cs, out_rows = together(ta, tb, cs, out_rows)
    e, es = sums(
        [
            [(wa, (0, 0)), (ra, (0, 0)), (qa, (0,)), (ta, ())],
            [(wb, (0, 0)), (rb, (0, 0)), (qb, (0,)), (tb, ())],
        ],
        at,
    )
    re = near(es)
    qc, qd, e = together(qc, qd, e)
    cs, ds_ = sums(
        [[(wc, (1, 0)), (rc, (1, 0)), (qc, (1,))], [(wd, (0, 1)), (rd, (0, 1)), (qd, (1,))]]
    )
    cs, ds_, re, dx_rows = together(cs, ds_, re, dx_rows)
    tc, td = swap(cs, 4), swap(ds_, 2)
    e = e + re
    e, g = e[: steps // 2], e[steps // 2 :]
    re, rg = far(e), far(g)
    e, g, tc, td = together(e, g, tc, td)
    f1, fs = sums(
        [
            [(wc, (0, 0)), (rc, (0, 0)), (qc, (0,)), (tc, ())],
            [(wd, (0, 0)), (rd, (0, 0)), (qd, (0,)), (td, ())],
        ],
        at,
    )
    rf = near(fs)
    f1, re, e = together(f1, re, e)
    e = e + re
    re = near(e)
    dx_rows, dx_specials = settle(after(dx_rows, e), ns)
    rf, dx_rows = together(rf, dx_rows)
    f1 = f1 + rf
    rf = far(f1)
    f1, rg, g = together(f1, rg, g)
    g = g + rg
    rg = near(g)
    rf, g = together(rf, g)
    f1 = f1 + rf
    rf = near(f1)
    re, rg, f1 = together(re, rg, f1)
    smem = pl.BlockSpec(memory_space=pltpu.SMEM)
    vmem = pl.BlockSpec(memory_space=pltpu.VMEM)
    d_fc1, d_fc2 = pl.pallas_call(
        finish_feed_kernel,
        in_specs=[smem, *[vmem] * 4],
        out_shape=[struct(n1, hidden, dtype=F32), struct(hidden // OWNERS, width, dtype=F32)],
        compiler_params=pltpu.CompilerParams(vmem_limit_bytes=60 * 2**20),
        cost_estimate=cost(2),
        name="finish_feed",
    )(at, e, re, g, rg)
    rf, d_fc1 = together(rf, d_fc1)
    done = pl.pallas_call(
        finish_kernel,
        in_specs=[smem, vmem, vmem],
        out_shape=[
            struct(n1, 3 * width, dtype=F32), struct(n1, width, dtype=F32),
            *[struct(1, n1, dtype=F32)] * 2, struct(2, n1, dtype=F32),
            *[struct(1, n1, dtype=F32)] * 4, struct(1, hidden // OWNERS, dtype=F32),
        ],
        compiler_params=pltpu.CompilerParams(vmem_limit_bytes=60 * 2**20),
        cost_estimate=cost(2),
        name="finish",
    )(at, f1.reshape(n1, -1), rf.reshape(n1, -1))
    d_qkv, d_proj, gain1, bias1, d_qv, gain2, bias2, d_fc2b, d_projb, d_fc1b = done

    def one(v):
        return v.reshape(-1)

    return (
        out_rows, out_specials, dx_rows, dx_specials,
        one(gain1), one(bias1), d_qkv, d_qv, d_proj, one(d_projb), one(gain2), one(bias2),
        d_fc1, one(d_fc1b), d_fc2, one(d_fc2b),
    )


def natural_sums(w1s, w1k, w2s, w2k, cs, ck, ds_, dk_, flat, small1, small2, db1):
    width = small1.shape[1]
    replicas = lax.axis_size("dp")

    def natural(sent, kept):
        if kept.ndim == 4:
            kept, sent = (v.transpose(0, 2, 1, 3).reshape(width // 2, -1) for v in (kept, sent))
        v = jnp.stack([kept, sent]).reshape(2, OWNERS // 2, -1, kept.shape[1])
        v = v.transpose(1, 0, 2, 3).reshape(-1, kept.shape[1])
        v = lax.psum_scatter(v, "dp", scatter_dimension=0, tiled=True)
        return lax.psum(v, "seq").astype(F32)

    d_fc1, d_fc2 = natural(w1s, w1k), natural(w2s, w2k)
    d_qk, d_vp = natural(cs, ck), natural(ds_, dk_)
    d_qkv = jnp.concatenate([d_qk[:, : 2 * width], d_vp[:, :width]], axis=1)
    d_proj = d_vp[:, width : 2 * width]
    flat = flat.reshape(3, width)
    vectors = jnp.concatenate([small1, flat[0:1], flat[2:3], small2, db1.reshape(-1, width)], axis=0)
    vectors = lax.psum(vectors, ("dp", "seq"))
    mine = lax.axis_index("dp")

    def shard(v):
        size = v.shape[-1] // replicas
        return lax.dynamic_slice_in_dim(v, mine * size, size, axis=v.ndim - 1)

    s = shard(vectors[:8])
    d_fc1b = shard(vectors[8:].reshape(-1))
    return s[0], s[1], d_qkv, s[2:4], d_proj, s[7], s[4], s[5], d_fc1, d_fc1b, d_fc2, s[6]


def solution(mesh):
    rows = P("dp", "seq", None)
    lead = P("dp", None, None)
    flat = P("dp")
    matrix = P("dp", None)
    return jax.shard_map(
        shards,
        mesh=mesh,
        in_specs=(rows, lead, matrix, *[P()] * 12, rows, lead),
        out_specs=(
            rows, lead, rows, lead, flat, flat, matrix, P(None, "dp"), matrix, flat, flat, flat,
            matrix, flat, matrix, flat,
        ),
        check_vma=False,
    )
```

time: 258 us -> 245 us (0.950)
  Pallas kernels: 120 us -> 108 us
  waiting for transfers between devices: 73.9 us -> 85.9 us
  starting transfers between devices: 43 us -> 34.9 us
  local copies, waits for them, and re-layouts: 17.2 us -> 11.3 us
    ppermute x12 -> x3, starting transfers between devices: 19.9 us -> 6.11 us  [shards(): lax.ppermute(block, 'seq', [(s, (s + k) % groups) for s in range(groups)])]
    pallas_call x15 -> x12, Pallas kernels: 118 us -> 105 us  [the longest x1 31.7 us: shards(): pl.pallas_call(partial(feed_kernel, images=n), grid_spec=pltpu.PrefetchSc...]
    all_to_all x0 -> x3, starting transfers between devices: none -> 12.2 us  [exchange(): return lax.all_to_all(x, 'seq', split_axis=0, concat_axis=0, tiled=True)]
    reshape x8 -> x1, local copies, waits for them, and re-layouts: 9.57 us -> 0.64 us  [shards(): vectors = jnp.concatenate([v.astype(F32) for v in vectors]).reshape(1, -1)]
    all_to_all x0 -> x3, waiting for transfers between devices: none -> 8.29 us  [exchange(): return lax.all_to_all(x, 'seq', split_axis=0, concat_axis=0, tiled=True)]
    ppermute x12, waiting for transfers between devices: 16.7 us -> 22.9 us  [swap(): lax.ppermute(v, 'dp', [(s, s ^ bit) for s in range(lax.axis_size('dp'))])]
    ppermute x2 -> x3, starting transfers between devices: 7.25 us -> 2.74 us  [far(): return lax.ppermute(v, 'seq', [(s, s ^ 2) for s in range(groups)])]
    ppermute x4 -> x5, waiting for transfers between devices: 23.1 us -> 19.9 us  [near(): return lax.ppermute(v, 'seq', [(s, s ^ 1) for s in range(groups)])]
  transfers between devices with their start and end apart: 30 -> 26, of which waited for: 12 -> 17; matrix products, arithmetic and copies ran while one was open for 5% -> 1% of each run, Pallas kernels for 44% -> 29%
where the time goes in v3:
time: 245 us; the launch traced here: 243 us
  Pallas kernels  108 us (44%)
  waiting for transfers between devices  85.9 us (35%)
  starting transfers between devices  34.9 us (14%)
  local copies, waits for them, and re-layouts  11.3 us (5%)
    pallas_call x1, Pallas kernels, shards(): pl.pallas_call(partial(feed_kernel, images=n), grid_spec=pltpu.PrefetchSc...  31.7 us
    pallas_call x1, Pallas kernels, shards(): pl.pallas_call(partial(heads_kernel, images=n, heads=heads, part=part, ns...  27.8 us
    ppermute x12, waiting for transfers between devices, swap(): lax.ppermute(v, 'dp', [(s, s ^ bit) for s in range(lax.axis_size('dp'))])  22.9 us
    pallas_call x6, Pallas kernels, sums(): pl.pallas_call(partial(sum_kernel, jobs=leads, pick=at is not None), in_s...  20.9 us
    ppermute x3, waiting for transfers between devices, shards(): lax.ppermute(block, 'seq', [(s, (s + k) % groups) for s in range(groups)])  20.1 us
    ppermute x5, waiting for transfers between devices, near(): return lax.ppermute(v, 'seq', [(s, s ^ 1) for s in range(groups)])  19.9 us
    pallas_call x1, Pallas kernels, shards(): pl.pallas_call(partial(forward_kernel, rows=rows, heads=heads), grid_spec...  15.2 us
    ppermute x3, waiting for transfers between devices, far(): return lax.ppermute(v, 'seq', [(s, s ^ 2) for s in range(groups)])  14.7 us
  transfers between devices with their start and end apart: 26, of which 17 were waited for; matrix products, arithmetic and copies ran while one was open for 1% of the time, Pallas kernels for 29%

profile of v3, /device:TPU:0, one launch (start us, length us, event | category | flops | bytes accessed | tf_op | source)
XLA Modules:
  0.0 243.3 jit_solution(14235566052226769310)
XLA Ops:
  0.7 1.3 constant_dynamic-slice_fusion
  2.1 5.1 %collective-permute-start.2 = (bf16[3,49,768]{2,1,0:T(8,128)(2,1)S(1)}, bf16[3,49,768]{2,1,0:T(8,128)(2,1)S(1)}, u32[]{:S(2)}, u32[]{:S(2)}) collective-permute-start(bf16[3,49,768]{2,1,0:T(8,128)(2,1)S(1)} %get-tuple-element.232), channel_id=1, source_target_pairs={{0,3},{1,0},{2,1},{3,2},{4,7},{5,4},{6,5},{7,6},{8,11},{9,8},{10,9... | collective-permute-start | bytes 677384 | tf_op jit(solution)/shard_map/ppermute | solution.py:475
  7.2 1.0 collective-permute-start
  8.3 0.7 copy.34.keep
  9.0 4.8 %collective-permute-done.2.x3 = bf16[3,49,768]{2,1,0:T(8,128)(2,1)S(1)} collective-permute-done((bf16[3,49,768]{2,1,0:T(8,128)(2,1)S(1)}, bf16[3,49,768]{2,1,0:T(8,128)(2,1)S(1)}, u32[]{:S(2)}, u32[]{:S(2)}) %collective-permute-start.2) | collective-permute-done | bytes 225824 | tf_op jit(solution)/shard_map/ppermute | solution.py:475
  13.8 15.3 %collective-permute-done.1.x2 = bf16[3,49,768]{2,1,0:T(8,128)(2,1)S(1)} collective-permute-done((bf16[3,49,768]{2,1,0:T(8,128)(2,1)S(1)}, bf16[3,49,768]{2,1,0:T(8,128)(2,1)S(1)}, u32[]{:S(2)}, u32[]{:S(2)}) %collective-permute-start.1) | collective-permute-done | bytes 225824 | tf_op jit(solution)/shard_map/ppermute | solution.py:475
  29.1 4.1 %all-to-all-start = ((bf16[12,49,768]{2,1,0:T(8,128)(2,1)}), bf16[12,49,768]{2,1,0:T(8,128)(2,1)S(1)}, u32[]{:S(2)}, u32[]{:S(2)}) async-start(bf16[12,49,768]{2,1,0:T(8,128)(2,1)} %param.32), calls=%async_computation | async-start | bytes 2064384 | tf_op jit(solution)/shard_map/all_to_all | solution.py:427
  33.3 0.6 reshape.90.g1.b1.bq.bp.g2.b2.gain
  33.9 0.6 pad_add_fusion.at.refs_0_
  34.5 15.2 %attention_forward.1 = (bf16[3,208,768]{2,1,0:T(8,128)(2,1)}, bf16[3,768,208]{2,1,0:T(8,128)(2,1)}, bf16[3,208,2304]{2,1,0:T(8,128)(2,1)}, bf16[3,6,416,208]{3,2...) custom-call(s32[2]{0:T(128)} %pad_add_fusion.at.refs_0_, ...), custom_call_target="tpu_custom_call" | custom-call | flops 4499999744 | bytes 1 | tf_op jit(solution)/shard_map/attention_forward/pallas_call | solution.py:494
  49.7 8.3 %all-to-all-done.g0.g1.g2.g3 = bf16[12,49,768]{2,1,0:T(8,128)(2,1)S(1)} async-done(((bf16[12,49,768]{2,1,0:T(8,128)(2,1)}), bf16[12,49,768]{2,1,0:T(8,128)(2,1)S(1)}, u32[]{:S(2)}, u32[]{:S(2)}) %all-to-all-start) | async-done | bytes 903200 | tf_op jit(solution)/shard_map/all_to_all | solution.py:427
  58.0 1.0 copy-done.8
  58.9 31.7 %feed_forward.1 = (bf16[12,51,768]{2,1,0:T(8,128)(2,1)}, f32[3,208,768]{2,1,0:T(8,128)}, bf16[3,208,768]{2,1,0:T(8,128)(2,1)}, bf16[1536,768]{1,0:T(8,128)(2,1)}...) custom-call(s32[2]{0:T(128)} %pad_add_fusion.at.refs_0_, ...), custom_call_target="tpu_custom_call" | custom-call | flops 8999999488 | bytes 1 | tf_op jit(solution)/shard_map/feed_forward/pallas_call | solution.py:525
  90.7 0.5 collective-permute-start.4
  91.2 3.7 %all-to-all-start.1 = ((bf16[12,51,768]{2,1,0:T(8,128)(2,1)}), bf16[12,51,768]{2,1,0:T(8,128)(2,1)S(1)}, u32[]{:S(2)}, u32[]{:S(2)}) async-start(bf16[12,51,768]{2,1,0:T(8,128)(2,1)} %get-tuple-element.154), calls=%async_computation.1 | async-start | bytes 2064384 | tf_op jit(solution)/shard_map/all_to_all | solution.py:427
  94.9 3.1 %collective-permute-done.3 = bf16[4,4,96,768]{3,2,1,0:T(8,128)(2,1)S(1)} collective-permute-done((bf16[4,4,96,768]{3,2,1,0:T(8,128)(2,1)}, bf16[4,4,96,768]{3,2,1,0:T(8,128)(2,1)S(1)}, u32[]{:S(2)}, u32[]{:S(2)}) %collective-permute-start.3) | collective-permute-done | bytes 2359328 | tf_op jit(solution)/shard_map/ppermute | solution.py:423
  98.1 0.9 collective-permute-done.4
  99.0 0.5 copy-done
  99.5 4.1 %sums.6 = (bf16[2,4,96,768]{3,2,1,0:T(8,128)(2,1)}, bf16[2,4,96,768]{3,2,1,0:T(8,128)(2,1)}) custom-call(bf16[2,2,4,96,768]{4,3,2,1,0:T(8,128)(2,1)} %bitcast.21, bf16[2,2,4,96,768]{4,3,2,1,0:T(8,128)(2,1)} %bitcast.24, bf16[2,2,4,96,768]{4,3,2,1,0:T(8,128)(2,1)} %bitcast.18, bf16[2,2,4,96,768]{4,3,2,1,0:T(8,128)(2,1)} %bitcast.5.refs_3_.refs_4_.refs_6_), custom_call_target="tpu_custom_call" | custom-call | flops 600000000 | bytes 1 | tf_op jit(solution)/shard_map/sums/pallas_call | solution.py:351
  103.6 1.6 collective-permute-start.5
  105.1 1.5 collective-permute-start.6
  106.7 27.8 %attention_backward.1 = (bf16[12,51,768]{2,1,0:T(8,128)(2,1)}, f32[2,768]{1,0:T(2,128)}, f32[1,2304]{1,0:T(1,128)}, bf16[384,1664]{1,0:T(8,128)(2,1)}, bf16[384,...) custom-call(s32[2]{0:T(128)} %pad_add_fusion.at.refs_0_, ...), custom_call_target="tpu_custom_call" | custom-call | flops 6600000000 | bytes 1 | tf_op jit(solution)/shard_map/attention_backward/pallas_call | solution.py:588
  134.5 1.0 copy-done.3
  135.5 1.0 copy-done.4
  136.5 3.2 %sums.7 = (bf16[4,96,768]{2,1,0:T(8,128)(2,1)}, bf16[4,96,768]{2,1,0:T(8,128)(2,1)}) custom-call(bf16[2,2,4,96,768]{4,3,2,1,0:T(8,128)(2,1)} %bitcast.22, bf16[2,2,4,96,768]{4,3,2,1,0:T(8,128)(2,1)} %bitcast.25, bf16[2,4,96,768]{3,2,1,0:T(8,128)(2,1)} %copy-done.3, bf16[2,2,4,96,768]{4,3,2,1,0:T(8,128)(2,1)} %bitcast.19, ...), custom_call_target="tpu_custom_call" | custom-call | flops 600000000 | bytes 1 | tf_op jit(solution)/shard_map/sums/pallas_call | solution.py:351
  139.9 0.5 collective-permute-start.10
  140.4 4.5 %all-to-all-start.2 = ((bf16[12,51,768]{2,1,0:T(8,128)(2,1)}), bf16[12,51,768]{2,1,0:T(8,128)(2,1)}, u32[]{:S(2)}, u32[]{:S(2)}) async-start(bf16[12,51,768]{2,1,0:T(8,128)(2,1)} %get-tuple-element.189), calls=%async_computation.2 | async-start | bytes 2064384 | tf_op jit(solution)/shard_map/all_to_all | solution.py:427
  144.9 0.6 collective-permute-start.7
  145.4 0.5 collective-permute-start.8
  146.0 1.1 copy-done.1
  147.0 0.4 copy-done.2
  147.4 2.9 %sums.8 = (bf16[2,2,48,1664]{3,2,1,0:T(8,128)(2,1)}, bf16[2,2,48,1664]{3,2,1,0:T(8,128)(2,1)}) custom-call(bf16[2,2,2,48,1664]{4,3,2,1,0:T(8,128)(2,1)} %bitcast.27, bf16[2,2,2,48,1664]{4,3,2,1,0:T(8,128)(2,1)} %bitcast.33, bf16[2,2,2,48,1664]{4,3,2,1,0:T(8,128)(2,1)} %bitcast.30, bf16[2,2,2,48,1664]{4,3,2,1,0:T(8,128)(2,1)} %bitcast.36), custom_call_target="tpu_custom_call" | custom-call | flops 600000000 | bytes 1 | tf_op jit(solution)/shard_map/sums/pallas_call | solution.py:351
  150.3 1.6 collective-permute-start.11
  151.9 1.5 collective-permute-start.12
  153.4 3.4 %settle.2 = (bf16[12,49,768]{2,1,0:T(8,128)(2,1)}, bf16[12,2,768]{2,1,0:T(2,128)(2,1)}) custom-call(bf16[12,51,768]{2,1,0:T(8,128)(2,1)} %copy-done.7), custom_call_target="tpu_custom_call" | custom-call | flops 600000000 | bytes 1 | tf_op jit(solution)/shard_map/settle/pallas_call | solution.py:433
  156.8 4.5 %collective-permute-done.7.refs_4_ = bf16[4,96,768]{2,1,0:T(8,128)(2,1)S(1)} collective-permute-done((bf16[4,96,768]{2,1,0:T(8,128)(2,1)}, bf16[4,96,768]{2,1,0:T(8,128)(2,1)S(1)}, u32[]{:S(2)}, u32[]{:S(2)}) %collective-permute-start.7) | collective-permute-done | bytes 589856 | tf_op jit(solution)/shard_map/ppermute | solution.py:423
  161.3 0.4 collective-permute-done.8.refs_8_
  161.8 0.4 copy-done.9
  162.1 4.7 %sums.9 = (bf16[4,96,768]{2,1,0:T(8,128)(2,1)}, bf16[4,96,768]{2,1,0:T(8,128)(2,1)}) custom-call(s32[2]{0:T(128)} %pad_add_fusion.at.refs_0_, bf16[2,2,4,96,768]{4,3,2,1,0:T(8,128)(2,1)} %bitcast.23, bf16[2,2,4,96,768]{4,3,2,1,0:T(8,128)(2,1)} %bitcast.26, bf16[2,4,96,768]{3,2,1,0:T(8,128)(2,1)} %copy-done.3, bf16[4,96,768]{2,1,0:T(8,128)(2,1)} %copy-done.9, ...), custom_call_target="tpu_custom_call" | custom-call | flops 600000000 | bytes 1 | tf_op jit(solution)/shard_map/sums/pallas_call | solution.py:351
  166.8 1.8 collective-permute-start.13
  168.6 5.5 %collective-permute-done.12.refs_5_.refs_7_ = bf16[2,2,48,1664]{3,2,1,0:T(8,128)(2,1)S(1)} collective-permute-done((bf16[2,2,48,1664]{3,2,1,0:T(8,128)(2,1)}, bf16[2,2,48,1664]{3,2,1,0:T(8,128)(2,1)S(1)}, u32[]{:S(2)}, u32[]{:S(2)}) %collective-permute-start.12) | collective-permute-done | bytes 639008 | tf_op jit(solution)/shard_map/ppermute | solution.py:423
  174.2 0.8 copy-done.6
  175.2 2.5 %sums.10 = (bf16[2,48,1664]{2,1,0:T(8,128)(2,1)}, bf16[2,48,1664]{2,1,0:T(8,128)(2,1)}) custom-call(bf16[2,2,2,48,1664]{4,3,2,1,0:T(8,128)(2,1)} %bitcast.28, bf16[2,2,2,48,1664]{4,3,2,1,0:T(8,128)(2,1)} %bitcast.34, bf16[2,2,48,1664]{3,2,1,0:T(8,128)(2,1)} %copy-done.5, bf16[2,2,2,48,1664]{4,3,2,1,0:T(8,128)(2,1)} %bitcast.31, ...), custom_call_target="tpu_custom_call" | custom-call | flops 600000000 | bytes 1 | tf_op jit(solution)/shard_map/sums/pallas_call | solution.py:351
  177.7 5.4 %collective-permute-done.13 = bf16[4,96,768]{2,1,0:T(8,128)(2,1)S(1)} collective-permute-done((bf16[4,96,768]{2,1,0:T(8,128)(2,1)}, bf16[4,96,768]{2,1,0:T(8,128)(2,1)S(1)}, u32[]{:S(2)}, u32[]{:S(2)}) %collective-permute-start.13) | collective-permute-done | bytes 589856 | tf_op jit(solution)/shard_map/ppermute | solution.py:634
  183.1 0.5 collective-permute-start.14
  183.6 0.5 collective-permute-start.15
  184.4 8.3 %collective-permute-done.14.refs_4_ = bf16[2,48,1664]{2,1,0:T(8,128)(2,1)S(1)} collective-permute-done((bf16[2,48,1664]{2,1,0:T(8,128)(2,1)}, bf16[2,48,1664]{2,1,0:T(8,128)(2,1)S(1)}, u32[]{:S(2)}, u32[]{:S(2)}) %collective-permute-start.14) | collective-permute-done | bytes 319520 | tf_op jit(solution)/shard_map/ppermute | solution.py:423
  192.7 0.7 copy-done.11
  193.6 3.5 %sums.11 = (bf16[2,48,1664]{2,1,0:T(8,128)(2,1)}, bf16[2,48,1664]{2,1,0:T(8,128)(2,1)}) custom-call(s32[2]{0:T(128)} %pad_add_fusion.at.refs_0_, bf16[2,2,2,48,1664]{4,3,2,1,0:T(8,128)(2,1)} %bitcast.29, bf16[2,2,2,48,1664]{4,3,2,1,0:T(8,128)(2,1)} %bitcast.35, bf16[2,2,48,1664]{3,2,1,0:T(8,128)(2,1)} %copy-done.5, bf16[2,48,1664]{2,1,0:T(8,128)(2,1)} %copy-done.11, ...), custom_call_target="tpu_custom_call" | custom-call | flops 600000000 | bytes 1 | tf_op jit(solution)/shard_map/sums/pallas_call | solution.py:351
  197.3 1.6 collective-permute-done.17
  198.9 3.5 %settle.3 = (bf16[12,49,768]{2,1,0:T(8,128)(2,1)}, bf16[12,2,768]{2,1,0:T(2,128)(2,1)}) custom-call(bf16[12,51,768]{2,1,0:T(8,128)(2,1)} %all-to-all-done.2.both), custom_call_target="tpu_custom_call" | custom-call | flops 600000000 | bytes 1 | tf_op jit(solution)/shard_map/settle/pallas_call | solution.py:433
  202.4 5.5 %collective-permute-done.16 = bf16[2,48,1664]{2,1,0:T(8,128)(2,1)S(1)} collective-permute-done((bf16[2,48,1664]{2,1,0:T(8,128)(2,1)}, bf16[2,48,1664]{2,1,0:T(8,128)(2,1)S(1)}, u32[]{:S(2)}, u32[]{:S(2)}) %collective-permute-start.16) | collective-permute-done | bytes 319520 | tf_op jit(solution)/shard_map/ppermute | solution.py:634
  208.0 2.6 %collective-permute-start.21 = (bf16[2,48,1664]{2,1,0:T(8,128)(2,1)S(1)}, bf16[2,48,1664]{2,1,0:T(8,128)(2,1)S(1)}, u32[]{:S(2)}, u32[]{:S(2)}) collective-permute-start(bf16[2,48,1664]{2,1,0:T(8,128)(2,1)S(1)} %add.54), channel_id=1, source_target_pairs={{0,2},{1,3},{2,0},{3,1},{4,6},{5,7},{6,4},{7,5},{8,10},{9,11},{10,... | collective-permute-start | bytes 958472 | tf_op jit(solution)/shard_map/ppermute | solution.py:637
  210.6 2.4 collective-permute-start.18
  213.0 8.0 %collective-permute-done.19 = bf16[2,96,768]{2,1,0:T(8,128)(2,1)S(1)} collective-permute-done((bf16[2,96,768]{2,1,0:T(8,128)(2,1)S(1)}, bf16[2,96,768]{2,1,0:T(8,128)(2,1)S(1)}, u32[]{:S(2)}, u32[]{:S(2)}) %collective-permute-start.19) | collective-permute-done | bytes 294944 | tf_op jit(solution)/shard_map/ppermute | solution.py:637
  221.2 5.2 %collective-permute-done.21 = bf16[2,48,1664]{2,1,0:T(8,128)(2,1)S(1)} collective-permute-done((bf16[2,48,1664]{2,1,0:T(8,128)(2,1)S(1)}, bf16[2,48,1664]{2,1,0:T(8,128)(2,1)S(1)}, u32[]{:S(2)}, u32[]{:S(2)}) %collective-permute-start.21) | collective-permute-done | bytes 319520 | tf_op jit(solution)/shard_map/ppermute | solution.py:637
  226.5 1.6 collective-permute-done.18.other_a
  228.2 6.3 %collective-permute-done.20.other_b = bf16[2,96,768]{2,1,0:T(8,128)(2,1)S(1)} collective-permute-done((bf16[2,96,768]{2,1,0:T(8,128)(2,1)S(1)}, bf16[2,96,768]{2,1,0:T(8,128)(2,1)S(1)}, u32[]{:S(2)}, u32[]{:S(2)}) %collective-permute-start.20) | collective-permute-done | bytes 294944 | tf_op jit(solution)/shard_map/ppermute | solution.py:634
  234.5 0.7 copy-done.29
  235.2 2.9 %finish_feed.1 = (f32[96,3072]{1,0:T(8,128)}, f32[384,768]{1,0:T(8,128)}) custom-call(s32[2]{0:T(128)} %pad_add_fusion.at.refs_0_, bf16[2,96,768]{2,1,0:T(8,128)(2,1)} %copy-done.15, bf16[2,96,768]{2,1,0:T(8,128)(2,1)} %copy-done.28, bf16[2,96,768]{2,1,0:T(8,128)(2,1)} %copy-done.16, bf16[2,96,768]{2,1,0:T(8,128)(2,1)} %copy-done.29), custom_call_target="tpu_custom_call" | custom-call | flops 600000000 | bytes 1 | tf_op jit(solution)/shard_map/finish_feed/pallas_call | solution.py:694
  238.1 1.0 collective-permute-done.22
  239.1 0.7 copy-done.27
  239.8 2.2 finish.1
  242.0 1.3 reduce.2
  (89 shorter events, 1.5 us)
Async XLA Ops:
  0.6 7.5 %copy-start.17 = (bf16[2,768]{1,0:T(2,128)(2,1)S(1)}, bf16[2,768]{1,0:T(2,128)(2,1)}, u32[]{:S(2)}) copy-start(bf16[2,768]{1,0:T(2,128)(2,1)} %param.23) | copy-start | bytes 9220
  0.7 7.5 %copy-start.18 = (bf16[3072]{0:T(1024)(128)(2,1)S(1)}, bf16[3072]{0:T(1024)(128)(2,1)}, u32[]{:S(2)}) copy-start(bf16[3072]{0:T(1024)(128)(2,1)} %param.29) | copy-start | bytes 18436
  0.7 7.6 %copy-start.19 = (bf16[768]{0:T(1024)(128)(2,1)S(1)}, bf16[768]{0:T(1024)(128)(2,1)}, u32[]{:S(2)}) copy-start(bf16[768]{0:T(1024)(128)(2,1)} %param.20) | copy-start | bytes 4612
  0.7 7.6 %copy-start.20 = (bf16[768]{0:T(1024)(128)(2,1)S(1)}, bf16[768]{0:T(1024)(128)(2,1)}, u32[]{:S(2)}) copy-start(bf16[768]{0:T(1024)(128)(2,1)} %param.21) | copy-start | bytes 4612
  0.7 7.6 %copy-start.25 = (s32[12,2]{0,1:T(2,128)S(1)}, s32[12,2]{0,1:T(2,128)}, u32[]{:S(2)}) copy-start(s32[12,2]{0,1:T(2,128)} %param.19) | copy-start | bytes 292
  2.0 31.2 %copy-start.21 = (bf16[768]{0:T(1024)(128)(2,1)S(1)}, bf16[768]{0:T(1024)(128)(2,1)}, u32[]{:S(2)}) copy-start(bf16[768]{0:T(1024)(128)(2,1)} %param.25) | copy-start | bytes 4612
  2.0 31.2 %copy-start.22 = (bf16[768]{0:T(1024)(128)(2,1)S(1)}, bf16[768]{0:T(1024)(128)(2,1)}, u32[]{:S(2)}) copy-start(bf16[768]{0:T(1024)(128)(2,1)} %param.26) | copy-start | bytes 4612
  2.0 31.2 %copy-start.23 = (bf16[768]{0:T(1024)(128)(2,1)S(1)}, bf16[768]{0:T(1024)(128)(2,1)}, u32[]{:S(2)}) copy-start(bf16[768]{0:T(1024)(128)(2,1)} %param.27) | copy-start | bytes 4612
  2.0 31.2 %copy-start.24 = (bf16[768]{0:T(1024)(128)(2,1)S(1)}, bf16[768]{0:T(1024)(128)(2,1)}, u32[]{:S(2)}) copy-start(bf16[768]{0:T(1024)(128)(2,1)} %param.31) | copy-start | bytes 4612
  2.1 11.8 %collective-permute-start.2 = (bf16[3,49,768]{2,1,0:T(8,128)(2,1)S(1)}, bf16[3,49,768]{2,1,0:T(8,128)(2,1)S(1)}, u32[]{:S(2)}, u32[]{:S(2)}) collective-permute-start(bf16[3,49,768]{2,1,0:T(8,128)(2,1)S(1)} %get-tuple-element.232), channel_id=1, source_target_pairs={{0,3},{1,0},{2,1},{3,2},{4,7},{5,4},{6,5},{7,6},{8,11},{9,8},{10,9... | collective-permute-start | bytes 677384 | tf_op jit(solution)/shard_map/ppermute | solution.py:475
  7.2 22.0 %collective-permute-start.1 = (bf16[3,49,768]{2,1,0:T(8,128)(2,1)S(1)}, bf16[3,49,768]{2,1,0:T(8,128)(2,1)S(1)}, u32[]{:S(2)}, u32[]{:S(2)}) collective-permute-start(bf16[3,49,768]{2,1,0:T(8,128)(2,1)S(1)} %get-tuple-element.233), channel_id=1, source_target_pairs={{0,2},{1,3},{2,0},{3,1},{4,6},{5,7},{6,4},{7,5},{8,10},{9,11},{10,... | collective-permute-start | bytes 677384 | tf_op jit(solution)/shard_map/ppermute | solution.py:475
  7.2 22.0 %collective-permute-start = (bf16[3,49,768]{2,1,0:T(8,128)(2,1)S(1)}, bf16[3,49,768]{2,1,0:T(8,128)(2,1)S(1)}, u32[]{:S(2)}, u32[]{:S(2)}) collective-permute-start(bf16[3,49,768]{2,1,0:T(8,128)(2,1)S(1)} %get-tuple-element.234), channel_id=1, source_target_pairs={{0,1},{1,2},{2,3},{3,0},{4,5},{5,6},{6,7},{7,4},{8,9},{9,10},{10,1... | collective-permute-start | bytes 677384 | tf_op jit(solution)/shard_map/ppermute | solution.py:475
  13.8 20.7 %copy-start.30 = (bf16[3,49,768]{2,1,0:T(8,128)(2,1)}, bf16[3,49,768]{2,1,0:T(8,128)(2,1)S(1)}, u32[]{:S(2)}) copy-start(bf16[3,49,768]{2,1,0:T(8,128)(2,1)S(1)} %collective-permute-done.2.x3) | copy-start | bytes 677380
  29.1 5.4 %copy-start.31 = (bf16[3,49,768]{2,1,0:T(8,128)(2,1)}, bf16[3,49,768]{2,1,0:T(8,128)(2,1)S(1)}, u32[]{:S(2)}) copy-start(bf16[3,49,768]{2,1,0:T(8,128)(2,1)S(1)} %collective-permute-done.1.x2) | copy-start | bytes 677380
  29.1 5.4 %copy-start.32 = (bf16[3,49,768]{2,1,0:T(8,128)(2,1)}, bf16[3,49,768]{2,1,0:T(8,128)(2,1)S(1)}, u32[]{:S(2)}) copy-start(bf16[3,49,768]{2,1,0:T(8,128)(2,1)S(1)} %collective-permute-done.x1) | copy-start | bytes 677380
  29.1 28.8 %all-to-all-start = ((bf16[12,49,768]{2,1,0:T(8,128)(2,1)}), bf16[12,49,768]{2,1,0:T(8,128)(2,1)S(1)}, u32[]{:S(2)}, u32[]{:S(2)}) async-start(bf16[12,49,768]{2,1,0:T(8,128)(2,1)} %param.32), calls=%async_computation | async-start | bytes 2064384 | tf_op jit(solution)/shard_map/all_to_all | solution.py:427
  58.0 1.0 copy-start.8
  90.7 7.4 %collective-permute-start.3 = (bf16[4,4,96,768]{3,2,1,0:T(8,128)(2,1)}, bf16[4,4,96,768]{3,2,1,0:T(8,128)(2,1)S(1)}, u32[]{:S(2)}, u32[]{:S(2)}) collective-permute-start(bf16[4,4,96,768]{3,2,1,0:T(8,128)(2,1)} %get-tuple-element.133), channel_id=1, source_target_pairs={{0,4},{4,0},{8,12},{12,8},{16,20},{20,16},{24,28},{28,24},{1,5},{5... | collective-permute-start | bytes 7077896 | tf_op jit(solution)/shard_map/ppermute | solution.py:423
  90.7 8.2 %collective-permute-start.4 = (bf16[1536,768]{1,0:T(8,128)(2,1)}, bf16[1536,768]{1,0:T(8,128)(2,1)}, u32[]{:S(2)}, u32[]{:S(2)}) collective-permute-start(bf16[1536,768]{1,0:T(8,128)(2,1)} %get-tuple-element.134), channel_id=1, source_target_pairs={{0,4},{4,0},{8,12},{12,8},{16,20},{20,16},{24,28},{28,24},{1,5},{5... | collective-permute-start | bytes 7077896 | tf_op jit(solution)/shard_map/ppermute | solution.py:423
  91.2 43.2 %all-to-all-start.1 = ((bf16[12,51,768]{2,1,0:T(8,128)(2,1)}), bf16[12,51,768]{2,1,0:T(8,128)(2,1)S(1)}, u32[]{:S(2)}, u32[]{:S(2)}) async-start(bf16[12,51,768]{2,1,0:T(8,128)(2,1)} %get-tuple-element.154), calls=%async_computation.1 | async-start | bytes 2064384 | tf_op jit(solution)/shard_map/all_to_all | solution.py:427
  98.1 1.4 copy-start
  103.6 30.9 %collective-permute-start.5 = (bf16[2,4,96,768]{3,2,1,0:T(8,128)(2,1)}, bf16[2,4,96,768]{3,2,1,0:T(8,128)(2,1)S(1)}, u32[]{:S(2)}, u32[]{:S(2)}) collective-permute-start(bf16[2,4,96,768]{3,2,1,0:T(8,128)(2,1)} %get-tuple-element.141), channel_id=1, source_target_pairs={{0,8},{4,12},{8,0},{12,4},{16,24},{20,28},{24,16},{28,20},{1,9},{5... | collective-permute-start | bytes 3538952 | tf_op jit(solution)/shard_map/ppermute | solution.py:423
  105.1 29.4 %collective-permute-start.6 = (bf16[2,4,96,768]{3,2,1,0:T(8,128)(2,1)}, bf16[2,4,96,768]{3,2,1,0:T(8,128)(2,1)S(1)}, u32[]{:S(2)}, u32[]{:S(2)}) collective-permute-start(bf16[2,4,96,768]{3,2,1,0:T(8,128)(2,1)} %get-tuple-element.142), channel_id=1, source_target_pairs={{0,16},{4,20},{8,24},{12,28},{16,0},{20,4},{24,8},{28,12},{1,17},{... | collective-permute-start | bytes 3538952 | tf_op jit(solution)/shard_map/ppermute | solution.py:423
  134.5 5.3 %copy-start.7 = (bf16[12,51,768]{2,1,0:T(8,128)(2,1)}, bf16[12,51,768]{2,1,0:T(8,128)(2,1)S(1)}, u32[]{:S(2)}) copy-start(bf16[12,51,768]{2,1,0:T(8,128)(2,1)S(1)} %all-to-all-done.1.both) | copy-start | bytes 2820100
  134.5 1.0 copy-start.3
  135.5 1.0 copy-start.4
  139.8 5.6 %copy-start.26 = (bf16[4,96,768]{2,1,0:T(8,128)(2,1)S(1)}, bf16[4,96,768]{2,1,0:T(8,128)(2,1)}, u32[]{:S(2)}) copy-start(bf16[4,96,768]{2,1,0:T(8,128)(2,1)} %get-tuple-element.164) | copy-start | bytes 1769476
  139.8 6.1 %collective-permute-start.9 = (bf16[384,1664]{1,0:T(8,128)(2,1)}, bf16[384,1664]{1,0:T(8,128)(2,1)S(1)}, u32[]{:S(2)}, u32[]{:S(2)}) collective-permute-start(bf16[384,1664]{1,0:T(8,128)(2,1)} %get-tuple-element.165), channel_id=1, source_target_pairs={{0,4},{4,0},{8,12},{12,8},{16,20},{20,16},{24,28},{28,24},{1,5},{5... | collective-permute-start | bytes 3833864 | tf_op jit(solution)/shard_map/ppermute | solution.py:423
  139.9 6.1 %collective-permute-start.10 = (bf16[384,1664]{1,0:T(8,128)(2,1)}, bf16[384,1664]{1,0:T(8,128)(2,1)S(1)}, u32[]{:S(2)}, u32[]{:S(2)}) collective-permute-start(bf16[384,1664]{1,0:T(8,128)(2,1)} %get-tuple-element.166), channel_id=1, source_target_pairs={{0,4},{4,0},{8,12},{12,8},{16,20},{20,16},{24,28},{28,24},{1,5},{5... | collective-permute-start | bytes 3833864 | tf_op jit(solution)/shard_map/ppermute | solution.py:423
  140.4 37.3 %all-to-all-start.2 = ((bf16[12,51,768]{2,1,0:T(8,128)(2,1)}), bf16[12,51,768]{2,1,0:T(8,128)(2,1)}, u32[]{:S(2)}, u32[]{:S(2)}) async-start(bf16[12,51,768]{2,1,0:T(8,128)(2,1)} %get-tuple-element.189), calls=%async_computation.2 | async-start | bytes 2064384 | tf_op jit(solution)/shard_map/all_to_all | solution.py:427
  144.9 16.5 %collective-permute-start.7 = (bf16[4,96,768]{2,1,0:T(8,128)(2,1)}, bf16[4,96,768]{2,1,0:T(8,128)(2,1)S(1)}, u32[]{:S(2)}, u32[]{:S(2)}) collective-permute-start(bf16[4,96,768]{2,1,0:T(8,128)(2,1)} %get-tuple-element.163), channel_id=1, source_target_pairs={{0,16},{4,20},{8,24},{12,28},{16,0},{20,4},{24,8},{28,12},{1,17},{... | collective-permute-start | bytes 1769480 | tf_op jit(solution)/shard_map/ppermute | solution.py:423
  145.4 16.3 %collective-permute-start.8 = (bf16[4,96,768]{2,1,0:T(8,128)(2,1)S(1)}, bf16[4,96,768]{2,1,0:T(8,128)(2,1)}, u32[]{:S(2)}, u32[]{:S(2)}) collective-permute-start(bf16[4,96,768]{2,1,0:T(8,128)(2,1)S(1)} %copy-done.26), channel_id=1, source_target_pairs={{0,8},{4,12},{8,0},{12,4},{16,24},{20,28},{24,16},{28,20},{1,9},{5... | collective-permute-start | bytes 1769480 | tf_op jit(solution)/shard_map/ppermute | solution.py:423
  146.0 1.1 copy-start.1
  146.0 1.4 copy-start.2
  150.3 23.8 %collective-permute-start.11 = (bf16[2,2,48,1664]{3,2,1,0:T(8,128)(2,1)}, bf16[2,2,48,1664]{3,2,1,0:T(8,128)(2,1)S(1)}, u32[]{:S(2)}, u32[]{:S(2)}) collective-permute-start(bf16[2,2,48,1664]{3,2,1,0:T(8,128)(2,1)} %get-tuple-element.173), channel_id=1, source_target_pairs={{0,8},{4,12},{8,0},{12,4},{16,24},{20,28},{24,16},{28,20},{1,9},{5... | collective-permute-start | bytes 1916936 | tf_op jit(solution)/shard_map/ppermute | solution.py:423
  151.9 22.3 %collective-permute-start.12 = (bf16[2,2,48,1664]{3,2,1,0:T(8,128)(2,1)}, bf16[2,2,48,1664]{3,2,1,0:T(8,128)(2,1)S(1)}, u32[]{:S(2)}, u32[]{:S(2)}) collective-permute-start(bf16[2,2,48,1664]{3,2,1,0:T(8,128)(2,1)} %get-tuple-element.179), channel_id=1, source_target_pairs={{0,16},{4,20},{8,24},{12,28},{16,0},{20,4},{24,8},{28,12},{1,17},{... | collective-permute-start | bytes 1916936 | tf_op jit(solution)/shard_map/ppermute | solution.py:423
  161.3 0.8 copy-start.9
  166.8 16.3 %collective-permute-start.13 = (bf16[4,96,768]{2,1,0:T(8,128)(2,1)}, bf16[4,96,768]{2,1,0:T(8,128)(2,1)S(1)}, u32[]{:S(2)}, u32[]{:S(2)}) collective-permute-start(bf16[4,96,768]{2,1,0:T(8,128)(2,1)} %get-tuple-element.188), channel_id=1, source_target_pairs={{0,1},{1,0},{2,3},{3,2},{4,5},{5,4},{6,7},{7,6},{8,9},{9,8},{10,11... | collective-permute-start | bytes 1769480 | tf_op jit(solution)/shard_map/ppermute | solution.py:634
  174.1 0.8 copy-start.6
  174.2 1.0 copy-start.5
  175.2 9.0 %copy-start.10 = (bf16[4,96,768]{2,1,0:T(8,128)(2,1)S(1)}, bf16[4,96,768]{2,1,0:T(8,128)(2,1)}, u32[]{:S(2)}) copy-start(bf16[4,96,768]{2,1,0:T(8,128)(2,1)} %get-tuple-element.184) | copy-start | bytes 1769476
  183.1 9.6 %collective-permute-start.14 = (bf16[2,48,1664]{2,1,0:T(8,128)(2,1)}, bf16[2,48,1664]{2,1,0:T(8,128)(2,1)S(1)}, u32[]{:S(2)}, u32[]{:S(2)}) collective-permute-start(bf16[2,48,1664]{2,1,0:T(8,128)(2,1)} %get-tuple-element.191), channel_id=1, source_target_pairs={{0,16},{4,20},{8,24},{12,28},{16,0},{20,4},{24,8},{28,12},{1,17},{... | collective-permute-start | bytes 958472 | tf_op jit(solution)/shard_map/ppermute | solution.py:423
  183.6 9.1 %collective-permute-start.15 = (bf16[2,48,1664]{2,1,0:T(8,128)(2,1)}, bf16[2,48,1664]{2,1,0:T(8,128)(2,1)S(1)}, u32[]{:S(2)}, u32[]{:S(2)}) collective-permute-start(bf16[2,48,1664]{2,1,0:T(8,128)(2,1)} %get-tuple-element.192), channel_id=1, source_target_pairs={{0,8},{4,12},{8,0},{12,4},{16,24},{20,28},{24,16},{28,20},{1,9},{5... | collective-permute-start | bytes 958472 | tf_op jit(solution)/shard_map/ppermute | solution.py:423
  184.4 14.5 %collective-permute-start.17 = (bf16[2,96,768]{2,1,0:T(8,128)(2,1)S(1)}, bf16[2,96,768]{2,1,0:T(8,128)(2,1)S(1)}, u32[]{:S(2)}, u32[]{:S(2)}) collective-permute-start(bf16[2,96,768]{2,1,0:T(8,128)(2,1)S(1)} %get-tuple-element.199), channel_id=1, source_target_pairs={{0,2},{1,3},{2,0},{3,1},{4,6},{5,7},{6,4},{7,5},{8,10},{9,11},{10,... | collective-permute-start | bytes 884744 | tf_op jit(solution)/shard_map/ppermute | solution.py:637
  192.7 0.7 copy-start.11
  192.7 0.8 copy-start.12
  197.1 10.8 %collective-permute-start.16 = (bf16[2,48,1664]{2,1,0:T(8,128)(2,1)}, bf16[2,48,1664]{2,1,0:T(8,128)(2,1)S(1)}, u32[]{:S(2)}, u32[]{:S(2)}) collective-permute-start(bf16[2,48,1664]{2,1,0:T(8,128)(2,1)} %get-tuple-element.195), channel_id=1, source_target_pairs={{0,1},{1,0},{2,3},{3,2},{4,5},{5,4},{6,7},{7,6},{8,9},{9,8},{10,11... | collective-permute-start | bytes 958472 | tf_op jit(solution)/shard_map/ppermute | solution.py:634
  197.2 23.8 %collective-permute-start.19 = (bf16[2,96,768]{2,1,0:T(8,128)(2,1)S(1)}, bf16[2,96,768]{2,1,0:T(8,128)(2,1)S(1)}, u32[]{:S(2)}, u32[]{:S(2)}) collective-permute-start(bf16[2,96,768]{2,1,0:T(8,128)(2,1)S(1)} %get-tuple-element.208), channel_id=1, source_target_pairs={{0,2},{1,3},{2,0},{3,1},{4,6},{5,7},{6,4},{7,5},{8,10},{9,11},{10,... | collective-permute-start | bytes 884744 | tf_op jit(solution)/shard_map/ppermute | solution.py:637
  198.9 11.7 %copy-start.15 = (bf16[2,96,768]{2,1,0:T(8,128)(2,1)}, bf16[2,96,768]{2,1,0:T(8,128)(2,1)S(1)}, u32[]{:S(2)}) copy-start(bf16[2,96,768]{2,1,0:T(8,128)(2,1)S(1)} %add.53.mine_a) | copy-start | bytes 884740
  198.9 9.0 %copy-start.14 = (bf16[2,48,1664]{2,1,0:T(8,128)(2,1)S(1)}, bf16[2,48,1664]{2,1,0:T(8,128)(2,1)}, u32[]{:S(2)}) copy-start(bf16[2,48,1664]{2,1,0:T(8,128)(2,1)} %get-tuple-element.205) | copy-start | bytes 958468
  208.0 18.3 %collective-permute-start.21 = (bf16[2,48,1664]{2,1,0:T(8,128)(2,1)S(1)}, bf16[2,48,1664]{2,1,0:T(8,128)(2,1)S(1)}, u32[]{:S(2)}, u32[]{:S(2)}) collective-permute-start(bf16[2,48,1664]{2,1,0:T(8,128)(2,1)S(1)} %add.54), channel_id=1, source_target_pairs={{0,2},{1,3},{2,0},{3,1},{4,6},{5,7},{6,4},{7,5},{8,10},{9,11},{10,... | collective-permute-start | bytes 958472 | tf_op jit(solution)/shard_map/ppermute | solution.py:637
  210.6 17.5 %collective-permute-start.18 = (bf16[2,96,768]{2,1,0:T(8,128)(2,1)S(1)}, bf16[2,96,768]{2,1,0:T(8,128)(2,1)S(1)}, u32[]{:S(2)}, u32[]{:S(2)}) collective-permute-start(bf16[2,96,768]{2,1,0:T(8,128)(2,1)S(1)} %add.53.mine_a), channel_id=1, source_target_pairs={{0,1},{1,0},{2,3},{3,2},{4,5},{5,4},{6,7},{7,6},{8,9},{9,8},{10,11... | collective-permute-start | bytes 884744 | tf_op jit(solution)/shard_map/ppermute | solution.py:634
  221.1 13.4 %copy-start.16 = (bf16[2,96,768]{2,1,0:T(8,128)(2,1)}, bf16[2,96,768]{2,1,0:T(8,128)(2,1)S(1)}, u32[]{:S(2)}) copy-start(bf16[2,96,768]{2,1,0:T(8,128)(2,1)S(1)} %add.55.mine_b) | copy-start | bytes 884740
  221.1 13.4 %collective-permute-start.20 = (bf16[2,96,768]{2,1,0:T(8,128)(2,1)S(1)}, bf16[2,96,768]{2,1,0:T(8,128)(2,1)S(1)}, u32[]{:S(2)}, u32[]{:S(2)}) collective-permute-start(bf16[2,96,768]{2,1,0:T(8,128)(2,1)S(1)} %add.55.mine_b), channel_id=1, source_target_pairs={{0,1},{1,0},{2,3},{3,2},{4,5},{5,4},{6,7},{7,6},{8,9},{9,8},{10,11... | collective-permute-start | bytes 884744 | tf_op jit(solution)/shard_map/ppermute | solution.py:634
  226.4 12.6 %copy-start.13 = (bf16[2,48,1664]{2,1,0:T(8,128)(2,1)}, bf16[2,48,1664]{2,1,0:T(8,128)(2,1)S(1)}, u32[]{:S(2)}) copy-start(bf16[2,48,1664]{2,1,0:T(8,128)(2,1)S(1)} %add.56) | copy-start | bytes 958468
  226.4 12.6 %collective-permute-start.22 = (bf16[2,48,1664]{2,1,0:T(8,128)(2,1)S(1)}, bf16[2,48,1664]{2,1,0:T(8,128)(2,1)S(1)}, u32[]{:S(2)}, u32[]{:S(2)}) collective-permute-start(bf16[2,48,1664]{2,1,0:T(8,128)(2,1)S(1)} %add.56), channel_id=1, source_target_pairs={{0,1},{1,0},{2,3},{3,2},{4,5},{5,4},{6,7},{7,6},{8,9},{9,8},{10,11... | collective-permute-start | bytes 958472 | tf_op jit(solution)/shard_map/ppermute | solution.py:634
  228.2 6.3 %copy-start.28 = (bf16[2,96,768]{2,1,0:T(8,128)(2,1)}, bf16[2,96,768]{2,1,0:T(8,128)(2,1)S(1)}, u32[]{:S(2)}) copy-start(bf16[2,96,768]{2,1,0:T(8,128)(2,1)S(1)} %collective-permute-done.18.other_a) | copy-start | bytes 884740
  234.5 0.7 copy-start.29
  239.1 0.7 copy-start.27

commit v4 on v3

--- a/solution.py
+++ b/solution.py
@@ -66,6 +66,17 @@
     for b in range(OWNERS):
         spot = pl.multiple_of(place(b ^ d) * n, n)
         ref[lead, pl.ds(spot, n), :] = value[b * n : (b + 1) * n]
+
+
+def unpacked(tall, i, images, part):
+    base = part // 16 * 16
+    rest = part - base
+    last = tall[images * base :, :].astype(F32)
+    row = last[:rest]
+    for j in range(1, images):
+        row = jnp.where(i == j, last[j * rest : (j + 1) * rest], row)
+    most = tall[pl.ds(pl.multiple_of(i * base, base), base), :].astype(F32)
+    return jnp.concatenate([most, row], axis=0)
 
 
 def forward_kernel(
@@ -79,7 +90,8 @@
     width = x0.shape[2]
     buf[...] = jnp.zeros_like(buf)
     buf[0:ns, :] = sp[0].astype(F32)
-    came = [ref[0].astype(F32) for ref in (x0, x1, x2, x3)]
+    came = [x0[0].astype(F32)]
+    came += [unpacked(ref, i, x1.shape[0] // part, part) for ref in (x1, x2, x3)]
     for s in range(len(came)):
         k = (at[0] - s) & 3
         near, far = (jnp.where((k & 1) == 0, came[j], came[j + 1]) for j in (0, 2))
@@ -125,7 +137,7 @@
     dout, dz, z, da2, acts, dus, across, *, images,
 ):
     t = pl.program_id(0)
-    part = g0.shape[1]
+    part = g0.shape[1] // images
     ns = sg.shape[1]
     padded = h.shape[1]
 
@@ -138,7 +150,7 @@
             dout[r : r + ns, :] = sg[i].astype(F32)
             for k, ref in enumerate((g0, g1, g2, g3)):
                 lo = r + ns + k * part
-                dout[lo : lo + part, :] = ref[i].astype(F32)
+                dout[lo : lo + part, :] = unpacked(ref.at[0], i, images, part)
             dz[r : r + padded, :] = (dout[r : r + padded, :] * m2).astype(BF)
             across[:, r : r + padded] = a2t[i]
         z[...] = jnp.zeros_like(z)
@@ -386,8 +398,8 @@
     for ref in vectors:
         ref[...] = flat[row : row + ref.shape[0]]
         row += ref.shape[0]
-    for j in range(long.shape[1] // n):
-        long[:, j * n : (j + 1) * n] = flat[row + j : row + j + 1]
+    parts = [flat[row + j : row + j + 1] for j in range(long.shape[0] // n)]
+    long[...] = jnp.concatenate(parts, axis=1).reshape(long.shape)
 
 
 def whole(shape, mode=None):
@@ -421,6 +433,15 @@
 
 def swap(v, bit):
     return lax.ppermute(v, "dp", [(s, s ^ bit) for s in range(lax.axis_size("dp"))])
+
+
+def pack(x, blocks):
+    images, part, width = x.shape
+    x = x.reshape(blocks, images // blocks, part, width)
+    base = part // 16 * 16
+    return jnp.concatenate(
+        [x[:, :, :base].reshape(blocks, -1, width), x[:, :, base:].reshape(blocks, -1, width)], axis=1
+    )
 
 
 def exchange(x):
@@ -471,10 +492,10 @@
 
     moved = []
     for k in range(1, groups):
-        block = lax.dynamic_slice_in_dim(patches, n * ((me + k) % groups), n)
+        block = pack(lax.dynamic_slice_in_dim(patches, n * ((me + k) % groups), n), 1)[0]
         moved.append(lax.ppermute(block, "seq", [(s, (s + k) % groups) for s in range(groups)]))
     moved = together(*moved)
-    grads = exchange(after(grad_patches, *moved))
+    grads = exchange(after(pack(grad_patches, groups), *moved))
     vectors = (
         fc1_bias, ln1_gain, ln1_bias, qv_bias[0], jnp.zeros_like(proj_bias), qv_bias[1], proj_bias,
         ln2_gain, ln2_bias, fc2_bias,
@@ -498,7 +519,7 @@
             grid=(n,),
             in_specs=[
                 pl.BlockSpec((1, part, width), lambda i, at, keep: (at[0] * n + i, 0, 0)),
-                *[per_image(0, part, width)] * (groups - 1),
+                *[whole((n * part, width))] * (groups - 1),
                 pl.BlockSpec((1, ns, width), lambda i, at, keep: (at[0] * n + i, 0, 0)),
                 vector(0), vector(1), whole(qkv_weight.shape), vector(2, 3),
                 whole(proj_weight.shape), vector(5), vector(6), vector(7),
@@ -529,7 +550,7 @@
             grid=(steps,),
             in_specs=[
                 *[
-                    pl.BlockSpec((n, part, width), lambda t, at, keep, k=k: (k, 0, 0), pipeline_mode=once)
+                    pl.BlockSpec((1, n * part, width), lambda t, at, keep, k=k: (k, 0, 0), pipeline_mode=once)
                     for k in range(groups)
                 ],
                 pl.BlockSpec((n, ns, width), lambda t, at, keep: (at[0], 0, 0)),
@@ -661,7 +682,7 @@
     cs, ds_ = sums(
         [[(wc, (1, 0)), (rc, (1, 0)), (qc, (1,))], [(wd, (0, 1)), (rd, (0, 1)), (qd, (1,))]]
     )
-    cs, ds_, re, dx_rows = together(cs, ds_, re, dx_rows)
+    cs, ds_, re = together(cs, ds_, re)
     tc, td = swap(cs, 4), swap(ds_, 2)
     e = e + re
     e, g = e[: steps // 2], e[steps // 2 :]
@@ -706,7 +727,7 @@
         out_shape=[
             struct(n1, 3 * width, dtype=F32), struct(n1, width, dtype=F32),
             *[struct(1, n1, dtype=F32)] * 2, struct(2, n1, dtype=F32),
-            *[struct(1, n1, dtype=F32)] * 4, struct(1, hidden // OWNERS, dtype=F32),
+            *[struct(1, n1, dtype=F32)] * 4, struct(hidden // OWNERS, dtype=F32),
         ],
         compiler_params=pltpu.CompilerParams(vmem_limit_bytes=60 * 2**20),
         cost_estimate=cost(2),

time: 245 us -> 238 us (0.971)
  waiting for transfers between devices: 85.9 us -> 65.2 us
  starting transfers between devices: 34.9 us -> 48.6 us
    ppermute x3, waiting for transfers between devices: 20.1 us -> 12.3 us  [shards(): lax.ppermute(block, 'seq', [(s, (s + k) % groups) for s in range(groups)])]
    ppermute x3, waiting for transfers between devices: 14.7 us -> 7.07 us  [far(): return lax.ppermute(v, 'seq', [(s, s ^ 2) for s in range(groups)])]
    ppermute x12, waiting for transfers between devices: 22.9 us -> 15.3 us  [swap(): lax.ppermute(v, 'dp', [(s, s ^ bit) for s in range(lax.axis_size('dp'))])]
    ppermute x5, starting transfers between devices: 4.38 us -> 9.98 us  [near(): return lax.ppermute(v, 'seq', [(s, s ^ 1) for s in range(groups)])]
    ppermute x3, starting transfers between devices: 2.74 us -> 7.05 us  [far(): return lax.ppermute(v, 'seq', [(s, s ^ 2) for s in range(groups)])]
    ppermute x5, waiting for transfers between devices: 19.9 us -> 23.7 us  [near(): return lax.ppermute(v, 'seq', [(s, s ^ 1) for s in range(groups)])]
    all_to_all x3, starting transfers between devices: 12.2 us -> 15.9 us  [exchange(): return lax.all_to_all(x, 'seq', split_axis=0, concat_axis=0, tiled=True)]
    unnamed x70 -> x71, local copies, waits for them, and re-layouts: 9.4 us -> 9.05 us
  transfers between devices with their start and end apart: 26 -> 26, of which waited for: 17 -> 16; matrix products, arithmetic and copies ran while one was open for 1% -> 2% of each run, Pallas kernels for 29% -> 30%
where the time goes in v4:
time: 238 us; the launch traced here: 237 us
  Pallas kernels  108 us (45%)
  waiting for transfers between devices  65.2 us (27%)
  starting transfers between devices  48.6 us (20%)
  local copies, waits for them, and re-layouts  11.8 us (5%)
    pallas_call x1, Pallas kernels, shards(): pl.pallas_call(partial(feed_kernel, images=n), grid_spec=pltpu.PrefetchSc...  31.7 us
    pallas_call x1, Pallas kernels, shards(): pl.pallas_call(partial(heads_kernel, images=n, heads=heads, part=part, ns...  27.8 us
    ppermute x5, waiting for transfers between devices, near(): return lax.ppermute(v, 'seq', [(s, s ^ 1) for s in range(groups)])  23.7 us
    pallas_call x6, Pallas kernels, sums(): pl.pallas_call(partial(sum_kernel, jobs=leads, pick=at is not None), in_s...  20.9 us
    all_to_all x3, starting transfers between devices, exchange(): return lax.all_to_all(x, 'seq', split_axis=0, concat_axis=0, tiled=True)  15.9 us
    ppermute x12, waiting for transfers between devices, swap(): lax.ppermute(v, 'dp', [(s, s ^ bit) for s in range(lax.axis_size('dp'))])  15.3 us
    pallas_call x1, Pallas kernels, shards(): pl.pallas_call(partial(forward_kernel, rows=rows, heads=heads), grid_spec...  15.2 us
    ppermute x3, waiting for transfers between devices, shards(): lax.ppermute(block, 'seq', [(s, (s + k) % groups) for s in range(groups)])  12.3 us
  transfers between devices with their start and end apart: 26, of which 16 were waited for; matrix products, arithmetic and copies ran while one was open for 2% of the time, Pallas kernels for 30%

profile of v4, /device:TPU:0, one launch (start us, length us, event | category | flops | bytes accessed | tf_op | source)
XLA Modules:
  0.0 236.9 jit_solution(13148020446681487050)
XLA Ops:
  0.7 1.3 constant_dynamic-slice_fusion
  1.9 0.2 copy_bitcast_fusion
  2.4 4.1 %collective-permute-start.1 = (bf16[147,768]{1,0:T(8,128)(2,1)S(1)}, bf16[147,768]{1,0:T(8,128)(2,1)S(1)}, u32[]{:S(2)}, u32[]{:S(2)}) collective-permute-start(bf16[147,768]{1,0:T(8,128)(2,1)S(1)} %maximum_bitcast_fusion.1), channel_id=1, source_target_pairs={{0,2},{1,3},{2,0},{3,1},{4,6},{5,7},{6,4},{7,5},{8,10},{9,11},{10,... | collective-permute-start | bytes 677384 | tf_op jit(solution)/shard_map/ppermute | solution.py:496
  6.7 1.4 collective-permute-start.2
  8.4 0.7 collective-permute-start
  9.3 0.7 copy.47.keep
  10.1 1.0 pad_maximum_fusion
  11.1 7.8 %collective-permute-done.1.x2 = bf16[147,768]{1,0:T(8,128)(2,1)S(1)} collective-permute-done((bf16[147,768]{1,0:T(8,128)(2,1)S(1)}, bf16[147,768]{1,0:T(8,128)(2,1)S(1)}, u32[]{:S(2)}, u32[]{:S(2)}) %collective-permute-start.1) | collective-permute-done | bytes 225824 | tf_op jit(solution)/shard_map/ppermute | solution.py:496
  18.9 4.5 %collective-permute-done.x1 = bf16[147,768]{1,0:T(8,128)(2,1)S(1)} collective-permute-done((bf16[147,768]{1,0:T(8,128)(2,1)S(1)}, bf16[147,768]{1,0:T(8,128)(2,1)S(1)}, u32[]{:S(2)}, u32[]{:S(2)}) %collective-permute-start) | collective-permute-done | bytes 225824 | tf_op jit(solution)/shard_map/ppermute | solution.py:496
  23.4 7.7 %all-to-all-start = ((bf16[4,147,768]{2,1,0:T(8,128)(2,1)}), bf16[4,147,768]{2,1,0:T(8,128)(2,1)S(1)}, u32[]{:S(2)}, u32[]{:S(2)}) async-start(bf16[4,147,768]{2,1,0:T(8,128)(2,1)} %pad_maximum_fusion), calls=%async_computation | async-start | bytes 1867776 | tf_op jit(solution)/shard_map/all_to_all | solution.py:448
  31.2 0.7 reshape.132.g1.b1.bq.bp.g2.b2.gain
  31.9 0.6 pad_add_fusion.at.refs_0_
  32.5 15.2 %attention_forward.1 = (bf16[3,208,768]{2,1,0:T(8,128)(2,1)}, bf16[3,768,208]{2,1,0:T(8,128)(2,1)}, bf16[3,208,2304]{2,1,0:T(8,128)(2,1)}, bf16[3,6,416,208]{3,2...) custom-call(s32[2]{0:T(128)} %pad_add_fusion.at.refs_0_, ...), custom_call_target="tpu_custom_call" | custom-call | flops 4499999744 | bytes 1 | tf_op jit(solution)/shard_map/attention_forward/pallas_call | solution.py:515
  47.7 6.9 %all-to-all-done.g0.g1.g2.g3 = bf16[4,147,768]{2,1,0:T(8,128)(2,1)S(1)} async-done(((bf16[4,147,768]{2,1,0:T(8,128)(2,1)}), bf16[4,147,768]{2,1,0:T(8,128)(2,1)S(1)}, u32[]{:S(2)}, u32[]{:S(2)}) %all-to-all-start) | async-done | bytes 903200 | tf_op jit(solution)/shard_map/all_to_all | solution.py:448
  54.6 1.0 copy-done.8
  55.6 31.7 %feed_forward.1 = (bf16[12,51,768]{2,1,0:T(8,128)(2,1)}, f32[3,208,768]{2,1,0:T(8,128)}, bf16[3,208,768]{2,1,0:T(8,128)(2,1)}, bf16[1536,768]{1,0:T(8,128)(2,1)}...) custom-call(s32[2]{0:T(128)} %pad_add_fusion.at.refs_0_, ...), custom_call_target="tpu_custom_call" | custom-call | flops 8999999488 | bytes 1 | tf_op jit(solution)/shard_map/feed_forward/pallas_call | solution.py:546
  87.4 0.5 collective-permute-start.4
  87.9 3.7 %all-to-all-start.1 = ((bf16[12,51,768]{2,1,0:T(8,128)(2,1)}), bf16[12,51,768]{2,1,0:T(8,128)(2,1)S(1)}, u32[]{:S(2)}, u32[]{:S(2)}) async-start(bf16[12,51,768]{2,1,0:T(8,128)(2,1)} %get-tuple-element.153), calls=%async_computation.1 | async-start | bytes 2064384 | tf_op jit(solution)/shard_map/all_to_all | solution.py:448
  91.6 3.1 %collective-permute-done.3 = bf16[4,4,96,768]{3,2,1,0:T(8,128)(2,1)S(1)} collective-permute-done((bf16[4,4,96,768]{3,2,1,0:T(8,128)(2,1)}, bf16[4,4,96,768]{3,2,1,0:T(8,128)(2,1)S(1)}, u32[]{:S(2)}, u32[]{:S(2)}) %collective-permute-start.3) | collective-permute-done | bytes 2359328 | tf_op jit(solution)/shard_map/ppermute | solution.py:435
  94.7 0.9 collective-permute-done.4
  95.6 0.6 copy-done
  96.2 4.0 %sums.6 = (bf16[2,4,96,768]{3,2,1,0:T(8,128)(2,1)}, bf16[2,4,96,768]{3,2,1,0:T(8,128)(2,1)}) custom-call(bf16[2,2,4,96,768]{4,3,2,1,0:T(8,128)(2,1)} %bitcast.48, bf16[2,2,4,96,768]{4,3,2,1,0:T(8,128)(2,1)} %bitcast.51, bf16[2,2,4,96,768]{4,3,2,1,0:T(8,128)(2,1)} %bitcast.45, bf16[2,2,4,96,768]{4,3,2,1,0:T(8,128)(2,1)} %bitcast.20.refs_3_.refs_4_.refs_6_), custom_call_target="tpu_custom_call" | custom-call | flops 600000000 | bytes 1 | tf_op jit(solution)/shard_map/sums/pallas_call | solution.py:363
  100.2 1.6 collective-permute-start.5
  101.8 1.5 collective-permute-start.6
  103.3 27.8 %attention_backward.1 = (bf16[12,51,768]{2,1,0:T(8,128)(2,1)}, f32[2,768]{1,0:T(2,128)}, f32[1,2304]{1,0:T(1,128)}, bf16[384,1664]{1,0:T(8,128)(2,1)}, bf16[384,...) custom-call(s32[2]{0:T(128)} %pad_add_fusion.at.refs_0_, ...), custom_call_target="tpu_custom_call" | custom-call | flops 6600000000 | bytes 1 | tf_op jit(solution)/shard_map/attention_backward/pallas_call | solution.py:609
  131.2 1.0 copy-done.3
  132.2 1.0 copy-done.4
  133.2 3.2 %sums.7 = (bf16[4,96,768]{2,1,0:T(8,128)(2,1)}, bf16[4,96,768]{2,1,0:T(8,128)(2,1)}) custom-call(bf16[2,2,4,96,768]{4,3,2,1,0:T(8,128)(2,1)} %bitcast.49, bf16[2,2,4,96,768]{4,3,2,1,0:T(8,128)(2,1)} %bitcast.52, bf16[2,4,96,768]{3,2,1,0:T(8,128)(2,1)} %copy-done.3, bf16[2,2,4,96,768]{4,3,2,1,0:T(8,128)(2,1)} %bitcast.46, ...), custom_call_target="tpu_custom_call" | custom-call | flops 600000000 | bytes 1 | tf_op jit(solution)/shard_map/sums/pallas_call | solution.py:363
  136.6 0.5 collective-permute-start.10
  137.1 0.5 collective-permute-start.7
  137.6 0.5 collective-permute-start.8
  138.1 4.5 %all-to-all-start.2 = ((bf16[12,51,768]{2,1,0:T(8,128)(2,1)}), bf16[12,51,768]{2,1,0:T(8,128)(2,1)}, u32[]{:S(2)}, u32[]{:S(2)}) async-start(bf16[12,51,768]{2,1,0:T(8,128)(2,1)} %get-tuple-element.194), calls=%async_computation.2 | async-start | bytes 2064384 | tf_op jit(solution)/shard_map/all_to_all | solution.py:448
  142.6 1.0 copy-done.1
  143.6 0.4 copy-done.2
  144.0 2.9 %sums.8 = (bf16[2,2,48,1664]{3,2,1,0:T(8,128)(2,1)}, bf16[2,2,48,1664]{3,2,1,0:T(8,128)(2,1)}) custom-call(bf16[2,2,2,48,1664]{4,3,2,1,0:T(8,128)(2,1)} %bitcast.54, bf16[2,2,2,48,1664]{4,3,2,1,0:T(8,128)(2,1)} %bitcast.60, bf16[2,2,2,48,1664]{4,3,2,1,0:T(8,128)(2,1)} %bitcast.57, bf16[2,2,2,48,1664]{4,3,2,1,0:T(8,128)(2,1)} %bitcast.63), custom_call_target="tpu_custom_call" | custom-call | flops 600000000 | bytes 1 | tf_op jit(solution)/shard_map/sums/pallas_call | solution.py:363
  146.9 1.6 collective-permute-start.11
  148.5 1.5 collective-permute-start.12
  150.0 3.4 %settle.2 = (bf16[12,49,768]{2,1,0:T(8,128)(2,1)}, bf16[12,2,768]{2,1,0:T(2,128)(2,1)}) custom-call(bf16[12,51,768]{2,1,0:T(8,128)(2,1)} %copy-done.7), custom_call_target="tpu_custom_call" | custom-call | flops 600000000 | bytes 1 | tf_op jit(solution)/shard_map/settle/pallas_call | solution.py:454
  153.5 0.6 collective-permute-done.8.refs_8_
  154.3 4.7 %sums.9 = (bf16[4,96,768]{2,1,0:T(8,128)(2,1)}, bf16[4,96,768]{2,1,0:T(8,128)(2,1)}) custom-call(s32[2]{0:T(128)} %pad_add_fusion.at.refs_0_, bf16[2,2,4,96,768]{4,3,2,1,0:T(8,128)(2,1)} %bitcast.50, bf16[2,2,4,96,768]{4,3,2,1,0:T(8,128)(2,1)} %bitcast.53, bf16[2,4,96,768]{3,2,1,0:T(8,128)(2,1)} %copy-done.3, bf16[4,96,768]{2,1,0:T(8,128)(2,1)} %copy-done.10, ...), custom_call_target="tpu_custom_call" | custom-call | flops 600000000 | bytes 1 | tf_op jit(solution)/shard_map/sums/pallas_call | solution.py:363
  158.9 1.7 collective-permute-start.13
  160.7 5.6 %collective-permute-done.12.refs_5_.refs_7_ = bf16[2,2,48,1664]{3,2,1,0:T(8,128)(2,1)S(1)} collective-permute-done((bf16[2,2,48,1664]{3,2,1,0:T(8,128)(2,1)}, bf16[2,2,48,1664]{3,2,1,0:T(8,128)(2,1)S(1)}, u32[]{:S(2)}, u32[]{:S(2)}) %collective-permute-start.12) | collective-permute-done | bytes 639008 | tf_op jit(solution)/shard_map/ppermute | solution.py:435
  166.5 0.6 copy-done.6
  167.1 0.2 copy-done.5
  167.3 2.5 %sums.10 = (bf16[2,48,1664]{2,1,0:T(8,128)(2,1)}, bf16[2,48,1664]{2,1,0:T(8,128)(2,1)}) custom-call(bf16[2,2,2,48,1664]{4,3,2,1,0:T(8,128)(2,1)} %bitcast.55, bf16[2,2,2,48,1664]{4,3,2,1,0:T(8,128)(2,1)} %bitcast.61, bf16[2,2,48,1664]{3,2,1,0:T(8,128)(2,1)} %copy-done.5, bf16[2,2,2,48,1664]{4,3,2,1,0:T(8,128)(2,1)} %bitcast.58, ...), custom_call_target="tpu_custom_call" | custom-call | flops 600000000 | bytes 1 | tf_op jit(solution)/shard_map/sums/pallas_call | solution.py:363
  169.8 7.9 %collective-permute-done.13 = bf16[4,96,768]{2,1,0:T(8,128)(2,1)S(1)} collective-permute-done((bf16[4,96,768]{2,1,0:T(8,128)(2,1)}, bf16[4,96,768]{2,1,0:T(8,128)(2,1)S(1)}, u32[]{:S(2)}, u32[]{:S(2)}) %collective-permute-start.13) | collective-permute-done | bytes 589856 | tf_op jit(solution)/shard_map/ppermute | solution.py:655
  177.8 0.5 collective-permute-start.14
  178.3 0.7 collective-permute-start.15
  179.1 1.7 collective-permute-start.17
  180.8 4.6 %collective-permute-done.14.refs_4_ = bf16[2,48,1664]{2,1,0:T(8,128)(2,1)S(1)} collective-permute-done((bf16[2,48,1664]{2,1,0:T(8,128)(2,1)}, bf16[2,48,1664]{2,1,0:T(8,128)(2,1)S(1)}, u32[]{:S(2)}, u32[]{:S(2)}) %collective-permute-start.14) | collective-permute-done | bytes 319520 | tf_op jit(solution)/shard_map/ppermute | solution.py:435
  185.5 0.7 copy-done.12
  186.3 3.5 %sums.11 = (bf16[2,48,1664]{2,1,0:T(8,128)(2,1)}, bf16[2,48,1664]{2,1,0:T(8,128)(2,1)}) custom-call(s32[2]{0:T(128)} %pad_add_fusion.at.refs_0_, bf16[2,2,2,48,1664]{4,3,2,1,0:T(8,128)(2,1)} %bitcast.56, bf16[2,2,2,48,1664]{4,3,2,1,0:T(8,128)(2,1)} %bitcast.62, bf16[2,2,48,1664]{3,2,1,0:T(8,128)(2,1)} %copy-done.5, bf16[2,48,1664]{2,1,0:T(8,128)(2,1)} %copy-done.12, ...), custom_call_target="tpu_custom_call" | custom-call | flops 600000000 | bytes 1 | tf_op jit(solution)/shard_map/sums/pallas_call | solution.py:363
  189.9 5.3 %collective-permute-start.19 = (bf16[2,96,768]{2,1,0:T(8,128)(2,1)S(1)}, bf16[2,96,768]{2,1,0:T(8,128)(2,1)S(1)}, u32[]{:S(2)}, u32[]{:S(2)}) collective-permute-start(bf16[2,96,768]{2,1,0:T(8,128)(2,1)S(1)} %get-tuple-element.206), channel_id=1, source_target_pairs={{0,2},{1,3},{2,0},{3,1},{4,6},{5,7},{6,4},{7,5},{8,10},{9,11},{10,... | collective-permute-start | bytes 884744 | tf_op jit(solution)/shard_map/ppermute | solution.py:658
  195.3 3.5 %settle.3 = (bf16[12,49,768]{2,1,0:T(8,128)(2,1)}, bf16[12,2,768]{2,1,0:T(2,128)(2,1)}) custom-call(bf16[12,51,768]{2,1,0:T(8,128)(2,1)} %all-to-all-done.2.both), custom_call_target="tpu_custom_call" | custom-call | flops 600000000 | bytes 1 | tf_op jit(solution)/shard_map/settle/pallas_call | solution.py:454
  198.8 6.9 %collective-permute-done.16 = bf16[2,48,1664]{2,1,0:T(8,128)(2,1)S(1)} collective-permute-done((bf16[2,48,1664]{2,1,0:T(8,128)(2,1)}, bf16[2,48,1664]{2,1,0:T(8,128)(2,1)S(1)}, u32[]{:S(2)}, u32[]{:S(2)}) %collective-permute-start.16) | collective-permute-done | bytes 319520 | tf_op jit(solution)/shard_map/ppermute | solution.py:655
  206.0 8.0 %collective-permute-start.20 = (bf16[2,96,768]{2,1,0:T(8,128)(2,1)S(1)}, bf16[2,96,768]{2,1,0:T(8,128)(2,1)S(1)}, u32[]{:S(2)}, u32[]{:S(2)}) collective-permute-start(bf16[2,96,768]{2,1,0:T(8,128)(2,1)S(1)} %add.55.mine_b), channel_id=1, source_target_pairs={{0,1},{1,0},{2,3},{3,2},{4,5},{5,4},{6,7},{7,6},{8,9},{9,8},{10,11... | collective-permute-start | bytes 884744 | tf_op jit(solution)/shard_map/ppermute | solution.py:655
  214.1 7.1 %collective-permute-done.21 = bf16[2,48,1664]{2,1,0:T(8,128)(2,1)S(1)} collective-permute-done((bf16[2,48,1664]{2,1,0:T(8,128)(2,1)S(1)}, bf16[2,48,1664]{2,1,0:T(8,128)(2,1)S(1)}, u32[]{:S(2)}, u32[]{:S(2)}) %collective-permute-start.21) | collective-permute-done | bytes 319520 | tf_op jit(solution)/shard_map/ppermute | solution.py:658
  221.3 1.3 collective-permute-done.18.other_a
  222.6 6.3 %collective-permute-done.20.other_b = bf16[2,96,768]{2,1,0:T(8,128)(2,1)S(1)} collective-permute-done((bf16[2,96,768]{2,1,0:T(8,128)(2,1)S(1)}, bf16[2,96,768]{2,1,0:T(8,128)(2,1)S(1)}, u32[]{:S(2)}, u32[]{:S(2)}) %collective-permute-start.20) | collective-permute-done | bytes 294944 | tf_op jit(solution)/shard_map/ppermute | solution.py:655
  228.9 0.7 copy-done.29
  229.6 2.9 %finish_feed.1 = (f32[96,3072]{1,0:T(8,128)}, f32[384,768]{1,0:T(8,128)}) custom-call(s32[2]{0:T(128)} %pad_add_fusion.at.refs_0_, bf16[2,96,768]{2,1,0:T(8,128)(2,1)} %copy-done.16, bf16[2,96,768]{2,1,0:T(8,128)(2,1)} %copy-done.28, bf16[2,96,768]{2,1,0:T(8,128)(2,1)} %copy-done.17, bf16[2,96,768]{2,1,0:T(8,128)(2,1)} %copy-done.29), custom_call_target="tpu_custom_call" | custom-call | flops 600000000 | bytes 1 | tf_op jit(solution)/shard_map/finish_feed/pallas_call | solution.py:715
  232.5 1.2 collective-permute-done.22
  233.7 0.7 copy-done.27
  234.5 2.2 finish.1
  (106 shorter events, 2.4 us)
Async XLA Ops:
  2.4 6.8 %copy-start.9 = (bf16[12,49,768]{2,1,0:T(8,128)(2,1)S(1)}, bf16[12,49,768]{2,1,0:T(8,128)(2,1)}, u32[]{:S(2)}) copy-start(bf16[12,49,768]{2,1,0:T(8,128)(2,1)} %param.32) | copy-start | bytes 2709508
  2.4 16.5 %collective-permute-start.1 = (bf16[147,768]{1,0:T(8,128)(2,1)S(1)}, bf16[147,768]{1,0:T(8,128)(2,1)S(1)}, u32[]{:S(2)}, u32[]{:S(2)}) collective-permute-start(bf16[147,768]{1,0:T(8,128)(2,1)S(1)} %maximum_bitcast_fusion.1), channel_id=1, source_target_pairs={{0,2},{1,3},{2,0},{3,1},{4,6},{5,7},{6,4},{7,5},{8,10},{9,11},{10,... | collective-permute-start | bytes 677384 | tf_op jit(solution)/shard_map/ppermute | solution.py:496
  6.7 12.3 %collective-permute-start.2 = (bf16[147,768]{1,0:T(8,128)(2,1)S(1)}, bf16[147,768]{1,0:T(8,128)(2,1)S(1)}, u32[]{:S(2)}, u32[]{:S(2)}) collective-permute-start(bf16[147,768]{1,0:T(8,128)(2,1)S(1)} %maximum_bitcast_fusion.2), channel_id=1, source_target_pairs={{0,3},{1,0},{2,1},{3,2},{4,7},{5,4},{6,5},{7,6},{8,11},{9,8},{10,9... | collective-permute-start | bytes 677384 | tf_op jit(solution)/shard_map/ppermute | solution.py:496
  8.1 1.2 copy-start.26
  8.1 1.9 copy-start.18
  8.2 1.8 copy-start.19
  8.2 1.8 copy-start.20
  8.2 1.8 copy-start.21
  8.4 15.0 %collective-permute-start = (bf16[147,768]{1,0:T(8,128)(2,1)S(1)}, bf16[147,768]{1,0:T(8,128)(2,1)S(1)}, u32[]{:S(2)}, u32[]{:S(2)}) collective-permute-start(bf16[147,768]{1,0:T(8,128)(2,1)S(1)} %maximum_bitcast_fusion), channel_id=1, source_target_pairs={{0,1},{1,2},{2,3},{3,0},{4,5},{5,6},{6,7},{7,4},{8,9},{9,10},{10,1... | collective-permute-start | bytes 677384 | tf_op jit(solution)/shard_map/ppermute | solution.py:496
  10.1 21.1 %copy-start.22 = (bf16[768]{0:T(1024)(128)(2,1)S(1)}, bf16[768]{0:T(1024)(128)(2,1)}, u32[]{:S(2)}) copy-start(bf16[768]{0:T(1024)(128)(2,1)} %param.25) | copy-start | bytes 4612
  10.1 21.1 %copy-start.23 = (bf16[768]{0:T(1024)(128)(2,1)S(1)}, bf16[768]{0:T(1024)(128)(2,1)}, u32[]{:S(2)}) copy-start(bf16[768]{0:T(1024)(128)(2,1)} %param.26) | copy-start | bytes 4612
  10.1 21.1 %copy-start.24 = (bf16[768]{0:T(1024)(128)(2,1)S(1)}, bf16[768]{0:T(1024)(128)(2,1)}, u32[]{:S(2)}) copy-start(bf16[768]{0:T(1024)(128)(2,1)} %param.27) | copy-start | bytes 4612
  10.1 21.1 %copy-start.25 = (bf16[768]{0:T(1024)(128)(2,1)S(1)}, bf16[768]{0:T(1024)(128)(2,1)}, u32[]{:S(2)}) copy-start(bf16[768]{0:T(1024)(128)(2,1)} %param.31) | copy-start | bytes 4612
  18.9 13.6 %copy-start.30 = (bf16[147,768]{1,0:T(8,128)(2,1)}, bf16[147,768]{1,0:T(8,128)(2,1)S(1)}, u32[]{:S(2)}) copy-start(bf16[147,768]{1,0:T(8,128)(2,1)S(1)} %collective-permute-done.1.x2) | copy-start | bytes 677380
  18.9 13.6 %copy-start.31 = (bf16[147,768]{1,0:T(8,128)(2,1)}, bf16[147,768]{1,0:T(8,128)(2,1)S(1)}, u32[]{:S(2)}) copy-start(bf16[147,768]{1,0:T(8,128)(2,1)S(1)} %collective-permute-done.2.x3) | copy-start | bytes 677380
  23.4 9.1 %copy-start.32 = (bf16[147,768]{1,0:T(8,128)(2,1)}, bf16[147,768]{1,0:T(8,128)(2,1)S(1)}, u32[]{:S(2)}) copy-start(bf16[147,768]{1,0:T(8,128)(2,1)S(1)} %collective-permute-done.x1) | copy-start | bytes 677380
  23.4 31.2 %all-to-all-start = ((bf16[4,147,768]{2,1,0:T(8,128)(2,1)}), bf16[4,147,768]{2,1,0:T(8,128)(2,1)S(1)}, u32[]{:S(2)}, u32[]{:S(2)}) async-start(bf16[4,147,768]{2,1,0:T(8,128)(2,1)} %pad_maximum_fusion), calls=%async_computation | async-start | bytes 1867776 | tf_op jit(solution)/shard_map/all_to_all | solution.py:448
  54.6 1.0 copy-start.8
  87.3 7.4 %collective-permute-start.3 = (bf16[4,4,96,768]{3,2,1,0:T(8,128)(2,1)}, bf16[4,4,96,768]{3,2,1,0:T(8,128)(2,1)S(1)}, u32[]{:S(2)}, u32[]{:S(2)}) collective-permute-start(bf16[4,4,96,768]{3,2,1,0:T(8,128)(2,1)} %get-tuple-element.132), channel_id=1, source_target_pairs={{0,4},{4,0},{8,12},{12,8},{16,20},{20,16},{24,28},{28,24},{1,5},{5... | collective-permute-start | bytes 7077896 | tf_op jit(solution)/shard_map/ppermute | solution.py:435
  87.4 8.2 %collective-permute-start.4 = (bf16[1536,768]{1,0:T(8,128)(2,1)}, bf16[1536,768]{1,0:T(8,128)(2,1)}, u32[]{:S(2)}, u32[]{:S(2)}) collective-permute-start(bf16[1536,768]{1,0:T(8,128)(2,1)} %get-tuple-element.133), channel_id=1, source_target_pairs={{0,4},{4,0},{8,12},{12,8},{16,20},{20,16},{24,28},{28,24},{1,5},{5... | collective-permute-start | bytes 7077896 | tf_op jit(solution)/shard_map/ppermute | solution.py:435
  87.9 43.3 %all-to-all-start.1 = ((bf16[12,51,768]{2,1,0:T(8,128)(2,1)}), bf16[12,51,768]{2,1,0:T(8,128)(2,1)S(1)}, u32[]{:S(2)}, u32[]{:S(2)}) async-start(bf16[12,51,768]{2,1,0:T(8,128)(2,1)} %get-tuple-element.153), calls=%async_computation.1 | async-start | bytes 2064384 | tf_op jit(solution)/shard_map/all_to_all | solution.py:448
  94.7 1.5 copy-start
  100.2 30.9 %collective-permute-start.5 = (bf16[2,4,96,768]{3,2,1,0:T(8,128)(2,1)}, bf16[2,4,96,768]{3,2,1,0:T(8,128)(2,1)S(1)}, u32[]{:S(2)}, u32[]{:S(2)}) collective-permute-start(bf16[2,4,96,768]{3,2,1,0:T(8,128)(2,1)} %get-tuple-element.140), channel_id=1, source_target_pairs={{0,8},{4,12},{8,0},{12,4},{16,24},{20,28},{24,16},{28,20},{1,9},{5... | collective-permute-start | bytes 3538952 | tf_op jit(solution)/shard_map/ppermute | solution.py:435
  101.8 29.4 %collective-permute-start.6 = (bf16[2,4,96,768]{3,2,1,0:T(8,128)(2,1)}, bf16[2,4,96,768]{3,2,1,0:T(8,128)(2,1)S(1)}, u32[]{:S(2)}, u32[]{:S(2)}) collective-permute-start(bf16[2,4,96,768]{3,2,1,0:T(8,128)(2,1)} %get-tuple-element.141), channel_id=1, source_target_pairs={{0,16},{4,20},{8,24},{12,28},{16,0},{20,4},{24,8},{28,12},{1,17},{... | collective-permute-start | bytes 3538952 | tf_op jit(solution)/shard_map/ppermute | solution.py:435
  131.1 5.3 %copy-start.7 = (bf16[12,51,768]{2,1,0:T(8,128)(2,1)}, bf16[12,51,768]{2,1,0:T(8,128)(2,1)S(1)}, u32[]{:S(2)}) copy-start(bf16[12,51,768]{2,1,0:T(8,128)(2,1)S(1)} %all-to-all-done.1.both) | copy-start | bytes 2820100
  131.2 1.0 copy-start.3
  132.2 1.0 copy-start.4
  136.5 6.1 %collective-permute-start.9 = (bf16[384,1664]{1,0:T(8,128)(2,1)}, bf16[384,1664]{1,0:T(8,128)(2,1)S(1)}, u32[]{:S(2)}, u32[]{:S(2)}) collective-permute-start(bf16[384,1664]{1,0:T(8,128)(2,1)} %get-tuple-element.164), channel_id=1, source_target_pairs={{0,4},{4,0},{8,12},{12,8},{16,20},{20,16},{24,28},{28,24},{1,5},{5... | collective-permute-start | bytes 3833864 | tf_op jit(solution)/shard_map/ppermute | solution.py:435
  136.6 6.0 %collective-permute-start.10 = (bf16[384,1664]{1,0:T(8,128)(2,1)}, bf16[384,1664]{1,0:T(8,128)(2,1)S(1)}, u32[]{:S(2)}, u32[]{:S(2)}) collective-permute-start(bf16[384,1664]{1,0:T(8,128)(2,1)} %get-tuple-element.165), channel_id=1, source_target_pairs={{0,4},{4,0},{8,12},{12,8},{16,20},{20,16},{24,28},{28,24},{1,5},{5... | collective-permute-start | bytes 3833864 | tf_op jit(solution)/shard_map/ppermute | solution.py:435
  137.1 16.4 %collective-permute-start.7 = (bf16[4,96,768]{2,1,0:T(8,128)(2,1)}, bf16[4,96,768]{2,1,0:T(8,128)(2,1)S(1)}, u32[]{:S(2)}, u32[]{:S(2)}) collective-permute-start(bf16[4,96,768]{2,1,0:T(8,128)(2,1)} %get-tuple-element.162), channel_id=1, source_target_pairs={{0,16},{4,20},{8,24},{12,28},{16,0},{20,4},{24,8},{28,12},{1,17},{... | collective-permute-start | bytes 1769480 | tf_op jit(solution)/shard_map/ppermute | solution.py:435
  137.6 16.5 %collective-permute-start.8 = (bf16[4,96,768]{2,1,0:T(8,128)(2,1)}, bf16[4,96,768]{2,1,0:T(8,128)(2,1)}, u32[]{:S(2)}, u32[]{:S(2)}) collective-permute-start(bf16[4,96,768]{2,1,0:T(8,128)(2,1)} %get-tuple-element.163), channel_id=1, source_target_pairs={{0,8},{4,12},{8,0},{12,4},{16,24},{20,28},{24,16},{28,20},{1,9},{5... | collective-permute-start | bytes 1769480 | tf_op jit(solution)/shard_map/ppermute | solution.py:435
  138.1 57.2 %all-to-all-start.2 = ((bf16[12,51,768]{2,1,0:T(8,128)(2,1)}), bf16[12,51,768]{2,1,0:T(8,128)(2,1)}, u32[]{:S(2)}, u32[]{:S(2)}) async-start(bf16[12,51,768]{2,1,0:T(8,128)(2,1)} %get-tuple-element.194), calls=%async_computation.2 | async-start | bytes 2064384 | tf_op jit(solution)/shard_map/all_to_all | solution.py:448
  142.6 1.1 copy-start.1
  142.6 1.4 copy-start.2
  146.9 19.6 %collective-permute-start.11 = (bf16[2,2,48,1664]{3,2,1,0:T(8,128)(2,1)}, bf16[2,2,48,1664]{3,2,1,0:T(8,128)(2,1)S(1)}, u32[]{:S(2)}, u32[]{:S(2)}) collective-permute-start(bf16[2,2,48,1664]{3,2,1,0:T(8,128)(2,1)} %get-tuple-element.172), channel_id=1, source_target_pairs={{0,8},{4,12},{8,0},{12,4},{16,24},{20,28},{24,16},{28,20},{1,9},{5... | collective-permute-start | bytes 1916936 | tf_op jit(solution)/shard_map/ppermute | solution.py:435
  148.5 17.8 %collective-permute-start.12 = (bf16[2,2,48,1664]{3,2,1,0:T(8,128)(2,1)}, bf16[2,2,48,1664]{3,2,1,0:T(8,128)(2,1)S(1)}, u32[]{:S(2)}, u32[]{:S(2)}) collective-permute-start(bf16[2,2,48,1664]{3,2,1,0:T(8,128)(2,1)} %get-tuple-element.178), channel_id=1, source_target_pairs={{0,16},{4,20},{8,24},{12,28},{16,0},{20,4},{24,8},{28,12},{1,17},{... | collective-permute-start | bytes 1916936 | tf_op jit(solution)/shard_map/ppermute | solution.py:435
  153.5 0.8 copy-start.10
  158.9 18.9 %collective-permute-start.13 = (bf16[4,96,768]{2,1,0:T(8,128)(2,1)}, bf16[4,96,768]{2,1,0:T(8,128)(2,1)S(1)}, u32[]{:S(2)}, u32[]{:S(2)}) collective-permute-start(bf16[4,96,768]{2,1,0:T(8,128)(2,1)} %get-tuple-element.187), channel_id=1, source_target_pairs={{0,1},{1,0},{2,3},{3,2},{4,5},{5,4},{6,7},{7,6},{8,9},{9,8},{10,11... | collective-permute-start | bytes 1769480 | tf_op jit(solution)/shard_map/ppermute | solution.py:655
  166.3 0.8 copy-start.6
  166.5 0.8 copy-start.5
  167.3 11.6 %copy-start.11 = (bf16[4,96,768]{2,1,0:T(8,128)(2,1)S(1)}, bf16[4,96,768]{2,1,0:T(8,128)(2,1)}, u32[]{:S(2)}) copy-start(bf16[4,96,768]{2,1,0:T(8,128)(2,1)} %get-tuple-element.183) | copy-start | bytes 1769476
  177.8 7.7 %collective-permute-start.14 = (bf16[2,48,1664]{2,1,0:T(8,128)(2,1)}, bf16[2,48,1664]{2,1,0:T(8,128)(2,1)S(1)}, u32[]{:S(2)}, u32[]{:S(2)}) collective-permute-start(bf16[2,48,1664]{2,1,0:T(8,128)(2,1)} %get-tuple-element.189), channel_id=1, source_target_pairs={{0,16},{4,20},{8,24},{12,28},{16,0},{20,4},{24,8},{28,12},{1,17},{... | collective-permute-start | bytes 958472 | tf_op jit(solution)/shard_map/ppermute | solution.py:435
  178.3 7.2 %collective-permute-start.15 = (bf16[2,48,1664]{2,1,0:T(8,128)(2,1)}, bf16[2,48,1664]{2,1,0:T(8,128)(2,1)S(1)}, u32[]{:S(2)}, u32[]{:S(2)}) collective-permute-start(bf16[2,48,1664]{2,1,0:T(8,128)(2,1)} %get-tuple-element.190), channel_id=1, source_target_pairs={{0,8},{4,12},{8,0},{12,4},{16,24},{20,28},{24,16},{28,20},{1,9},{5... | collective-permute-start | bytes 958472 | tf_op jit(solution)/shard_map/ppermute | solution.py:435
  179.1 16.1 %collective-permute-start.17 = (bf16[2,96,768]{2,1,0:T(8,128)(2,1)S(1)}, bf16[2,96,768]{2,1,0:T(8,128)(2,1)S(1)}, u32[]{:S(2)}, u32[]{:S(2)}) collective-permute-start(bf16[2,96,768]{2,1,0:T(8,128)(2,1)S(1)} %get-tuple-element.197), channel_id=1, source_target_pairs={{0,2},{1,3},{2,0},{3,1},{4,6},{5,7},{6,4},{7,5},{8,10},{9,11},{10,... | collective-permute-start | bytes 884744 | tf_op jit(solution)/shard_map/ppermute | solution.py:658
  185.4 0.7 copy-start.12
  185.5 0.8 copy-start.13
  189.8 15.9 %copy-start.14 = (bf16[2,48,1664]{2,1,0:T(8,128)(2,1)S(1)}, bf16[2,48,1664]{2,1,0:T(8,128)(2,1)}, u32[]{:S(2)}) copy-start(bf16[2,48,1664]{2,1,0:T(8,128)(2,1)} %get-tuple-element.203) | copy-start | bytes 958468
  189.8 15.9 %collective-permute-start.16 = (bf16[2,48,1664]{2,1,0:T(8,128)(2,1)}, bf16[2,48,1664]{2,1,0:T(8,128)(2,1)S(1)}, u32[]{:S(2)}, u32[]{:S(2)}) collective-permute-start(bf16[2,48,1664]{2,1,0:T(8,128)(2,1)} %get-tuple-element.193), channel_id=1, source_target_pairs={{0,1},{1,0},{2,3},{3,2},{4,5},{5,4},{6,7},{7,6},{8,9},{9,8},{10,11... | collective-permute-start | bytes 958472 | tf_op jit(solution)/shard_map/ppermute | solution.py:655
  189.9 16.0 %collective-permute-start.19 = (bf16[2,96,768]{2,1,0:T(8,128)(2,1)S(1)}, bf16[2,96,768]{2,1,0:T(8,128)(2,1)S(1)}, u32[]{:S(2)}, u32[]{:S(2)}) collective-permute-start(bf16[2,96,768]{2,1,0:T(8,128)(2,1)S(1)} %get-tuple-element.206), channel_id=1, source_target_pairs={{0,2},{1,3},{2,0},{3,1},{4,6},{5,7},{6,4},{7,5},{8,10},{9,11},{10,... | collective-permute-start | bytes 884744 | tf_op jit(solution)/shard_map/ppermute | solution.py:658
  195.3 10.7 %copy-start.16 = (bf16[2,96,768]{2,1,0:T(8,128)(2,1)}, bf16[2,96,768]{2,1,0:T(8,128)(2,1)S(1)}, u32[]{:S(2)}) copy-start(bf16[2,96,768]{2,1,0:T(8,128)(2,1)S(1)} %add.53.mine_a) | copy-start | bytes 884740
  205.8 15.4 %collective-permute-start.21 = (bf16[2,48,1664]{2,1,0:T(8,128)(2,1)S(1)}, bf16[2,48,1664]{2,1,0:T(8,128)(2,1)S(1)}, u32[]{:S(2)}, u32[]{:S(2)}) collective-permute-start(bf16[2,48,1664]{2,1,0:T(8,128)(2,1)S(1)} %add.54), channel_id=1, source_target_pairs={{0,2},{1,3},{2,0},{3,1},{4,6},{5,7},{6,4},{7,5},{8,10},{9,11},{10,... | collective-permute-start | bytes 958472 | tf_op jit(solution)/shard_map/ppermute | solution.py:658
  205.9 16.8 %collective-permute-start.18 = (bf16[2,96,768]{2,1,0:T(8,128)(2,1)S(1)}, bf16[2,96,768]{2,1,0:T(8,128)(2,1)S(1)}, u32[]{:S(2)}, u32[]{:S(2)}) collective-permute-start(bf16[2,96,768]{2,1,0:T(8,128)(2,1)S(1)} %add.53.mine_a), channel_id=1, source_target_pairs={{0,1},{1,0},{2,3},{3,2},{4,5},{5,4},{6,7},{7,6},{8,9},{9,8},{10,11... | collective-permute-start | bytes 884744 | tf_op jit(solution)/shard_map/ppermute | solution.py:655
  206.0 22.9 %copy-start.17 = (bf16[2,96,768]{2,1,0:T(8,128)(2,1)}, bf16[2,96,768]{2,1,0:T(8,128)(2,1)S(1)}, u32[]{:S(2)}) copy-start(bf16[2,96,768]{2,1,0:T(8,128)(2,1)S(1)} %add.55.mine_b) | copy-start | bytes 884740
  206.0 22.9 %collective-permute-start.20 = (bf16[2,96,768]{2,1,0:T(8,128)(2,1)S(1)}, bf16[2,96,768]{2,1,0:T(8,128)(2,1)S(1)}, u32[]{:S(2)}, u32[]{:S(2)}) collective-permute-start(bf16[2,96,768]{2,1,0:T(8,128)(2,1)S(1)} %add.55.mine_b), channel_id=1, source_target_pairs={{0,1},{1,0},{2,3},{3,2},{4,5},{5,4},{6,7},{7,6},{8,9},{9,8},{10,11... | collective-permute-start | bytes 884744 | tf_op jit(solution)/shard_map/ppermute | solution.py:655
  221.2 12.5 %copy-start.15 = (bf16[2,48,1664]{2,1,0:T(8,128)(2,1)}, bf16[2,48,1664]{2,1,0:T(8,128)(2,1)S(1)}, u32[]{:S(2)}) copy-start(bf16[2,48,1664]{2,1,0:T(8,128)(2,1)S(1)} %add.56) | copy-start | bytes 958468
  221.2 12.5 %collective-permute-start.22 = (bf16[2,48,1664]{2,1,0:T(8,128)(2,1)S(1)}, bf16[2,48,1664]{2,1,0:T(8,128)(2,1)S(1)}, u32[]{:S(2)}, u32[]{:S(2)}) collective-permute-start(bf16[2,48,1664]{2,1,0:T(8,128)(2,1)S(1)} %add.56), channel_id=1, source_target_pairs={{0,1},{1,0},{2,3},{3,2},{4,5},{5,4},{6,7},{7,6},{8,9},{9,8},{10,11... | collective-permute-start | bytes 958472 | tf_op jit(solution)/shard_map/ppermute | solution.py:655
  222.6 6.3 %copy-start.28 = (bf16[2,96,768]{2,1,0:T(8,128)(2,1)}, bf16[2,96,768]{2,1,0:T(8,128)(2,1)S(1)}, u32[]{:S(2)}) copy-start(bf16[2,96,768]{2,1,0:T(8,128)(2,1)S(1)} %collective-permute-done.18.other_a) | copy-start | bytes 884740
  228.9 0.7 copy-start.29
  233.7 0.7 copy-start.27

commit v5 on v4

--- a/solution.py
+++ b/solution.py
@@ -338,14 +338,11 @@
         values.append(total)
     if pick:
         values = [jnp.where(even, *values), jnp.where(even, *values[::-1])]
-    pieces = len(outs) // len(values)
-    for k, ref in enumerate(outs):
-        v, n = values[k // pieces], ref.shape[0]
-        lo = k % pieces * n if pieces > 1 else 0
-        ref[...] = (v if pieces == 1 else v[lo : lo + n]).astype(BF).reshape(ref.shape)
-
-
-def sums(jobs, at=None, mib=60, pieces=1):
+    for ref, v in zip(outs, values):
+        ref[...] = v.astype(BF)
+
+
+def sums(jobs, at=None, mib=63):
     arrays, bufs, out_shapes, leads = [], [], [], []
     for job in jobs:
         leads.append([])
@@ -355,7 +352,7 @@
             leads[-1].append(index)
             arrays.append(v)
             bufs.append(pltpu.VMEM(kept, BF))
-        out_shapes += [struct(kept[0] // pieces, *kept[1:])] * pieces
+        out_shapes.append(struct(*kept))
     specs = [ANY] * len(arrays)
     if at is not None:
         specs.insert(0, pl.BlockSpec(memory_space=pltpu.SMEM))
@@ -371,14 +368,13 @@
     )(*arrays)
 
 
-def finish_feed_kernel(at, mine_a, other_a, mine_b, other_b, fc1, fc2):
+def finish_feed_kernel(at, mine, other, *refs):
+    fc1, fc2 = refs[-2:]
     even = (at[0] & 1) == 0
     n = fc1.shape[0]
     width = fc2.shape[1]
-    half = mine_a.shape[0]
-    for m in range(2 * half):
-        mine, other = (mine_a, other_a) if m < half else (mine_b, other_b)
-        p, q = mine[m % half].astype(F32), other[m % half].astype(F32)
+    for m in range(mine.shape[0]):
+        p, q = mine[m].astype(F32), other[m].astype(F32)
         fc1[:, m * width : (m + 1) * width] = jnp.where(even, p, q)
         fc2[m * n : (m + 1) * n, :] = jnp.where(even, q, p)
 
@@ -406,7 +402,7 @@
     return pl.BlockSpec(shape, lambda *_: (0,) * len(shape), pipeline_mode=mode)
 
 
-def params(mib=60):
+def params(mib=63):
     return pltpu.CompilerParams(
         dimension_semantics=("arbitrary",), vmem_limit_bytes=mib * 2**20
     )
@@ -528,7 +524,7 @@
             scratch_shapes=[pltpu.VMEM((padded, width), F32)],
         ),
         out_shape=[struct(n, *shape, dtype=dtype) for shape, dtype in shapes],
-        compiler_params=params(60),
+        compiler_params=params(63),
         cost_estimate=cost(15),
         name="attention_forward",
     )(
@@ -581,7 +577,7 @@
             *[struct(hidden // 2, width)] * 2, *[struct(steps, steps, width // OWNERS, chunk)] * 2,
             struct(1, hidden, dtype=F32), struct(4, width, dtype=F32),
         ],
-        compiler_params=params(60),
+        compiler_params=params(63),
         cost_estimate=cost(30),
         name="feed_forward",
     )(
@@ -595,7 +591,7 @@
         ra, rb = swap(w1s, 1), swap(w2s, 1)
         ra, rb = together(ra, rb)
         wa, wb, ra, rb = (v.reshape(2, 2, steps, n1, chunk) for v in (w1k, w2k, ra, rb))
-        as_, bs = sums([[(wa, x_half), (ra, x_half)], [(wb, y_half), (rb, y_half)]], mib=60)
+        as_, bs = sums([[(wa, x_half), (ra, x_half)], [(wb, y_half), (rb, y_half)]], mib=63)
         dy, as_, bs = together(dy, as_, bs)
         qa, qb = swap(as_, 2), swap(bs, 4)
     out_rows = exchange(out_rows)
@@ -633,7 +629,7 @@
             struct(images, part + ns, width), struct(2, width, dtype=F32),
             struct(1, 3 * width, dtype=F32), *[struct(half, wide)] * 4,
         ],
-        compiler_params=params(60),
+        compiler_params=params(63),
         cost_estimate=cost(22),
         name="attention_backward",
     )(at, dy, prob, qkv, proj_weight, qkv_weight, xs, dh, vectors, a1t, ot, small2, db1)
@@ -668,8 +664,7 @@
     wc, wd, rc, rd = (v.reshape(2, 2, 2, n1 // 2, -1) for v in (ck, dk_, rc, rd))
     cs, ds_ = sums([[(wc, x_half), (rc, x_half)], [(wd, y_half), (rd, y_half)]])
     qc, qd = swap(cs, 2), swap(ds_, 4)
-    out_rows, out_specials = settle(after(out_rows, cs), ns)
-    ta, tb, cs, out_rows = together(ta, tb, cs, out_rows)
+    ta, tb, cs = together(ta, tb, cs)
     e, es = sums(
         [
             [(wa, (0, 0)), (ra, (0, 0)), (qa, (0,)), (ta, ())],
@@ -678,9 +673,11 @@
         at,
     )
     re = near(es)
-    qc, qd, e = together(qc, qd, e)
+    out_rows, out_specials = settle(after(out_rows, e), ns)
+    qc, qd, e, out_rows = together(qc, qd, e, out_rows)
     cs, ds_ = sums(
-        [[(wc, (1, 0)), (rc, (1, 0)), (qc, (1,))], [(wd, (0, 1)), (rd, (0, 1)), (qd, (1,))]]
+        [[(wc, (1, 0)), (rc, (1, 0)), (qc, (1,))], [(wd, (0, 1)), (rd, (0, 1)), (qd, (1,))]],
+        mib=60,
     )
     cs, ds_, re = together(cs, ds_, re)
     tc, td = swap(cs, 4), swap(ds_, 2)
@@ -694,6 +691,7 @@
             [(wd, (0, 0)), (rd, (0, 0)), (qd, (0,)), (td, ())],
         ],
         at,
+        mib=60,
     )
     rf = near(fs)
     f1, re, e = together(f1, re, e)
@@ -709,17 +707,29 @@
     rf, g = together(rf, g)
     f1 = f1 + rf
     rf = near(f1)
-    re, rg, f1 = together(re, rg, f1)
+    re, f1 = together(re, f1)
     smem = pl.BlockSpec(memory_space=pltpu.SMEM)
     vmem = pl.BlockSpec(memory_space=pltpu.VMEM)
-    d_fc1, d_fc2 = pl.pallas_call(
-        finish_feed_kernel,
-        in_specs=[smem, *[vmem] * 4],
-        out_shape=[struct(n1, hidden, dtype=F32), struct(hidden // OWNERS, width, dtype=F32)],
-        compiler_params=pltpu.CompilerParams(vmem_limit_bytes=60 * 2**20),
-        cost_estimate=cost(2),
-        name="finish_feed",
-    )(at, e, re, g, rg)
+
+    def finish_feed(k, mine, other, *before):
+        return pl.pallas_call(
+            finish_feed_kernel,
+            grid=(1,),
+            in_specs=[smem, whole(mine.shape), whole(other.shape), *[ANY] * len(before)],
+            out_specs=[
+                pl.BlockSpec((n1, hidden // 2), lambda i: (0, k)),
+                pl.BlockSpec((hidden // OWNERS // 2, width), lambda i: (k, 0)),
+            ],
+            out_shape=[struct(n1, hidden, dtype=F32), struct(hidden // OWNERS, width, dtype=F32)],
+            input_output_aliases={3 + j: j for j in range(len(before))},
+            compiler_params=params(60),
+            cost_estimate=cost(2),
+            name="finish_feed",
+        )(at, mine, other, *before)
+
+    d_fc1, d_fc2 = finish_feed(0, e, re)
+    rg, d_fc1, d_fc2 = together(rg, d_fc1, d_fc2)
+    d_fc1, d_fc2 = finish_feed(1, g, rg, d_fc1, d_fc2)
     rf, d_fc1 = together(rf, d_fc1)
     done = pl.pallas_call(
         finish_kernel,

time: 238 us -> 235 us (0.987)
  starting transfers between devices: 48.6 us -> 38.7 us
  waiting for transfers between devices: 65.2 us -> 75.1 us
  local copies, waits for them, and re-layouts: 11.8 us -> 7.86 us
    ppermute x5, starting transfers between devices: 9.98 us -> 2.38 us  [near(): return lax.ppermute(v, 'seq', [(s, s ^ 1) for s in range(groups)])]
    ppermute x3, waiting for transfers between devices: 7.07 us -> 13.2 us  [far(): return lax.ppermute(v, 'seq', [(s, s ^ 2) for s in range(groups)])]
    ppermute x3, starting transfers between devices: 7.05 us -> 2.95 us  [far(): return lax.ppermute(v, 'seq', [(s, s ^ 2) for s in range(groups)])]
    unnamed x71 -> x55, local copies, waits for them, and re-layouts: 9.05 us -> 5.09 us
    ppermute x12, waiting for transfers between devices: 15.3 us -> 18.9 us  [swap(): lax.ppermute(v, 'dp', [(s, s ^ bit) for s in range(lax.axis_size('dp'))])]
  transfers between devices with their start and end apart: 26 -> 26, of which waited for: 16 -> 17; matrix products, arithmetic and copies ran while one was open for 2% -> 2% of each run, Pallas kernels for 30% -> 31%
where the time goes in v5:
time: 235 us; the launch traced here: 234 us
  Pallas kernels  109 us (46%)
  waiting for transfers between devices  75.1 us (32%)
  starting transfers between devices  38.7 us (16%)
  local copies, waits for them, and re-layouts  7.86 us (3%)
    pallas_call x1, Pallas kernels, shards(): pl.pallas_call(partial(feed_kernel, images=n), grid_spec=pltpu.PrefetchSc...  31.7 us
    pallas_call x1, Pallas kernels, shards(): pl.pallas_call(partial(heads_kernel, images=n, heads=heads, part=part, ns...  27.9 us
    ppermute x5, waiting for transfers between devices, near(): return lax.ppermute(v, 'seq', [(s, s ^ 1) for s in range(groups)])  23.8 us
    pallas_call x6, Pallas kernels, sums(): pl.pallas_call(partial(sum_kernel, jobs=leads, pick=at is not None), in_s...  20.9 us
    ppermute x12, waiting for transfers between devices, swap(): lax.ppermute(v, 'dp', [(s, s ^ bit) for s in range(lax.axis_size('dp'))])  18.9 us
    all_to_all x3, starting transfers between devices, exchange(): return lax.all_to_all(x, 'seq', split_axis=0, concat_axis=0, tiled=True)  16.6 us
    pallas_call x1, Pallas kernels, shards(): pl.pallas_call(partial(forward_kernel, rows=rows, heads=heads), grid_spec...  15.2 us
    ppermute x3, waiting for transfers between devices, far(): return lax.ppermute(v, 'seq', [(s, s ^ 2) for s in range(groups)])  13.2 us
  transfers between devices with their start and end apart: 26, of which 17 were waited for; matrix products, arithmetic and copies ran while one was open for 2% of the time, Pallas kernels for 31%

profile of v5, /device:TPU:0, one launch (start us, length us, event | category | flops | bytes accessed | tf_op | source)
XLA Modules:
  0.0 234.5 jit_solution(15127328421803973693)
XLA Ops:
  0.7 1.3 constant_dynamic-slice_fusion
  1.9 0.2 copy_bitcast_fusion
  2.4 4.1 %collective-permute-start.1 = (bf16[147,768]{1,0:T(8,128)(2,1)S(1)}, bf16[147,768]{1,0:T(8,128)(2,1)S(1)}, u32[]{:S(2)}, u32[]{:S(2)}) collective-permute-start(bf16[147,768]{1,0:T(8,128)(2,1)S(1)} %maximum_bitcast_fusion.1), channel_id=1, source_target_pairs={{0,2},{1,3},{2,0},{3,1},{4,6},{5,7},{6,4},{7,5},{8,10},{9,11},{10,... | collective-permute-start | bytes 677384 | tf_op jit(solution)/shard_map/ppermute | solution.py:492
  6.7 1.4 collective-permute-start.2
  8.1 0.1 copy.55
  8.4 0.7 collective-permute-start
  9.3 0.7 copy.49.keep
  10.1 1.0 pad_maximum_fusion
  11.1 7.8 %collective-permute-done.1.x2 = bf16[147,768]{1,0:T(8,128)(2,1)S(1)} collective-permute-done((bf16[147,768]{1,0:T(8,128)(2,1)S(1)}, bf16[147,768]{1,0:T(8,128)(2,1)S(1)}, u32[]{:S(2)}, u32[]{:S(2)}) %collective-permute-start.1) | collective-permute-done | bytes 225824 | tf_op jit(solution)/shard_map/ppermute | solution.py:492
  18.9 4.5 %collective-permute-done.x1 = bf16[147,768]{1,0:T(8,128)(2,1)S(1)} collective-permute-done((bf16[147,768]{1,0:T(8,128)(2,1)S(1)}, bf16[147,768]{1,0:T(8,128)(2,1)S(1)}, u32[]{:S(2)}, u32[]{:S(2)}) %collective-permute-start) | collective-permute-done | bytes 225824 | tf_op jit(solution)/shard_map/ppermute | solution.py:492
  23.4 7.7 %all-to-all-start = ((bf16[4,147,768]{2,1,0:T(8,128)(2,1)}), bf16[4,147,768]{2,1,0:T(8,128)(2,1)S(1)}, u32[]{:S(2)}, u32[]{:S(2)}) async-start(bf16[4,147,768]{2,1,0:T(8,128)(2,1)} %pad_maximum_fusion), calls=%async_computation | async-start | bytes 1867776 | tf_op jit(solution)/shard_map/all_to_all | solution.py:444
  31.2 0.6 reshape.132.g1.b1.bq.bp.g2.b2.gain
  31.9 0.6 pad_add_fusion.at.refs_0_
  32.5 15.2 %attention_forward.1 = (bf16[3,208,768]{2,1,0:T(8,128)(2,1)}, bf16[3,768,208]{2,1,0:T(8,128)(2,1)}, bf16[3,208,2304]{2,1,0:T(8,128)(2,1)}, bf16[3,6,416,208]{3,2...) custom-call(s32[2]{0:T(128)} %pad_add_fusion.at.refs_0_, ...), custom_call_target="tpu_custom_call" | custom-call | flops 4499999744 | bytes 1 | tf_op jit(solution)/shard_map/attention_forward/pallas_call | solution.py:511
  47.7 6.9 %all-to-all-done.g0.g1.g2.g3 = bf16[4,147,768]{2,1,0:T(8,128)(2,1)S(1)} async-done(((bf16[4,147,768]{2,1,0:T(8,128)(2,1)}), bf16[4,147,768]{2,1,0:T(8,128)(2,1)S(1)}, u32[]{:S(2)}, u32[]{:S(2)}) %all-to-all-start) | async-done | bytes 903200 | tf_op jit(solution)/shard_map/all_to_all | solution.py:444
  54.6 0.9 copy-done.2
  55.5 31.7 %feed_forward.1 = (bf16[12,51,768]{2,1,0:T(8,128)(2,1)}, f32[3,208,768]{2,1,0:T(8,128)}, bf16[3,208,768]{2,1,0:T(8,128)(2,1)}, bf16[1536,768]{1,0:T(8,128)(2,1)}...) custom-call(s32[2]{0:T(128)} %pad_add_fusion.at.refs_0_, ...), custom_call_target="tpu_custom_call" | custom-call | flops 8999999488 | bytes 1 | tf_op jit(solution)/shard_map/feed_forward/pallas_call | solution.py:542
  87.3 0.5 collective-permute-start.4
  87.8 4.4 %all-to-all-start.1 = ((bf16[12,51,768]{2,1,0:T(8,128)(2,1)}), bf16[12,51,768]{2,1,0:T(8,128)(2,1)}, u32[]{:S(2)}, u32[]{:S(2)}) async-start(bf16[12,51,768]{2,1,0:T(8,128)(2,1)} %get-tuple-element.157), calls=%async_computation.1 | async-start | bytes 2064384 | tf_op jit(solution)/shard_map/all_to_all | solution.py:444
  92.3 3.3 %collective-permute-done.4 = bf16[1536,768]{1,0:T(8,128)(2,1)} collective-permute-done((bf16[1536,768]{1,0:T(8,128)(2,1)}, bf16[1536,768]{1,0:T(8,128)(2,1)}, u32[]{:S(2)}, u32[]{:S(2)}) %collective-permute-start.4) | collective-permute-done | bytes 2359328 | tf_op jit(solution)/shard_map/ppermute | solution.py:431
  95.6 4.0 %sums.6 = (bf16[2,4,96,768]{3,2,1,0:T(8,128)(2,1)}, bf16[2,4,96,768]{3,2,1,0:T(8,128)(2,1)}) custom-call(bf16[2,2,4,96,768]{4,3,2,1,0:T(8,128)(2,1)} %bitcast.48, bf16[2,2,4,96,768]{4,3,2,1,0:T(8,128)(2,1)} %bitcast.18.refs_1_.refs_2_, bf16[2,2,4,96,768]{4,3,2,1,0:T(8,128)(2,1)} %bitcast.45, bf16[2,2,4,96,768]{4,3,2,1,0:T(8,128)(2,1)} %bitcast.20.refs_3_.refs_4_.refs_6_), custom_call_target="tpu_custom_call" | custom-call | flops 600000000 | bytes 1 | tf_op jit(solution)/shard_map/sums/pallas_call | solution.py:360
  99.6 1.6 collective-permute-start.5
  101.2 1.5 collective-permute-start.6
  102.7 27.9 %attention_backward.1 = (bf16[12,51,768]{2,1,0:T(8,128)(2,1)}, f32[2,768]{1,0:T(2,128)}, f32[1,2304]{1,0:T(1,128)}, bf16[384,1664]{1,0:T(8,128)(2,1)}, bf16[384,...) custom-call(s32[2]{0:T(128)} %pad_add_fusion.at.refs_0_, ...), custom_call_target="tpu_custom_call" | custom-call | flops 6600000000 | bytes 1 | tf_op jit(solution)/shard_map/attention_backward/pallas_call | solution.py:605
  130.6 3.2 %sums.7 = (bf16[4,96,768]{2,1,0:T(8,128)(2,1)}, bf16[4,96,768]{2,1,0:T(8,128)(2,1)}) custom-call(bf16[2,2,4,96,768]{4,3,2,1,0:T(8,128)(2,1)} %bitcast.49, bf16[2,2,4,96,768]{4,3,2,1,0:T(8,128)(2,1)} %bitcast.18.refs_1_.refs_2_, bf16[2,4,96,768]{3,2,1,0:T(8,128)(2,1)} %collective-permute-done.5.refs_2_.refs_3_, bf16[2,2,4,96,768]{4,3,2,1,0:T(8,128)(2,1)} %bitcast.46, ...), custom_call_target="tpu_custom_call" | custom-call | flops 600000000 | bytes 1 | tf_op jit(solution)/shard_map/sums/pallas_call | solution.py:360
  133.9 0.5 collective-permute-start.8
  134.4 0.5 collective-permute-start.11
  135.0 0.5 collective-permute-start.12
  135.5 4.5 %all-to-all-start.2 = ((bf16[12,51,768]{2,1,0:T(8,128)(2,1)}), bf16[12,51,768]{2,1,0:T(8,128)(2,1)}, u32[]{:S(2)}, u32[]{:S(2)}) async-start(bf16[12,51,768]{2,1,0:T(8,128)(2,1)} %get-tuple-element.198), calls=%async_computation.2 | async-start | bytes 2064384 | tf_op jit(solution)/shard_map/all_to_all | solution.py:444
  140.0 2.9 %sums.8 = (bf16[2,2,48,1664]{3,2,1,0:T(8,128)(2,1)}, bf16[2,2,48,1664]{3,2,1,0:T(8,128)(2,1)}) custom-call(bf16[2,2,2,48,1664]{4,3,2,1,0:T(8,128)(2,1)} %bitcast.51, bf16[2,2,2,48,1664]{4,3,2,1,0:T(8,128)(2,1)} %bitcast.22.refs_1_.refs_2_, bf16[2,2,2,48,1664]{4,3,2,1,0:T(8,128)(2,1)} %bitcast.54, bf16[2,2,2,48,1664]{4,3,2,1,0:T(8,128)(2,1)} %bitcast.24.refs_3_.refs_4_.refs_6_), custom_call_target="tpu_custom_call" | custom-call | flops 600000000 | bytes 1 | tf_op jit(solution)/shard_map/sums/pallas_call | solution.py:360
  142.9 1.7 collective-permute-start.10
  144.5 1.4 collective-permute-start.9
  145.9 5.0 %collective-permute-done.11.refs_4_ = bf16[4,96,768]{2,1,0:T(8,128)(2,1)} collective-permute-done((bf16[4,96,768]{2,1,0:T(8,128)(2,1)}, bf16[4,96,768]{2,1,0:T(8,128)(2,1)}, u32[]{:S(2)}, u32[]{:S(2)}) %collective-permute-start.11) | collective-permute-done | bytes 589856 | tf_op jit(solution)/shard_map/ppermute | solution.py:431
  150.9 0.6 collective-permute-done.12.refs_8_
  151.5 4.6 %sums.9 = (bf16[4,96,768]{2,1,0:T(8,128)(2,1)}, bf16[4,96,768]{2,1,0:T(8,128)(2,1)}) custom-call(s32[2]{0:T(128)} %pad_add_fusion.at.refs_0_, bf16[2,2,4,96,768]{4,3,2,1,0:T(8,128)(2,1)} %bitcast.50, bf16[2,2,4,96,768]{4,3,2,1,0:T(8,128)(2,1)} %bitcast.18.refs_1_.refs_2_, bf16[2,4,96,768]{3,2,1,0:T(8,128)(2,1)} %collective-permute-done.5.refs_2_.refs_3_, ...), custom_call_target="tpu_custom_call" | custom-call | flops 600000000 | bytes 1 | tf_op jit(solution)/shard_map/sums/pallas_call | solution.py:360
  156.3 3.4 %settle.2 = (bf16[12,49,768]{2,1,0:T(8,128)(2,1)}, bf16[12,2,768]{2,1,0:T(2,128)(2,1)}) custom-call(bf16[12,51,768]{2,1,0:T(8,128)(2,1)} %all-to-all-done.1.both), custom_call_target="tpu_custom_call" | custom-call | flops 600000000 | bytes 1 | tf_op jit(solution)/shard_map/settle/pallas_call | solution.py:450
  159.6 4.0 %collective-permute-done.10.refs_5_.refs_7_ = bf16[2,2,48,1664]{3,2,1,0:T(8,128)(2,1)S(1)} collective-permute-done((bf16[2,2,48,1664]{3,2,1,0:T(8,128)(2,1)}, bf16[2,2,48,1664]{3,2,1,0:T(8,128)(2,1)S(1)}, u32[]{:S(2)}, u32[]{:S(2)}) %collective-permute-start.10) | collective-permute-done | bytes 639008 | tf_op jit(solution)/shard_map/ppermute | solution.py:431
  163.7 0.4 collective-permute-done.9.refs_2_.refs_3_
  164.0 0.5 copy-done
  164.5 2.5 %sums.10 = (bf16[2,48,1664]{2,1,0:T(8,128)(2,1)}, bf16[2,48,1664]{2,1,0:T(8,128)(2,1)}) custom-call(bf16[2,2,2,48,1664]{4,3,2,1,0:T(8,128)(2,1)} %bitcast.52, bf16[2,2,2,48,1664]{4,3,2,1,0:T(8,128)(2,1)} %bitcast.22.refs_1_.refs_2_, bf16[2,2,48,1664]{3,2,1,0:T(8,128)(2,1)} %collective-permute-done.9.refs_2_.refs_3_, bf16[2,2,2,48,1664]{4,3,2,1,0:T(8,128)(2,1)} %bitcast.55, ...), custom_call_target="tpu_custom_call" | custom-call | flops 600000000 | bytes 1 | tf_op jit(solution)/shard_map/sums/pallas_call | solution.py:360
  167.0 6.9 %collective-permute-done.13 = bf16[4,96,768]{2,1,0:T(8,128)(2,1)S(1)} collective-permute-done((bf16[4,96,768]{2,1,0:T(8,128)(2,1)}, bf16[4,96,768]{2,1,0:T(8,128)(2,1)S(1)}, u32[]{:S(2)}, u32[]{:S(2)}) %collective-permute-start.13) | collective-permute-done | bytes 589856 | tf_op jit(solution)/shard_map/ppermute | solution.py:651
  173.9 1.4 collective-permute-start.14
  175.4 0.8 collective-permute-start.15
  176.2 0.1 add.52
  176.4 0.6 collective-permute-start.17
  177.0 4.2 %collective-permute-done.14.refs_4_ = bf16[2,48,1664]{2,1,0:T(8,128)(2,1)S(1)} collective-permute-done((bf16[2,48,1664]{2,1,0:T(8,128)(2,1)}, bf16[2,48,1664]{2,1,0:T(8,128)(2,1)S(1)}, u32[]{:S(2)}, u32[]{:S(2)}) %collective-permute-start.14) | collective-permute-done | bytes 319520 | tf_op jit(solution)/shard_map/ppermute | solution.py:431
  181.1 1.4 collective-permute-done.15.refs_8_
  182.6 0.7 copy-done.6
  183.3 3.5 %sums.11 = (bf16[2,48,1664]{2,1,0:T(8,128)(2,1)}, bf16[2,48,1664]{2,1,0:T(8,128)(2,1)}) custom-call(s32[2]{0:T(128)} %pad_add_fusion.at.refs_0_, bf16[2,2,2,48,1664]{4,3,2,1,0:T(8,128)(2,1)} %bitcast.53, bf16[2,2,2,48,1664]{4,3,2,1,0:T(8,128)(2,1)} %bitcast.22.refs_1_.refs_2_, bf16[2,2,48,1664]{3,2,1,0:T(8,128)(2,1)} %collective-permute-done.9.refs_2_.refs_3_, ...), custom_call_target="tpu_custom_call" | custom-call | flops 600000000 | bytes 1 | tf_op jit(solution)/shard_map/sums/pallas_call | solution.py:360
  186.9 2.3 collective-permute-start.19
  189.2 0.4 collective-permute-done.17
  189.7 3.5 %settle.3 = (bf16[12,49,768]{2,1,0:T(8,128)(2,1)}, bf16[12,2,768]{2,1,0:T(2,128)(2,1)}) custom-call(bf16[12,51,768]{2,1,0:T(8,128)(2,1)} %all-to-all-done.2.both), custom_call_target="tpu_custom_call" | custom-call | flops 600000000 | bytes 1 | tf_op jit(solution)/shard_map/settle/pallas_call | solution.py:450
  193.2 8.9 %collective-permute-done.16 = bf16[2,48,1664]{2,1,0:T(8,128)(2,1)S(1)} collective-permute-done((bf16[2,48,1664]{2,1,0:T(8,128)(2,1)}, bf16[2,48,1664]{2,1,0:T(8,128)(2,1)S(1)}, u32[]{:S(2)}, u32[]{:S(2)}) %collective-permute-start.16) | collective-permute-done | bytes 319520 | tf_op jit(solution)/shard_map/ppermute | solution.py:651
  202.3 2.1 collective-permute-start.18
  204.6 12.8 %collective-permute-done.20 = bf16[2,48,1664]{2,1,0:T(8,128)(2,1)S(1)} collective-permute-done((bf16[2,48,1664]{2,1,0:T(8,128)(2,1)S(1)}, bf16[2,48,1664]{2,1,0:T(8,128)(2,1)S(1)}, u32[]{:S(2)}, u32[]{:S(2)}) %collective-permute-start.20) | collective-permute-done | bytes 319520 | tf_op jit(solution)/shard_map/ppermute | solution.py:654
  217.5 1.6 collective-permute-done.18.other
  219.1 0.7 copy-done.21
  219.8 2.2 finish_feed.2
  222.0 3.4 %collective-permute-done.22.other = bf16[2,96,768]{2,1,0:T(8,128)(2,1)S(1)} collective-permute-done((bf16[2,96,768]{2,1,0:T(8,128)(2,1)S(1)}, bf16[2,96,768]{2,1,0:T(8,128)(2,1)S(1)}, u32[]{:S(2)}, u32[]{:S(2)}) %collective-permute-start.22) | collective-permute-done | bytes 294944 | tf_op jit(solution)/shard_map/ppermute | solution.py:651
  225.4 0.7 copy-done.9
  226.1 2.2 finish_feed.3
  228.3 3.0 %collective-permute-done.21 = bf16[2,48,1664]{2,1,0:T(8,128)(2,1)S(1)} collective-permute-done((bf16[2,48,1664]{2,1,0:T(8,128)(2,1)S(1)}, bf16[2,48,1664]{2,1,0:T(8,128)(2,1)S(1)}, u32[]{:S(2)}, u32[]{:S(2)}) %collective-permute-start.21) | collective-permute-done | bytes 319520 | tf_op jit(solution)/shard_map/ppermute | solution.py:651
  231.3 0.7 copy-done.20
  232.1 2.2 finish.1
  (91 shorter events, 1.6 us)
Async XLA Ops:
  2.4 16.5 %collective-permute-start.1 = (bf16[147,768]{1,0:T(8,128)(2,1)S(1)}, bf16[147,768]{1,0:T(8,128)(2,1)S(1)}, u32[]{:S(2)}, u32[]{:S(2)}) collective-permute-start(bf16[147,768]{1,0:T(8,128)(2,1)S(1)} %maximum_bitcast_fusion.1), channel_id=1, source_target_pairs={{0,2},{1,3},{2,0},{3,1},{4,6},{5,7},{6,4},{7,5},{8,10},{9,11},{10,... | collective-permute-start | bytes 677384 | tf_op jit(solution)/shard_map/ppermute | solution.py:492
  6.6 2.5 %copy-start.3 = (bf16[12,49,768]{2,1,0:T(8,128)(2,1)S(1)}, bf16[12,49,768]{2,1,0:T(8,128)(2,1)}, u32[]{:S(2)}) copy-start(bf16[12,49,768]{2,1,0:T(8,128)(2,1)} %param.32) | copy-start | bytes 2709508
  6.7 12.3 %collective-permute-start.2 = (bf16[147,768]{1,0:T(8,128)(2,1)S(1)}, bf16[147,768]{1,0:T(8,128)(2,1)S(1)}, u32[]{:S(2)}, u32[]{:S(2)}) collective-permute-start(bf16[147,768]{1,0:T(8,128)(2,1)S(1)} %maximum_bitcast_fusion.2), channel_id=1, source_target_pairs={{0,3},{1,0},{2,1},{3,2},{4,7},{5,4},{6,5},{7,6},{8,11},{9,8},{10,9... | collective-permute-start | bytes 677384 | tf_op jit(solution)/shard_map/ppermute | solution.py:492
  8.3 0.9 copy-start.19
  8.4 1.6 copy-start.11
  8.4 1.6 copy-start.12
  8.4 1.6 copy-start.13
  8.4 1.7 copy-start.14
  8.4 15.0 %collective-permute-start = (bf16[147,768]{1,0:T(8,128)(2,1)S(1)}, bf16[147,768]{1,0:T(8,128)(2,1)S(1)}, u32[]{:S(2)}, u32[]{:S(2)}) collective-permute-start(bf16[147,768]{1,0:T(8,128)(2,1)S(1)} %maximum_bitcast_fusion), channel_id=1, source_target_pairs={{0,1},{1,2},{2,3},{3,0},{4,5},{5,6},{6,7},{7,4},{8,9},{9,10},{10,1... | collective-permute-start | bytes 677384 | tf_op jit(solution)/shard_map/ppermute | solution.py:492
  11.1 20.0 %copy-start.15 = (bf16[768]{0:T(1024)(128)(2,1)S(1)}, bf16[768]{0:T(1024)(128)(2,1)}, u32[]{:S(2)}) copy-start(bf16[768]{0:T(1024)(128)(2,1)} %param.25) | copy-start | bytes 4612
  11.1 20.0 %copy-start.16 = (bf16[768]{0:T(1024)(128)(2,1)S(1)}, bf16[768]{0:T(1024)(128)(2,1)}, u32[]{:S(2)}) copy-start(bf16[768]{0:T(1024)(128)(2,1)} %param.26) | copy-start | bytes 4612
  11.1 20.1 %copy-start.17 = (bf16[768]{0:T(1024)(128)(2,1)S(1)}, bf16[768]{0:T(1024)(128)(2,1)}, u32[]{:S(2)}) copy-start(bf16[768]{0:T(1024)(128)(2,1)} %param.27) | copy-start | bytes 4612
  11.1 20.1 %copy-start.18 = (bf16[768]{0:T(1024)(128)(2,1)S(1)}, bf16[768]{0:T(1024)(128)(2,1)}, u32[]{:S(2)}) copy-start(bf16[768]{0:T(1024)(128)(2,1)} %param.31) | copy-start | bytes 4612
  18.9 12.9 %copy-start.22 = (bf16[147,768]{1,0:T(8,128)(2,1)}, bf16[147,768]{1,0:T(8,128)(2,1)S(1)}, u32[]{:S(2)}) copy-start(bf16[147,768]{1,0:T(8,128)(2,1)S(1)} %collective-permute-done.1.x2) | copy-start | bytes 677380
  18.9 12.9 %copy-start.23 = (bf16[147,768]{1,0:T(8,128)(2,1)}, bf16[147,768]{1,0:T(8,128)(2,1)S(1)}, u32[]{:S(2)}) copy-start(bf16[147,768]{1,0:T(8,128)(2,1)S(1)} %collective-permute-done.2.x3) | copy-start | bytes 677380
  23.4 8.5 %copy-start.24 = (bf16[147,768]{1,0:T(8,128)(2,1)}, bf16[147,768]{1,0:T(8,128)(2,1)S(1)}, u32[]{:S(2)}) copy-start(bf16[147,768]{1,0:T(8,128)(2,1)S(1)} %collective-permute-done.x1) | copy-start | bytes 677380
  23.4 31.2 %all-to-all-start = ((bf16[4,147,768]{2,1,0:T(8,128)(2,1)}), bf16[4,147,768]{2,1,0:T(8,128)(2,1)S(1)}, u32[]{:S(2)}, u32[]{:S(2)}) async-start(bf16[4,147,768]{2,1,0:T(8,128)(2,1)} %pad_maximum_fusion), calls=%async_computation | async-start | bytes 1867776 | tf_op jit(solution)/shard_map/all_to_all | solution.py:444
  54.6 0.9 copy-start.2
  87.3 5.0 %collective-permute-start.3 = (bf16[4,4,96,768]{3,2,1,0:T(8,128)(2,1)}, bf16[4,4,96,768]{3,2,1,0:T(8,128)(2,1)}, u32[]{:S(2)}, u32[]{:S(2)}) collective-permute-start(bf16[4,4,96,768]{3,2,1,0:T(8,128)(2,1)} %get-tuple-element.136), channel_id=1, source_target_pairs={{0,4},{4,0},{8,12},{12,8},{16,20},{20,16},{24,28},{28,24},{1,5},{5... | collective-permute-start | bytes 7077896 | tf_op jit(solution)/shard_map/ppermute | solution.py:431
  87.3 8.2 %collective-permute-start.4 = (bf16[1536,768]{1,0:T(8,128)(2,1)}, bf16[1536,768]{1,0:T(8,128)(2,1)}, u32[]{:S(2)}, u32[]{:S(2)}) collective-permute-start(bf16[1536,768]{1,0:T(8,128)(2,1)} %get-tuple-element.137), channel_id=1, source_target_pairs={{0,4},{4,0},{8,12},{12,8},{16,20},{20,16},{24,28},{28,24},{1,5},{5... | collective-permute-start | bytes 7077896 | tf_op jit(solution)/shard_map/ppermute | solution.py:431
  87.8 42.7 %all-to-all-start.1 = ((bf16[12,51,768]{2,1,0:T(8,128)(2,1)}), bf16[12,51,768]{2,1,0:T(8,128)(2,1)}, u32[]{:S(2)}, u32[]{:S(2)}) async-start(bf16[12,51,768]{2,1,0:T(8,128)(2,1)} %get-tuple-element.157), calls=%async_computation.1 | async-start | bytes 2064384 | tf_op jit(solution)/shard_map/all_to_all | solution.py:444
  99.6 31.0 %collective-permute-start.5 = (bf16[2,4,96,768]{3,2,1,0:T(8,128)(2,1)}, bf16[2,4,96,768]{3,2,1,0:T(8,128)(2,1)}, u32[]{:S(2)}, u32[]{:S(2)}) collective-permute-start(bf16[2,4,96,768]{3,2,1,0:T(8,128)(2,1)} %get-tuple-element.144), channel_id=1, source_target_pairs={{0,8},{4,12},{8,0},{12,4},{16,24},{20,28},{24,16},{28,20},{1,9},{5... | collective-permute-start | bytes 3538952 | tf_op jit(solution)/shard_map/ppermute | solution.py:431
  101.2 29.4 %collective-permute-start.6 = (bf16[2,4,96,768]{3,2,1,0:T(8,128)(2,1)}, bf16[2,4,96,768]{3,2,1,0:T(8,128)(2,1)}, u32[]{:S(2)}, u32[]{:S(2)}) collective-permute-start(bf16[2,4,96,768]{3,2,1,0:T(8,128)(2,1)} %get-tuple-element.145), channel_id=1, source_target_pairs={{0,16},{4,20},{8,24},{12,28},{16,0},{20,4},{24,8},{28,12},{1,17},{... | collective-permute-start | bytes 3538952 | tf_op jit(solution)/shard_map/ppermute | solution.py:431
  133.9 6.1 %collective-permute-start.7 = (bf16[384,1664]{1,0:T(8,128)(2,1)}, bf16[384,1664]{1,0:T(8,128)(2,1)}, u32[]{:S(2)}, u32[]{:S(2)}) collective-permute-start(bf16[384,1664]{1,0:T(8,128)(2,1)} %get-tuple-element.166), channel_id=1, source_target_pairs={{0,4},{4,0},{8,12},{12,8},{16,20},{20,16},{24,28},{28,24},{1,5},{5... | collective-permute-start | bytes 3833864 | tf_op jit(solution)/shard_map/ppermute | solution.py:431
  133.9 6.0 %collective-permute-start.8 = (bf16[384,1664]{1,0:T(8,128)(2,1)}, bf16[384,1664]{1,0:T(8,128)(2,1)}, u32[]{:S(2)}, u32[]{:S(2)}) collective-permute-start(bf16[384,1664]{1,0:T(8,128)(2,1)} %get-tuple-element.167), channel_id=1, source_target_pairs={{0,4},{4,0},{8,12},{12,8},{16,20},{20,16},{24,28},{28,24},{1,5},{5... | collective-permute-start | bytes 3833864 | tf_op jit(solution)/shard_map/ppermute | solution.py:431
  134.4 16.5 %collective-permute-start.11 = (bf16[4,96,768]{2,1,0:T(8,128)(2,1)}, bf16[4,96,768]{2,1,0:T(8,128)(2,1)}, u32[]{:S(2)}, u32[]{:S(2)}) collective-permute-start(bf16[4,96,768]{2,1,0:T(8,128)(2,1)} %get-tuple-element.176), channel_id=1, source_target_pairs={{0,16},{4,20},{8,24},{12,28},{16,0},{20,4},{24,8},{28,12},{1,17},{... | collective-permute-start | bytes 1769480 | tf_op jit(solution)/shard_map/ppermute | solution.py:431
  135.0 16.5 %collective-permute-start.12 = (bf16[4,96,768]{2,1,0:T(8,128)(2,1)}, bf16[4,96,768]{2,1,0:T(8,128)(2,1)}, u32[]{:S(2)}, u32[]{:S(2)}) collective-permute-start(bf16[4,96,768]{2,1,0:T(8,128)(2,1)} %get-tuple-element.177), channel_id=1, source_target_pairs={{0,8},{4,12},{8,0},{12,4},{16,24},{20,28},{24,16},{28,20},{1,9},{5... | collective-permute-start | bytes 1769480 | tf_op jit(solution)/shard_map/ppermute | solution.py:431
  135.5 54.2 %all-to-all-start.2 = ((bf16[12,51,768]{2,1,0:T(8,128)(2,1)}), bf16[12,51,768]{2,1,0:T(8,128)(2,1)}, u32[]{:S(2)}, u32[]{:S(2)}) async-start(bf16[12,51,768]{2,1,0:T(8,128)(2,1)} %get-tuple-element.198), calls=%async_computation.2 | async-start | bytes 2064384 | tf_op jit(solution)/shard_map/all_to_all | solution.py:444
  142.9 20.8 %collective-permute-start.10 = (bf16[2,2,48,1664]{3,2,1,0:T(8,128)(2,1)}, bf16[2,2,48,1664]{3,2,1,0:T(8,128)(2,1)S(1)}, u32[]{:S(2)}, u32[]{:S(2)}) collective-permute-start(bf16[2,2,48,1664]{3,2,1,0:T(8,128)(2,1)} %get-tuple-element.175), channel_id=1, source_target_pairs={{0,16},{4,20},{8,24},{12,28},{16,0},{20,4},{24,8},{28,12},{1,17},{... | collective-permute-start | bytes 1916936 | tf_op jit(solution)/shard_map/ppermute | solution.py:431
  144.5 19.5 %collective-permute-start.9 = (bf16[2,2,48,1664]{3,2,1,0:T(8,128)(2,1)}, bf16[2,2,48,1664]{3,2,1,0:T(8,128)(2,1)}, u32[]{:S(2)}, u32[]{:S(2)}) collective-permute-start(bf16[2,2,48,1664]{3,2,1,0:T(8,128)(2,1)} %get-tuple-element.174), channel_id=1, source_target_pairs={{0,8},{4,12},{8,0},{12,4},{16,24},{20,28},{24,16},{28,20},{1,9},{5... | collective-permute-start | bytes 1916936 | tf_op jit(solution)/shard_map/ppermute | solution.py:431
  156.2 17.8 %collective-permute-start.13 = (bf16[4,96,768]{2,1,0:T(8,128)(2,1)}, bf16[4,96,768]{2,1,0:T(8,128)(2,1)S(1)}, u32[]{:S(2)}, u32[]{:S(2)}) collective-permute-start(bf16[4,96,768]{2,1,0:T(8,128)(2,1)} %get-tuple-element.191), channel_id=1, source_target_pairs={{0,1},{1,0},{2,3},{3,2},{4,5},{5,4},{6,7},{7,6},{8,9},{9,8},{10,11... | collective-permute-start | bytes 1769480 | tf_op jit(solution)/shard_map/ppermute | solution.py:651
  163.7 0.8 copy-start
  164.5 11.7 %copy-start.4 = (bf16[4,96,768]{2,1,0:T(8,128)(2,1)S(1)}, bf16[4,96,768]{2,1,0:T(8,128)(2,1)}, u32[]{:S(2)}) copy-start(bf16[4,96,768]{2,1,0:T(8,128)(2,1)} %get-tuple-element.187) | copy-start | bytes 1769476
  173.9 7.2 %collective-permute-start.14 = (bf16[2,48,1664]{2,1,0:T(8,128)(2,1)}, bf16[2,48,1664]{2,1,0:T(8,128)(2,1)S(1)}, u32[]{:S(2)}, u32[]{:S(2)}) collective-permute-start(bf16[2,48,1664]{2,1,0:T(8,128)(2,1)} %get-tuple-element.193), channel_id=1, source_target_pairs={{0,16},{4,20},{8,24},{12,28},{16,0},{20,4},{24,8},{28,12},{1,17},{... | collective-permute-start | bytes 958472 | tf_op jit(solution)/shard_map/ppermute | solution.py:431
  175.4 7.2 %collective-permute-start.15 = (bf16[2,48,1664]{2,1,0:T(8,128)(2,1)}, bf16[2,48,1664]{2,1,0:T(8,128)(2,1)S(1)}, u32[]{:S(2)}, u32[]{:S(2)}) collective-permute-start(bf16[2,48,1664]{2,1,0:T(8,128)(2,1)} %get-tuple-element.194), channel_id=1, source_target_pairs={{0,8},{4,12},{8,0},{12,4},{16,24},{20,28},{24,16},{28,20},{1,9},{5... | collective-permute-start | bytes 958472 | tf_op jit(solution)/shard_map/ppermute | solution.py:431
  176.4 13.3 %collective-permute-start.17 = (bf16[2,96,768]{2,1,0:T(8,128)(2,1)S(1)}, bf16[2,96,768]{2,1,0:T(8,128)(2,1)S(1)}, u32[]{:S(2)}, u32[]{:S(2)}) collective-permute-start(bf16[2,96,768]{2,1,0:T(8,128)(2,1)S(1)} %get-tuple-element.201), channel_id=1, source_target_pairs={{0,2},{1,3},{2,0},{3,1},{4,6},{5,7},{6,4},{7,5},{8,10},{9,11},{10,... | collective-permute-start | bytes 884744 | tf_op jit(solution)/shard_map/ppermute | solution.py:654
  181.1 1.4 copy-start.5
  182.6 0.7 copy-start.6
  186.8 15.3 %collective-permute-start.16 = (bf16[2,48,1664]{2,1,0:T(8,128)(2,1)}, bf16[2,48,1664]{2,1,0:T(8,128)(2,1)S(1)}, u32[]{:S(2)}, u32[]{:S(2)}) collective-permute-start(bf16[2,48,1664]{2,1,0:T(8,128)(2,1)} %get-tuple-element.197), channel_id=1, source_target_pairs={{0,1},{1,0},{2,3},{3,2},{4,5},{5,4},{6,7},{7,6},{8,9},{9,8},{10,11... | collective-permute-start | bytes 958472 | tf_op jit(solution)/shard_map/ppermute | solution.py:651
  186.9 17.5 %collective-permute-start.19 = (bf16[2,96,768]{2,1,0:T(8,128)(2,1)S(1)}, bf16[2,96,768]{2,1,0:T(8,128)(2,1)S(1)}, u32[]{:S(2)}, u32[]{:S(2)}) collective-permute-start(bf16[2,96,768]{2,1,0:T(8,128)(2,1)S(1)} %get-tuple-element.211), channel_id=1, source_target_pairs={{0,2},{1,3},{2,0},{3,1},{4,6},{5,7},{6,4},{7,5},{8,10},{9,11},{10,... | collective-permute-start | bytes 884744 | tf_op jit(solution)/shard_map/ppermute | solution.py:654
  189.7 12.6 %copy-start.10 = (bf16[2,96,768]{2,1,0:T(8,128)(2,1)}, bf16[2,96,768]{2,1,0:T(8,128)(2,1)S(1)}, u32[]{:S(2)}) copy-start(bf16[2,96,768]{2,1,0:T(8,128)(2,1)S(1)} %add.53.mine) | copy-start | bytes 884740
  189.7 12.4 %copy-start.8 = (bf16[2,48,1664]{2,1,0:T(8,128)(2,1)S(1)}, bf16[2,48,1664]{2,1,0:T(8,128)(2,1)}, u32[]{:S(2)}) copy-start(bf16[2,48,1664]{2,1,0:T(8,128)(2,1)} %get-tuple-element.207) | copy-start | bytes 958468
  202.2 15.1 %collective-permute-start.20 = (bf16[2,48,1664]{2,1,0:T(8,128)(2,1)S(1)}, bf16[2,48,1664]{2,1,0:T(8,128)(2,1)S(1)}, u32[]{:S(2)}, u32[]{:S(2)}) collective-permute-start(bf16[2,48,1664]{2,1,0:T(8,128)(2,1)S(1)} %add.54), channel_id=1, source_target_pairs={{0,2},{1,3},{2,0},{3,1},{4,6},{5,7},{6,4},{7,5},{8,10},{9,11},{10,... | collective-permute-start | bytes 958472 | tf_op jit(solution)/shard_map/ppermute | solution.py:654
  202.3 16.8 %collective-permute-start.18 = (bf16[2,96,768]{2,1,0:T(8,128)(2,1)S(1)}, bf16[2,96,768]{2,1,0:T(8,128)(2,1)S(1)}, u32[]{:S(2)}, u32[]{:S(2)}) collective-permute-start(bf16[2,96,768]{2,1,0:T(8,128)(2,1)S(1)} %add.53.mine), channel_id=1, source_target_pairs={{0,1},{1,0},{2,3},{3,2},{4,5},{5,4},{6,7},{7,6},{8,9},{9,8},{10,11... | collective-permute-start | bytes 884744 | tf_op jit(solution)/shard_map/ppermute | solution.py:651
  204.5 17.5 %copy-start.1 = (bf16[2,96,768]{2,1,0:T(8,128)(2,1)}, bf16[2,96,768]{2,1,0:T(8,128)(2,1)S(1)}, u32[]{:S(2)}) copy-start(bf16[2,96,768]{2,1,0:T(8,128)(2,1)S(1)} %add.55.mine) | copy-start | bytes 884740
  204.5 20.9 %collective-permute-start.22 = (bf16[2,96,768]{2,1,0:T(8,128)(2,1)S(1)}, bf16[2,96,768]{2,1,0:T(8,128)(2,1)S(1)}, u32[]{:S(2)}, u32[]{:S(2)}) collective-permute-start(bf16[2,96,768]{2,1,0:T(8,128)(2,1)S(1)} %add.55.mine), channel_id=1, source_target_pairs={{0,1},{1,0},{2,3},{3,2},{4,5},{5,4},{6,7},{7,6},{8,9},{9,8},{10,11... | collective-permute-start | bytes 884744 | tf_op jit(solution)/shard_map/ppermute | solution.py:651
  217.5 10.8 %copy-start.7 = (bf16[2,48,1664]{2,1,0:T(8,128)(2,1)}, bf16[2,48,1664]{2,1,0:T(8,128)(2,1)S(1)}, u32[]{:S(2)}) copy-start(bf16[2,48,1664]{2,1,0:T(8,128)(2,1)S(1)} %add.56) | copy-start | bytes 958468
  217.5 13.9 %collective-permute-start.21 = (bf16[2,48,1664]{2,1,0:T(8,128)(2,1)S(1)}, bf16[2,48,1664]{2,1,0:T(8,128)(2,1)S(1)}, u32[]{:S(2)}, u32[]{:S(2)}) collective-permute-start(bf16[2,48,1664]{2,1,0:T(8,128)(2,1)S(1)} %add.56), channel_id=1, source_target_pairs={{0,1},{1,0},{2,3},{3,2},{4,5},{5,4},{6,7},{7,6},{8,9},{9,8},{10,11... | collective-permute-start | bytes 958472 | tf_op jit(solution)/shard_map/ppermute | solution.py:651
  219.1 0.7 copy-start.21
  225.4 0.7 copy-start.9
  231.3 0.7 copy-start.20

commit v6 on v5

--- a/solution.py
+++ b/solution.py
@@ -132,17 +132,21 @@
 
 
 def feed_kernel(
-    at, keep, g0, g1, g2, g3, sg, h, a2, a2t, w1, b1, w2, b2, gain,
+    at, keep, g0, g1, g2, g3, sg, h_any, a2, a2t_any, w1, b1, w2, b2, gain,
     out, dh, dy, w2s, w2k, w1s, w1k, db1, small,
-    dout, dz, z, da2, acts, dus, across, *, images,
+    dout, dz, z, da2, acts, dus, across, h, a2t, sems, *, images,
 ):
     t = pl.program_id(0)
+    fetch_h = pltpu.make_async_copy(h_any, h, sems.at[0])
+    fetch_a2t = pltpu.make_async_copy(a2t_any, a2t, sems.at[1])
     part = g0.shape[1] // images
     ns = sg.shape[1]
     padded = h.shape[1]
 
     @pl.when(t == 0)
     def _():
+        fetch_a2t.start()
+        fetch_h.start()
         for i in range(images):
             m2 = keep[at[0] * images + i, 1].astype(F32) * KEEP
             r = i * padded
@@ -152,7 +156,6 @@
                 lo = r + ns + k * part
                 dout[lo : lo + part, :] = unpacked(ref.at[0], i, images, part)
             dz[r : r + padded, :] = (dout[r : r + padded, :] * m2).astype(BF)
-            across[:, r : r + padded] = a2t[i]
         z[...] = jnp.zeros_like(z)
         da2[...] = jnp.zeros_like(da2)
 
@@ -171,6 +174,13 @@
     db1[...] = db
     z[...] += dot(acts[...], wb)
     da2[...] += dot_nt(dus[...], wa)
+
+    @pl.when(t == 0)
+    def _():
+        fetch_a2t.wait()
+        for i in range(images):
+            across[:, i * padded : (i + 1) * padded] = a2t[i]
+
     half = across.shape[0] // 2
     w1k[...] = dot(across[:half, :], dus[...]).astype(BF).reshape(w1k.shape)
     w1s[...] = dot(across[half:, :], dus[...]).astype(BF).reshape(w1s.shape)
@@ -181,6 +191,7 @@
 
     @pl.when(t == pl.num_programs(0) - 1)
     def _():
+        fetch_h.wait()
         gains = gain[...].astype(F32)
         sums = [jnp.zeros((1, dout.shape[1]), F32) for _ in range(4)]
         for i in range(images):
@@ -207,8 +218,8 @@
 
 def heads_kernel(
     at, dy, prob, qkv, wp_any, wq_any, xs, dh, gain, a1t_any, ot_any, small2, db1,
-    out, small, flat, cs, ck, ds_, dk_,
-    buf, dqkv, dys, wp, wq, a1t, ot, a1, o, cols, sems, *, images, heads, part, ns,
+    out, small, flat, cs_any, ck, ds_any, dk_,
+    buf, dqkv, dys, wp, wq, a1t, ot, a1, o, cols, cs, ds_, sems, *, images, heads, part, ns,
 ):
     i = pl.program_id(0)
     width = dy.shape[2]
@@ -291,6 +302,10 @@
         fetches[2].wait()
         fetches[3].wait()
 
+    send = [
+        pltpu.make_async_copy(cs, cs_any, sems.at[4]),
+        pltpu.make_async_copy(ds_, ds_any, sems.at[5]),
+    ]
     half = cs.shape[0]
     for step, lo, c_ref, d_ref in ((images, half, cs, ds_), (images + 1, 0, ck, dk_)):
 
@@ -305,6 +320,8 @@
             d_ref[:, :width] = dot(a1[...], dqkv[:, 2 * width :]).astype(BF)
             d_ref[:, width : 2 * width] = dot(o[...], dys[...]).astype(BF)
             d_ref[:, 2 * width :] = cols[lo : lo + half, :].astype(BF)
+            for copy in send:
+                copy.start() if lo else copy.wait()
 
 
 def settle_kernel(both, rows, specials):
@@ -550,7 +567,7 @@
                     for k in range(groups)
                 ],
                 pl.BlockSpec((n, ns, width), lambda t, at, keep: (at[0], 0, 0)),
-                whole(h.shape, once), whole(a2.shape, once), whole(a2t.shape, once),
+                ANY, whole(a2.shape, once), ANY,
                 pl.BlockSpec((width, chunk), lambda t, at, keep: (0, owner(t, at))),
                 pl.BlockSpec((1, chunk), lambda t, at, keep: (0, owner(t, at))),
                 pl.BlockSpec((chunk, width), lambda t, at, keep: (owner(t, at), 0)),
@@ -568,7 +585,8 @@
                 pltpu.VMEM((total, width), F32), pltpu.VMEM((total, width), BF),
                 pltpu.VMEM((total, width), F32), pltpu.VMEM((total, width), F32),
                 pltpu.VMEM((total, chunk), BF), pltpu.VMEM((total, chunk), BF),
-                pltpu.VMEM((width, total), BF),
+                pltpu.VMEM((width, total), BF), pltpu.VMEM(h.shape, F32), pltpu.VMEM(a2t.shape, BF),
+                pltpu.SemaphoreType.DMA((2,)),
             ],
         ),
         out_shape=[
@@ -615,14 +633,15 @@
             ],
             out_specs=[
                 whole((images, part + ns, width)), whole((2, width)), whole((1, 3 * width)),
-                *[whole((half, wide))] * 4,
+                ANY, whole((half, wide)), ANY, whole((half, wide)),
             ],
             scratch_shapes=[
                 pltpu.VMEM((padded, width), F32), pltpu.VMEM((total, 3 * width), BF),
                 pltpu.VMEM((total, width), BF), pltpu.VMEM(proj_weight.shape, BF),
                 pltpu.VMEM(qkv_weight.shape, BF), pltpu.VMEM(a1t.shape, BF), pltpu.VMEM(ot.shape, BF),
                 pltpu.VMEM((half, total), BF), pltpu.VMEM((half, total), BF),
-                pltpu.VMEM((width, COLUMNS), F32), pltpu.SemaphoreType.DMA((4,)),
+                pltpu.VMEM((width, COLUMNS), F32), pltpu.VMEM((half, wide), BF),
+                pltpu.VMEM((half, wide), BF), pltpu.SemaphoreType.DMA((6,)),
             ],
         ),
         out_shape=[

time: 235 us -> 234 us (level)
  transfers between devices with their start and end apart: 26 -> 26, of which waited for: 17 -> 17; matrix products, arithmetic and copies ran while one was open for 2% -> 2% of each run, Pallas kernels for 31% -> 30%
where the time goes in v6:
time: 234 us; the launch traced here: 233 us
  Pallas kernels  108 us (46%)
  waiting for transfers between devices  76 us (32%)
  starting transfers between devices  38.3 us (16%)
  local copies, waits for them, and re-layouts  7.4 us (3%)
    pallas_call x1, Pallas kernels, shards(): pl.pallas_call(partial(feed_kernel, images=n), grid_spec=pltpu.PrefetchSc...  31.2 us
    pallas_call x1, Pallas kernels, shards(): pl.pallas_call(partial(heads_kernel, images=n, heads=heads, part=part, ns...  27 us
    ppermute x5, waiting for transfers between devices, near(): return lax.ppermute(v, 'seq', [(s, s ^ 1) for s in range(groups)])  24.2 us
    pallas_call x6, Pallas kernels, sums(): pl.pallas_call(partial(sum_kernel, jobs=leads, pick=at is not None), in_s...  20.9 us
    ppermute x12, waiting for transfers between devices, swap(): lax.ppermute(v, 'dp', [(s, s ^ bit) for s in range(lax.axis_size('dp'))])  19.4 us
    all_to_all x3, starting transfers between devices, exchange(): return lax.all_to_all(x, 'seq', split_axis=0, concat_axis=0, tiled=True)  16.6 us
    pallas_call x1, Pallas kernels, shards(): pl.pallas_call(partial(forward_kernel, rows=rows, heads=heads), grid_spec...  15.2 us
    ppermute x3, waiting for transfers between devices, far(): return lax.ppermute(v, 'seq', [(s, s ^ 2) for s in range(groups)])  13.3 us
  transfers between devices with their start and end apart: 26, of which 17 were waited for; matrix products, arithmetic and copies ran while one was open for 2% of the time, Pallas kernels for 30%

profile of v6, /device:TPU:0, one launch (start us, length us, event | category | flops | bytes accessed | tf_op | source)
XLA Modules:
  0.0 233.1 jit_solution(10404953739547672222)
XLA Ops:
  0.7 1.3 constant_dynamic-slice_fusion
  1.9 0.2 copy_bitcast_fusion
  2.2 0.1 slice.50
  2.4 4.1 %collective-permute-start.1 = (bf16[147,768]{1,0:T(8,128)(2,1)S(1)}, bf16[147,768]{1,0:T(8,128)(2,1)S(1)}, u32[]{:S(2)}, u32[]{:S(2)}) collective-permute-start(bf16[147,768]{1,0:T(8,128)(2,1)S(1)} %maximum_bitcast_fusion.1), channel_id=1, source_target_pairs={{0,2},{1,3},{2,0},{3,1},{4,6},{5,7},{6,4},{7,5},{8,10},{9,11},{10,... | collective-permute-start | bytes 677384 | tf_op jit(solution)/shard_map/ppermute | solution.py:509
  6.7 1.4 collective-permute-start.2
  8.1 0.1 copy.55
  8.4 0.7 collective-permute-start
  9.3 0.7 copy.49.keep
  10.1 1.0 pad_maximum_fusion
  11.1 7.8 %collective-permute-done.1.x2 = bf16[147,768]{1,0:T(8,128)(2,1)S(1)} collective-permute-done((bf16[147,768]{1,0:T(8,128)(2,1)S(1)}, bf16[147,768]{1,0:T(8,128)(2,1)S(1)}, u32[]{:S(2)}, u32[]{:S(2)}) %collective-permute-start.1) | collective-permute-done | bytes 225824 | tf_op jit(solution)/shard_map/ppermute | solution.py:509
  18.9 4.5 %collective-permute-done.x1 = bf16[147,768]{1,0:T(8,128)(2,1)S(1)} collective-permute-done((bf16[147,768]{1,0:T(8,128)(2,1)S(1)}, bf16[147,768]{1,0:T(8,128)(2,1)S(1)}, u32[]{:S(2)}, u32[]{:S(2)}) %collective-permute-start) | collective-permute-done | bytes 225824 | tf_op jit(solution)/shard_map/ppermute | solution.py:509
  23.4 7.7 %all-to-all-start = ((bf16[4,147,768]{2,1,0:T(8,128)(2,1)}), bf16[4,147,768]{2,1,0:T(8,128)(2,1)S(1)}, u32[]{:S(2)}, u32[]{:S(2)}) async-start(bf16[4,147,768]{2,1,0:T(8,128)(2,1)} %pad_maximum_fusion), calls=%async_computation | async-start | bytes 1867776 | tf_op jit(solution)/shard_map/all_to_all | solution.py:461
  31.2 0.6 reshape.132.g1.b1.bq.bp.g2.b2.gain
  31.9 0.6 pad_add_fusion.at.refs_0_
  32.5 15.2 %attention_forward.1 = (bf16[3,208,768]{2,1,0:T(8,128)(2,1)}, bf16[3,768,208]{2,1,0:T(8,128)(2,1)}, bf16[3,208,2304]{2,1,0:T(8,128)(2,1)}, bf16[3,6,416,208]{3,2...) custom-call(s32[2]{0:T(128)} %pad_add_fusion.at.refs_0_, ...), custom_call_target="tpu_custom_call" | custom-call | flops 4499999744 | bytes 1 | tf_op jit(solution)/shard_map/attention_forward/pallas_call | solution.py:528
  47.7 6.9 %all-to-all-done.g0.g1.g2.g3 = bf16[4,147,768]{2,1,0:T(8,128)(2,1)S(1)} async-done(((bf16[4,147,768]{2,1,0:T(8,128)(2,1)}), bf16[4,147,768]{2,1,0:T(8,128)(2,1)S(1)}, u32[]{:S(2)}, u32[]{:S(2)}) %all-to-all-start) | async-done | bytes 903200 | tf_op jit(solution)/shard_map/all_to_all | solution.py:461
  54.6 0.9 copy-done.2
  55.5 31.2 %feed_forward.1 = (bf16[12,51,768]{2,1,0:T(8,128)(2,1)}, f32[3,208,768]{2,1,0:T(8,128)}, bf16[3,208,768]{2,1,0:T(8,128)(2,1)}, bf16[1536,768]{1,0:T(8,128)(2,1)}...) custom-call(s32[2]{0:T(128)} %pad_add_fusion.at.refs_0_, ...), custom_call_target="tpu_custom_call" | custom-call | flops 8999999488 | bytes 1 | tf_op jit(solution)/shard_map/feed_forward/pallas_call | solution.py:559
  86.9 0.5 collective-permute-start.4
  87.4 4.4 %all-to-all-start.1 = ((bf16[12,51,768]{2,1,0:T(8,128)(2,1)}), bf16[12,51,768]{2,1,0:T(8,128)(2,1)}, u32[]{:S(2)}, u32[]{:S(2)}) async-start(bf16[12,51,768]{2,1,0:T(8,128)(2,1)} %get-tuple-element.157), calls=%async_computation.1 | async-start | bytes 2064384 | tf_op jit(solution)/shard_map/all_to_all | solution.py:461
  91.8 3.3 %collective-permute-done.4 = bf16[1536,768]{1,0:T(8,128)(2,1)} collective-permute-done((bf16[1536,768]{1,0:T(8,128)(2,1)}, bf16[1536,768]{1,0:T(8,128)(2,1)}, u32[]{:S(2)}, u32[]{:S(2)}) %collective-permute-start.4) | collective-permute-done | bytes 2359328 | tf_op jit(solution)/shard_map/ppermute | solution.py:448
  95.1 4.0 %sums.6 = (bf16[2,4,96,768]{3,2,1,0:T(8,128)(2,1)}, bf16[2,4,96,768]{3,2,1,0:T(8,128)(2,1)}) custom-call(bf16[2,2,4,96,768]{4,3,2,1,0:T(8,128)(2,1)} %bitcast.48, bf16[2,2,4,96,768]{4,3,2,1,0:T(8,128)(2,1)} %bitcast.18.refs_1_.refs_2_, bf16[2,2,4,96,768]{4,3,2,1,0:T(8,128)(2,1)} %bitcast.45, bf16[2,2,4,96,768]{4,3,2,1,0:T(8,128)(2,1)} %bitcast.20.refs_3_.refs_4_.refs_6_), custom_call_target="tpu_custom_call" | custom-call | flops 600000000 | bytes 1 | tf_op jit(solution)/shard_map/sums/pallas_call | solution.py:377
  99.2 1.6 collective-permute-start.5
  100.7 1.5 collective-permute-start.6
  102.2 27.0 %attention_backward.1 = (bf16[12,51,768]{2,1,0:T(8,128)(2,1)}, f32[2,768]{1,0:T(2,128)}, f32[1,2304]{1,0:T(1,128)}, bf16[384,1664]{1,0:T(8,128)(2,1)}, bf16[384,...) custom-call(s32[2]{0:T(128)} %pad_add_fusion.at.refs_0_, ...), custom_call_target="tpu_custom_call" | custom-call | flops 6600000000 | bytes 1 | tf_op jit(solution)/shard_map/attention_backward/pallas_call | solution.py:623
  129.3 3.2 %sums.7 = (bf16[4,96,768]{2,1,0:T(8,128)(2,1)}, bf16[4,96,768]{2,1,0:T(8,128)(2,1)}) custom-call(bf16[2,2,4,96,768]{4,3,2,1,0:T(8,128)(2,1)} %bitcast.49, bf16[2,2,4,96,768]{4,3,2,1,0:T(8,128)(2,1)} %bitcast.18.refs_1_.refs_2_, bf16[2,4,96,768]{3,2,1,0:T(8,128)(2,1)} %collective-permute-done.5.refs_2_.refs_3_, bf16[2,2,4,96,768]{4,3,2,1,0:T(8,128)(2,1)} %bitcast.46, ...), custom_call_target="tpu_custom_call" | custom-call | flops 600000000 | bytes 1 | tf_op jit(solution)/shard_map/sums/pallas_call | solution.py:377
  132.6 0.5 collective-permute-start.8
  133.1 1.0 collective-permute-start.11
  134.1 0.6 collective-permute-start.12
  134.7 4.5 %all-to-all-start.2 = ((bf16[12,51,768]{2,1,0:T(8,128)(2,1)}), bf16[12,51,768]{2,1,0:T(8,128)(2,1)}, u32[]{:S(2)}, u32[]{:S(2)}) async-start(bf16[12,51,768]{2,1,0:T(8,128)(2,1)} %get-tuple-element.198), calls=%async_computation.2 | async-start | bytes 2064384 | tf_op jit(solution)/shard_map/all_to_all | solution.py:461
  139.2 2.9 %sums.8 = (bf16[2,2,48,1664]{3,2,1,0:T(8,128)(2,1)}, bf16[2,2,48,1664]{3,2,1,0:T(8,128)(2,1)}) custom-call(bf16[2,2,2,48,1664]{4,3,2,1,0:T(8,128)(2,1)} %bitcast.51, bf16[2,2,2,48,1664]{4,3,2,1,0:T(8,128)(2,1)} %bitcast.22.refs_1_.refs_2_, bf16[2,2,2,48,1664]{4,3,2,1,0:T(8,128)(2,1)} %bitcast.54, bf16[2,2,2,48,1664]{4,3,2,1,0:T(8,128)(2,1)} %bitcast.24.refs_3_.refs_4_.refs_6_), custom_call_target="tpu_custom_call" | custom-call | flops 600000000 | bytes 1 | tf_op jit(solution)/shard_map/sums/pallas_call | solution.py:377
  142.1 1.1 collective-permute-start.10
  143.2 1.4 collective-permute-start.9
  144.6 5.0 %collective-permute-done.11.refs_4_ = bf16[4,96,768]{2,1,0:T(8,128)(2,1)} collective-permute-done((bf16[4,96,768]{2,1,0:T(8,128)(2,1)}, bf16[4,96,768]{2,1,0:T(8,128)(2,1)}, u32[]{:S(2)}, u32[]{:S(2)}) %collective-permute-start.11) | collective-permute-done | bytes 589856 | tf_op jit(solution)/shard_map/ppermute | solution.py:448
  149.6 1.0 collective-permute-done.12.refs_8_
  150.6 4.6 %sums.9 = (bf16[4,96,768]{2,1,0:T(8,128)(2,1)}, bf16[4,96,768]{2,1,0:T(8,128)(2,1)}) custom-call(s32[2]{0:T(128)} %pad_add_fusion.at.refs_0_, bf16[2,2,4,96,768]{4,3,2,1,0:T(8,128)(2,1)} %bitcast.50, bf16[2,2,4,96,768]{4,3,2,1,0:T(8,128)(2,1)} %bitcast.18.refs_1_.refs_2_, bf16[2,4,96,768]{3,2,1,0:T(8,128)(2,1)} %collective-permute-done.5.refs_2_.refs_3_, ...), custom_call_target="tpu_custom_call" | custom-call | flops 600000000 | bytes 1 | tf_op jit(solution)/shard_map/sums/pallas_call | solution.py:377
  155.4 3.4 %settle.2 = (bf16[12,49,768]{2,1,0:T(8,128)(2,1)}, bf16[12,2,768]{2,1,0:T(2,128)(2,1)}) custom-call(bf16[12,51,768]{2,1,0:T(8,128)(2,1)} %all-to-all-done.1.both), custom_call_target="tpu_custom_call" | custom-call | flops 600000000 | bytes 1 | tf_op jit(solution)/shard_map/settle/pallas_call | solution.py:467
  158.8 3.6 %collective-permute-done.10.refs_5_.refs_7_ = bf16[2,2,48,1664]{3,2,1,0:T(8,128)(2,1)S(1)} collective-permute-done((bf16[2,2,48,1664]{3,2,1,0:T(8,128)(2,1)}, bf16[2,2,48,1664]{3,2,1,0:T(8,128)(2,1)S(1)}, u32[]{:S(2)}, u32[]{:S(2)}) %collective-permute-start.10) | collective-permute-done | bytes 639008 | tf_op jit(solution)/shard_map/ppermute | solution.py:448
  162.3 0.8 collective-permute-done.9.refs_2_.refs_3_
  163.2 2.5 %sums.10 = (bf16[2,48,1664]{2,1,0:T(8,128)(2,1)}, bf16[2,48,1664]{2,1,0:T(8,128)(2,1)}) custom-call(bf16[2,2,2,48,1664]{4,3,2,1,0:T(8,128)(2,1)} %bitcast.52, bf16[2,2,2,48,1664]{4,3,2,1,0:T(8,128)(2,1)} %bitcast.22.refs_1_.refs_2_, bf16[2,2,48,1664]{3,2,1,0:T(8,128)(2,1)} %collective-permute-done.9.refs_2_.refs_3_, bf16[2,2,2,48,1664]{4,3,2,1,0:T(8,128)(2,1)} %bitcast.55, ...), custom_call_target="tpu_custom_call" | custom-call | flops 600000000 | bytes 1 | tf_op jit(solution)/shard_map/sums/pallas_call | solution.py:377
  165.7 7.3 %collective-permute-done.13 = bf16[4,96,768]{2,1,0:T(8,128)(2,1)S(1)} collective-permute-done((bf16[4,96,768]{2,1,0:T(8,128)(2,1)}, bf16[4,96,768]{2,1,0:T(8,128)(2,1)S(1)}, u32[]{:S(2)}, u32[]{:S(2)}) %collective-permute-start.13) | collective-permute-done | bytes 589856 | tf_op jit(solution)/shard_map/ppermute | solution.py:670
  173.0 1.0 collective-permute-start.14
  174.0 0.8 collective-permute-start.15
  174.8 0.1 add.52
  175.0 0.6 collective-permute-start.17
  175.6 4.6 %collective-permute-done.14.refs_4_ = bf16[2,48,1664]{2,1,0:T(8,128)(2,1)S(1)} collective-permute-done((bf16[2,48,1664]{2,1,0:T(8,128)(2,1)}, bf16[2,48,1664]{2,1,0:T(8,128)(2,1)S(1)}, u32[]{:S(2)}, u32[]{:S(2)}) %collective-permute-start.14) | collective-permute-done | bytes 319520 | tf_op jit(solution)/shard_map/ppermute | solution.py:448
  180.2 1.0 collective-permute-done.15.refs_8_
  181.2 0.7 copy-done.6
  181.9 3.5 %sums.11 = (bf16[2,48,1664]{2,1,0:T(8,128)(2,1)}, bf16[2,48,1664]{2,1,0:T(8,128)(2,1)}) custom-call(s32[2]{0:T(128)} %pad_add_fusion.at.refs_0_, bf16[2,2,2,48,1664]{4,3,2,1,0:T(8,128)(2,1)} %bitcast.53, bf16[2,2,2,48,1664]{4,3,2,1,0:T(8,128)(2,1)} %bitcast.22.refs_1_.refs_2_, bf16[2,2,48,1664]{3,2,1,0:T(8,128)(2,1)} %collective-permute-done.9.refs_2_.refs_3_, ...), custom_call_target="tpu_custom_call" | custom-call | flops 600000000 | bytes 1 | tf_op jit(solution)/shard_map/sums/pallas_call | solution.py:377
  185.6 2.3 collective-permute-start.19
  187.8 0.4 collective-permute-done.17
  188.4 3.5 %settle.3 = (bf16[12,49,768]{2,1,0:T(8,128)(2,1)}, bf16[12,2,768]{2,1,0:T(2,128)(2,1)}) custom-call(bf16[12,51,768]{2,1,0:T(8,128)(2,1)} %all-to-all-done.2.both), custom_call_target="tpu_custom_call" | custom-call | flops 600000000 | bytes 1 | tf_op jit(solution)/shard_map/settle/pallas_call | solution.py:467
  191.9 8.9 %collective-permute-done.16 = bf16[2,48,1664]{2,1,0:T(8,128)(2,1)S(1)} collective-permute-done((bf16[2,48,1664]{2,1,0:T(8,128)(2,1)}, bf16[2,48,1664]{2,1,0:T(8,128)(2,1)S(1)}, u32[]{:S(2)}, u32[]{:S(2)}) %collective-permute-start.16) | collective-permute-done | bytes 319520 | tf_op jit(solution)/shard_map/ppermute | solution.py:670
  201.0 2.1 collective-permute-start.18
  203.2 12.9 %collective-permute-done.20 = bf16[2,48,1664]{2,1,0:T(8,128)(2,1)S(1)} collective-permute-done((bf16[2,48,1664]{2,1,0:T(8,128)(2,1)S(1)}, bf16[2,48,1664]{2,1,0:T(8,128)(2,1)S(1)}, u32[]{:S(2)}, u32[]{:S(2)}) %collective-permute-start.20) | collective-permute-done | bytes 319520 | tf_op jit(solution)/shard_map/ppermute | solution.py:673
  216.3 1.5 collective-permute-done.18.other
  217.7 0.7 copy-done.21
  218.5 2.2 finish_feed.2
  220.6 3.4 %collective-permute-done.22.other = bf16[2,96,768]{2,1,0:T(8,128)(2,1)S(1)} collective-permute-done((bf16[2,96,768]{2,1,0:T(8,128)(2,1)S(1)}, bf16[2,96,768]{2,1,0:T(8,128)(2,1)S(1)}, u32[]{:S(2)}, u32[]{:S(2)}) %collective-permute-start.22) | collective-permute-done | bytes 294944 | tf_op jit(solution)/shard_map/ppermute | solution.py:670
  224.1 0.7 copy-done.9
  224.8 2.2 finish_feed.3
  226.9 3.0 %collective-permute-done.21 = bf16[2,48,1664]{2,1,0:T(8,128)(2,1)S(1)} collective-permute-done((bf16[2,48,1664]{2,1,0:T(8,128)(2,1)S(1)}, bf16[2,48,1664]{2,1,0:T(8,128)(2,1)S(1)}, u32[]{:S(2)}, u32[]{:S(2)}) %collective-permute-start.21) | collective-permute-done | bytes 319520 | tf_op jit(solution)/shard_map/ppermute | solution.py:670
  230.0 0.7 copy-done.20
  230.7 2.2 finish.1
  (91 shorter events, 1.5 us)
Async XLA Ops:
  2.4 16.5 %collective-permute-start.1 = (bf16[147,768]{1,0:T(8,128)(2,1)S(1)}, bf16[147,768]{1,0:T(8,128)(2,1)S(1)}, u32[]{:S(2)}, u32[]{:S(2)}) collective-permute-start(bf16[147,768]{1,0:T(8,128)(2,1)S(1)} %maximum_bitcast_fusion.1), channel_id=1, source_target_pairs={{0,2},{1,3},{2,0},{3,1},{4,6},{5,7},{6,4},{7,5},{8,10},{9,11},{10,... | collective-permute-start | bytes 677384 | tf_op jit(solution)/shard_map/ppermute | solution.py:509
  6.6 2.5 %copy-start.3 = (bf16[12,49,768]{2,1,0:T(8,128)(2,1)S(1)}, bf16[12,49,768]{2,1,0:T(8,128)(2,1)}, u32[]{:S(2)}) copy-start(bf16[12,49,768]{2,1,0:T(8,128)(2,1)} %param.32) | copy-start | bytes 2709508
  6.7 12.3 %collective-permute-start.2 = (bf16[147,768]{1,0:T(8,128)(2,1)S(1)}, bf16[147,768]{1,0:T(8,128)(2,1)S(1)}, u32[]{:S(2)}, u32[]{:S(2)}) collective-permute-start(bf16[147,768]{1,0:T(8,128)(2,1)S(1)} %maximum_bitcast_fusion.2), channel_id=1, source_target_pairs={{0,3},{1,0},{2,1},{3,2},{4,7},{5,4},{6,5},{7,6},{8,11},{9,8},{10,9... | collective-permute-start | bytes 677384 | tf_op jit(solution)/shard_map/ppermute | solution.py:509
  8.3 0.9 copy-start.19
  8.4 1.6 copy-start.11
  8.4 1.6 copy-start.12
  8.4 1.6 copy-start.13
  8.4 1.7 copy-start.14
  8.4 15.0 %collective-permute-start = (bf16[147,768]{1,0:T(8,128)(2,1)S(1)}, bf16[147,768]{1,0:T(8,128)(2,1)S(1)}, u32[]{:S(2)}, u32[]{:S(2)}) collective-permute-start(bf16[147,768]{1,0:T(8,128)(2,1)S(1)} %maximum_bitcast_fusion), channel_id=1, source_target_pairs={{0,1},{1,2},{2,3},{3,0},{4,5},{5,6},{6,7},{7,4},{8,9},{9,10},{10,1... | collective-permute-start | bytes 677384 | tf_op jit(solution)/shard_map/ppermute | solution.py:509
  11.1 20.0 %copy-start.15 = (bf16[768]{0:T(1024)(128)(2,1)S(1)}, bf16[768]{0:T(1024)(128)(2,1)}, u32[]{:S(2)}) copy-start(bf16[768]{0:T(1024)(128)(2,1)} %param.25) | copy-start | bytes 4612
  11.1 20.0 %copy-start.16 = (bf16[768]{0:T(1024)(128)(2,1)S(1)}, bf16[768]{0:T(1024)(128)(2,1)}, u32[]{:S(2)}) copy-start(bf16[768]{0:T(1024)(128)(2,1)} %param.26) | copy-start | bytes 4612
  11.1 20.1 %copy-start.17 = (bf16[768]{0:T(1024)(128)(2,1)S(1)}, bf16[768]{0:T(1024)(128)(2,1)}, u32[]{:S(2)}) copy-start(bf16[768]{0:T(1024)(128)(2,1)} %param.27) | copy-start | bytes 4612
  11.1 20.1 %copy-start.18 = (bf16[768]{0:T(1024)(128)(2,1)S(1)}, bf16[768]{0:T(1024)(128)(2,1)}, u32[]{:S(2)}) copy-start(bf16[768]{0:T(1024)(128)(2,1)} %param.31) | copy-start | bytes 4612
  18.9 12.9 %copy-start.22 = (bf16[147,768]{1,0:T(8,128)(2,1)}, bf16[147,768]{1,0:T(8,128)(2,1)S(1)}, u32[]{:S(2)}) copy-start(bf16[147,768]{1,0:T(8,128)(2,1)S(1)} %collective-permute-done.1.x2) | copy-start | bytes 677380
  18.9 12.9 %copy-start.23 = (bf16[147,768]{1,0:T(8,128)(2,1)}, bf16[147,768]{1,0:T(8,128)(2,1)S(1)}, u32[]{:S(2)}) copy-start(bf16[147,768]{1,0:T(8,128)(2,1)S(1)} %collective-permute-done.2.x3) | copy-start | bytes 677380
  23.4 8.5 %copy-start.24 = (bf16[147,768]{1,0:T(8,128)(2,1)}, bf16[147,768]{1,0:T(8,128)(2,1)S(1)}, u32[]{:S(2)}) copy-start(bf16[147,768]{1,0:T(8,128)(2,1)S(1)} %collective-permute-done.x1) | copy-start | bytes 677380
  23.4 31.2 %all-to-all-start = ((bf16[4,147,768]{2,1,0:T(8,128)(2,1)}), bf16[4,147,768]{2,1,0:T(8,128)(2,1)S(1)}, u32[]{:S(2)}, u32[]{:S(2)}) async-start(bf16[4,147,768]{2,1,0:T(8,128)(2,1)} %pad_maximum_fusion), calls=%async_computation | async-start | bytes 1867776 | tf_op jit(solution)/shard_map/all_to_all | solution.py:461
  54.6 0.9 copy-start.2
  86.8 5.0 %collective-permute-start.3 = (bf16[4,4,96,768]{3,2,1,0:T(8,128)(2,1)}, bf16[4,4,96,768]{3,2,1,0:T(8,128)(2,1)}, u32[]{:S(2)}, u32[]{:S(2)}) collective-permute-start(bf16[4,4,96,768]{3,2,1,0:T(8,128)(2,1)} %get-tuple-element.136), channel_id=1, source_target_pairs={{0,4},{4,0},{8,12},{12,8},{16,20},{20,16},{24,28},{28,24},{1,5},{5... | collective-permute-start | bytes 7077896 | tf_op jit(solution)/shard_map/ppermute | solution.py:448
  86.9 8.2 %collective-permute-start.4 = (bf16[1536,768]{1,0:T(8,128)(2,1)}, bf16[1536,768]{1,0:T(8,128)(2,1)}, u32[]{:S(2)}, u32[]{:S(2)}) collective-permute-start(bf16[1536,768]{1,0:T(8,128)(2,1)} %get-tuple-element.137), channel_id=1, source_target_pairs={{0,4},{4,0},{8,12},{12,8},{16,20},{20,16},{24,28},{28,24},{1,5},{5... | collective-permute-start | bytes 7077896 | tf_op jit(solution)/shard_map/ppermute | solution.py:448
  87.4 41.9 %all-to-all-start.1 = ((bf16[12,51,768]{2,1,0:T(8,128)(2,1)}), bf16[12,51,768]{2,1,0:T(8,128)(2,1)}, u32[]{:S(2)}, u32[]{:S(2)}) async-start(bf16[12,51,768]{2,1,0:T(8,128)(2,1)} %get-tuple-element.157), calls=%async_computation.1 | async-start | bytes 2064384 | tf_op jit(solution)/shard_map/all_to_all | solution.py:461
  99.2 30.1 %collective-permute-start.5 = (bf16[2,4,96,768]{3,2,1,0:T(8,128)(2,1)}, bf16[2,4,96,768]{3,2,1,0:T(8,128)(2,1)}, u32[]{:S(2)}, u32[]{:S(2)}) collective-permute-start(bf16[2,4,96,768]{3,2,1,0:T(8,128)(2,1)} %get-tuple-element.144), channel_id=1, source_target_pairs={{0,8},{4,12},{8,0},{12,4},{16,24},{20,28},{24,16},{28,20},{1,9},{5... | collective-permute-start | bytes 3538952 | tf_op jit(solution)/shard_map/ppermute | solution.py:448
  100.7 28.5 %collective-permute-start.6 = (bf16[2,4,96,768]{3,2,1,0:T(8,128)(2,1)}, bf16[2,4,96,768]{3,2,1,0:T(8,128)(2,1)}, u32[]{:S(2)}, u32[]{:S(2)}) collective-permute-start(bf16[2,4,96,768]{3,2,1,0:T(8,128)(2,1)} %get-tuple-element.145), channel_id=1, source_target_pairs={{0,16},{4,20},{8,24},{12,28},{16,0},{20,4},{24,8},{28,12},{1,17},{... | collective-permute-start | bytes 3538952 | tf_op jit(solution)/shard_map/ppermute | solution.py:448
  132.5 6.6 %collective-permute-start.7 = (bf16[384,1664]{1,0:T(8,128)(2,1)}, bf16[384,1664]{1,0:T(8,128)(2,1)}, u32[]{:S(2)}, u32[]{:S(2)}) collective-permute-start(bf16[384,1664]{1,0:T(8,128)(2,1)} %get-tuple-element.166), channel_id=1, source_target_pairs={{0,4},{4,0},{8,12},{12,8},{16,20},{20,16},{24,28},{28,24},{1,5},{5... | collective-permute-start | bytes 3833864 | tf_op jit(solution)/shard_map/ppermute | solution.py:448
  132.6 6.6 %collective-permute-start.8 = (bf16[384,1664]{1,0:T(8,128)(2,1)}, bf16[384,1664]{1,0:T(8,128)(2,1)}, u32[]{:S(2)}, u32[]{:S(2)}) collective-permute-start(bf16[384,1664]{1,0:T(8,128)(2,1)} %get-tuple-element.167), channel_id=1, source_target_pairs={{0,4},{4,0},{8,12},{12,8},{16,20},{20,16},{24,28},{28,24},{1,5},{5... | collective-permute-start | bytes 3833864 | tf_op jit(solution)/shard_map/ppermute | solution.py:448
  133.1 16.5 %collective-permute-start.11 = (bf16[4,96,768]{2,1,0:T(8,128)(2,1)}, bf16[4,96,768]{2,1,0:T(8,128)(2,1)}, u32[]{:S(2)}, u32[]{:S(2)}) collective-permute-start(bf16[4,96,768]{2,1,0:T(8,128)(2,1)} %get-tuple-element.176), channel_id=1, source_target_pairs={{0,16},{4,20},{8,24},{12,28},{16,0},{20,4},{24,8},{28,12},{1,17},{... | collective-permute-start | bytes 1769480 | tf_op jit(solution)/shard_map/ppermute | solution.py:448
  134.1 16.5 %collective-permute-start.12 = (bf16[4,96,768]{2,1,0:T(8,128)(2,1)}, bf16[4,96,768]{2,1,0:T(8,128)(2,1)}, u32[]{:S(2)}, u32[]{:S(2)}) collective-permute-start(bf16[4,96,768]{2,1,0:T(8,128)(2,1)} %get-tuple-element.177), channel_id=1, source_target_pairs={{0,8},{4,12},{8,0},{12,4},{16,24},{20,28},{24,16},{28,20},{1,9},{5... | collective-permute-start | bytes 1769480 | tf_op jit(solution)/shard_map/ppermute | solution.py:448
  134.7 53.7 %all-to-all-start.2 = ((bf16[12,51,768]{2,1,0:T(8,128)(2,1)}), bf16[12,51,768]{2,1,0:T(8,128)(2,1)}, u32[]{:S(2)}, u32[]{:S(2)}) async-start(bf16[12,51,768]{2,1,0:T(8,128)(2,1)} %get-tuple-element.198), calls=%async_computation.2 | async-start | bytes 2064384 | tf_op jit(solution)/shard_map/all_to_all | solution.py:461
  142.1 20.2 %collective-permute-start.10 = (bf16[2,2,48,1664]{3,2,1,0:T(8,128)(2,1)}, bf16[2,2,48,1664]{3,2,1,0:T(8,128)(2,1)S(1)}, u32[]{:S(2)}, u32[]{:S(2)}) collective-permute-start(bf16[2,2,48,1664]{3,2,1,0:T(8,128)(2,1)} %get-tuple-element.175), channel_id=1, source_target_pairs={{0,16},{4,20},{8,24},{12,28},{16,0},{20,4},{24,8},{28,12},{1,17},{... | collective-permute-start | bytes 1916936 | tf_op jit(solution)/shard_map/ppermute | solution.py:448
  143.2 20.0 %collective-permute-start.9 = (bf16[2,2,48,1664]{3,2,1,0:T(8,128)(2,1)}, bf16[2,2,48,1664]{3,2,1,0:T(8,128)(2,1)}, u32[]{:S(2)}, u32[]{:S(2)}) collective-permute-start(bf16[2,2,48,1664]{3,2,1,0:T(8,128)(2,1)} %get-tuple-element.174), channel_id=1, source_target_pairs={{0,8},{4,12},{8,0},{12,4},{16,24},{20,28},{24,16},{28,20},{1,9},{5... | collective-permute-start | bytes 1916936 | tf_op jit(solution)/shard_map/ppermute | solution.py:448
  155.3 17.7 %collective-permute-start.13 = (bf16[4,96,768]{2,1,0:T(8,128)(2,1)}, bf16[4,96,768]{2,1,0:T(8,128)(2,1)S(1)}, u32[]{:S(2)}, u32[]{:S(2)}) collective-permute-start(bf16[4,96,768]{2,1,0:T(8,128)(2,1)} %get-tuple-element.191), channel_id=1, source_target_pairs={{0,1},{1,0},{2,3},{3,2},{4,5},{5,4},{6,7},{7,6},{8,9},{9,8},{10,11... | collective-permute-start | bytes 1769480 | tf_op jit(solution)/shard_map/ppermute | solution.py:670
  162.3 0.8 copy-start
  163.2 11.7 %copy-start.4 = (bf16[4,96,768]{2,1,0:T(8,128)(2,1)S(1)}, bf16[4,96,768]{2,1,0:T(8,128)(2,1)}, u32[]{:S(2)}) copy-start(bf16[4,96,768]{2,1,0:T(8,128)(2,1)} %get-tuple-element.187) | copy-start | bytes 1769476
  173.0 7.2 %collective-permute-start.14 = (bf16[2,48,1664]{2,1,0:T(8,128)(2,1)}, bf16[2,48,1664]{2,1,0:T(8,128)(2,1)S(1)}, u32[]{:S(2)}, u32[]{:S(2)}) collective-permute-start(bf16[2,48,1664]{2,1,0:T(8,128)(2,1)} %get-tuple-element.193), channel_id=1, source_target_pairs={{0,16},{4,20},{8,24},{12,28},{16,0},{20,4},{24,8},{28,12},{1,17},{... | collective-permute-start | bytes 958472 | tf_op jit(solution)/shard_map/ppermute | solution.py:448
  174.0 7.2 %collective-permute-start.15 = (bf16[2,48,1664]{2,1,0:T(8,128)(2,1)}, bf16[2,48,1664]{2,1,0:T(8,128)(2,1)S(1)}, u32[]{:S(2)}, u32[]{:S(2)}) collective-permute-start(bf16[2,48,1664]{2,1,0:T(8,128)(2,1)} %get-tuple-element.194), channel_id=1, source_target_pairs={{0,8},{4,12},{8,0},{12,4},{16,24},{20,28},{24,16},{28,20},{1,9},{5... | collective-permute-start | bytes 958472 | tf_op jit(solution)/shard_map/ppermute | solution.py:448
  175.0 13.3 %collective-permute-start.17 = (bf16[2,96,768]{2,1,0:T(8,128)(2,1)S(1)}, bf16[2,96,768]{2,1,0:T(8,128)(2,1)S(1)}, u32[]{:S(2)}, u32[]{:S(2)}) collective-permute-start(bf16[2,96,768]{2,1,0:T(8,128)(2,1)S(1)} %get-tuple-element.201), channel_id=1, source_target_pairs={{0,2},{1,3},{2,0},{3,1},{4,6},{5,7},{6,4},{7,5},{8,10},{9,11},{10,... | collective-permute-start | bytes 884744 | tf_op jit(solution)/shard_map/ppermute | solution.py:673
  180.2 1.0 copy-start.5
  181.2 0.7 copy-start.6
  185.5 15.3 %collective-permute-start.16 = (bf16[2,48,1664]{2,1,0:T(8,128)(2,1)}, bf16[2,48,1664]{2,1,0:T(8,128)(2,1)S(1)}, u32[]{:S(2)}, u32[]{:S(2)}) collective-permute-start(bf16[2,48,1664]{2,1,0:T(8,128)(2,1)} %get-tuple-element.197), channel_id=1, source_target_pairs={{0,1},{1,0},{2,3},{3,2},{4,5},{5,4},{6,7},{7,6},{8,9},{9,8},{10,11... | collective-permute-start | bytes 958472 | tf_op jit(solution)/shard_map/ppermute | solution.py:670
  185.6 17.5 %collective-permute-start.19 = (bf16[2,96,768]{2,1,0:T(8,128)(2,1)S(1)}, bf16[2,96,768]{2,1,0:T(8,128)(2,1)S(1)}, u32[]{:S(2)}, u32[]{:S(2)}) collective-permute-start(bf16[2,96,768]{2,1,0:T(8,128)(2,1)S(1)} %get-tuple-element.211), channel_id=1, source_target_pairs={{0,2},{1,3},{2,0},{3,1},{4,6},{5,7},{6,4},{7,5},{8,10},{9,11},{10,... | collective-permute-start | bytes 884744 | tf_op jit(solution)/shard_map/ppermute | solution.py:673
  188.3 12.6 %copy-start.10 = (bf16[2,96,768]{2,1,0:T(8,128)(2,1)}, bf16[2,96,768]{2,1,0:T(8,128)(2,1)S(1)}, u32[]{:S(2)}) copy-start(bf16[2,96,768]{2,1,0:T(8,128)(2,1)S(1)} %add.53.mine) | copy-start | bytes 884740
  188.3 12.5 %copy-start.8 = (bf16[2,48,1664]{2,1,0:T(8,128)(2,1)S(1)}, bf16[2,48,1664]{2,1,0:T(8,128)(2,1)}, u32[]{:S(2)}) copy-start(bf16[2,48,1664]{2,1,0:T(8,128)(2,1)} %get-tuple-element.207) | copy-start | bytes 958468
  200.9 15.2 %collective-permute-start.20 = (bf16[2,48,1664]{2,1,0:T(8,128)(2,1)S(1)}, bf16[2,48,1664]{2,1,0:T(8,128)(2,1)S(1)}, u32[]{:S(2)}, u32[]{:S(2)}) collective-permute-start(bf16[2,48,1664]{2,1,0:T(8,128)(2,1)S(1)} %add.54), channel_id=1, source_target_pairs={{0,2},{1,3},{2,0},{3,1},{4,6},{5,7},{6,4},{7,5},{8,10},{9,11},{10,... | collective-permute-start | bytes 958472 | tf_op jit(solution)/shard_map/ppermute | solution.py:673
  201.0 16.8 %collective-permute-start.18 = (bf16[2,96,768]{2,1,0:T(8,128)(2,1)S(1)}, bf16[2,96,768]{2,1,0:T(8,128)(2,1)S(1)}, u32[]{:S(2)}, u32[]{:S(2)}) collective-permute-start(bf16[2,96,768]{2,1,0:T(8,128)(2,1)S(1)} %add.53.mine), channel_id=1, source_target_pairs={{0,1},{1,0},{2,3},{3,2},{4,5},{5,4},{6,7},{7,6},{8,9},{9,8},{10,11... | collective-permute-start | bytes 884744 | tf_op jit(solution)/shard_map/ppermute | solution.py:670
  203.1 17.5 %copy-start.1 = (bf16[2,96,768]{2,1,0:T(8,128)(2,1)}, bf16[2,96,768]{2,1,0:T(8,128)(2,1)S(1)}, u32[]{:S(2)}) copy-start(bf16[2,96,768]{2,1,0:T(8,128)(2,1)S(1)} %add.55.mine) | copy-start | bytes 884740
  203.1 20.9 %collective-permute-start.22 = (bf16[2,96,768]{2,1,0:T(8,128)(2,1)S(1)}, bf16[2,96,768]{2,1,0:T(8,128)(2,1)S(1)}, u32[]{:S(2)}, u32[]{:S(2)}) collective-permute-start(bf16[2,96,768]{2,1,0:T(8,128)(2,1)S(1)} %add.55.mine), channel_id=1, source_target_pairs={{0,1},{1,0},{2,3},{3,2},{4,5},{5,4},{6,7},{7,6},{8,9},{9,8},{10,11... | collective-permute-start | bytes 884744 | tf_op jit(solution)/shard_map/ppermute | solution.py:670
  216.2 10.8 %copy-start.7 = (bf16[2,48,1664]{2,1,0:T(8,128)(2,1)}, bf16[2,48,1664]{2,1,0:T(8,128)(2,1)S(1)}, u32[]{:S(2)}) copy-start(bf16[2,48,1664]{2,1,0:T(8,128)(2,1)S(1)} %add.56) | copy-start | bytes 958468
  216.2 13.8 %collective-permute-start.21 = (bf16[2,48,1664]{2,1,0:T(8,128)(2,1)S(1)}, bf16[2,48,1664]{2,1,0:T(8,128)(2,1)S(1)}, u32[]{:S(2)}, u32[]{:S(2)}) collective-permute-start(bf16[2,48,1664]{2,1,0:T(8,128)(2,1)S(1)} %add.56), channel_id=1, source_target_pairs={{0,1},{1,0},{2,3},{3,2},{4,5},{5,4},{6,7},{7,6},{8,9},{9,8},{10,11... | collective-permute-start | bytes 958472 | tf_op jit(solution)/shard_map/ppermute | solution.py:670
  217.7 0.7 copy-start.21
  224.1 0.7 copy-start.9
  230.0 0.7 copy-start.20

commit v7 on v6

--- a/solution.py
+++ b/solution.py
@@ -218,8 +218,8 @@
 
 def heads_kernel(
     at, dy, prob, qkv, wp_any, wq_any, xs, dh, gain, a1t_any, ot_any, small2, db1,
-    out, small, flat, cs_any, ck, ds_any, dk_,
-    buf, dqkv, dys, wp, wq, a1t, ot, a1, o, cols, cs, ds_, sems, *, images, heads, part, ns,
+    out_any, small, flat, cs_any, ck_any, ds_any, dk_,
+    buf, dqkv, dys, wp, wq, a1t, ot, a1, o, cols, cs, ds_, out, ck, sems, *, images, heads, part, ns,
 ):
     i = pl.program_id(0)
     width = dy.shape[2]
@@ -305,7 +305,9 @@
     send = [
         pltpu.make_async_copy(cs, cs_any, sems.at[4]),
         pltpu.make_async_copy(ds_, ds_any, sems.at[5]),
+        pltpu.make_async_copy(out, out_any, sems.at[6]),
     ]
+    send_ck = pltpu.make_async_copy(ck, ck_any, sems.at[7])
     half = cs.shape[0]
     for step, lo, c_ref, d_ref in ((images, half, cs, ds_), (images + 1, 0, ck, dk_)):
 
@@ -317,11 +319,15 @@
                 o[:, lanes] = ot[n, lo : lo + half, :]
             c_ref[:, : 2 * width] = dot(a1[...], dqkv[:, : 2 * width]).astype(BF)
             c_ref[:, 2 * width :] = jnp.zeros((half, COLUMNS), BF)
+            if not lo:
+                send_ck.start()
             d_ref[:, :width] = dot(a1[...], dqkv[:, 2 * width :]).astype(BF)
             d_ref[:, width : 2 * width] = dot(o[...], dys[...]).astype(BF)
             d_ref[:, 2 * width :] = cols[lo : lo + half, :].astype(BF)
             for copy in send:
                 copy.start() if lo else copy.wait()
+            if not lo:
+                send_ck.wait()
 
 
 def settle_kernel(both, rows, specials):
@@ -632,8 +638,8 @@
                 whole((1, hidden)),
             ],
             out_specs=[
-                whole((images, part + ns, width)), whole((2, width)), whole((1, 3 * width)),
-                ANY, whole((half, wide)), ANY, whole((half, wide)),
+                ANY, whole((2, width)), whole((1, 3 * width)),
+                ANY, ANY, ANY, whole((half, wide)),
             ],
             scratch_shapes=[
                 pltpu.VMEM((padded, width), F32), pltpu.VMEM((total, 3 * width), BF),
@@ -641,7 +647,8 @@
                 pltpu.VMEM(qkv_weight.shape, BF), pltpu.VMEM(a1t.shape, BF), pltpu.VMEM(ot.shape, BF),
                 pltpu.VMEM((half, total), BF), pltpu.VMEM((half, total), BF),
                 pltpu.VMEM((width, COLUMNS), F32), pltpu.VMEM((half, wide), BF),
-                pltpu.VMEM((half, wide), BF), pltpu.SemaphoreType.DMA((6,)),
+                pltpu.VMEM((half, wide), BF), pltpu.VMEM((images, part + ns, width), BF),
+                pltpu.VMEM((half, wide), BF), pltpu.SemaphoreType.DMA((8,)),
             ],
         ),
         out_shape=[

time: 234 us -> 233 us (level)
  transfers between devices with their start and end apart: 26 -> 26, of which waited for: 17 -> 18; matrix products, arithmetic and copies ran while one was open for 2% -> 2% of each run, Pallas kernels for 30% -> 30%
where the time goes in v7:
time: 233 us
  Pallas kernels  107 us (46%)
  waiting for transfers between devices  76.2 us (33%)
  starting transfers between devices  38.2 us (16%)
  local copies, waits for them, and re-layouts  7.4 us (3%)
    pallas_call x1, Pallas kernels, shards(): pl.pallas_call(partial(feed_kernel, images=n), grid_spec=pltpu.PrefetchSc...  31.2 us
    pallas_call x1, Pallas kernels, shards(): pl.pallas_call(partial(heads_kernel, images=n, heads=heads, part=part, ns...  26.4 us
    ppermute x5, waiting for transfers between devices, near(): return lax.ppermute(v, 'seq', [(s, s ^ 1) for s in range(groups)])  24 us
    pallas_call x6, Pallas kernels, sums(): pl.pallas_call(partial(sum_kernel, jobs=leads, pick=at is not None), in_s...  20.9 us
    ppermute x12, waiting for transfers between devices, swap(): lax.ppermute(v, 'dp', [(s, s ^ bit) for s in range(lax.axis_size('dp'))])  20 us
    all_to_all x3, starting transfers between devices, exchange(): return lax.all_to_all(x, 'seq', split_axis=0, concat_axis=0, tiled=True)  16.6 us
    pallas_call x1, Pallas kernels, shards(): pl.pallas_call(partial(forward_kernel, rows=rows, heads=heads), grid_spec...  15.2 us
    ppermute x3, waiting for transfers between devices, far(): return lax.ppermute(v, 'seq', [(s, s ^ 2) for s in range(groups)])  13 us
  transfers between devices with their start and end apart: 26, of which 18 were waited for; matrix products, arithmetic and copies ran while one was open for 2% of the time, Pallas kernels for 30%

profile of v7, /device:TPU:0, one launch (start us, length us, event | category | flops | bytes accessed | tf_op | source)
XLA Modules:
  0.0 232.7 jit_solution(11562099239709001513)
XLA Ops:
  0.7 1.3 constant_dynamic-slice_fusion
  1.9 0.2 copy_bitcast_fusion
  2.4 4.1 %collective-permute-start.1 = (bf16[147,768]{1,0:T(8,128)(2,1)S(1)}, bf16[147,768]{1,0:T(8,128)(2,1)S(1)}, u32[]{:S(2)}, u32[]{:S(2)}) collective-permute-start(bf16[147,768]{1,0:T(8,128)(2,1)S(1)} %maximum_bitcast_fusion.1), channel_id=1, source_target_pairs={{0,2},{1,3},{2,0},{3,1},{4,6},{5,7},{6,4},{7,5},{8,10},{9,11},{10,... | collective-permute-start | bytes 677384 | tf_op jit(solution)/shard_map/ppermute | solution.py:515
  6.7 1.4 collective-permute-start.2
  8.4 0.7 collective-permute-start
  9.3 0.7 copy.49.keep
  10.1 1.0 pad_maximum_fusion
  11.1 7.8 %collective-permute-done.1.x2 = bf16[147,768]{1,0:T(8,128)(2,1)S(1)} collective-permute-done((bf16[147,768]{1,0:T(8,128)(2,1)S(1)}, bf16[147,768]{1,0:T(8,128)(2,1)S(1)}, u32[]{:S(2)}, u32[]{:S(2)}) %collective-permute-start.1) | collective-permute-done | bytes 225824 | tf_op jit(solution)/shard_map/ppermute | solution.py:515
  18.9 4.5 %collective-permute-done.x1 = bf16[147,768]{1,0:T(8,128)(2,1)S(1)} collective-permute-done((bf16[147,768]{1,0:T(8,128)(2,1)S(1)}, bf16[147,768]{1,0:T(8,128)(2,1)S(1)}, u32[]{:S(2)}, u32[]{:S(2)}) %collective-permute-start) | collective-permute-done | bytes 225824 | tf_op jit(solution)/shard_map/ppermute | solution.py:515
  23.4 7.7 %all-to-all-start = ((bf16[4,147,768]{2,1,0:T(8,128)(2,1)}), bf16[4,147,768]{2,1,0:T(8,128)(2,1)S(1)}, u32[]{:S(2)}, u32[]{:S(2)}) async-start(bf16[4,147,768]{2,1,0:T(8,128)(2,1)} %pad_maximum_fusion), calls=%async_computation | async-start | bytes 1867776 | tf_op jit(solution)/shard_map/all_to_all | solution.py:467
  31.2 0.6 reshape.132.g1.b1.bq.bp.g2.b2.gain
  31.9 0.6 pad_add_fusion.at.refs_0_
  32.5 15.2 %attention_forward.1 = (bf16[3,208,768]{2,1,0:T(8,128)(2,1)}, bf16[3,768,208]{2,1,0:T(8,128)(2,1)}, bf16[3,208,2304]{2,1,0:T(8,128)(2,1)}, bf16[3,6,416,208]{3,2...) custom-call(s32[2]{0:T(128)} %pad_add_fusion.at.refs_0_, ...), custom_call_target="tpu_custom_call" | custom-call | flops 4499999744 | bytes 1 | tf_op jit(solution)/shard_map/attention_forward/pallas_call | solution.py:534
  47.7 6.9 %all-to-all-done.g0.g1.g2.g3 = bf16[4,147,768]{2,1,0:T(8,128)(2,1)S(1)} async-done(((bf16[4,147,768]{2,1,0:T(8,128)(2,1)}), bf16[4,147,768]{2,1,0:T(8,128)(2,1)S(1)}, u32[]{:S(2)}, u32[]{:S(2)}) %all-to-all-start) | async-done | bytes 903200 | tf_op jit(solution)/shard_map/all_to_all | solution.py:467
  54.6 0.9 copy-done.2
  55.5 31.2 %feed_forward.1 = (bf16[12,51,768]{2,1,0:T(8,128)(2,1)}, f32[3,208,768]{2,1,0:T(8,128)}, bf16[3,208,768]{2,1,0:T(8,128)(2,1)}, bf16[1536,768]{1,0:T(8,128)(2,1)}...) custom-call(s32[2]{0:T(128)} %pad_add_fusion.at.refs_0_, ...), custom_call_target="tpu_custom_call" | custom-call | flops 8999999488 | bytes 1 | tf_op jit(solution)/shard_map/feed_forward/pallas_call | solution.py:565
  86.9 0.5 collective-permute-start.4
  87.4 4.4 %all-to-all-start.1 = ((bf16[12,51,768]{2,1,0:T(8,128)(2,1)}), bf16[12,51,768]{2,1,0:T(8,128)(2,1)}, u32[]{:S(2)}, u32[]{:S(2)}) async-start(bf16[12,51,768]{2,1,0:T(8,128)(2,1)} %get-tuple-element.157), calls=%async_computation.1 | async-start | bytes 2064384 | tf_op jit(solution)/shard_map/all_to_all | solution.py:467
  91.8 3.3 %collective-permute-done.4 = bf16[1536,768]{1,0:T(8,128)(2,1)} collective-permute-done((bf16[1536,768]{1,0:T(8,128)(2,1)}, bf16[1536,768]{1,0:T(8,128)(2,1)}, u32[]{:S(2)}, u32[]{:S(2)}) %collective-permute-start.4) | collective-permute-done | bytes 2359328 | tf_op jit(solution)/shard_map/ppermute | solution.py:454
  95.1 4.0 %sums.6 = (bf16[2,4,96,768]{3,2,1,0:T(8,128)(2,1)}, bf16[2,4,96,768]{3,2,1,0:T(8,128)(2,1)}) custom-call(bf16[2,2,4,96,768]{4,3,2,1,0:T(8,128)(2,1)} %bitcast.48, bf16[2,2,4,96,768]{4,3,2,1,0:T(8,128)(2,1)} %bitcast.18.refs_1_.refs_2_, bf16[2,2,4,96,768]{4,3,2,1,0:T(8,128)(2,1)} %bitcast.45, bf16[2,2,4,96,768]{4,3,2,1,0:T(8,128)(2,1)} %bitcast.20.refs_3_.refs_4_.refs_6_), custom_call_target="tpu_custom_call" | custom-call | flops 600000000 | bytes 1 | tf_op jit(solution)/shard_map/sums/pallas_call | solution.py:383
  99.2 1.6 collective-permute-start.5
  100.7 1.5 collective-permute-start.6
  102.2 26.4 %attention_backward.1 = (bf16[12,51,768]{2,1,0:T(8,128)(2,1)}, f32[2,768]{1,0:T(2,128)}, f32[1,2304]{1,0:T(1,128)}, bf16[384,1664]{1,0:T(8,128)(2,1)}, bf16[384,...) custom-call(s32[2]{0:T(128)} %pad_add_fusion.at.refs_0_, ...), custom_call_target="tpu_custom_call" | custom-call | flops 6600000000 | bytes 1 | tf_op jit(solution)/shard_map/attention_backward/pallas_call | solution.py:629
  128.7 0.1 collective-permute-done.6.refs_5_.refs_7_
  128.8 3.2 %sums.7 = (bf16[4,96,768]{2,1,0:T(8,128)(2,1)}, bf16[4,96,768]{2,1,0:T(8,128)(2,1)}) custom-call(bf16[2,2,4,96,768]{4,3,2,1,0:T(8,128)(2,1)} %bitcast.49, bf16[2,2,4,96,768]{4,3,2,1,0:T(8,128)(2,1)} %bitcast.18.refs_1_.refs_2_, bf16[2,4,96,768]{3,2,1,0:T(8,128)(2,1)} %collective-permute-done.5.refs_2_.refs_3_, bf16[2,2,4,96,768]{4,3,2,1,0:T(8,128)(2,1)} %bitcast.46, ...), custom_call_target="tpu_custom_call" | custom-call | flops 600000000 | bytes 1 | tf_op jit(solution)/shard_map/sums/pallas_call | solution.py:383
  132.1 0.5 collective-permute-start.8
  132.6 1.5 collective-permute-start.11
  134.1 0.6 collective-permute-start.12
  134.7 4.5 %all-to-all-start.2 = ((bf16[12,51,768]{2,1,0:T(8,128)(2,1)}), bf16[12,51,768]{2,1,0:T(8,128)(2,1)}, u32[]{:S(2)}, u32[]{:S(2)}) async-start(bf16[12,51,768]{2,1,0:T(8,128)(2,1)} %get-tuple-element.198), calls=%async_computation.2 | async-start | bytes 2064384 | tf_op jit(solution)/shard_map/all_to_all | solution.py:467
  139.2 2.9 %sums.8 = (bf16[2,2,48,1664]{3,2,1,0:T(8,128)(2,1)}, bf16[2,2,48,1664]{3,2,1,0:T(8,128)(2,1)}) custom-call(bf16[2,2,2,48,1664]{4,3,2,1,0:T(8,128)(2,1)} %bitcast.51, bf16[2,2,2,48,1664]{4,3,2,1,0:T(8,128)(2,1)} %bitcast.22.refs_1_.refs_2_, bf16[2,2,2,48,1664]{4,3,2,1,0:T(8,128)(2,1)} %bitcast.54, bf16[2,2,2,48,1664]{4,3,2,1,0:T(8,128)(2,1)} %bitcast.24.refs_3_.refs_4_.refs_6_), custom_call_target="tpu_custom_call" | custom-call | flops 600000000 | bytes 1 | tf_op jit(solution)/shard_map/sums/pallas_call | solution.py:383
  142.1 0.5 collective-permute-start.10
  142.6 1.5 collective-permute-start.9
  144.1 5.0 %collective-permute-done.11.refs_4_ = bf16[4,96,768]{2,1,0:T(8,128)(2,1)} collective-permute-done((bf16[4,96,768]{2,1,0:T(8,128)(2,1)}, bf16[4,96,768]{2,1,0:T(8,128)(2,1)}, u32[]{:S(2)}, u32[]{:S(2)}) %collective-permute-start.11) | collective-permute-done | bytes 589856 | tf_op jit(solution)/shard_map/ppermute | solution.py:454
  149.1 1.5 collective-permute-done.12.refs_8_
  150.6 4.6 %sums.9 = (bf16[4,96,768]{2,1,0:T(8,128)(2,1)}, bf16[4,96,768]{2,1,0:T(8,128)(2,1)}) custom-call(s32[2]{0:T(128)} %pad_add_fusion.at.refs_0_, bf16[2,2,4,96,768]{4,3,2,1,0:T(8,128)(2,1)} %bitcast.50, bf16[2,2,4,96,768]{4,3,2,1,0:T(8,128)(2,1)} %bitcast.18.refs_1_.refs_2_, bf16[2,4,96,768]{3,2,1,0:T(8,128)(2,1)} %collective-permute-done.5.refs_2_.refs_3_, ...), custom_call_target="tpu_custom_call" | custom-call | flops 600000000 | bytes 1 | tf_op jit(solution)/shard_map/sums/pallas_call | solution.py:383
  155.4 3.4 %settle.2 = (bf16[12,49,768]{2,1,0:T(8,128)(2,1)}, bf16[12,2,768]{2,1,0:T(2,128)(2,1)}) custom-call(bf16[12,51,768]{2,1,0:T(8,128)(2,1)} %all-to-all-done.1.both), custom_call_target="tpu_custom_call" | custom-call | flops 600000000 | bytes 1 | tf_op jit(solution)/shard_map/settle/pallas_call | solution.py:473
  158.8 3.1 %collective-permute-done.10.refs_5_.refs_7_ = bf16[2,2,48,1664]{3,2,1,0:T(8,128)(2,1)S(1)} collective-permute-done((bf16[2,2,48,1664]{3,2,1,0:T(8,128)(2,1)}, bf16[2,2,48,1664]{3,2,1,0:T(8,128)(2,1)S(1)}, u32[]{:S(2)}, u32[]{:S(2)}) %collective-permute-start.10) | collective-permute-done | bytes 639008 | tf_op jit(solution)/shard_map/ppermute | solution.py:454
  161.8 1.3 collective-permute-done.9.refs_2_.refs_3_
  163.2 2.5 %sums.10 = (bf16[2,48,1664]{2,1,0:T(8,128)(2,1)}, bf16[2,48,1664]{2,1,0:T(8,128)(2,1)}) custom-call(bf16[2,2,2,48,1664]{4,3,2,1,0:T(8,128)(2,1)} %bitcast.52, bf16[2,2,2,48,1664]{4,3,2,1,0:T(8,128)(2,1)} %bitcast.22.refs_1_.refs_2_, bf16[2,2,48,1664]{3,2,1,0:T(8,128)(2,1)} %collective-permute-done.9.refs_2_.refs_3_, bf16[2,2,2,48,1664]{4,3,2,1,0:T(8,128)(2,1)} %bitcast.55, ...), custom_call_target="tpu_custom_call" | custom-call | flops 600000000 | bytes 1 | tf_op jit(solution)/shard_map/sums/pallas_call | solution.py:383
  165.7 7.3 %collective-permute-done.13 = bf16[4,96,768]{2,1,0:T(8,128)(2,1)S(1)} collective-permute-done((bf16[4,96,768]{2,1,0:T(8,128)(2,1)}, bf16[4,96,768]{2,1,0:T(8,128)(2,1)S(1)}, u32[]{:S(2)}, u32[]{:S(2)}) %collective-permute-start.13) | collective-permute-done | bytes 589856 | tf_op jit(solution)/shard_map/ppermute | solution.py:677
  173.0 0.6 collective-permute-start.14
  173.6 0.8 collective-permute-start.15
  174.4 0.1 add.52
  174.6 0.6 collective-permute-start.17
  175.1 5.1 %collective-permute-done.14.refs_4_ = bf16[2,48,1664]{2,1,0:T(8,128)(2,1)S(1)} collective-permute-done((bf16[2,48,1664]{2,1,0:T(8,128)(2,1)}, bf16[2,48,1664]{2,1,0:T(8,128)(2,1)S(1)}, u32[]{:S(2)}, u32[]{:S(2)}) %collective-permute-start.14) | collective-permute-done | bytes 319520 | tf_op jit(solution)/shard_map/ppermute | solution.py:454
  180.2 0.6 collective-permute-done.15.refs_8_
  180.9 0.6 copy-done.6
  181.5 3.5 %sums.11 = (bf16[2,48,1664]{2,1,0:T(8,128)(2,1)}, bf16[2,48,1664]{2,1,0:T(8,128)(2,1)}) custom-call(s32[2]{0:T(128)} %pad_add_fusion.at.refs_0_, bf16[2,2,2,48,1664]{4,3,2,1,0:T(8,128)(2,1)} %bitcast.53, bf16[2,2,2,48,1664]{4,3,2,1,0:T(8,128)(2,1)} %bitcast.22.refs_1_.refs_2_, bf16[2,2,48,1664]{3,2,1,0:T(8,128)(2,1)} %collective-permute-done.9.refs_2_.refs_3_, ...), custom_call_target="tpu_custom_call" | custom-call | flops 600000000 | bytes 1 | tf_op jit(solution)/shard_map/sums/pallas_call | solution.py:383
  185.2 2.3 collective-permute-start.19
  187.4 0.4 collective-permute-done.17
  187.9 3.5 %settle.3 = (bf16[12,49,768]{2,1,0:T(8,128)(2,1)}, bf16[12,2,768]{2,1,0:T(2,128)(2,1)}) custom-call(bf16[12,51,768]{2,1,0:T(8,128)(2,1)} %all-to-all-done.2.both), custom_call_target="tpu_custom_call" | custom-call | flops 600000000 | bytes 1 | tf_op jit(solution)/shard_map/settle/pallas_call | solution.py:473
  191.4 8.9 %collective-permute-done.16 = bf16[2,48,1664]{2,1,0:T(8,128)(2,1)S(1)} collective-permute-done((bf16[2,48,1664]{2,1,0:T(8,128)(2,1)}, bf16[2,48,1664]{2,1,0:T(8,128)(2,1)S(1)}, u32[]{:S(2)}, u32[]{:S(2)}) %collective-permute-start.16) | collective-permute-done | bytes 319520 | tf_op jit(solution)/shard_map/ppermute | solution.py:677
  200.4 0.2 collective-permute-start.20
  200.6 2.3 %collective-permute-start.18 = (bf16[2,96,768]{2,1,0:T(8,128)(2,1)S(1)}, bf16[2,96,768]{2,1,0:T(8,128)(2,1)S(1)}, u32[]{:S(2)}, u32[]{:S(2)}) collective-permute-start(bf16[2,96,768]{2,1,0:T(8,128)(2,1)S(1)} %add.53.mine), channel_id=1, source_target_pairs={{0,1},{1,0},{2,3},{3,2},{4,5},{5,4},{6,7},{7,6},{8,9},{9,8},{10,11... | collective-permute-start | bytes 884744 | tf_op jit(solution)/shard_map/ppermute | solution.py:677
  203.1 12.6 %collective-permute-done.20 = bf16[2,48,1664]{2,1,0:T(8,128)(2,1)S(1)} collective-permute-done((bf16[2,48,1664]{2,1,0:T(8,128)(2,1)S(1)}, bf16[2,48,1664]{2,1,0:T(8,128)(2,1)S(1)}, u32[]{:S(2)}, u32[]{:S(2)}) %collective-permute-start.20) | collective-permute-done | bytes 319520 | tf_op jit(solution)/shard_map/ppermute | solution.py:680
  215.9 1.8 collective-permute-done.18.other
  217.7 0.7 copy-done.21
  218.4 2.2 finish_feed.2
  220.6 3.4 %collective-permute-done.22.other = bf16[2,96,768]{2,1,0:T(8,128)(2,1)S(1)} collective-permute-done((bf16[2,96,768]{2,1,0:T(8,128)(2,1)S(1)}, bf16[2,96,768]{2,1,0:T(8,128)(2,1)S(1)}, u32[]{:S(2)}, u32[]{:S(2)}) %collective-permute-start.22) | collective-permute-done | bytes 294944 | tf_op jit(solution)/shard_map/ppermute | solution.py:677
  224.0 0.7 copy-done.9
  224.7 2.2 finish_feed.3
  226.9 2.6 %collective-permute-done.21 = bf16[2,48,1664]{2,1,0:T(8,128)(2,1)S(1)} collective-permute-done((bf16[2,48,1664]{2,1,0:T(8,128)(2,1)S(1)}, bf16[2,48,1664]{2,1,0:T(8,128)(2,1)S(1)}, u32[]{:S(2)}, u32[]{:S(2)}) %collective-permute-start.21) | collective-permute-done | bytes 319520 | tf_op jit(solution)/shard_map/ppermute | solution.py:677
  229.5 0.7 copy-done.20
  230.3 2.2 finish.1
  (91 shorter events, 1.8 us)
Async XLA Ops:
  2.4 16.5 %collective-permute-start.1 = (bf16[147,768]{1,0:T(8,128)(2,1)S(1)}, bf16[147,768]{1,0:T(8,128)(2,1)S(1)}, u32[]{:S(2)}, u32[]{:S(2)}) collective-permute-start(bf16[147,768]{1,0:T(8,128)(2,1)S(1)} %maximum_bitcast_fusion.1), channel_id=1, source_target_pairs={{0,2},{1,3},{2,0},{3,1},{4,6},{5,7},{6,4},{7,5},{8,10},{9,11},{10,... | collective-permute-start | bytes 677384 | tf_op jit(solution)/shard_map/ppermute | solution.py:515
  6.6 2.5 %copy-start.3 = (bf16[12,49,768]{2,1,0:T(8,128)(2,1)S(1)}, bf16[12,49,768]{2,1,0:T(8,128)(2,1)}, u32[]{:S(2)}) copy-start(bf16[12,49,768]{2,1,0:T(8,128)(2,1)} %param.32) | copy-start | bytes 2709508
  6.7 12.3 %collective-permute-start.2 = (bf16[147,768]{1,0:T(8,128)(2,1)S(1)}, bf16[147,768]{1,0:T(8,128)(2,1)S(1)}, u32[]{:S(2)}, u32[]{:S(2)}) collective-permute-start(bf16[147,768]{1,0:T(8,128)(2,1)S(1)} %maximum_bitcast_fusion.2), channel_id=1, source_target_pairs={{0,3},{1,0},{2,1},{3,2},{4,7},{5,4},{6,5},{7,6},{8,11},{9,8},{10,9... | collective-permute-start | bytes 677384 | tf_op jit(solution)/shard_map/ppermute | solution.py:515
  8.3 0.9 copy-start.19
  8.4 1.6 copy-start.11
  8.4 1.6 copy-start.12
  8.4 1.6 copy-start.13
  8.4 1.7 copy-start.14
  8.4 15.0 %collective-permute-start = (bf16[147,768]{1,0:T(8,128)(2,1)S(1)}, bf16[147,768]{1,0:T(8,128)(2,1)S(1)}, u32[]{:S(2)}, u32[]{:S(2)}) collective-permute-start(bf16[147,768]{1,0:T(8,128)(2,1)S(1)} %maximum_bitcast_fusion), channel_id=1, source_target_pairs={{0,1},{1,2},{2,3},{3,0},{4,5},{5,6},{6,7},{7,4},{8,9},{9,10},{10,1... | collective-permute-start | bytes 677384 | tf_op jit(solution)/shard_map/ppermute | solution.py:515
  11.1 20.0 %copy-start.15 = (bf16[768]{0:T(1024)(128)(2,1)S(1)}, bf16[768]{0:T(1024)(128)(2,1)}, u32[]{:S(2)}) copy-start(bf16[768]{0:T(1024)(128)(2,1)} %param.25) | copy-start | bytes 4612
  11.1 20.0 %copy-start.16 = (bf16[768]{0:T(1024)(128)(2,1)S(1)}, bf16[768]{0:T(1024)(128)(2,1)}, u32[]{:S(2)}) copy-start(bf16[768]{0:T(1024)(128)(2,1)} %param.26) | copy-start | bytes 4612
  11.1 20.1 %copy-start.17 = (bf16[768]{0:T(1024)(128)(2,1)S(1)}, bf16[768]{0:T(1024)(128)(2,1)}, u32[]{:S(2)}) copy-start(bf16[768]{0:T(1024)(128)(2,1)} %param.27) | copy-start | bytes 4612
  11.1 20.1 %copy-start.18 = (bf16[768]{0:T(1024)(128)(2,1)S(1)}, bf16[768]{0:T(1024)(128)(2,1)}, u32[]{:S(2)}) copy-start(bf16[768]{0:T(1024)(128)(2,1)} %param.31) | copy-start | bytes 4612
  18.9 12.9 %copy-start.22 = (bf16[147,768]{1,0:T(8,128)(2,1)}, bf16[147,768]{1,0:T(8,128)(2,1)S(1)}, u32[]{:S(2)}) copy-start(bf16[147,768]{1,0:T(8,128)(2,1)S(1)} %collective-permute-done.1.x2) | copy-start | bytes 677380
  18.9 12.9 %copy-start.23 = (bf16[147,768]{1,0:T(8,128)(2,1)}, bf16[147,768]{1,0:T(8,128)(2,1)S(1)}, u32[]{:S(2)}) copy-start(bf16[147,768]{1,0:T(8,128)(2,1)S(1)} %collective-permute-done.2.x3) | copy-start | bytes 677380
  23.4 8.5 %copy-start.24 = (bf16[147,768]{1,0:T(8,128)(2,1)}, bf16[147,768]{1,0:T(8,128)(2,1)S(1)}, u32[]{:S(2)}) copy-start(bf16[147,768]{1,0:T(8,128)(2,1)S(1)} %collective-permute-done.x1) | copy-start | bytes 677380
  23.4 31.2 %all-to-all-start = ((bf16[4,147,768]{2,1,0:T(8,128)(2,1)}), bf16[4,147,768]{2,1,0:T(8,128)(2,1)S(1)}, u32[]{:S(2)}, u32[]{:S(2)}) async-start(bf16[4,147,768]{2,1,0:T(8,128)(2,1)} %pad_maximum_fusion), calls=%async_computation | async-start | bytes 1867776 | tf_op jit(solution)/shard_map/all_to_all | solution.py:467
  54.6 0.9 copy-start.2
  86.8 5.0 %collective-permute-start.3 = (bf16[4,4,96,768]{3,2,1,0:T(8,128)(2,1)}, bf16[4,4,96,768]{3,2,1,0:T(8,128)(2,1)}, u32[]{:S(2)}, u32[]{:S(2)}) collective-permute-start(bf16[4,4,96,768]{3,2,1,0:T(8,128)(2,1)} %get-tuple-element.136), channel_id=1, source_target_pairs={{0,4},{4,0},{8,12},{12,8},{16,20},{20,16},{24,28},{28,24},{1,5},{5... | collective-permute-start | bytes 7077896 | tf_op jit(solution)/shard_map/ppermute | solution.py:454
  86.9 8.2 %collective-permute-start.4 = (bf16[1536,768]{1,0:T(8,128)(2,1)}, bf16[1536,768]{1,0:T(8,128)(2,1)}, u32[]{:S(2)}, u32[]{:S(2)}) collective-permute-start(bf16[1536,768]{1,0:T(8,128)(2,1)} %get-tuple-element.137), channel_id=1, source_target_pairs={{0,4},{4,0},{8,12},{12,8},{16,20},{20,16},{24,28},{28,24},{1,5},{5... | collective-permute-start | bytes 7077896 | tf_op jit(solution)/shard_map/ppermute | solution.py:454
  87.4 41.3 %all-to-all-start.1 = ((bf16[12,51,768]{2,1,0:T(8,128)(2,1)}), bf16[12,51,768]{2,1,0:T(8,128)(2,1)}, u32[]{:S(2)}, u32[]{:S(2)}) async-start(bf16[12,51,768]{2,1,0:T(8,128)(2,1)} %get-tuple-element.157), calls=%async_computation.1 | async-start | bytes 2064384 | tf_op jit(solution)/shard_map/all_to_all | solution.py:467
  99.2 29.5 %collective-permute-start.5 = (bf16[2,4,96,768]{3,2,1,0:T(8,128)(2,1)}, bf16[2,4,96,768]{3,2,1,0:T(8,128)(2,1)}, u32[]{:S(2)}, u32[]{:S(2)}) collective-permute-start(bf16[2,4,96,768]{3,2,1,0:T(8,128)(2,1)} %get-tuple-element.144), channel_id=1, source_target_pairs={{0,8},{4,12},{8,0},{12,4},{16,24},{20,28},{24,16},{28,20},{1,9},{5... | collective-permute-start | bytes 3538952 | tf_op jit(solution)/shard_map/ppermute | solution.py:454
  100.7 28.0 %collective-permute-start.6 = (bf16[2,4,96,768]{3,2,1,0:T(8,128)(2,1)}, bf16[2,4,96,768]{3,2,1,0:T(8,128)(2,1)}, u32[]{:S(2)}, u32[]{:S(2)}) collective-permute-start(bf16[2,4,96,768]{3,2,1,0:T(8,128)(2,1)} %get-tuple-element.145), channel_id=1, source_target_pairs={{0,16},{4,20},{8,24},{12,28},{16,0},{20,4},{24,8},{28,12},{1,17},{... | collective-permute-start | bytes 3538952 | tf_op jit(solution)/shard_map/ppermute | solution.py:454
  132.0 7.1 %collective-permute-start.7 = (bf16[384,1664]{1,0:T(8,128)(2,1)}, bf16[384,1664]{1,0:T(8,128)(2,1)}, u32[]{:S(2)}, u32[]{:S(2)}) collective-permute-start(bf16[384,1664]{1,0:T(8,128)(2,1)} %get-tuple-element.166), channel_id=1, source_target_pairs={{0,4},{4,0},{8,12},{12,8},{16,20},{20,16},{24,28},{28,24},{1,5},{5... | collective-permute-start | bytes 3833864 | tf_op jit(solution)/shard_map/ppermute | solution.py:454
  132.1 7.1 %collective-permute-start.8 = (bf16[384,1664]{1,0:T(8,128)(2,1)}, bf16[384,1664]{1,0:T(8,128)(2,1)}, u32[]{:S(2)}, u32[]{:S(2)}) collective-permute-start(bf16[384,1664]{1,0:T(8,128)(2,1)} %get-tuple-element.167), channel_id=1, source_target_pairs={{0,4},{4,0},{8,12},{12,8},{16,20},{20,16},{24,28},{28,24},{1,5},{5... | collective-permute-start | bytes 3833864 | tf_op jit(solution)/shard_map/ppermute | solution.py:454
  132.6 16.5 %collective-permute-start.11 = (bf16[4,96,768]{2,1,0:T(8,128)(2,1)}, bf16[4,96,768]{2,1,0:T(8,128)(2,1)}, u32[]{:S(2)}, u32[]{:S(2)}) collective-permute-start(bf16[4,96,768]{2,1,0:T(8,128)(2,1)} %get-tuple-element.176), channel_id=1, source_target_pairs={{0,16},{4,20},{8,24},{12,28},{16,0},{20,4},{24,8},{28,12},{1,17},{... | collective-permute-start | bytes 1769480 | tf_op jit(solution)/shard_map/ppermute | solution.py:454
  134.1 16.5 %collective-permute-start.12 = (bf16[4,96,768]{2,1,0:T(8,128)(2,1)}, bf16[4,96,768]{2,1,0:T(8,128)(2,1)}, u32[]{:S(2)}, u32[]{:S(2)}) collective-permute-start(bf16[4,96,768]{2,1,0:T(8,128)(2,1)} %get-tuple-element.177), channel_id=1, source_target_pairs={{0,8},{4,12},{8,0},{12,4},{16,24},{20,28},{24,16},{28,20},{1,9},{5... | collective-permute-start | bytes 1769480 | tf_op jit(solution)/shard_map/ppermute | solution.py:454
  134.7 53.2 %all-to-all-start.2 = ((bf16[12,51,768]{2,1,0:T(8,128)(2,1)}), bf16[12,51,768]{2,1,0:T(8,128)(2,1)}, u32[]{:S(2)}, u32[]{:S(2)}) async-start(bf16[12,51,768]{2,1,0:T(8,128)(2,1)} %get-tuple-element.198), calls=%async_computation.2 | async-start | bytes 2064384 | tf_op jit(solution)/shard_map/all_to_all | solution.py:467
  142.1 19.8 %collective-permute-start.10 = (bf16[2,2,48,1664]{3,2,1,0:T(8,128)(2,1)}, bf16[2,2,48,1664]{3,2,1,0:T(8,128)(2,1)S(1)}, u32[]{:S(2)}, u32[]{:S(2)}) collective-permute-start(bf16[2,2,48,1664]{3,2,1,0:T(8,128)(2,1)} %get-tuple-element.175), channel_id=1, source_target_pairs={{0,16},{4,20},{8,24},{12,28},{16,0},{20,4},{24,8},{28,12},{1,17},{... | collective-permute-start | bytes 1916936 | tf_op jit(solution)/shard_map/ppermute | solution.py:454
  142.6 20.6 %collective-permute-start.9 = (bf16[2,2,48,1664]{3,2,1,0:T(8,128)(2,1)}, bf16[2,2,48,1664]{3,2,1,0:T(8,128)(2,1)}, u32[]{:S(2)}, u32[]{:S(2)}) collective-permute-start(bf16[2,2,48,1664]{3,2,1,0:T(8,128)(2,1)} %get-tuple-element.174), channel_id=1, source_target_pairs={{0,8},{4,12},{8,0},{12,4},{16,24},{20,28},{24,16},{28,20},{1,9},{5... | collective-permute-start | bytes 1916936 | tf_op jit(solution)/shard_map/ppermute | solution.py:454
  155.3 17.7 %collective-permute-start.13 = (bf16[4,96,768]{2,1,0:T(8,128)(2,1)}, bf16[4,96,768]{2,1,0:T(8,128)(2,1)S(1)}, u32[]{:S(2)}, u32[]{:S(2)}) collective-permute-start(bf16[4,96,768]{2,1,0:T(8,128)(2,1)} %get-tuple-element.191), channel_id=1, source_target_pairs={{0,1},{1,0},{2,3},{3,2},{4,5},{5,4},{6,7},{7,6},{8,9},{9,8},{10,11... | collective-permute-start | bytes 1769480 | tf_op jit(solution)/shard_map/ppermute | solution.py:677
  161.8 1.3 copy-start
  163.2 11.2 %copy-start.4 = (bf16[4,96,768]{2,1,0:T(8,128)(2,1)S(1)}, bf16[4,96,768]{2,1,0:T(8,128)(2,1)}, u32[]{:S(2)}) copy-start(bf16[4,96,768]{2,1,0:T(8,128)(2,1)} %get-tuple-element.187) | copy-start | bytes 1769476
  173.0 7.2 %collective-permute-start.14 = (bf16[2,48,1664]{2,1,0:T(8,128)(2,1)}, bf16[2,48,1664]{2,1,0:T(8,128)(2,1)S(1)}, u32[]{:S(2)}, u32[]{:S(2)}) collective-permute-start(bf16[2,48,1664]{2,1,0:T(8,128)(2,1)} %get-tuple-element.193), channel_id=1, source_target_pairs={{0,16},{4,20},{8,24},{12,28},{16,0},{20,4},{24,8},{28,12},{1,17},{... | collective-permute-start | bytes 958472 | tf_op jit(solution)/shard_map/ppermute | solution.py:454
  173.6 7.2 %collective-permute-start.15 = (bf16[2,48,1664]{2,1,0:T(8,128)(2,1)}, bf16[2,48,1664]{2,1,0:T(8,128)(2,1)S(1)}, u32[]{:S(2)}, u32[]{:S(2)}) collective-permute-start(bf16[2,48,1664]{2,1,0:T(8,128)(2,1)} %get-tuple-element.194), channel_id=1, source_target_pairs={{0,8},{4,12},{8,0},{12,4},{16,24},{20,28},{24,16},{28,20},{1,9},{5... | collective-permute-start | bytes 958472 | tf_op jit(solution)/shard_map/ppermute | solution.py:454
  174.6 13.3 %collective-permute-start.17 = (bf16[2,96,768]{2,1,0:T(8,128)(2,1)S(1)}, bf16[2,96,768]{2,1,0:T(8,128)(2,1)S(1)}, u32[]{:S(2)}, u32[]{:S(2)}) collective-permute-start(bf16[2,96,768]{2,1,0:T(8,128)(2,1)S(1)} %get-tuple-element.201), channel_id=1, source_target_pairs={{0,2},{1,3},{2,0},{3,1},{4,6},{5,7},{6,4},{7,5},{8,10},{9,11},{10,... | collective-permute-start | bytes 884744 | tf_op jit(solution)/shard_map/ppermute | solution.py:680
  180.2 0.7 copy-start.5
  180.8 0.7 copy-start.6
  185.1 15.3 %collective-permute-start.16 = (bf16[2,48,1664]{2,1,0:T(8,128)(2,1)}, bf16[2,48,1664]{2,1,0:T(8,128)(2,1)S(1)}, u32[]{:S(2)}, u32[]{:S(2)}) collective-permute-start(bf16[2,48,1664]{2,1,0:T(8,128)(2,1)} %get-tuple-element.197), channel_id=1, source_target_pairs={{0,1},{1,0},{2,3},{3,2},{4,5},{5,4},{6,7},{7,6},{8,9},{9,8},{10,11... | collective-permute-start | bytes 958472 | tf_op jit(solution)/shard_map/ppermute | solution.py:677
  185.2 17.8 %collective-permute-start.19 = (bf16[2,96,768]{2,1,0:T(8,128)(2,1)S(1)}, bf16[2,96,768]{2,1,0:T(8,128)(2,1)S(1)}, u32[]{:S(2)}, u32[]{:S(2)}) collective-permute-start(bf16[2,96,768]{2,1,0:T(8,128)(2,1)S(1)} %get-tuple-element.211), channel_id=1, source_target_pairs={{0,2},{1,3},{2,0},{3,1},{4,6},{5,7},{6,4},{7,5},{8,10},{9,11},{10,... | collective-permute-start | bytes 884744 | tf_op jit(solution)/shard_map/ppermute | solution.py:680
  187.9 12.7 %copy-start.10 = (bf16[2,96,768]{2,1,0:T(8,128)(2,1)}, bf16[2,96,768]{2,1,0:T(8,128)(2,1)S(1)}, u32[]{:S(2)}) copy-start(bf16[2,96,768]{2,1,0:T(8,128)(2,1)S(1)} %add.53.mine) | copy-start | bytes 884740
  187.9 12.4 %copy-start.8 = (bf16[2,48,1664]{2,1,0:T(8,128)(2,1)S(1)}, bf16[2,48,1664]{2,1,0:T(8,128)(2,1)}, u32[]{:S(2)}) copy-start(bf16[2,48,1664]{2,1,0:T(8,128)(2,1)} %get-tuple-element.207) | copy-start | bytes 958468
  200.4 15.3 %collective-permute-start.20 = (bf16[2,48,1664]{2,1,0:T(8,128)(2,1)S(1)}, bf16[2,48,1664]{2,1,0:T(8,128)(2,1)S(1)}, u32[]{:S(2)}, u32[]{:S(2)}) collective-permute-start(bf16[2,48,1664]{2,1,0:T(8,128)(2,1)S(1)} %add.54), channel_id=1, source_target_pairs={{0,2},{1,3},{2,0},{3,1},{4,6},{5,7},{6,4},{7,5},{8,10},{9,11},{10,... | collective-permute-start | bytes 958472 | tf_op jit(solution)/shard_map/ppermute | solution.py:680
  200.6 17.0 %collective-permute-start.18 = (bf16[2,96,768]{2,1,0:T(8,128)(2,1)S(1)}, bf16[2,96,768]{2,1,0:T(8,128)(2,1)S(1)}, u32[]{:S(2)}, u32[]{:S(2)}) collective-permute-start(bf16[2,96,768]{2,1,0:T(8,128)(2,1)S(1)} %add.53.mine), channel_id=1, source_target_pairs={{0,1},{1,0},{2,3},{3,2},{4,5},{5,4},{6,7},{7,6},{8,9},{9,8},{10,11... | collective-permute-start | bytes 884744 | tf_op jit(solution)/shard_map/ppermute | solution.py:677
  203.1 17.5 %copy-start.1 = (bf16[2,96,768]{2,1,0:T(8,128)(2,1)}, bf16[2,96,768]{2,1,0:T(8,128)(2,1)S(1)}, u32[]{:S(2)}) copy-start(bf16[2,96,768]{2,1,0:T(8,128)(2,1)S(1)} %add.55.mine) | copy-start | bytes 884740
  203.1 20.9 %collective-permute-start.22 = (bf16[2,96,768]{2,1,0:T(8,128)(2,1)S(1)}, bf16[2,96,768]{2,1,0:T(8,128)(2,1)S(1)}, u32[]{:S(2)}, u32[]{:S(2)}) collective-permute-start(bf16[2,96,768]{2,1,0:T(8,128)(2,1)S(1)} %add.55.mine), channel_id=1, source_target_pairs={{0,1},{1,0},{2,3},{3,2},{4,5},{5,4},{6,7},{7,6},{8,9},{9,8},{10,11... | collective-permute-start | bytes 884744 | tf_op jit(solution)/shard_map/ppermute | solution.py:677
  215.8 11.0 %copy-start.7 = (bf16[2,48,1664]{2,1,0:T(8,128)(2,1)}, bf16[2,48,1664]{2,1,0:T(8,128)(2,1)S(1)}, u32[]{:S(2)}) copy-start(bf16[2,48,1664]{2,1,0:T(8,128)(2,1)S(1)} %add.56) | copy-start | bytes 958468
  215.8 13.7 %collective-permute-start.21 = (bf16[2,48,1664]{2,1,0:T(8,128)(2,1)S(1)}, bf16[2,48,1664]{2,1,0:T(8,128)(2,1)S(1)}, u32[]{:S(2)}, u32[]{:S(2)}) collective-permute-start(bf16[2,48,1664]{2,1,0:T(8,128)(2,1)S(1)} %add.56), channel_id=1, source_target_pairs={{0,1},{1,0},{2,3},{3,2},{4,5},{5,4},{6,7},{7,6},{8,9},{9,8},{10,11... | collective-permute-start | bytes 958472 | tf_op jit(solution)/shard_map/ppermute | solution.py:677
  217.7 0.7 copy-start.21
  224.0 0.7 copy-start.9
  229.5 0.7 copy-start.20
